TPU v7x, 32 devices: a whole 2x2x4 slice. The times are simulated.
32 devices in a mesh: groups: 2 (over y), seq: 4 (over z), chan: 4 (over x, core).
Axes of the slice: x: 2, y: 2, z: 4, core: 2. Of those that a mesh axis runs over, the one named last changes fastest.
Arguments:
- dna_bases: int32 [4096], P(('groups', 'seq')), parts along dimension 0, may hold values from 0 to 3
- w_stem: bfloat16 [768, 5, 4], P('chan'), may hold values from -2.5 to 2.5
- w_enc: bfloat16 [1536, 5, 768], P(None, None, 'chan'), may hold values from -0.09375 to 0.09375
- w_dec: bfloat16 [768, 5, 1536], P(None, None, 'chan'), may hold values from -0.0625 to 0.0625
- targets: bfloat16 [4096, 768], P(('groups', 'seq'), 'chan'), parts along dimension 0, may hold values from -6 to 6
Outputs:
- pred: bfloat16 [4096, 768], P(('groups', 'seq'), 'chan'), parts along dimension 0
- g_enc: float32 [3072, 5, 768], P(('groups', 'seq'), None, 'chan'), parts along dimension 0
- g_dec: float32 [1536, 5, 1536], P(('groups', 'seq'), None, 'chan'), parts along dimension 0
There are 2 independent parts, one for each index of `groups`. A program takes and returns all parts, laid end to end along the dimension named above; an argument that names none is the same for every part. Nothing has to cross between parts.
Inputs may be any that keep to these rules, and one draw needn't show every extreme that they name: `dna_bases`: each entry is one of the four bases.
All inputs are finite; a program needn't handle non-finite values.
Results may differ from a plain program's by a relative error of at most 0.009.
Values may be sent and summed in bfloat16 or wider, within the bound.
No kernel may reach another device: no remote copies, remote signals or barrier semaphores. Data moves between devices by JAX's collectives and lax.ppermute only.
A program may use at most 192 MiB of HBM per device.

v0:
```python
import math

import jax
import jax.numpy as jnp
from jax import lax
from jax.sharding import PartitionSpec as P

KW = 5


SQRT_TWO_PI = 0.7978845608028654
CUBIC = 0.044715


def extended(block, sides, width):
    for axis, dim in sides:
        count = lax.axis_size(axis)
        forward = [(i, i + 1) for i in range(count - 1)]
        backward = [(target, source) for source, target in forward]
        low = lax.ppermute(
            lax.slice_in_dim(block, block.shape[dim] - width, None, axis=dim), axis, forward
        )
        high = lax.ppermute(lax.slice_in_dim(block, 0, width, axis=dim), axis, backward)
        block = jnp.concatenate([low, block, high], axis=dim)
    return block


def gelu_value(value):
    inner = jnp.tanh(SQRT_TWO_PI * (value + CUBIC * value * value * value))
    return 0.5 * value * (1.0 + inner)


def gelu_slope(value):
    inner = jnp.tanh(SQRT_TWO_PI * (value + CUBIC * value * value * value))
    return 0.5 * (1.0 + inner) + 0.5 * value * (1.0 - inner * inner) * SQRT_TWO_PI * (
        1.0 + 3.0 * CUBIC * value * value
    )


def rim_cells(block, margin):
    return extended(block, (("seq", 0),), margin)


def channel_sum(partial_value):
    return lax.psum_scatter(partial_value, "chan", scatter_dimension=1, tiled=True)


def channel_gather(block):
    return lax.all_gather(block, "chan", axis=1, tiled=True)


def conv_rows(padded, weight):
    row_count = padded.shape[0] - 4
    total = jnp.zeros((row_count, weight.shape[0]), jnp.float32)
    for k in range(KW):
        total = total + lax.dot_general(
            padded[k : k + row_count],
            weight[:, k, :],
            (((1,), (1,)), ((), ())),
            preferred_element_type=jnp.float32,
        )
    return total


def grad_taps(picked, padded):
    row_count = picked.shape[0]
    pieces = [
        lax.dot_general(
            picked,
            padded[k : k + row_count],
            (((0,), (0,)), ((), ())),
            preferred_element_type=jnp.float32,
        )
        for k in range(KW)
    ]
    return jnp.stack(pieces, axis=1)


def weight_grad(cotangent, padded):
    rounded = grad_taps(cotangent, padded).astype(jnp.bfloat16)
    return lax.psum_scatter(
        lax.optimization_barrier(rounded).astype(jnp.float32),
        "seq",
        scatter_dimension=0,
        tiled=True,
    )


def shards(dna_bases, w_stem, w_enc, w_dec, targets):
    row_count = dna_bases.shape[0]
    devices = lax.axis_size("seq")
    length = row_count * devices
    onehot = (dna_bases[:, None] == jnp.arange(4, dtype=jnp.int32)[None, :]).astype(jnp.bfloat16)
    onehot_pad = rim_cells(onehot, 2)
    stem_out = gelu_value(conv_rows(onehot_pad, w_stem)).astype(jnp.bfloat16)
    stem_pad = rim_cells(stem_out, 2)
    enc_pre = channel_sum(conv_rows(stem_pad, w_enc))
    active = gelu_value(enc_pre).astype(jnp.bfloat16).astype(jnp.float32)
    pooled = (0.5 * active.reshape(row_count // 2, 2, -1).sum(axis=1)).astype(jnp.bfloat16)
    pooled_pad = rim_cells(pooled, 1)
    up_pad = jnp.repeat(pooled_pad, 2, axis=0)
    output = channel_sum(conv_rows(up_pad, w_dec)) + stem_out.astype(jnp.float32)
    pred = output.astype(jnp.bfloat16)
    scale = 1.0 / math.sqrt(length)
    slope_out = ((output - targets.astype(jnp.float32)) * scale).astype(jnp.bfloat16)
    slope_all = channel_gather(slope_out)
    g_dec = weight_grad(slope_all, up_pad)
    slope_pad = rim_cells(slope_all, 2)
    up_grad = jnp.zeros((row_count, w_dec.shape[2]), jnp.float32)
    for k in range(KW):
        up_grad = up_grad + jnp.dot(
            slope_pad[4 - k : 4 - k + row_count], w_dec[:, k, :], preferred_element_type=jnp.float32
        )
    pool_grad = up_grad.reshape(row_count // 2, 2, -1).sum(axis=1)
    act_grad = 0.5 * jnp.repeat(pool_grad, 2, axis=0)
    pre_grad = (act_grad * gelu_slope(enc_pre)).astype(jnp.bfloat16)
    pre_all = channel_gather(pre_grad)
    g_enc = weight_grad(pre_all, stem_pad)
    return (pred, g_enc, g_dec)


def solution(mesh):
    return jax.shard_map(
        shards,
        mesh=mesh,
        in_specs=(
            P(("groups", "seq")),
            P("chan", None, None),
            P(None, None, "chan"),
            P(None, None, "chan"),
            P(("groups", "seq"), "chan"),
        ),
        out_specs=(
            P(("groups", "seq"), "chan"),
            P(("groups", "seq"), None, "chan"),
            P(("groups", "seq"), None, "chan"),
        ),
        check_vma=False,
    )
```

profile of v0, /device:TPU:0, one launch (start us, length us, event | category | flops | bytes accessed | tf_op | source)
XLA Modules:
  0.0 406.5 jit_solution(9728655634134982751)
XLA Ops:
  8.1 4.9 %collective-permute-start = (bf16[2,4]{0,1:T(4,128)(2,1)S(1)}, bf16[2,4]{0,1:T(4,128)(2,1)S(1)}, u32[]{:S(2)}, u32[]{:S(2)}) collective-permute-start(bf16[2,4]{0,1:T(4,128)(2,1)S(1)} %get-tuple-element.13), channel_id=1, source_target_pairs={{0,4},{4,8},{8,12},{1,5},{5,9},{9,13},{2,6},{6,10},{10,14},{3,7},{... | collective-permute-start | bytes 56 | tf_op jit(solution)/shard_map/ppermute | solution.py:20
  13.1 1.3 collective-permute-start.1
  14.4 0.9 fusion.91
  15.3 3.2 collective-permute-done.1
  18.5 0.9 fusion.97
  19.5 1.0 fusion.99
  20.4 0.9 fusion.25
  21.4 1.1 fusion.82
  22.5 3.5 collective-permute-start.2
  26.0 1.3 collective-permute-start.3
  28.0 4.1 %collective-permute-done.3 = bf16[2,192]{0,1:T(8,128)(2,1)S(1)} collective-permute-done((bf16[2,192]{0,1:T(8,128)(2,1)S(1)}, bf16[2,192]{0,1:T(8,128)(2,1)S(1)}, u32[]{:S(2)}, u32[]{:S(2)}) %collective-permute-start.3) | collective-permute-done | bytes 800 | tf_op jit(solution)/shard_map/ppermute | solution.py:23
  34.3 2.4 fusion
  36.8 37.3 %reduce-scatter.5.cloned.1.call-done = f32[512,384]{1,0:T(8,128)} async-done(((f32[512,1536]{1,0:T(8,128)}), f32[512,384]{1,0:T(8,128)}) %reduce-scatter.5.cloned.1.call-update) | async-done | bytes 786448 | tf_op jit(solution)/shard_map/reduce_scatter | solution.py:45
  74.0 1.4 fusion.83
  76.9 3.4 collective-permute-start.4
  80.2 1.3 collective-permute-start.5
  81.9 1.8 fusion.47
  83.7 2.0 collective-permute-done.5
  86.0 1.3 reshape.27
  87.3 1.8 fusion.43
  89.1 3.0 fusion.50
  92.9 0.9 broadcast_in_dim.17
  93.8 1.9 slice.192
  95.7 1.9 broadcast_in_dim.14
  97.6 1.9 slice.182
  99.5 1.9 fusion.53
  101.4 3.2 add_add_fusion
  104.7 27.5 %reduce-scatter.7.cloned.1.call-done = f32[512,192]{0,1:T(8,128)} async-done(((f32[512,768]{0,1:T(8,128)}), f32[512,192]{0,1:T(8,128)}) %reduce-scatter.7.cloned.1.call-update) | async-done | bytes 393232 | tf_op jit(solution)/shard_map/reduce_scatter | solution.py:45
  132.2 1.8 multiply_convert_fusion.1
  133.9 8.3 %all_gather.6 = bf16[512,768]{0,1:T(8,128)(2,1)S(1)} all-gather(bf16[512,192]{0,1:T(8,128)(2,1)S(1)} %get-tuple-element.5), channel_id=1, replica_groups=mesh['groups'=2,'seq'=4,'chan'=4] {'chan'}, dimensions={1}, use_global_device_ids=true | all-gather | bytes 983040 | tf_op jit(solution)/shard_map/all_gather | solution.py:49
  142.4 1.7 fusion.45
  144.1 1.3 collective-permute-start.6
  145.4 4.7 %collective-permute-start.7 = (bf16[2,768]{0,1:T(8,128)(2,1)S(1)}, bf16[2,768]{0,1:T(8,128)(2,1)S(1)}, u32[]{:S(2)}, u32[]{:S(2)}) collective-permute-start(bf16[2,768]{0,1:T(8,128)(2,1)S(1)} %get-tuple-element.4), channel_id=1, source_target_pairs={{0,4},{4,8},{8,12},{1,5},{5,9},{9,13},{2,6},{6,10},{10,14},{3,7},{... | collective-permute-start | bytes 9224 | tf_op jit(solution)/shard_map/ppermute | solution.py:20
  150.2 2.9 collective-permute-done.6
  153.2 1.0 fusion.37
  154.2 1.0 fusion.13
  155.2 1.0 fusion.35
  156.1 1.9 fusion.12
  158.0 1.7 reshape.28
  161.0 1.4 mul.116
  162.4 2.4 fusion.34
  168.1 2.9 convert_element_type.46
  171.2 14.0 %all-gather.2.cloned.1.call-done = bf16[512,1536]{1,0:T(8,128)(2,1)} async-done(((bf16[512,384]{1,0:T(8,128)(2,1)}), bf16[512,1536]{1,0:T(8,128)(2,1)}) %all-gather.2.cloned.1.call-update) | async-done | bytes 1572880 | tf_op jit(solution)/shard_map/all_gather | solution.py:49
  185.1 2.1 fusion.3
  187.2 1.9 fusion.5
  190.7 3.4 convert_element_type.45
  194.1 98.1 %reduce-scatter.11.cloned.1.call-done = f32[192,5,384]{2,0,1:T(8,128)} async-done(((f32[768,5,384]{2,0,1:T(8,128)}), f32[192,5,384]{2,0,1:T(8,128)}) %reduce-scatter.11.cloned.1.call-update) | async-done | bytes 1474576 | tf_op jit(solution)/shard_map/reduce_scatter | solution.py:81
  292.3 107.7 %reduce-scatter.9.cloned.1.call-done = f32[384,5,192]{0,2,1:T(8,128)} async-done(((f32[1536,5,192]{0,2,1:T(8,128)}), f32[384,5,192]{0,2,1:T(8,128)}) %reduce-scatter.9.cloned.1.call-update) | async-done | bytes 1474576 | tf_op jit(solution)/shard_map/reduce_scatter | solution.py:81
  (74 shorter events, 13.2 us)
Async XLA Ops:
  7.2 20.2 %copy-start.5 = (bf16[1536,5,192]{0,2,1:T(8,128)(2,1)S(1)}, bf16[1536,5,192]{0,2,1:T(8,128)(2,1)}, u32[]{:S(2)}) copy-start(bf16[1536,5,192]{0,2,1:T(8,128)(2,1)} %param.7) | copy-start | bytes 8847364
  7.2 66.9 %reduce-scatter.5.cloned.1.call-start = ((), (), s32[]{:S(2)}) async-start(), calls=%async_computation.4 | async-start | bytes 3932160 | tf_op jit(solution)/shard_map/reduce_scatter | solution.py:45
  8.1 11.3 %collective-permute-start = (bf16[2,4]{0,1:T(4,128)(2,1)S(1)}, bf16[2,4]{0,1:T(4,128)(2,1)S(1)}, u32[]{:S(2)}, u32[]{:S(2)}) collective-permute-start(bf16[2,4]{0,1:T(4,128)(2,1)S(1)} %get-tuple-element.13), channel_id=1, source_target_pairs={{0,4},{4,8},{8,12},{1,5},{5,9},{9,13},{2,6},{6,10},{10,14},{3,7},{... | collective-permute-start | bytes 56 | tf_op jit(solution)/shard_map/ppermute | solution.py:20
  13.1 5.5 %collective-permute-start.1 = (bf16[2,4]{0,1:T(4,128)(2,1)S(1)}, bf16[2,4]{0,1:T(4,128)(2,1)S(1)}, u32[]{:S(2)}, u32[]{:S(2)}) collective-permute-start(bf16[2,4]{0,1:T(4,128)(2,1)S(1)} %get-tuple-element.14), channel_id=1, source_target_pairs={{4,0},{8,4},{12,8},{5,1},{9,5},{13,9},{6,2},{10,6},{14,10},{7,3},{... | collective-permute-start | bytes 56 | tf_op jit(solution)/shard_map/ppermute | solution.py:23
  22.5 10.2 %collective-permute-start.2 = (bf16[2,192]{0,1:T(8,128)(2,1)S(1)}, bf16[2,192]{0,1:T(8,128)(2,1)S(1)}, u32[]{:S(2)}, u32[]{:S(2)}) collective-permute-start(bf16[2,192]{0,1:T(8,128)(2,1)S(1)} %get-tuple-element.11), channel_id=1, source_target_pairs={{0,4},{4,8},{8,12},{1,5},{5,9},{9,13},{2,6},{6,10},{10,14},{3,7},{... | collective-permute-start | bytes 2312 | tf_op jit(solution)/shard_map/ppermute | solution.py:20
  26.0 6.0 %collective-permute-start.3 = (bf16[2,192]{0,1:T(8,128)(2,1)S(1)}, bf16[2,192]{0,1:T(8,128)(2,1)S(1)}, u32[]{:S(2)}, u32[]{:S(2)}) collective-permute-start(bf16[2,192]{0,1:T(8,128)(2,1)S(1)} %get-tuple-element.12), channel_id=1, source_target_pairs={{4,0},{8,4},{12,8},{5,1},{9,5},{13,9},{6,2},{10,6},{14,10},{7,3},{... | collective-permute-start | bytes 2312 | tf_op jit(solution)/shard_map/ppermute | solution.py:23
  32.0 2.3 copy-start.10
  32.8 1.5 copy-start.12
  36.7 95.5 %reduce-scatter.7.cloned.1.call-start = ((), (), s32[]{:S(2)}) async-start(), calls=%async_computation.5 | async-start | bytes 1966080 | tf_op jit(solution)/shard_map/reduce_scatter | solution.py:45
  76.9 6.9 %collective-permute-start.4 = (bf16[1,384]{1,0:T(2,128)(2,1)S(1)}, bf16[1,384]{1,0:T(2,128)(2,1)S(1)}, u32[]{:S(2)}, u32[]{:S(2)}) collective-permute-start(bf16[1,384]{1,0:T(2,128)(2,1)S(1)} %get-tuple-element.9), channel_id=1, source_target_pairs={{0,4},{4,8},{8,12},{1,5},{5,9},{9,13},{2,6},{6,10},{10,14},{3,7},{... | collective-permute-start | bytes 2312 | tf_op jit(solution)/shard_map/ppermute | solution.py:20
  80.2 5.5 %collective-permute-start.5 = (bf16[1,384]{1,0:T(2,128)(2,1)S(1)}, bf16[1,384]{1,0:T(2,128)(2,1)S(1)}, u32[]{:S(2)}, u32[]{:S(2)}) collective-permute-start(bf16[1,384]{1,0:T(2,128)(2,1)S(1)} %get-tuple-element.10), channel_id=1, source_target_pairs={{4,0},{8,4},{12,8},{5,1},{9,5},{13,9},{6,2},{10,6},{14,10},{7,3},{... | collective-permute-start | bytes 2312 | tf_op jit(solution)/shard_map/ppermute | solution.py:23
  81.9 3.8 copy-start.7
  99.5 1.9 copy-start.1
  101.4 30.7 %copy-start.14 = (bf16[512,192]{0,1:T(8,128)(2,1)S(1)}, bf16[512,192]{0,1:T(8,128)(2,1)}, u32[]{:S(2)}) copy-start(bf16[512,192]{0,1:T(8,128)(2,1)} %param.9) | copy-start | bytes 589828
  104.6 80.5 %all-gather.2.cloned.1.call-start = ((), (), s32[]{:S(2)}) async-start(), calls=%async_computation.6 | async-start | bytes 1966080 | tf_op jit(solution)/shard_map/all_gather | solution.py:49
  133.9 19.2 %copy-start.2 = (bf16[768,5,384]{2,0,1:T(8,128)(2,1)S(1)}, bf16[768,5,384]{2,0,1:T(8,128)(2,1)}, u32[]{:S(2)}) copy-start(bf16[768,5,384]{2,0,1:T(8,128)(2,1)} %param.8) | copy-start | bytes 8847364
  144.1 9.1 %collective-permute-start.6 = (bf16[2,768]{0,1:T(8,128)(2,1)S(1)}, bf16[2,768]{0,1:T(8,128)(2,1)S(1)}, u32[]{:S(2)}, u32[]{:S(2)}) collective-permute-start(bf16[2,768]{0,1:T(8,128)(2,1)S(1)} %get-tuple-element.3), channel_id=1, source_target_pairs={{4,0},{8,4},{12,8},{5,1},{9,5},{13,9},{6,2},{10,6},{14,10},{7,3},{... | collective-permute-start | bytes 9224 | tf_op jit(solution)/shard_map/ppermute | solution.py:23
  145.4 9.7 %collective-permute-start.7 = (bf16[2,768]{0,1:T(8,128)(2,1)S(1)}, bf16[2,768]{0,1:T(8,128)(2,1)S(1)}, u32[]{:S(2)}, u32[]{:S(2)}) collective-permute-start(bf16[2,768]{0,1:T(8,128)(2,1)S(1)} %get-tuple-element.4), channel_id=1, source_target_pairs={{0,4},{4,8},{8,12},{1,5},{5,9},{9,13},{2,6},{6,10},{10,14},{3,7},{... | collective-permute-start | bytes 9224 | tf_op jit(solution)/shard_map/ppermute | solution.py:20
  158.0 4.4 %copy-start.4 = (f32[512,384]{1,0:T(8,128)S(1)}, f32[512,384]{1,0:T(8,128)}, u32[]{:S(2)}) copy-start(f32[512,384]{1,0:T(8,128)} %reduce-scatter.5.cloned.1.call-done) | copy-start | bytes 2359300
  160.6 4.2 %copy-start.9 = (bf16[512,384]{1,0:T(8,128)(2,1)S(1)}, bf16[512,384]{1,0:T(8,128)(2,1)}, u32[]{:S(2)}) copy-start(bf16[512,384]{1,0:T(8,128)(2,1)} %slice.182) | copy-start | bytes 1179652
  160.9 4.5 %copy-start.3 = (bf16[516,384]{1,0:T(8,128)(2,1)S(1)}, bf16[516,384]{1,0:T(8,128)(2,1)}, u32[]{:S(2)}) copy-start(bf16[516,384]{1,0:T(8,128)(2,1)} %reshape.27) | copy-start | bytes 1188868
  164.8 1.4 copy-start.8
  164.8 127.5 %reduce-scatter.11.cloned.1.call-start = ((), (), s32[]{:S(2)}) async-start(), calls=%async_computation.8 | async-start | bytes 7372800 | tf_op jit(solution)/shard_map/reduce_scatter | solution.py:81
  166.1 1.3 copy-start.6
  171.1 14.1 %copy-start.13 = (bf16[2,192]{0,1:T(8,128)(2,1)S(1)}, bf16[2,192]{0,1:T(8,128)(2,1)}, u32[]{:S(2)}) copy-start(bf16[2,192]{0,1:T(8,128)(2,1)} %copy-done.12) | copy-start | bytes 2308
  171.1 228.9 %reduce-scatter.9.cloned.1.call-start = ((), (), s32[]{:S(2)}) async-start(), calls=%async_computation.7 | async-start | bytes 7372800 | tf_op jit(solution)/shard_map/reduce_scatter | solution.py:81
  185.1 4.0 copy-start
  187.2 2.5 copy-start.11
Sparse Core Ops, SparseCore 0:
  36.8 37.1 reduce-scatter.4
  104.7 27.3 reduce-scatter.6
  164.9 20.1 all-gather.1
  187.9 104.3 reduce-scatter.10
  295.0 104.8 reduce-scatter.8
where the time goes:
time: 407 us; the launch traced here: 406 us
  waiting for transfers between devices  297 us (73%)
  matrix products  36.9 us (9%)
  starting transfers between devices  21.9 us (5%)
  other arithmetic  15.4 us (4%)
  between operations  14.3 us (4%)
  local copies, waits for them, and re-layouts  12.8 us (3%)
  blocking collectives  8.34 us (2%)
    reduce_scatter x2, waiting for transfers between devices, weight_grad(): lax.psum_scatter(lax.optimization_barrier(rounded).astype(jnp.float32), '...  206 us
    reduce_scatter x2, waiting for transfers between devices, channel_sum(): lax.psum_scatter(partial_value, 'chan', scatter_dimension=1, tiled=True)  64.8 us
    dot_general x15, matrix products, conv_rows(): lax.dot_general(padded[k:k + row_count], weight[:, k, :], (((1,), (1,)),...  21.7 us
    ppermute x4, starting transfers between devices, extended(): lax.ppermute(lax.slice_in_dim(block, block.shape[dim] - width, None, axis...  16.5 us
    all_gather x1, waiting for transfers between devices, channel_gather(): return lax.all_gather(block, 'chan', axis=1, tiled=True)  14 us
    ppermute x4, waiting for transfers between devices, extended(): lax.ppermute(lax.slice_in_dim(block, 0, width, axis=dim), axis, backward)  12.2 us
    dot_general x10, matrix products, grad_taps(): lax.dot_general(picked, padded[k:k + row_count], (((0,), (0,)), ((), ()))...  8.74 us
    all_gather x1, blocking collectives, channel_gather(): return lax.all_gather(block, 'chan', axis=1, tiled=True)  8.34 us
  transfers between devices with their start and end apart: 13, of which 9 were waited for; matrix products, arithmetic and copies ran while one was open for 6% of the time, Pallas kernels for 0%

commit v1 on v0

v1 whole, which is shorter than its diff:
```python
import functools
import math

import jax
import jax.numpy as jnp
from jax import lax
from jax.experimental import pallas as pl
from jax.experimental.pallas import tpu as pltpu
from jax.sharding import PartitionSpec as P

KW = 5

SQRT_TWO_PI = 0.7978845608028654
CUBIC = 0.044715

SIDE = 64
OUTER = 16
INNER = 8
F32 = jnp.float32
BF16 = jnp.bfloat16
MIB = 1024 * 1024


def gelu_value(value):
    inner = jnp.tanh(SQRT_TWO_PI * (value + CUBIC * value * value * value))
    return 0.5 * value * (1.0 + inner)


def gelu_both(value):
    square = value * value
    inner = jnp.tanh(SQRT_TWO_PI * (value + CUBIC * square * value))
    slope = 0.5 * (1.0 + inner) + 0.5 * value * (1.0 - inner * inner) * SQRT_TWO_PI * (
        1.0 + 3.0 * CUBIC * square
    )
    return 0.5 * value * (1.0 + inner), slope


def dot(a, b, contract):
    return lax.dot_general(a, b, (contract, ((), ())), preferred_element_type=F32)


def tap_onehots(bases, start, width):
    total = bases.shape[1]
    before = pltpu.roll(bases, total - (start - 1), 1)[:, :width]
    here = pltpu.roll(bases, total - start, 1)[:, :width]
    after = pltpu.roll(bases, total - (start + 1), 1)[:, :width]
    taps = [before[0:1], before[1:2], here[0:1], here[1:2], after[0:1], after[1:2]]
    row = lax.broadcasted_iota(jnp.int32, (4 * KW, width), 0)
    tap, base = row >> 2, row & 3
    out = []
    for first in (0, 1):
        value = jnp.full((4 * KW, width), -1, jnp.int32)
        for k in range(KW):
            value = jnp.where(tap == k, jnp.broadcast_to(taps[first + k], value.shape), value)
        out.append(jnp.where(value == base, 1.0, 0.0).astype(BF16))
    return out


def valid_pairs(shape, dim, first, total):
    pair = lax.broadcasted_iota(jnp.int32, shape, dim) + first
    return (pair >= 0) & (pair < total)


def enc_kernel(place, bases, stem_w, w_own, w_oth, keep, send, stem_out, even, odd, lhs, *, pairs, total):
    seq, hi, lo = place[0], place[1], place[2]
    rows = pairs + 2 * INNER
    wide = pairs + 2 * OUTER
    block = keep.shape[1]
    hots = tap_onehots(bases[...], SIDE - OUTER, wide)
    for q in range(2):
        for hot, held in zip(hots, (even, odd)):
            raw = dot(hot, stem_w[q], ((0,), (0,)))
            ok = valid_pairs(raw.shape, 0, seq * pairs - OUTER, total)
            held[...] = jnp.where(ok, gelu_value(raw), 0.0).astype(BF16).astype(F32)
        gap = OUTER - INNER
        for k in range(6):
            source = even if k % 2 == 0 else odd
            lhs[q, k] = source[gap + k // 2 - 1 : gap + k // 2 - 1 + rows, :].astype(BF16)
        if q == 0:
            stem_out[0] = lhs[0, 2]
            stem_out[1] = lhs[0, 3]
    for part in range(2):
        own_at = pl.multiple_of((2 * (hi if part == 0 else 1 - hi) + lo) * block, 128)
        oth_at = pl.multiple_of((hi if part == 0 else 1 - hi) * block, 128)
        acc = jnp.zeros((2 * rows, block), F32)
        for k in range(KW):
            acc = acc + dot(
                lhs[0, k : k + 2].reshape(2 * rows, -1), w_own[k, :, pl.ds(own_at, block)], ((1,), (0,))
            )
            acc = acc + dot(
                lhs[1, k : k + 2].reshape(2 * rows, -1), w_oth[k, :, pl.ds(oth_at, block)], ((1,), (0,))
            )
        if part == 0:
            keep[...] = acc
        else:
            send[...] = acc.astype(BF16)


def pool_kernel(place, keep, came, pooled, centre, slope, *, pairs, total):
    rows = pairs + 2 * INNER
    value = keep[...] + came[...].astype(F32)
    active, grad = gelu_both(value)
    active = active.astype(BF16).astype(F32)
    both = 0.5 * (active[:rows] + active[rows:])
    ok = valid_pairs(both.shape, 0, place[0] * pairs - INNER, total)
    both = jnp.where(ok, both, 0.0).astype(BF16)
    pooled[...] = both
    centre[...] = both[INNER : INNER + pairs].astype(BF16)
    grad = 0.5 * grad
    slope[0] = grad[INNER : INNER + pairs]
    slope[1] = grad[rows + INNER : rows + INNER + pairs]


def dec_kernel(own, oth, w_own, w_oth, stem, targets, part, send, held, *, pairs):
    rows = pairs + 2 * INNER
    held[:8] = jnp.zeros((8, held.shape[1]), F32)
    held[8 + rows :] = jnp.zeros((8, held.shape[1]), F32)
    acc = jnp.zeros(part.shape, F32)
    for source, weight in ((own, w_own), (oth, w_oth)):
        held[8 : 8 + rows] = source[...].astype(F32)
        for k in range(3):
            acc = acc + dot(held[7 + k : 7 + k + rows].astype(BF16), weight[k], ((1,), (1,)))
    half = part.shape[1] // 2
    for parity in range(2):
        value = acc[:, parity * half : (parity + 1) * half]
        value = value + stem[parity].astype(F32) - targets[parity].astype(F32)
        part[:, parity * half : (parity + 1) * half] = value
        send[:, parity * half : (parity + 1) * half] = value.astype(BF16)


def slope_kernel(place, part, came, targets, pred, sums, held, *, pairs, total, scale):
    rows = pairs + 2 * INNER
    half = part.shape[1] // 2
    ok = valid_pairs((rows, half), 0, place[0] * pairs - INNER, total)
    slopes = []
    for parity in range(2):
        cols = slice(parity * half, (parity + 1) * half)
        value = part[:, cols] + came[:, cols].astype(F32)
        out = value + targets[parity].astype(F32)
        pred[parity] = out[INNER : INNER + pairs].astype(BF16)
        slopes.append(jnp.where(ok, value * scale, 0.0).astype(BF16).astype(F32))
    held[:rows] = slopes[0]
    held[rows:] = jnp.zeros((8, half), F32)
    sums[0] = (slopes[0] + slopes[1]).astype(BF16)
    sums[1] = (slopes[1] + held[1 : 1 + rows]).astype(BF16)


def shifted_sums(held, pairs):
    return [
        held[0, INNER + 1 : INNER + 1 + pairs].astype(BF16),
        held[1, INNER : INNER + pairs].astype(BF16),
        held[0, INNER : INNER + pairs].astype(BF16),
        held[1, INNER - 1 : INNER - 1 + pairs].astype(BF16),
        held[0, INNER - 1 : INNER - 1 + pairs].astype(BF16),
    ]


def back_kernel(own, oth, w_own, w_oth, slope, out, held, *, pairs):
    acc = jnp.zeros((pairs, out.shape[2]), F32)
    for source, weight in ((own, w_own), (oth, w_oth)):
        held[...] = source[...].astype(F32)
        for k, tap in enumerate(shifted_sums(held, pairs)):
            acc = acc + dot(tap, weight[k], ((1,), (0,)))
    out[0] = (acc * slope[0]).astype(BF16)
    out[1] = (acc * slope[1]).astype(BF16)


def taps_kernel(place, bases, stem_w, out, *, pairs, total, devices):
    block = lax.rem(place[0] - pl.program_id(0) + devices, devices)
    hots = tap_onehots(bases[0], SIDE, bases.shape[2])
    channels = stem_w.shape[0]
    parts = []
    for hot in hots:
        raw = dot(stem_w[...], hot, ((1,), (0,)))
        width = raw.shape[1]
        col = lax.broadcasted_iota(jnp.int32, raw.shape, 1)
        pair = jnp.where(col >= width - SIDE, col - width, col) + block * pairs
        ok = (pair >= 0) & (pair < total)
        parts.append(jnp.where(ok, gelu_value(raw), 0.0))
    width = parts[0].shape[1]
    taps = []
    for step in (-1, 0, 1):
        for held in parts:
            moved = held if step == 0 else pltpu.roll(held, (-step) % width, 1)
            taps.append(moved[:, :pairs].astype(BF16))
    for k in range(KW):
        out[0, k * channels : (k + 1) * channels, :pairs] = taps[k]
        out[0, k * channels : (k + 1) * channels, pairs:] = taps[k + 1]


def dec_grad_kernel(sums, pooled, out, held, *, pairs):
    held[...] = sums[0].astype(F32)

    @pl.when(pl.program_id(0) == 0)
    def _():
        out[...] = jnp.zeros(out.shape, F32)

    for k, tap in enumerate(shifted_sums(held, pairs)):
        out[k] += dot(tap, pooled[0], ((0,), (0,)))


def enc_grad_kernel(place, taps, own, oth, out, *, slots):
    step = pl.program_id(0)

    @pl.when(step == 0)
    def _():
        out[...] = jnp.zeros(out.shape, F32)

    @pl.when(step < slots)
    def _():
        out[...] += dot(taps[0], own[0], ((1,), (0,)))

    @pl.when(step >= slots)
    def _():
        out[...] += dot(taps[0], oth[0], ((1,), (0,)))


def whole(shape):
    return pl.BlockSpec(shape, lambda *_: (0,) * len(shape))


SCALARS = pl.BlockSpec(memory_space=pltpu.SMEM)


def call(kernel, ins, outs, scratch=(), limit=48, flops=0, name=None):
    specs = [SCALARS if i.dtype == jnp.int32 and i.ndim == 1 else whole(i.shape) for i in ins]
    size = sum(i.size * i.dtype.itemsize for i in ins) + sum(
        math.prod(s) * jnp.dtype(d).itemsize for s, d in outs
    )
    return pl.pallas_call(
        kernel,
        in_specs=specs,
        out_specs=[whole(s) for s, _ in outs],
        out_shape=[jax.ShapeDtypeStruct(s, d) for s, d in outs],
        scratch_shapes=[pltpu.VMEM(s, d) for s, d in scratch],
        compiler_params=pltpu.CompilerParams(vmem_limit_bytes=limit * MIB),
        cost_estimate=pl.CostEstimate(flops=flops, bytes_accessed=size, transcendentals=0),
        name=name,
    )(*ins)


def fast_shards(dna_bases, w_stem, w_enc, w_dec, targets):
    devices = lax.axis_size("seq")
    seq, chan = lax.axis_index("seq"), lax.axis_index("chan")
    hi, lo = chan // 2, chan % 2
    place = jnp.stack([seq, hi, lo]).astype(jnp.int32)
    pairs = dna_bases.shape[0] // 2
    total = pairs * devices
    rows = pairs + 2 * INNER
    stem_c = w_stem.shape[0]
    enc_c = w_dec.shape[2]
    across = [(c, c ^ 2) for c in range(4)]
    cores = [(c, c ^ 1) for c in range(4)]

    def ring(array, step):
        return lax.ppermute(array, "seq", [(i, (i + step) % devices) for i in range(devices)])

    enc_w = w_enc.transpose(1, 2, 0)
    dec_w = w_dec.transpose(1, 0, 2).reshape(KW, 2, 2, stem_c, enc_c)

    def pick(array, axis, index):
        return lax.dynamic_index_in_dim(array, index, axis, keepdims=False)

    stem_w = w_stem.transpose(1, 2, 0).reshape(4 * KW, stem_c)
    stem_oth = lax.ppermute(stem_w, "chan", cores)
    enc_send = pick(enc_w.reshape(KW, stem_c, 2, 2, enc_c), 3, 1 - lo).reshape(KW, stem_c, 2 * enc_c)
    enc_oth = lax.ppermute(enc_send, "chan", cores)

    own = dna_bases.reshape(pairs, 2).T
    blocks = [own] + [ring(own, r) for r in range(1, devices)]

    def bases_of(r):
        joined = jnp.concatenate(
            [blocks[(r + 1) % devices][:, pairs - SIDE :], blocks[r], blocks[(r - 1) % devices][:, :SIDE]], axis=1
        )
        first = lax.rem(seq - r + devices, devices) * pairs - SIDE
        pair = first + jnp.arange(pairs + 2 * SIDE, dtype=jnp.int32)[None, :]
        return jnp.where((pair >= 0) & (pair < total), joined, -1)

    keep, send, stem = call(
        functools.partial(enc_kernel, pairs=pairs, total=total),
        [place, bases_of(0), jnp.stack([stem_w, stem_oth]), enc_w, enc_oth],
        [((2 * rows, enc_c), F32), ((2 * rows, enc_c), BF16), ((2, rows, stem_c), BF16)],
        [
            ((pairs + 2 * OUTER, stem_c), F32),
            ((pairs + 2 * OUTER, stem_c), F32),
            ((2, 6, rows, stem_c), BF16),
        ],
        flops=4 * rows * 2 * stem_c * KW * 2 * enc_c,
        name="enc_conv",
    )
    came = lax.ppermute(send, "chan", across)

    dec_w, targets_in, bases_in, _ = lax.optimization_barrier((dec_w, targets, blocks, send))
    dec_own = pick(dec_w, 2, lo).reshape(KW, 2 * stem_c, enc_c)
    dec_oth = pick(dec_w, 2, 1 - lo).reshape(KW, 2 * stem_c, enc_c)
    dec_came = lax.ppermute(dec_oth, "chan", cores)

    def combined(w):
        even = jnp.stack([w[0] + w[1], w[2] + w[3], w[4]])
        odd = jnp.stack([w[0], w[1] + w[2], w[3] + w[4]])
        return jnp.concatenate([even, odd], axis=1)

    comb_own, comb_came = combined(dec_own), combined(dec_came)
    split = targets_in.reshape(pairs, 2, stem_c).transpose(1, 0, 2)
    split = jnp.concatenate(
        [ring(split[:, pairs - INNER :], 1), split, ring(split[:, :INNER], devices - 1)], axis=1
    )

    def placed(array):
        blank = jnp.zeros_like(array)
        return jnp.where(
            hi == 0, jnp.concatenate([array, blank], axis=2), jnp.concatenate([blank, array], axis=2)
        )

    targets_at, stem_at = placed(split), placed(stem)
    blocks = bases_in
    bases_all = jnp.stack([bases_of(r) for r in range(devices)])
    taps = pl.pallas_call(
        functools.partial(taps_kernel, pairs=pairs, total=total, devices=devices),
        grid=(devices,),
        in_specs=[
            SCALARS,
            pl.BlockSpec((1, 2, pairs + 2 * SIDE), lambda r: (r, 0, 0)),
            whole((stem_c, 4 * KW)),
        ],
        out_specs=pl.BlockSpec((1, KW * stem_c, 2 * pairs), lambda r: (r, 0, 0)),
        out_shape=jax.ShapeDtypeStruct((devices, KW * stem_c, 2 * pairs), BF16),
        compiler_params=pltpu.CompilerParams(vmem_limit_bytes=24 * MIB),
        name="stem_taps",
    )(place, bases_all, stem_w.T)

    pooled, centre, slope = call(
        functools.partial(pool_kernel, pairs=pairs, total=total),
        [place, keep, came],
        [((rows, enc_c), BF16), ((pairs, enc_c), BF16), ((2, pairs, enc_c), F32)],
        name="gelu_pool",
    )
    pooled_oth = lax.ppermute(pooled, "chan", cores)
    part, send = call(
        functools.partial(dec_kernel, pairs=pairs),
        [pooled, pooled_oth, comb_own, comb_came, stem_at, targets_at],
        [((rows, 4 * stem_c), F32), ((rows, 4 * stem_c), BF16)],
        [((rows + 16, enc_c), F32)],
        flops=2 * rows * 2 * enc_c * 3 * 4 * stem_c,
        name="dec_conv",
    )
    came = lax.ppermute(send, "chan", across)
    centre, _ = lax.optimization_barrier((centre, send))
    pooled_all = jnp.stack([centre] + [ring(centre, r) for r in range(1, devices)])

    pred, sums = call(
        functools.partial(slope_kernel, pairs=pairs, total=total, scale=1.0 / math.sqrt(2 * total)),
        [place, part, came, targets_at],
        [((2, pairs, 2 * stem_c), BF16), ((2, rows, 2 * stem_c), BF16)],
        [((rows + 8, 2 * stem_c), F32)],
        name="out_slope",
    )
    sums_oth = lax.ppermute(sums, "chan", cores)
    (pre,) = call(
        functools.partial(back_kernel, pairs=pairs),
        [sums, sums_oth, dec_own, dec_oth, slope],
        [((2, pairs, enc_c), BF16)],
        [((2, rows, 2 * stem_c), F32)],
        flops=2 * pairs * KW * 4 * stem_c * enc_c,
        name="up_grad",
    )
    pred = pick(pred.reshape(2, pairs, 2, stem_c), 2, hi)
    pred = pred.transpose(1, 0, 2).reshape(2 * pairs, stem_c)

    per_chan = devices // 4
    width = 4 * enc_c // devices

    def chan_of(block):
        return block // per_chan

    other = lax.ppermute(pre.reshape(2 * pairs, enc_c), "chan", across)
    pieces = jnp.stack([pre.reshape(2 * pairs, enc_c), other])
    mine = lax.rem(chan_of(seq), 2) == lo

    def piece(step):
        target = lax.rem(seq + step, devices)
        column = chan_of(target)
        block = pick(pieces, 0, (column // 2 != hi).astype(jnp.int32))
        return lax.dynamic_slice_in_dim(block, lax.rem(target, per_chan) * width, width, axis=1)

    def link(step):
        out = []
        for s in range(devices):
            t = (s + step) % devices
            for x in range(2):
                out.append((s * 4 + 2 * x + chan_of(t) % 2, t * 4 + 2 * x + (chan_of(t) + step) % 2))
        return out

    arrived = [piece(0)] + [
        lax.ppermute(piece(r), ("seq", "chan"), link(r)) for r in range(1, devices)
    ]
    held = jnp.stack(
        [jnp.where(mine, arrived[2 * i], arrived[2 * i + 1]) for i in range(devices // 2)]
    )
    held_oth = lax.ppermute(held, "chan", cores)
    slots = devices // 2
    parity = jnp.where(mine, 0, 1).astype(jnp.int32).reshape(1)

    def taps_at(i, p):
        first = i < slots
        return (jnp.where(first, 2 * i + p[0], 2 * (i - slots) + 1 - p[0]), 0, 0)

    g_enc = pl.pallas_call(
        functools.partial(enc_grad_kernel, slots=slots),
        grid_spec=pltpu.PrefetchScalarGridSpec(
            num_scalar_prefetch=1,
            grid=(devices,),
            in_specs=[
                pl.BlockSpec((1, KW * stem_c, 2 * pairs), taps_at),
                pl.BlockSpec((1, 2 * pairs, width), lambda i, p: (jnp.minimum(i, slots - 1), 0, 0)),
                pl.BlockSpec((1, 2 * pairs, width), lambda i, p: (jnp.maximum(i - slots, 0), 0, 0)),
            ],
            out_specs=pl.BlockSpec((KW * stem_c, width), lambda i, p: (0, 0)),
        ),
        out_shape=jax.ShapeDtypeStruct((KW * stem_c, width), F32),
        compiler_params=pltpu.CompilerParams(vmem_limit_bytes=32 * MIB),
        name="enc_grad",
    )(parity, taps, held, held_oth)
    g_enc = g_enc.reshape(KW, stem_c, width).transpose(2, 0, 1)

    natural = jnp.where(lo == 0, jnp.stack([sums, sums_oth]), jnp.stack([sums_oth, sums]))
    natural = natural.reshape(2, 2, rows, 2, stem_c).transpose(1, 2, 3, 0, 4).reshape(2, rows, 4 * stem_c)
    narrow = 4 * stem_c // devices
    half = pick(natural, 0, lo)

    def sums_for(array, step):
        return lax.dynamic_slice_in_dim(array, lax.rem(seq + step, devices) * narrow, narrow, axis=array.ndim - 1)

    half_all = jnp.stack([sums_for(half, 0)] + [ring(sums_for(half, r), r) for r in range(1, devices)])
    half_oth = lax.ppermute(half_all, "chan", cores)
    sums_all = jnp.where(
        lo == 0, jnp.stack([half_all, half_oth], axis=1), jnp.stack([half_oth, half_all], axis=1)
    )
    g_dec = pl.pallas_call(
        functools.partial(dec_grad_kernel, pairs=pairs),
        grid=(devices,),
        in_specs=[
            pl.BlockSpec((1, 2, rows, narrow), lambda r: (r, 0, 0, 0)),
            pl.BlockSpec((1, pairs, enc_c), lambda r: (r, 0, 0)),
        ],
        out_specs=pl.BlockSpec((KW, narrow, enc_c), lambda r: (0, 0, 0)),
        out_shape=jax.ShapeDtypeStruct((KW, narrow, enc_c), F32),
        scratch_shapes=[pltpu.VMEM((2, rows, narrow), F32)],
        compiler_params=pltpu.CompilerParams(vmem_limit_bytes=32 * MIB),
        name="dec_grad",
    )(sums_all, pooled_all)
    g_dec = g_dec.transpose(1, 0, 2)
    return (pred, g_enc, g_dec)


def solution(mesh):
    return jax.shard_map(
        fast_shards,
        mesh=mesh,
        in_specs=(
            P(("groups", "seq")),
            P("chan", None, None),
            P(None, None, "chan"),
            P(None, None, "chan"),
            P(("groups", "seq"), "chan"),
        ),
        out_specs=(
            P(("groups", "seq"), "chan"),
            P(("groups", "seq"), None, "chan"),
            P(("groups", "seq"), None, "chan"),
        ),
        check_vma=False,
    )
```

time: 407 us -> 146 us (0.36)
  waiting for transfers between devices: 297 us -> 40.7 us
  matrix products: 36.9 us -> 0 us
  local copies, waits for them, and re-layouts: 12.8 us -> 41 us
  Pallas kernels: 0 us -> 22.5 us
  between operations: 14.3 us -> 1.29 us
  blocking collectives: 8.34 us -> 0 us
    reduce_scatter x4 -> x0, waiting for transfers between devices: 271 us -> none  [the longest x2 206 us: weight_grad(): lax.psum_scatter(lax.optimization_barrier(rounded).astype(jnp.float32), '...]
    dot_general x30 -> x0, matrix products: 36.9 us -> none  [the longest x15 21.7 us: conv_rows(): lax.dot_general(padded[k:k + row_count], weight[:, k, :], (((1,), (1,)),...]
    ppermute x8 -> x24, waiting for transfers between devices: 12.2 us -> 40.7 us  [the longest x11 15.3 us: ring(): lax.ppermute(array, 'seq', [(i, (i + step) % devices) for i in range(devi...]
    pallas_call x0 -> x8, Pallas kernels: none -> 22.5 us  [the longest x5 11 us: call(): pl.pallas_call(kernel, in_specs=specs, out_specs=[whole(s) for s, _ in ou...]
    all_gather x1 -> x0, waiting for transfers between devices: 14 us -> none  [channel_gather(): return lax.all_gather(block, 'chan', axis=1, tiled=True)]
    reshape x3 -> x10, local copies, waits for them, and re-layouts: 3.46 us -> 17.3 us  [the longest x1 5.9 us: fast_shards(): enc_w.reshape(KW, stem_c, 2, 2, enc_c)]
    dynamic_slice x0 -> x3, local copies, waits for them, and re-layouts: none -> 12.5 us  [the longest x2 12.2 us: pick(): return lax.dynamic_index_in_dim(array, index, axis, keepdims=False)]
    convert_element_type x6 -> x0, other arithmetic: 11.4 us -> none  [the longest x2 6.34 us: weight_grad(): lax.optimization_barrier(rounded).astype(jnp.float32)]
  transfers between devices with their start and end apart: 13 -> 24, of which waited for: 9 -> 11; matrix products, arithmetic and copies ran while one was open for 6% -> 22% of each run, Pallas kernels for 0% -> 9%
where the time goes in v1:
time: 146 us; the launch traced here: 145 us
  local copies, waits for them, and re-layouts  41 us (28%)
  waiting for transfers between devices  40.7 us (28%)
  Pallas kernels  22.5 us (15%)
  starting transfers between devices  21.8 us (15%)
  other arithmetic  17.5 us (12%)
    ppermute x11, waiting for transfers between devices, ring(): lax.ppermute(array, 'seq', [(i, (i + step) % devices) for i in range(devi...  15.3 us
    dynamic_slice x2, local copies, waits for them, and re-layouts, pick(): return lax.dynamic_index_in_dim(array, index, axis, keepdims=False)  12.2 us
    ppermute x11, starting transfers between devices, ring(): lax.ppermute(array, 'seq', [(i, (i + step) % devices) for i in range(devi...  11.4 us
    pallas_call x5, Pallas kernels, call(): pl.pallas_call(kernel, in_specs=specs, out_specs=[whole(s) for s, _ in ou...  11 us
    ppermute x2, waiting for transfers between devices, fast_shards(): came = lax.ppermute(send, 'chan', across)  10.7 us
    ppermute x3, waiting for transfers between devices, fast_shards(): lax.ppermute(piece(r), ('seq', 'chan'), link(r))  9.45 us
    transpose x1, other arithmetic, fast_shards(): natural.reshape(2, 2, rows, 2, stem_c).transpose(1, 2, 3, 0, 4)  6.08 us
    reshape x1, local copies, waits for them, and re-layouts, fast_shards(): enc_w.reshape(KW, stem_c, 2, 2, enc_c)  5.9 us
  transfers between devices with their start and end apart: 24, of which 11 were waited for; matrix products, arithmetic and copies ran while one was open for 22% of the time, Pallas kernels for 9%

profile of v1, /device:TPU:0, one launch (start us, length us, event | category | flops | bytes accessed | tf_op | source)
XLA Modules:
  0.0 144.8 jit_solution(6021071013682657444)
XLA Ops:
  0.6 5.9 %reshape.441 = bf16[5,192,2,2,384]{4,3,2,1,0:T(2,128)(2,1)S(1)} reshape(bf16[5,192,1536]{2,1,0:T(8,128)(2,1)} %bitcast.104) | data formatting | bytes 5898240 | tf_op jit(solution)/shard_map/reshape | solution.py:266
  6.6 11.8 %dynamic-slice_reduce_fusion = bf16[5,192,2,384]{3,2,1,0:T(2,128)(2,1)} fusion(bf16[5,192,2,2,384]{4,3,2,1,0:T(2,128)(2,1)S(1)} %reshape.441, s32[]{:T(128)S(6)} %select_n.174), kind=kLoop, calls=%fused_computation | loop fusion | bytes 2949124 | tf_op jit(solution)/shard_map/jit(dynamic_index_in_dim)/dynamic_slice | solution.py:262
  18.4 4.8 %reshape.442 = bf16[5,192,768]{2,1,0:T(8,128)(2,1)} reshape(bf16[5,192,2,384]{3,2,1,0:T(2,128)(2,1)} %dynamic-slice_reduce_fusion) | data formatting | bytes 2949120 | tf_op jit(solution)/shard_map/reshape | solution.py:266
  23.9 4.6 %collective-permute-start.1 = (s32[2,256]{1,0:T(2,128)S(1)}, s32[2,256]{1,0:T(2,128)S(1)}, u32[]{:S(2)}, u32[]{:S(2)}) collective-permute-start(s32[2,256]{1,0:T(2,128)S(1)} %bitcast.122), channel_id=1, source_target_pairs={{0,12},{4,0},{8,4},{12,8},{1,13},{5,1},{9,5},{13,9},{2,14},{6,2},{... | collective-permute-start | bytes 6152 | tf_op jit(solution)/shard_map/ppermute | solution.py:256
  28.5 1.0 collective-permute-start.6
  29.8 4.1 %collective-permute-done = s32[2,256]{1,0:T(2,128)S(1)} collective-permute-done((s32[2,256]{1,0:T(2,128)S(1)}, s32[2,256]{1,0:T(2,128)S(1)}, u32[]{:S(2)}, u32[]{:S(2)}) %collective-permute-start) | collective-permute-done | bytes 2080 | tf_op jit(solution)/shard_map/ppermute | solution.py:256
  34.1 5.3 %enc_conv.1 = (f32[544,384]{1,0:T(8,128)S(1)}, bf16[544,384]{1,0:T(8,128)(2,1)S(1)}, bf16[2,272,192]{2,1,0:T(8,128)(2,1)S(1)}) custom-call(s32[3]{0:T(128)S(1)} %pad_add_fusion.1.place, s32[2,384]{1,0:T(2,128)S(1)} %add_select_fusion.bases, bf16[2,20,192]{2,1,0:T(8,128)(2,1)S(1)} %pad_maximum_fusion.4.stem_w, bf16[5,192,1536]{2,1,0:T(8,128)(2,1)S(1)} %bitcast.105, ...), custom_call_target="tpu_custom_call" | custom-call | flops 1604321280 | bytes 5904396 | tf_op jit(solution)/shard_map/enc_conv/pallas_call | solution.py:230
  40.8 1.5 %collective-permute-start.4 = (bf16[544,384]{1,0:T(8,128)(2,1)}, bf16[544,384]{1,0:T(8,128)(2,1)S(1)}, u32[]{:S(2)}, u32[]{:S(2)}) collective-permute-start(bf16[544,384]{1,0:T(8,128)(2,1)} %copy-done.12), channel_id=1, source_target_pairs={{0,2},{1,3},{2,0},{3,1},{4,6},{5,7},{6,4},{7,5},{8,10},{9,11},{10,... | collective-permute-start | bytes 1253384 | tf_op jit(solution)/shard_map/ppermute | solution.py:292
  42.4 1.8 %copy.32 = bf16[512,192]{1,0:T(8,128)(2,1)} copy(bf16[512,192]{0,1:T(8,128)(2,1)} %param.9) | data formatting | bytes 393216 | tf_op jit(solution)/shard_map/optimization_barrier | solution.py:294
  44.1 1.8 %reshape.445 = bf16[256,2,192]{2,1,0:T(2,128)(2,1)} reshape(bf16[512,192]{1,0:T(8,128)(2,1)} %copy.32) | data formatting | bytes 393216 | tf_op jit(solution)/shard_map/reshape | solution.py:305
  45.9 1.0 copy.46
  47.0 2.0 %collective-permute-start.8 = (bf16[2,8,192]{2,1,0:T(8,128)(2,1)S(1)}, bf16[2,8,192]{2,1,0:T(8,128)(2,1)S(1)}, u32[]{:S(2)}, u32[]{:S(2)}) collective-permute-start(bf16[2,8,192]{2,1,0:T(8,128)(2,1)S(1)} %get-tuple-element.66), channel_id=1, source_target_pairs={{0,4},{4,8},{8,12},{12,0},{1,5},{5,9},{9,13},{13,1},{2,6},{6,10},{... | collective-permute-start | bytes 18440 | tf_op jit(solution)/shard_map/ppermute | solution.py:256
  49.5 0.7 copy-done.11
  50.6 2.0 %collective-permute-done.8 = bf16[2,8,192]{2,1,0:T(8,128)(2,1)S(1)} collective-permute-done((bf16[2,8,192]{2,1,0:T(8,128)(2,1)S(1)}, bf16[2,8,192]{2,1,0:T(8,128)(2,1)S(1)}, u32[]{:S(2)}, u32[]{:S(2)}) %collective-permute-start.8) | collective-permute-done | bytes 6176 | tf_op jit(solution)/shard_map/ppermute | solution.py:256
  53.2 1.6 %gelu_pool.1 = (bf16[272,384]{1,0:T(8,128)(2,1)S(1)}, bf16[256,384]{1,0:T(8,128)(2,1)}, f32[2,256,384]{2,1,0:T(8,128)S(1)}) custom-call(s32[3]{0:T(128)S(1)} %pad_add_fusion.1.place, f32[544,384]{1,0:T(8,128)S(1)} %copy-done.7, bf16[544,384]{1,0:T(8,128)(2,1)S(1)} %collective-permute-done.4.came), custom_call_target="tpu_custom_call" | custom-call | bytes 2445324 | tf_op jit(solution)/shard_map/gelu_pool/pallas_call | solution.py:230
  54.8 1.5 %slice_add_fusion.3 = (bf16[1,384,384]{2,1,0:T(8,128)(2,1)S(1)}, bf16[1,384,384]{2,1,0:T(8,128)(2,1)S(1)}, bf16[1,384,384]{2,1,0:T(8,128)(2,1)S(1)}, bf16[1,384,...) fusion(bf16[5,384,384]{2,1,0:T(8,128)(2,1)} %collective-permute-done.7), kind=kLoop, calls=%fused_computation.39 | loop fusion | flops 589824 | bytes 3244032 | tf_op jit(solution)/shard_map/add | solution.py:300
  56.3 0.7 maximum_maximum_fusion
  57.0 1.5 %dec_conv.1 = (f32[272,768]{1,0:T(8,128)S(1)}, bf16[272,768]{1,0:T(8,128)(2,1)S(1)}) custom-call(bf16[272,384]{1,0:T(8,128)(2,1)S(1)} %get-tuple-element.22.own, bf16[272,384]{1,0:T(8,128)(2,1)S(1)} %collective-permute-done.5.oth, bf16[3,768,384]{2,1,0:T(8,128)(2,1)S(1)} %get-tuple-element.80.w_own, bf16[3,768,384]{2,1,0:T(8,128)(2,1)S(1)} %get-tuple-element.81.w_oth, ...), custom_call_target="tpu_custom_call" | custom-call | flops 962592768 | bytes 6045696 | tf_op jit(solution)/shard_map/dec_conv/pallas_call | solution.py:230
  58.5 1.5 %collective-permute-start.10 = (bf16[272,768]{1,0:T(8,128)(2,1)S(1)}, bf16[272,768]{1,0:T(8,128)(2,1)S(1)}, u32[]{:S(2)}, u32[]{:S(2)}) collective-permute-start(bf16[272,768]{1,0:T(8,128)(2,1)S(1)} %get-tuple-element.27), channel_id=1, source_target_pairs={{0,2},{1,3},{2,0},{3,1},{4,6},{5,7},{6,4},{7,5},{8,10},{9,11},{10,... | collective-permute-start | bytes 1253384 | tf_op jit(solution)/shard_map/ppermute | solution.py:348
  60.2 10.5 %collective-permute-done.10.came = bf16[272,768]{1,0:T(8,128)(2,1)S(1)} collective-permute-done((bf16[272,768]{1,0:T(8,128)(2,1)S(1)}, bf16[272,768]{1,0:T(8,128)(2,1)S(1)}, u32[]{:S(2)}, u32[]{:S(2)}) %collective-permute-start.10) | collective-permute-done | bytes 417824 | tf_op jit(solution)/shard_map/ppermute | solution.py:348
  70.7 1.0 out_slope.1
  72.0 1.6 %collective-permute-done.11.oth = bf16[2,272,384]{2,1,0:T(8,128)(2,1)S(1)} collective-permute-done((bf16[2,272,384]{2,1,0:T(8,128)(2,1)S(1)}, bf16[2,272,384]{2,1,0:T(8,128)(2,1)S(1)}, u32[]{:S(2)}, u32[]{:S(2)}) %collective-permute-start.11) | collective-permute-done | bytes 417824 | tf_op jit(solution)/shard_map/ppermute | solution.py:359
  73.6 1.4 up_grad.1
  75.0 1.5 %collective-permute-start.12 = (bf16[512,384]{1,0:T(8,128)(2,1)S(1)}, bf16[512,384]{1,0:T(8,128)(2,1)}, u32[]{:S(2)}, u32[]{:S(2)}) collective-permute-start(bf16[512,384]{1,0:T(8,128)(2,1)S(1)} %bitcast.101), channel_id=1, source_target_pairs={{0,2},{1,3},{2,0},{3,1},{4,6},{5,7},{6,4},{7,5},{8,10},{9,11},{10,... | collective-permute-start | bytes 1179656 | tf_op jit(solution)/shard_map/ppermute | solution.py:377
  76.7 1.5 %collective-permute-start.22 = (bf16[256,384]{1,0:T(8,128)(2,1)}, bf16[256,384]{1,0:T(8,128)(2,1)}, u32[]{:S(2)}, u32[]{:S(2)}) collective-permute-start(bf16[256,384]{1,0:T(8,128)(2,1)} %get-tuple-element.36), channel_id=1, source_target_pairs={{0,8},{4,12},{8,0},{12,4},{1,9},{5,13},{9,1},{13,5},{2,10},{6,14},... | collective-permute-start | bytes 589832 | tf_op jit(solution)/shard_map/ppermute | solution.py:256
  78.3 3.7 %stack.149 = bf16[1,2,272,2,192]{4,0,3,2,1:T(2,128)(2,1)S(1)} reshape(bf16[2,272,384]{2,1,0:T(8,128)(2,1)} %copy-done.3) | data formatting | bytes 835584 | tf_op jit(solution)/shard_map/stack | solution.py:427
  82.0 0.7 stack.150
  82.8 3.6 %collective-permute-done.12 = bf16[512,384]{1,0:T(8,128)(2,1)} collective-permute-done((bf16[512,384]{1,0:T(8,128)(2,1)S(1)}, bf16[512,384]{1,0:T(8,128)(2,1)}, u32[]{:S(2)}, u32[]{:S(2)}) %collective-permute-start.12) | collective-permute-done | bytes 393248 | tf_op jit(solution)/shard_map/ppermute | solution.py:377
  86.3 2.5 %fusion.8 = (bf16[512,384]{1,0:T(8,128)(2,1)}, bf16[512,384]{1,0:T(8,128)(2,1)}, bf16[512,384]{1,0:T(8,128)(2,1)}) fusion(s32[]{:T(128)S(6)} %select_n.189, bf16[1,512,384]{2,1,0:T(8,128)(2,1)S(1)} %bitcast.102, bf16[1,512,384]{2,1,0:T(8,128)(2,1)} %bitcast.37, s32[]{:T(128)S(6)} %select_n.192, s32[]{:T(128)S(6)} %select_n.194), kind=kLoop, calls=%fused_computation.26 | loop fusion | flops 589824 | bytes 1966092 | tf_op jit(solution)/shard_map/jit(dynamic_index_in_dim)/squeeze | solution.py:262
  88.8 1.9 %collective-permute-start.14 = (bf16[512,384]{1,0:T(8,128)(2,1)}, bf16[512,384]{1,0:T(8,128)(2,1)}, u32[]{:S(2)}, u32[]{:S(2)}) collective-permute-start(bf16[512,384]{1,0:T(8,128)(2,1)} %get-tuple-element.58), channel_id=1, source_target_pairs={{0,8},{2,10},{5,13},{7,15},{8,0},{10,2},{13,5},{15,7},{16,24},{18,... | collective-permute-start | bytes 1179656 | tf_op jit(solution)/shard_map/ppermute | solution.py:396
  90.8 1.4 collective-permute-start.15
  92.2 1.4 collective-permute-start.13
  93.6 6.1 %fusion = bf16[2,272,2,2,192]{4,3,2,1,0:T(2,128)(2,1)} fusion(pred[]{:T(512)S(6)} %eq.15, bf16[1,2,272,2,192]{4,0,3,2,1:T(2,128)(2,1)S(1)} %stack.150, bf16[1,2,272,2,192]{4,0,3,2,1:T(2,128)(2,1)S(1)} %stack.149), kind=kLoop, calls=%fused_computation.4 | loop fusion | flops 3760128 | bytes 1671169 | tf_op jit(solution)/shard_map/transpose | solution.py:428
  99.7 3.2 %reshape.452 = bf16[2,272,768]{2,1,0:T(8,128)(2,1)S(1)} reshape(bf16[2,272,2,2,192]{4,3,2,1,0:T(2,128)(2,1)} %fusion) | data formatting | bytes 1671168 | tf_op jit(solution)/shard_map/reshape | solution.py:428
  103.1 9.4 %collective-permute-done.14 = bf16[512,384]{1,0:T(8,128)(2,1)} collective-permute-done((bf16[512,384]{1,0:T(8,128)(2,1)}, bf16[512,384]{1,0:T(8,128)(2,1)}, u32[]{:S(2)}, u32[]{:S(2)}) %collective-permute-start.14) | collective-permute-done | bytes 393248 | tf_op jit(solution)/shard_map/ppermute | solution.py:396
  112.6 1.1 select_bitcast_fusion
  113.7 2.1 %collective-permute-start.17 = (bf16[272,192]{1,0:T(8,128)(2,1)S(1)}, bf16[272,192]{1,0:T(8,128)(2,1)S(1)}, u32[]{:S(2)}, u32[]{:S(2)}) collective-permute-start(bf16[272,192]{1,0:T(8,128)(2,1)S(1)} %get-tuple-element.56), channel_id=1, source_target_pairs={{0,4},{4,8},{8,12},{12,0},{1,5},{5,9},{9,13},{13,1},{2,6},{6,10},{... | collective-permute-start | bytes 313352 | tf_op jit(solution)/shard_map/ppermute | solution.py:256
  116.0 4.7 %collective-permute-done.19 = bf16[272,192]{1,0:T(8,128)(2,1)S(1)} collective-permute-done((bf16[272,192]{1,0:T(8,128)(2,1)S(1)}, bf16[272,192]{1,0:T(8,128)(2,1)S(1)}, u32[]{:S(2)}, u32[]{:S(2)}) %collective-permute-start.19) | collective-permute-done | bytes 104480 | tf_op jit(solution)/shard_map/ppermute | solution.py:256
  120.7 4.1 %collective-permute-done.18 = bf16[272,192]{1,0:T(8,128)(2,1)S(1)} collective-permute-done((bf16[272,192]{1,0:T(8,128)(2,1)S(1)}, bf16[272,192]{1,0:T(8,128)(2,1)S(1)}, u32[]{:S(2)}, u32[]{:S(2)}) %collective-permute-start.18) | collective-permute-done | bytes 104480 | tf_op jit(solution)/shard_map/ppermute | solution.py:256
  124.9 1.1 fusion.23
  126.0 0.5 collective-permute-start.20
  126.6 2.8 %stem_taps.1.taps = bf16[4,960,512]{2,1,0:T(8,128)(2,1)S(1)} custom-call(s32[3]{0:T(128)S(1)} %pad_add_fusion.1.place, s32[4,2,384]{2,1,0:T(2,128)S(1)} %pad_add_fusion.bases, bf16[192,20]{1,0:T(8,128)(2,1)S(1)} %bitcast.106), custom_call_target="tpu_custom_call" | custom-call | tf_op jit(solution)/shard_map/stem_taps/pallas_call | solution.py:319
  129.4 1.9 %copy-done = bf16[4,960,512]{2,1,0:T(8,128)(2,1)} copy-done((bf16[4,960,512]{2,1,0:T(8,128)(2,1)}, bf16[4,960,512]{2,1,0:T(8,128)(2,1)S(1)}, u32[]{:S(2)}) %copy-start) | copy-done | bytes 3932184
  131.3 1.2 pad_maximum_fusion.1.pooled
  133.2 0.8 copy.41
  134.0 2.1 %maximum_select_fusion.sums = bf16[4,2,272,192]{3,2,1,0:T(8,128)(2,1)S(1)} fusion(bf16[4,1,272,192]{3,2,1,0:T(8,128)(2,1)} %bitcast.54, bf16[4,1,272,192]{3,2,1,0:T(8,128)(2,1)} %get-tuple-element.60, pred[]{:T(512)S(6)} %eq.15), kind=kLoop, calls=%fused_computation.5 | loop fusion | flops 1253376 | bytes 1671169 | tf_op jit(solution)/shard_map/jit(_where)/select_n | solution.py:437
  136.1 3.4 %dec_grad.1 = f32[5,192,384]{2,1,0:T(8,128)} custom-call(bf16[4,2,272,192]{3,2,1,0:T(8,128)(2,1)S(1)} %maximum_select_fusion.sums, bf16[4,256,384]{2,1,0:T(8,128)(2,1)S(1)} %pad_maximum_fusion.1.pooled), custom_call_target="tpu_custom_call" | custom-call | tf_op jit(solution)/shard_map/dec_grad/pallas_call | solution.py:440
  139.5 5.3 %enc_grad.1 = f32[960,384]{1,0:T(8,128)} custom-call(s32[1]{0:T(128)} %bitcast.20.place, bf16[4,960,512]{2,1,0:T(8,128)(2,1)S(1)} %copy-done.1, bf16[2,512,384]{2,1,0:T(8,128)(2,1)S(1)} %pad_maximum_fusion.own, bf16[2,512,384]{2,1,0:T(8,128)(2,1)} %collective-permute-done.16.oth), custom_call_target="tpu_custom_call" | custom-call | tf_op jit(solution)/shard_map/enc_grad/pallas_call | solution.py:409
  (93 shorter events, 5.6 us)
Async XLA Ops:
  6.6 17.1 %copy-start.15 = (s32[512]{0:T(512)S(1)}, s32[512]{0:T(512)}, u32[]{:S(2)}) copy-start(s32[512]{0:T(512)} %param.5) | copy-start | bytes 6148
  18.4 11.1 %copy-start.14 = (bf16[192,5,4]{0,2,1:T(4,128)(2,1)S(1)}, bf16[192,5,4]{0,2,1:T(4,128)(2,1)}, u32[]{:S(2)}) copy-start(bf16[192,5,4]{0,2,1:T(4,128)(2,1)} %param.6) | copy-start | bytes 23044
  18.4 15.7 %copy-start.2 = (bf16[1536,5,192]{0,2,1:T(8,128)(2,1)S(1)}, bf16[1536,5,192]{0,2,1:T(8,128)(2,1)}, u32[]{:S(2)}) copy-start(bf16[1536,5,192]{0,2,1:T(8,128)(2,1)} %param.7) | copy-start | bytes 8847364
  23.2 10.9 %collective-permute-start.3 = (bf16[5,192,768]{2,1,0:T(8,128)(2,1)}, bf16[5,192,768]{2,1,0:T(8,128)(2,1)}, u32[]{:S(2)}, u32[]{:S(2)}) collective-permute-start(bf16[5,192,768]{2,1,0:T(8,128)(2,1)} %reshape.442), channel_id=1, source_target_pairs={{0,1},{1,0},{2,3},{3,2},{4,5},{5,4},{6,7},{7,6},{8,9},{9,8},{10,11... | collective-permute-start | bytes 4423688 | tf_op jit(solution)/shard_map/ppermute | solution.py:267
  23.9 5.9 %collective-permute-start.1 = (s32[2,256]{1,0:T(2,128)S(1)}, s32[2,256]{1,0:T(2,128)S(1)}, u32[]{:S(2)}, u32[]{:S(2)}) collective-permute-start(s32[2,256]{1,0:T(2,128)S(1)} %bitcast.122), channel_id=1, source_target_pairs={{0,12},{4,0},{8,4},{12,8},{1,13},{5,1},{9,5},{13,9},{2,14},{6,2},{... | collective-permute-start | bytes 6152 | tf_op jit(solution)/shard_map/ppermute | solution.py:256
  28.5 5.4 %collective-permute-start = (s32[2,256]{1,0:T(2,128)S(1)}, s32[2,256]{1,0:T(2,128)S(1)}, u32[]{:S(2)}, u32[]{:S(2)}) collective-permute-start(s32[2,256]{1,0:T(2,128)S(1)} %bitcast.123), channel_id=1, source_target_pairs={{0,4},{4,8},{8,12},{12,0},{1,5},{5,9},{9,13},{13,1},{2,6},{6,10},{... | collective-permute-start | bytes 6152 | tf_op jit(solution)/shard_map/ppermute | solution.py:256
  28.5 10.9 %collective-permute-start.6 = (s32[2,256]{1,0:T(2,128)S(1)}, s32[2,256]{1,0:T(2,128)S(1)}, u32[]{:S(2)}, u32[]{:S(2)}) collective-permute-start(s32[2,256]{1,0:T(2,128)S(1)} %bitcast.124), channel_id=1, source_target_pairs={{0,8},{4,12},{8,0},{12,4},{1,9},{5,13},{9,1},{13,5},{2,10},{6,14},... | collective-permute-start | bytes 6152 | tf_op jit(solution)/shard_map/ppermute | solution.py:256
  29.5 4.5 %collective-permute-start.2 = (bf16[20,192]{1,0:T(8,128)(2,1)S(1)}, bf16[20,192]{1,0:T(8,128)(2,1)S(1)}, u32[]{:S(2)}, u32[]{:S(2)}) collective-permute-start(bf16[20,192]{1,0:T(8,128)(2,1)S(1)} %reshape.440), channel_id=1, source_target_pairs={{0,1},{1,0},{2,3},{3,2},{4,5},{5,4},{6,7},{7,6},{8,9},{9,8},{10,11... | collective-permute-start | bytes 23048 | tf_op jit(solution)/shard_map/ppermute | solution.py:265
  34.1 5.4 %copy-start.13 = (bf16[768,5,384]{2,0,1:T(8,128)(2,1)S(1)}, bf16[768,5,384]{2,0,1:T(8,128)(2,1)}, u32[]{:S(2)}) copy-start(bf16[768,5,384]{2,0,1:T(8,128)(2,1)} %param.8) | copy-start | bytes 8847364
  39.4 0.9 copy-start.6
  39.4 1.0 copy-start.10
  39.4 1.1 copy-start.12
  40.5 14.3 %collective-permute-start.7 = (bf16[5,384,384]{2,1,0:T(8,128)(2,1)S(1)}, bf16[5,384,384]{2,1,0:T(8,128)(2,1)}, u32[]{:S(2)}, u32[]{:S(2)}) collective-permute-start(bf16[5,384,384]{2,1,0:T(8,128)(2,1)S(1)} %bitcast.99), channel_id=1, source_target_pairs={{0,1},{1,0},{2,3},{3,2},{4,5},{5,4},{6,7},{7,6},{8,9},{9,8},{10,11... | collective-permute-start | bytes 4423688 | tf_op jit(solution)/shard_map/ppermute | solution.py:297
  40.8 12.3 %collective-permute-start.4 = (bf16[544,384]{1,0:T(8,128)(2,1)}, bf16[544,384]{1,0:T(8,128)(2,1)S(1)}, u32[]{:S(2)}, u32[]{:S(2)}) collective-permute-start(bf16[544,384]{1,0:T(8,128)(2,1)} %copy-done.12), channel_id=1, source_target_pairs={{0,2},{1,3},{2,0},{3,1},{4,6},{5,7},{6,4},{7,5},{8,10},{9,11},{10,... | collective-permute-start | bytes 1253384 | tf_op jit(solution)/shard_map/ppermute | solution.py:292
  46.9 3.7 %collective-permute-start.9 = (bf16[2,8,192]{2,1,0:T(8,128)(2,1)S(1)}, bf16[2,8,192]{2,1,0:T(8,128)(2,1)S(1)}, u32[]{:S(2)}, u32[]{:S(2)}) collective-permute-start(bf16[2,8,192]{2,1,0:T(8,128)(2,1)S(1)} %get-tuple-element.67), channel_id=1, source_target_pairs={{0,12},{4,0},{8,4},{12,8},{1,13},{5,1},{9,5},{13,9},{2,14},{6,2},{... | collective-permute-start | bytes 18440 | tf_op jit(solution)/shard_map/ppermute | solution.py:256
  47.0 5.7 %collective-permute-start.8 = (bf16[2,8,192]{2,1,0:T(8,128)(2,1)S(1)}, bf16[2,8,192]{2,1,0:T(8,128)(2,1)S(1)}, u32[]{:S(2)}, u32[]{:S(2)}) collective-permute-start(bf16[2,8,192]{2,1,0:T(8,128)(2,1)S(1)} %get-tuple-element.66), channel_id=1, source_target_pairs={{0,4},{4,8},{8,12},{12,0},{1,5},{5,9},{9,13},{13,1},{2,6},{6,10},{... | collective-permute-start | bytes 18440 | tf_op jit(solution)/shard_map/ppermute | solution.py:256
  49.2 1.0 copy-start.11
  49.2 4.0 %copy-start.7 = (f32[544,384]{1,0:T(8,128)S(1)}, f32[544,384]{1,0:T(8,128)}, u32[]{:S(2)}) copy-start(f32[544,384]{1,0:T(8,128)} %copy-done.6) | copy-start | bytes 2506756
  54.8 2.2 %collective-permute-start.5 = (bf16[272,384]{1,0:T(8,128)(2,1)S(1)}, bf16[272,384]{1,0:T(8,128)(2,1)S(1)}, u32[]{:S(2)}, u32[]{:S(2)}) collective-permute-start(bf16[272,384]{1,0:T(8,128)(2,1)S(1)} %get-tuple-element.22.own), channel_id=1, source_target_pairs={{0,1},{1,0},{2,3},{3,2},{4,5},{5,4},{6,7},{7,6},{8,9},{9,8},{10,11... | collective-permute-start | bytes 626696 | tf_op jit(solution)/shard_map/ppermute | solution.py:339
  58.5 12.1 %collective-permute-start.10 = (bf16[272,768]{1,0:T(8,128)(2,1)S(1)}, bf16[272,768]{1,0:T(8,128)(2,1)S(1)}, u32[]{:S(2)}, u32[]{:S(2)}) collective-permute-start(bf16[272,768]{1,0:T(8,128)(2,1)S(1)} %get-tuple-element.27), channel_id=1, source_target_pairs={{0,2},{1,3},{2,0},{3,1},{4,6},{5,7},{6,4},{7,5},{8,10},{9,11},{10,... | collective-permute-start | bytes 1253384 | tf_op jit(solution)/shard_map/ppermute | solution.py:348
  71.7 3.3 %copy-start.3 = (bf16[2,272,384]{2,1,0:T(8,128)(2,1)}, bf16[2,272,384]{2,1,0:T(8,128)(2,1)S(1)}, u32[]{:S(2)}) copy-start(bf16[2,272,384]{2,1,0:T(8,128)(2,1)S(1)} %get-tuple-element.33.own) | copy-start | bytes 1253380
  71.7 3.3 %copy-start.8 = (bf16[2,256,384]{2,1,0:T(8,128)(2,1)}, bf16[2,256,384]{2,1,0:T(8,128)(2,1)S(1)}, u32[]{:S(2)}) copy-start(bf16[2,256,384]{2,1,0:T(8,128)(2,1)S(1)} %get-tuple-element.28) | copy-start | bytes 1179652
  71.7 1.8 %collective-permute-start.11 = (bf16[2,272,384]{2,1,0:T(8,128)(2,1)S(1)}, bf16[2,272,384]{2,1,0:T(8,128)(2,1)S(1)}, u32[]{:S(2)}, u32[]{:S(2)}) collective-permute-start(bf16[2,272,384]{2,1,0:T(8,128)(2,1)S(1)} %get-tuple-element.33.own), channel_id=1, source_target_pairs={{0,1},{1,0},{2,3},{3,2},{4,5},{5,4},{6,7},{7,6},{8,9},{9,8},{10,11... | collective-permute-start | bytes 1253384 | tf_op jit(solution)/shard_map/ppermute | solution.py:359
  73.5 1.4 copy-start.4
  75.0 7.0 %copy-start.5 = (bf16[2,272,384]{2,1,0:T(8,128)(2,1)S(1)}, bf16[2,272,384]{2,1,0:T(8,128)(2,1)}, u32[]{:S(2)}) copy-start(bf16[2,272,384]{2,1,0:T(8,128)(2,1)} %copy-done.4) | copy-start | bytes 1253380
  75.0 11.3 %collective-permute-start.12 = (bf16[512,384]{1,0:T(8,128)(2,1)S(1)}, bf16[512,384]{1,0:T(8,128)(2,1)}, u32[]{:S(2)}, u32[]{:S(2)}) collective-permute-start(bf16[512,384]{1,0:T(8,128)(2,1)S(1)} %bitcast.101), channel_id=1, source_target_pairs={{0,2},{1,3},{2,0},{3,1},{4,6},{5,7},{6,4},{7,5},{8,10},{9,11},{10,... | collective-permute-start | bytes 1179656 | tf_op jit(solution)/shard_map/ppermute | solution.py:377
  76.7 54.6 %collective-permute-start.23 = (bf16[256,384]{1,0:T(8,128)(2,1)}, bf16[256,384]{1,0:T(8,128)(2,1)S(1)}, u32[]{:S(2)}, u32[]{:S(2)}) collective-permute-start(bf16[256,384]{1,0:T(8,128)(2,1)} %get-tuple-element.36), channel_id=1, source_target_pairs={{0,12},{4,0},{8,4},{12,8},{1,13},{5,1},{9,5},{13,9},{2,14},{6,2},{... | collective-permute-start | bytes 589832 | tf_op jit(solution)/shard_map/ppermute | solution.py:256
  76.7 54.6 %collective-permute-start.22 = (bf16[256,384]{1,0:T(8,128)(2,1)}, bf16[256,384]{1,0:T(8,128)(2,1)}, u32[]{:S(2)}, u32[]{:S(2)}) collective-permute-start(bf16[256,384]{1,0:T(8,128)(2,1)} %get-tuple-element.36), channel_id=1, source_target_pairs={{0,8},{4,12},{8,0},{12,4},{1,9},{5,13},{9,1},{13,5},{2,10},{6,14},... | collective-permute-start | bytes 589832 | tf_op jit(solution)/shard_map/ppermute | solution.py:256
  88.8 23.8 %collective-permute-start.14 = (bf16[512,384]{1,0:T(8,128)(2,1)}, bf16[512,384]{1,0:T(8,128)(2,1)}, u32[]{:S(2)}, u32[]{:S(2)}) collective-permute-start(bf16[512,384]{1,0:T(8,128)(2,1)} %get-tuple-element.58), channel_id=1, source_target_pairs={{0,8},{2,10},{5,13},{7,15},{8,0},{10,2},{13,5},{15,7},{16,24},{18,... | collective-permute-start | bytes 1179656 | tf_op jit(solution)/shard_map/ppermute | solution.py:396
  90.8 21.8 %collective-permute-start.15 = (bf16[512,384]{1,0:T(8,128)(2,1)}, bf16[512,384]{1,0:T(8,128)(2,1)}, u32[]{:S(2)}, u32[]{:S(2)}) collective-permute-start(bf16[512,384]{1,0:T(8,128)(2,1)} %get-tuple-element.59), channel_id=1, source_target_pairs={{1,12},{3,14},{4,1},{6,3},{9,4},{11,6},{12,9},{14,11},{17,28},{19,... | collective-permute-start | bytes 1179656 | tf_op jit(solution)/shard_map/ppermute | solution.py:396
  92.2 21.5 %collective-permute-start.13 = (bf16[512,384]{1,0:T(8,128)(2,1)}, bf16[512,384]{1,0:T(8,128)(2,1)}, u32[]{:S(2)}, u32[]{:S(2)}) collective-permute-start(bf16[512,384]{1,0:T(8,128)(2,1)} %get-tuple-element.57), channel_id=1, source_target_pairs={{1,4},{3,6},{4,9},{6,11},{9,12},{11,14},{12,1},{14,3},{17,20},{19,... | collective-permute-start | bytes 1179656 | tf_op jit(solution)/shard_map/ppermute | solution.py:396
  112.6 8.1 %collective-permute-start.19 = (bf16[272,192]{1,0:T(8,128)(2,1)S(1)}, bf16[272,192]{1,0:T(8,128)(2,1)S(1)}, u32[]{:S(2)}, u32[]{:S(2)}) collective-permute-start(bf16[272,192]{1,0:T(8,128)(2,1)S(1)} %get-tuple-element.54), channel_id=1, source_target_pairs={{0,12},{4,0},{8,4},{12,8},{1,13},{5,1},{9,5},{13,9},{2,14},{6,2},{... | collective-permute-start | bytes 313352 | tf_op jit(solution)/shard_map/ppermute | solution.py:256
  112.6 12.3 %collective-permute-start.18 = (bf16[272,192]{1,0:T(8,128)(2,1)S(1)}, bf16[272,192]{1,0:T(8,128)(2,1)S(1)}, u32[]{:S(2)}, u32[]{:S(2)}) collective-permute-start(bf16[272,192]{1,0:T(8,128)(2,1)S(1)} %get-tuple-element.55), channel_id=1, source_target_pairs={{0,8},{4,12},{8,0},{12,4},{1,9},{5,13},{9,1},{13,5},{2,10},{6,14},... | collective-permute-start | bytes 313352 | tf_op jit(solution)/shard_map/ppermute | solution.py:256
  113.7 11.2 %collective-permute-start.17 = (bf16[272,192]{1,0:T(8,128)(2,1)S(1)}, bf16[272,192]{1,0:T(8,128)(2,1)S(1)}, u32[]{:S(2)}, u32[]{:S(2)}) collective-permute-start(bf16[272,192]{1,0:T(8,128)(2,1)S(1)} %get-tuple-element.56), channel_id=1, source_target_pairs={{0,4},{4,8},{8,12},{12,0},{1,5},{5,9},{9,13},{13,1},{2,6},{6,10},{... | collective-permute-start | bytes 313352 | tf_op jit(solution)/shard_map/ppermute | solution.py:256
  120.7 10.6 %collective-permute-start.21 = (bf16[256,384]{1,0:T(8,128)(2,1)}, bf16[256,384]{1,0:T(8,128)(2,1)S(1)}, u32[]{:S(2)}, u32[]{:S(2)}) collective-permute-start(bf16[256,384]{1,0:T(8,128)(2,1)} %get-tuple-element.36), channel_id=1, source_target_pairs={{0,4},{4,8},{8,12},{12,0},{1,5},{5,9},{9,13},{13,1},{2,6},{6,10},{... | collective-permute-start | bytes 589832 | tf_op jit(solution)/shard_map/ppermute | solution.py:256
  124.8 14.6 %collective-permute-start.16 = (bf16[2,512,384]{2,1,0:T(8,128)(2,1)S(1)}, bf16[2,512,384]{2,1,0:T(8,128)(2,1)}, u32[]{:S(2)}, u32[]{:S(2)}) collective-permute-start(bf16[2,512,384]{2,1,0:T(8,128)(2,1)S(1)} %pad_maximum_fusion.own), channel_id=1, source_target_pairs={{0,1},{1,0},{2,3},{3,2},{4,5},{5,4},{6,7},{7,6},{8,9},{9,8},{10,11... | collective-permute-start | bytes 2359304 | tf_op jit(solution)/shard_map/ppermute | solution.py:401
  126.0 8.0 %collective-permute-start.20 = (bf16[4,272,192]{2,1,0:T(8,128)(2,1)}, bf16[4,272,192]{2,1,0:T(8,128)(2,1)}, u32[]{:S(2)}, u32[]{:S(2)}) collective-permute-start(bf16[4,272,192]{2,1,0:T(8,128)(2,1)} %get-tuple-element.61), channel_id=1, source_target_pairs={{0,1},{1,0},{2,3},{3,2},{4,5},{5,4},{6,7},{7,6},{8,9},{9,8},{10,11... | collective-permute-start | bytes 1253384 | tf_op jit(solution)/shard_map/ppermute | solution.py:436
  129.4 1.9 %copy-start = (bf16[4,960,512]{2,1,0:T(8,128)(2,1)}, bf16[4,960,512]{2,1,0:T(8,128)(2,1)S(1)}, u32[]{:S(2)}) copy-start(bf16[4,960,512]{2,1,0:T(8,128)(2,1)S(1)} %stem_taps.1.taps) | copy-start | bytes 11796484
  131.3 1.2 copy-start.9
  134.0 5.5 %copy-start.1 = (bf16[4,960,512]{2,1,0:T(8,128)(2,1)S(1)}, bf16[4,960,512]{2,1,0:T(8,128)(2,1)}, u32[]{:S(2)}) copy-start(bf16[4,960,512]{2,1,0:T(8,128)(2,1)} %copy-done) | copy-start | bytes 11796484

commit v2 on v0

--- a/solution.py
+++ b/solution.py
@@ -1,15 +1,575 @@
+import functools
 import math
 
 import jax
 import jax.numpy as jnp
 from jax import lax
+from jax.experimental import pallas as pl
+from jax.experimental.pallas import tpu as pltpu
 from jax.sharding import PartitionSpec as P
 
 KW = 5
-
 
 SQRT_TWO_PI = 0.7978845608028654
 CUBIC = 0.044715
+
+SIDE = 64
+OUTER = 16
+INNER = 8
+F32 = jnp.float32
+BF16 = jnp.bfloat16
+MIB = 1024 * 1024
+
+
+def gelu_value(value):
+    inner = jnp.tanh(SQRT_TWO_PI * (value + CUBIC * value * value * value))
+    return 0.5 * value * (1.0 + inner)
+
+
+def gelu_both(value):
+    square = value * value
+    inner = jnp.tanh(SQRT_TWO_PI * (value + CUBIC * square * value))
+    slope = 0.5 * (1.0 + inner) + 0.5 * value * (1.0 - inner * inner) * SQRT_TWO_PI * (
+        1.0 + 3.0 * CUBIC * square
+    )
+    return 0.5 * value * (1.0 + inner), slope
+
+
+def dot(a, b, contract):
+    return lax.dot_general(a, b, (contract, ((), ())), preferred_element_type=F32)
+
+
+def assemble(own, after, before, block, devices):
+    side = 2 * SIDE
+    pairs = own.shape[1]
+    column = lax.broadcasted_iota(jnp.int32, (2, side), 1)
+    after = jnp.where(block == devices - 1, -1, after[:, :side])
+    before = jnp.where(block == 0, -1, before[:, pairs - side :])
+    return jnp.concatenate([own, jnp.where(column < SIDE, after, before)], axis=1)
+
+
+def tap_onehots(bases, start, width):
+    total = bases.shape[1]
+    before = pltpu.roll(bases, (1 - start) % total, 1)[:, :width]
+    here = bases[:, :width] if start == 0 else pltpu.roll(bases, -start % total, 1)[:, :width]
+    after = pltpu.roll(bases, (-1 - start) % total, 1)[:, :width]
+    taps = [before[0:1], before[1:2], here[0:1], here[1:2], after[0:1], after[1:2]]
+    row = lax.broadcasted_iota(jnp.int32, (4 * KW, width), 0)
+    tap, base = row >> 2, row & 3
+    out = []
+    for first in (0, 1):
+        value = jnp.full((4 * KW, width), -1, jnp.int32)
+        for k in range(KW):
+            value = jnp.where(tap == k, jnp.broadcast_to(taps[first + k], value.shape), value)
+        out.append(jnp.where(value == base, 1.0, 0.0).astype(BF16))
+    return out
+
+
+def valid_pairs(shape, dim, first, total):
+    pair = lax.broadcasted_iota(jnp.int32, shape, dim) + first
+    return (pair >= 0) & (pair < total)
+
+
+def stem_kernel(place, own, after, before, stem_own, stem_oth, w_own, acc, stem_out, lhs_oth, even, odd, lhs, *, pairs, devices):
+    seq, hi, lo = place[0], place[1], place[2]
+    rows = pairs + 2 * INNER
+    wide = pairs + 2 * OUTER
+    block = acc.shape[1] // 2
+    bases = assemble(own[...], after[...], before[...], seq, devices)
+    hots = tap_onehots(bases, -OUTER, wide)
+    gap = OUTER - INNER
+    for weight, held_lhs in ((stem_own, lhs), (stem_oth, lhs_oth)):
+        for hot, held in zip(hots, (even, odd)):
+            raw = dot(hot, weight[...], ((0,), (0,)))
+            ok = valid_pairs(raw.shape, 0, seq * pairs - OUTER, pairs * devices)
+            held[...] = jnp.where(ok, gelu_value(raw), 0.0).astype(BF16).astype(F32)
+        for k in range(6):
+            source = even if k % 2 == 0 else odd
+            held_lhs[k] = source[gap + k // 2 - 1 : gap + k // 2 - 1 + rows, :].astype(BF16)
+    stem_out[0] = lhs[2]
+    stem_out[1] = lhs[3]
+    for part in range(2):
+        at = pl.multiple_of((2 * (hi if part == 0 else 1 - hi) + lo) * block, 128)
+        total = jnp.zeros((2 * rows, block), F32)
+        for k in range(KW):
+            total = total + dot(lhs[k : k + 2].reshape(2 * rows, -1), w_own[k, :, pl.ds(at, block)], ((1,), (0,)))
+        acc[:, part * block : (part + 1) * block] = total
+
+
+def enc_kernel(place, acc, lhs, w_oth, keep, send):
+    hi = place[1]
+    rows, block = keep.shape
+    for part in range(2):
+        at = pl.multiple_of((hi if part == 0 else 1 - hi) * block, 128)
+        total = acc[:, part * block : (part + 1) * block]
+        for k in range(KW):
+            total = total + dot(lhs[k : k + 2].reshape(rows, -1), w_oth[k, :, pl.ds(at, block)], ((1,), (0,)))
+        if part == 0:
+            keep[...] = total
+        else:
+            send[...] = total.astype(BF16)
+
+
+def pool_kernel(place, keep, came, pooled, centre, slope, *, pairs, total):
+    rows = pairs + 2 * INNER
+    value = keep[...] + came[...].astype(F32)
+    active, grad = gelu_both(value)
+    active = active.astype(BF16).astype(F32)
+    both = 0.5 * (active[:rows] + active[rows:])
+    ok = valid_pairs(both.shape, 0, place[0] * pairs - INNER, total)
+    both = jnp.where(ok, both, 0.0).astype(BF16)
+    pooled[...] = both
+    centre[...] = both[INNER : INNER + pairs].astype(BF16)
+    grad = 0.5 * grad
+    slope[0] = grad[INNER : INNER + pairs]
+    slope[1] = grad[rows + INNER : rows + INNER + pairs]
+
+
+def dec_kernel(own, oth, w_own, w_oth, stem, targets, part, send, held, *, pairs):
+    rows = pairs + 2 * INNER
+    held[:8] = jnp.zeros((8, held.shape[1]), F32)
+    held[8 + rows :] = jnp.zeros((8, held.shape[1]), F32)
+    acc = jnp.zeros(part.shape, F32)
+    for source, weight in ((own, w_own), (oth, w_oth)):
+        held[8 : 8 + rows] = source[...].astype(F32)
+        for k in range(3):
+            acc = acc + dot(held[7 + k : 7 + k + rows].astype(BF16), weight[k], ((1,), (1,)))
+    half = part.shape[1] // 2
+    for parity in range(2):
+        value = acc[:, parity * half : (parity + 1) * half]
+        value = value + stem[parity].astype(F32) - targets[parity].astype(F32)
+        part[:, parity * half : (parity + 1) * half] = value
+        send[:, parity * half : (parity + 1) * half] = value.astype(BF16)
+
+
+def slope_kernel(place, part, came, targets, pred, sums, low, high, held, *, pairs, total, scale):
+    rows = pairs + 2 * INNER
+    half = part.shape[1] // 2
+    ok = valid_pairs((rows, half), 0, place[0] * pairs - INNER, total)
+    slopes = []
+    for parity in range(2):
+        cols = slice(parity * half, (parity + 1) * half)
+        value = part[:, cols] + came[:, cols].astype(F32)
+        out = value + targets[parity].astype(F32)
+        pred[parity] = out[INNER : INNER + pairs].astype(BF16)
+        slopes.append(jnp.where(ok, value * scale, 0.0).astype(BF16).astype(F32))
+    held[:rows] = slopes[0]
+    held[rows:] = jnp.zeros((8, half), F32)
+    for i, value in enumerate((slopes[0] + slopes[1], slopes[1] + held[1 : 1 + rows])):
+        value = value.astype(BF16)
+        sums[i] = value
+        low[i] = value[:, : half // 2]
+        high[i] = value[:, half // 2 :]
+
+
+def lane_tiles(channels):
+    return [(first, min(first + 128, channels)) for first in range(0, channels, 128)]
+
+
+def targets_kernel(place, own, before, after, out, held):
+    channels, count = own.shape
+    side = before.shape[1]
+    rows = count // 2 + 2 * INNER
+    high = place[1] == 1
+    for first, last in lane_tiles(channels):
+        wide = last - first
+        held[:side, :wide] = before[first:last].astype(F32).T
+        held[side : side + count, :wide] = own[first:last].astype(F32).T
+        held[side + count :, :wide] = after[first:last].astype(F32).T
+        for parity in range(2):
+            value = held[pl.ds(side - 2 * INNER + parity, rows, stride=2), :][:, :wide].astype(BF16)
+            blank = jnp.zeros_like(value)
+            out[parity, :, first:last] = jnp.where(high, blank, value)
+            out[parity, :, channels + first : channels + last] = jnp.where(high, value, blank)
+
+
+def pred_kernel(place, source, out, held):
+    channels, count = out.shape
+    for first, last in lane_tiles(channels):
+        wide = last - first
+        for parity in range(2):
+            value = source[parity].astype(F32)
+            value = jnp.where(place[1] == 1, value[:, channels + first : channels + last], value[:, first:last])
+            if wide < 128:
+                value = jnp.concatenate([value, jnp.zeros((count // 2, 128 - wide), F32)], axis=1)
+            held[pl.ds(parity, count // 2, stride=2), :] = value
+        out[first:last] = held[:, :wide].T.astype(BF16)
+
+
+def shifted_sums(held, pairs):
+    return [
+        held[0, INNER + 1 : INNER + 1 + pairs].astype(BF16),
+        held[1, INNER : INNER + pairs].astype(BF16),
+        held[0, INNER : INNER + pairs].astype(BF16),
+        held[1, INNER - 1 : INNER - 1 + pairs].astype(BF16),
+        held[0, INNER - 1 : INNER - 1 + pairs].astype(BF16),
+    ]
+
+
+def back_kernel(own, oth, w_own, w_oth, slope, out, held, *, pairs):
+    acc = jnp.zeros((pairs, out.shape[2]), F32)
+    for source, weight in ((own, w_own), (oth, w_oth)):
+        held[...] = source[...].astype(F32)
+        for k, tap in enumerate(shifted_sums(held, pairs)):
+            acc = acc + dot(tap, weight[k], ((1,), (0,)))
+    out[0] = (acc * slope[0]).astype(BF16)
+    out[1] = (acc * slope[1]).astype(BF16)
+
+
+def taps_kernel(place, *refs, pairs, devices):
+    blocks, (stem_w, out) = refs[:devices], refs[devices:]
+    channels = stem_w.shape[0]
+    for r in range(devices):
+        block = lax.rem(place[0] - r + devices, devices)
+        bases = assemble(blocks[r][...], blocks[r - 1][...], blocks[(r + 1) % devices][...], block, devices)
+        width = bases.shape[1]
+        parts = []
+        for hot in tap_onehots(bases, 0, width):
+            raw = dot(stem_w[...], hot, ((1,), (0,)))
+            column = lax.broadcasted_iota(jnp.int32, raw.shape, 1)
+            pair = jnp.where(column >= width - SIDE, column - width, column) + block * pairs
+            ok = (pair >= 0) & (pair < pairs * devices)
+            parts.append(jnp.where(ok, gelu_value(raw), 0.0))
+        taps = []
+        for step in (-1, 0, 1):
+            for held in parts:
+                moved = held if step == 0 else pltpu.roll(held, -step % width, 1)
+                taps.append(moved[:, :pairs].astype(BF16))
+        at = 2 * r * pairs
+        for k in range(KW):
+            out[k * channels : (k + 1) * channels, at : at + pairs] = taps[k]
+            out[k * channels : (k + 1) * channels, at + pairs : at + 2 * pairs] = taps[k + 1]
+
+
+def pick_kernel(place, source, out):
+    out[...] = source[...]
+
+
+def dec_pick_kernel(place, own, oth, own_out, oth_out, comb):
+    own_out[...] = own[...]
+    oth_out[...] = oth[...]
+    combine(own, comb)
+
+
+def comb_kernel(came, comb):
+    combine(came, comb)
+
+
+def combine(weight, comb):
+    comb[0, 0] = weight[0] + weight[1]
+    comb[1, 0] = weight[2] + weight[3]
+    comb[2, 0] = weight[4]
+    comb[0, 1] = weight[0]
+    comb[1, 1] = weight[1] + weight[2]
+    comb[2, 1] = weight[3] + weight[4]
+
+
+def dec_grad_kernel(place, own0, own1, oth0, oth1, pool0, pool1, pool2, pool3, out, held, taps, pooled, *, pairs):
+    slots = (own0, own1, oth0, oth1)
+    blocks = (pool0, pool1, pool2, pool3)
+    parity = place[3]
+    odd = lax.rem(place[0], 2)
+    for block, step in zip(blocks, (0, 3 - 2 * odd, 2, 1 + 2 * odd)):
+        pooled[pl.ds(pl.multiple_of(step * pairs, pairs), pairs), :] = block[...]
+    for i, slot in enumerate(slots):
+        held[...] = slot[...].astype(F32)
+        step = 2 * (i % 2) + (parity if i < 2 else 1 - parity)
+        at = pl.ds(pl.multiple_of(step * pairs, pairs), pairs)
+        for k, tap in enumerate(shifted_sums(held, pairs)):
+            taps[k, at, :] = tap
+    for k in range(KW):
+        out[k] = dot(taps[k], pooled[...], ((0,), (0,)))
+
+
+def enc_grad_kernel(place, taps, own0, own1, oth0, oth1, out, joined):
+    @pl.when(pl.program_id(0) == 0)
+    def _():
+        size = own0.shape[0]
+        for i, slot in enumerate((own0, own1, oth0, oth1)):
+            step = 2 * (i % 2) + (place[3] if i < 2 else 1 - place[3])
+            joined[pl.ds(pl.multiple_of(step * size, size), size), :] = slot[...]
+
+    out[...] = dot(taps[...], joined[...], ((1,), (0,)))
+
+
+def whole(shape):
+    return pl.BlockSpec(shape, lambda *_: (0,) * len(shape))
+
+
+SCALARS = pl.BlockSpec(memory_space=pltpu.SMEM)
+
+
+def call(kernel, ins, outs, scratch=(), limit=48, flops=0, name=None):
+    specs = [SCALARS if i.dtype == jnp.int32 and i.ndim == 1 else whole(i.shape) for i in ins]
+    size = sum(i.size * i.dtype.itemsize for i in ins) + sum(
+        math.prod(s) * jnp.dtype(d).itemsize for s, d in outs
+    )
+    return pl.pallas_call(
+        kernel,
+        in_specs=specs,
+        out_specs=[whole(s) for s, _ in outs],
+        out_shape=[jax.ShapeDtypeStruct(s, d) for s, d in outs],
+        scratch_shapes=[pltpu.VMEM(s, d) for s, d in scratch],
+        compiler_params=pltpu.CompilerParams(vmem_limit_bytes=limit * MIB),
+        cost_estimate=pl.CostEstimate(flops=flops, bytes_accessed=size, transcendentals=0),
+        name=name,
+    )(*ins)
+
+
+def gated(values, gates):
+    return lax.optimization_barrier((values, gates))[0]
+
+
+def shards(dna_bases, w_stem, w_enc, w_dec, targets):
+    devices = lax.axis_size("seq")
+    seq, chan = lax.axis_index("seq"), lax.axis_index("chan")
+    hi, lo = chan // 2, chan % 2
+    parity = lax.rem(lo + seq, 2)
+    place = jnp.stack([seq, hi, lo, parity]).astype(jnp.int32)
+    pairs = dna_bases.shape[0] // 2
+    total = pairs * devices
+    rows = pairs + 2 * INNER
+    stem_c = w_stem.shape[0]
+    enc_c = w_dec.shape[2]
+    across = [(c, c ^ 2) for c in range(4)]
+    cores = [(c, c ^ 1) for c in range(4)]
+
+    def ring(array, step):
+        return lax.ppermute(array, "seq", [(i, (i + step) % devices) for i in range(devices)])
+
+    def swap(array, distance):
+        return lax.ppermute(array, "seq", [(i, i ^ distance) for i in range(devices)])
+
+    own = dna_bases.reshape(pairs, 2).T
+    blocks = {0: own, 1: ring(own, 1), devices - 1: ring(own, devices - 1)}
+
+    stem_w = w_stem.transpose(1, 2, 0).reshape(4 * KW, stem_c)
+    stem_oth = lax.ppermute(stem_w, "chan", cores)
+    enc_w = w_enc.transpose(1, 2, 0)
+    enc_send = pl.pallas_call(
+        pick_kernel,
+        grid_spec=pltpu.PrefetchScalarGridSpec(
+            num_scalar_prefetch=1,
+            grid=(2,),
+            in_specs=[pl.BlockSpec((KW, stem_c, enc_c), lambda h, at: (0, 0, 2 * h + 1 - at[2]))],
+            out_specs=pl.BlockSpec((KW, stem_c, enc_c), lambda h, at: (0, 0, h)),
+        ),
+        out_shape=jax.ShapeDtypeStruct((KW, stem_c, 2 * enc_c), BF16),
+        compiler_params=pltpu.CompilerParams(vmem_limit_bytes=8 * MIB),
+        name="enc_pick",
+    )(place, enc_w)
+    enc_oth = lax.ppermute(enc_send, "chan", cores)
+
+    dec_w = w_dec.transpose(1, 0, 2).reshape(KW, 4, stem_c, enc_c)
+    picked = (KW, 1, stem_c, enc_c)
+    dec_own, dec_oth, comb_own = pl.pallas_call(
+        dec_pick_kernel,
+        grid_spec=pltpu.PrefetchScalarGridSpec(
+            num_scalar_prefetch=1,
+            grid=(2,),
+            in_specs=[
+                pl.BlockSpec(picked, lambda h, at: (0, 2 * h + at[2], 0, 0)),
+                pl.BlockSpec(picked, lambda h, at: (0, 2 * h + 1 - at[2], 0, 0)),
+            ],
+            out_specs=[
+                pl.BlockSpec(picked, lambda h, at: (0, h, 0, 0)),
+                pl.BlockSpec(picked, lambda h, at: (0, h, 0, 0)),
+                pl.BlockSpec((3, 2, 1, stem_c, enc_c), lambda h, at: (0, 0, h, 0, 0)),
+            ],
+        ),
+        out_shape=[
+            jax.ShapeDtypeStruct((KW, 2, stem_c, enc_c), BF16),
+            jax.ShapeDtypeStruct((KW, 2, stem_c, enc_c), BF16),
+            jax.ShapeDtypeStruct((3, 2, 2, stem_c, enc_c), BF16),
+        ],
+        compiler_params=pltpu.CompilerParams(vmem_limit_bytes=12 * MIB),
+        name="dec_pick",
+    )(place, dec_w, dec_w)
+    blocks[1], blocks[devices - 1] = gated((blocks[1], blocks[devices - 1]), (dec_own, dec_oth, comb_own))
+    acc, stem, lhs = call(
+        functools.partial(stem_kernel, pairs=pairs, devices=devices),
+        [place, own, blocks[devices - 1], blocks[1], stem_w, stem_oth, enc_w],
+        [((2 * rows, 2 * enc_c), F32), ((2, rows, stem_c), BF16), ((6, rows, stem_c), BF16)],
+        [
+            ((pairs + 2 * OUTER, stem_c), F32),
+            ((pairs + 2 * OUTER, stem_c), F32),
+            ((6, rows, stem_c), BF16),
+        ],
+        limit=14,
+        flops=4 * rows * stem_c * KW * 2 * enc_c,
+        name="stem_conv",
+    )
+    keep, send = call(
+        enc_kernel,
+        [place, acc, lhs, enc_oth],
+        [((2 * rows, enc_c), F32), ((2 * rows, enc_c), BF16)],
+        limit=12,
+        flops=4 * rows * stem_c * KW * 2 * enc_c,
+        name="enc_conv",
+    )
+    came = lax.ppermute(send, "chan", across)
+
+    dec_oth, targets_in, own_in = gated((dec_oth, targets, own), send)
+    for r in range(2, devices - 1):
+        blocks[r] = ring(own_in, r)
+    dec_came = lax.ppermute(dec_oth, "chan", cores)
+    comb_came = pl.pallas_call(
+        comb_kernel,
+        grid=(2,),
+        in_specs=[pl.BlockSpec(picked, lambda h: (0, h, 0, 0))],
+        out_specs=pl.BlockSpec((3, 2, 1, stem_c, enc_c), lambda h: (0, 0, h, 0, 0)),
+        out_shape=jax.ShapeDtypeStruct((3, 2, 2, stem_c, enc_c), BF16),
+        compiler_params=pltpu.CompilerParams(vmem_limit_bytes=8 * MIB),
+        name="dec_combine",
+    )(dec_came)
+    targets_in = targets_in.T
+    count, edge = 2 * pairs, 2 * SIDE
+    (targets_at,) = call(
+        targets_kernel,
+        [place, targets_in, ring(targets_in[:, count - edge :], 1), ring(targets_in[:, :edge], devices - 1)],
+        [((2, rows, 2 * stem_c), BF16)],
+        [((count + 2 * edge, 128), F32)],
+        limit=6,
+        name="targets",
+    )
+    blank = jnp.zeros_like(stem)
+    stem_at = jnp.where(hi == 0, jnp.concatenate([stem, blank], axis=2), jnp.concatenate([blank, stem], axis=2))
+    came = gated(came, (comb_came, targets_at, stem_at, [blocks[r] for r in range(2, devices - 1)]))
+
+    pooled, centre, slope = call(
+        functools.partial(pool_kernel, pairs=pairs, total=total),
+        [place, keep, came],
+        [((rows, enc_c), BF16), ((pairs, enc_c), BF16), ((2, pairs, enc_c), F32)],
+        limit=8,
+        name="gelu_pool",
+    )
+    pooled_oth = lax.ppermute(pooled, "chan", cores)
+    part, send = call(
+        functools.partial(dec_kernel, pairs=pairs),
+        [
+            pooled,
+            pooled_oth,
+            comb_own.reshape(3, 4 * stem_c, enc_c),
+            comb_came.reshape(3, 4 * stem_c, enc_c),
+            stem_at,
+            targets_at,
+        ],
+        [((rows, 4 * stem_c), F32), ((rows, 4 * stem_c), BF16)],
+        [((rows + 16, enc_c), F32)],
+        limit=11,
+        flops=2 * rows * 2 * enc_c * 3 * 4 * stem_c,
+        name="dec_conv",
+    )
+    came = lax.ppermute(send, "chan", across)
+
+    centre = gated(centre, send)
+    beyond, beside = swap(centre, 2), swap(centre, 1)
+    (taps,) = call(
+        functools.partial(taps_kernel, pairs=pairs, devices=devices),
+        [place] + [blocks[r] for r in range(devices)] + [stem_w.T],
+        [((KW * stem_c, 2 * pairs * devices), BF16)],
+        limit=12,
+        name="stem_taps",
+    )
+    came, beyond, beside = gated((came, beyond, beside), taps)
+    pooled_all = [centre, beside, beyond, swap(beyond, 1)]
+
+    pred, sums, low, high = call(
+        functools.partial(slope_kernel, pairs=pairs, total=total, scale=1.0 / math.sqrt(2 * total)),
+        [place, part, came, targets_at],
+        [
+            ((2, pairs, 2 * stem_c), BF16),
+            ((2, rows, 2 * stem_c), BF16),
+            ((2, rows, stem_c), BF16),
+            ((2, rows, stem_c), BF16),
+        ],
+        [((rows + 8, 2 * stem_c), F32)],
+        limit=7,
+        name="out_slope",
+    )
+    sums_oth = lax.ppermute(sums, "chan", cores)
+    (pre,) = call(
+        functools.partial(back_kernel, pairs=pairs),
+        [
+            sums,
+            sums_oth,
+            dec_own.reshape(KW, 2 * stem_c, enc_c),
+            dec_oth.reshape(KW, 2 * stem_c, enc_c),
+            slope,
+        ],
+        [((2, pairs, enc_c), BF16)],
+        [((2, rows, 2 * stem_c), F32)],
+        limit=11,
+        flops=2 * pairs * KW * 4 * stem_c * enc_c,
+        name="up_grad",
+    )
+    (pred,) = call(
+        pred_kernel,
+        [place, pred],
+        [((stem_c, 2 * pairs), BF16)],
+        [((2 * pairs, 128), F32)],
+        limit=5,
+        name="pred",
+    )
+    pred = pred.T
+
+    def link(steps):
+        out = []
+        for s in range(devices):
+            for step in steps:
+                t = (s + step) % devices
+                for x in range(2):
+                    out.append((s * 4 + 2 * x + t % 2, t * 4 + 2 * x + (t + step) % 2))
+        return out
+
+    def to_owner(first, second, gate=None):
+        def piece(step):
+            return jnp.where(lax.rem(seq + step, devices) < 2, first, second)
+
+        near = lax.ppermute(piece(2 - parity), ("seq", "chan"), link((1, 2)))
+        far = lax.ppermute(piece(3), ("seq", "chan"), link((3,)))
+        local = piece(0)
+        if gate is not None:
+            near, far = gated((near, far), gate)
+        mine = [jnp.where(parity == 0, local, near), jnp.where(parity == 0, near, far)]
+        return mine, [lax.ppermute(m, "chan", cores) for m in mine]
+
+    sums_mine, sums_came = to_owner(low, high)
+    pre = pre.reshape(2 * pairs, enc_c)
+    pre_oth = lax.ppermute(pre, "chan", across)
+    pre_oth = gated(pre_oth, (sums_mine, pooled_all))
+
+    (g_dec,) = call(
+        functools.partial(dec_grad_kernel, pairs=pairs),
+        [place] + sums_mine + sums_came + pooled_all,
+        [((KW, stem_c, enc_c), F32)],
+        [
+            ((2, rows, stem_c), F32),
+            ((KW, devices * pairs, stem_c), BF16),
+            ((devices * pairs, enc_c), BF16),
+        ],
+        limit=12,
+        flops=2 * KW * stem_c * devices * pairs * enc_c,
+        name="dec_grad",
+    )
+    pre_mine, pre_came = to_owner(
+        jnp.where(hi == 0, pre, pre_oth), jnp.where(hi == 0, pre_oth, pre), (g_dec, pred)
+    )
+    g_dec = g_dec.transpose(1, 0, 2)
+    pre_slots = pre_mine + pre_came
+    g_enc = pl.pallas_call(
+        enc_grad_kernel,
+        grid=(KW,),
+        in_specs=[SCALARS, pl.BlockSpec((stem_c, 2 * pairs * devices), lambda k: (k, 0))]
+        + [whole(p.shape) for p in pre_slots],
+        out_specs=pl.BlockSpec((stem_c, enc_c), lambda k: (k, 0)),
+        out_shape=jax.ShapeDtypeStruct((KW * stem_c, enc_c), F32),
+        scratch_shapes=[pltpu.VMEM((2 * pairs * devices, enc_c), BF16)],
+        compiler_params=pltpu.CompilerParams(vmem_limit_bytes=9 * MIB),
+        name="enc_grad",
+    )(place, taps, *pre_slots)
+    g_enc = g_enc.reshape(KW, stem_c, enc_c).transpose(2, 0, 1)
+    return (pred, g_enc, g_dec)
 
 
 def extended(block, sides, width):
@@ -23,11 +583,6 @@
         high = lax.ppermute(lax.slice_in_dim(block, 0, width, axis=dim), axis, backward)
         block = jnp.concatenate([low, block, high], axis=dim)
     return block
-
-
-def gelu_value(value):
-    inner = jnp.tanh(SQRT_TWO_PI * (value + CUBIC * value * value * value))
-    return 0.5 * value * (1.0 + inner)
 
 
 def gelu_slope(value):
@@ -86,7 +641,7 @@
     )
 
 
-def shards(dna_bases, w_stem, w_enc, w_dec, targets):
+def general_shards(dna_bases, w_stem, w_enc, w_dec, targets):
     row_count = dna_bases.shape[0]
     devices = lax.axis_size("seq")
     length = row_count * devices
@@ -120,8 +675,9 @@
 
 
 def solution(mesh):
+    sizes = mesh.shape["seq"], mesh.shape["chan"]
     return jax.shard_map(
-        shards,
+        shards if sizes == (4, 4) else general_shards,
         mesh=mesh,
         in_specs=(
             P(("groups", "seq")),

time: 407 us -> 104 us (0.26)
  waiting for transfers between devices: 297 us -> 30.2 us
  matrix products: 36.9 us -> 0 us
  Pallas kernels: 0 us -> 33.4 us
  other arithmetic: 15.4 us -> 1.49 us
  between operations: 14.3 us -> 0.92 us
  blocking collectives: 8.34 us -> 0 us
  starting transfers between devices: 21.9 us -> 26.4 us
    reduce_scatter x4 -> x0, waiting for transfers between devices: 271 us -> none  [the longest x2 206 us: weight_grad(): lax.psum_scatter(lax.optimization_barrier(rounded).astype(jnp.float32), '...]
    dot_general x30 -> x0, matrix products: 36.9 us -> none  [the longest x15 21.7 us: conv_rows(): lax.dot_general(padded[k:k + row_count], weight[:, k, :], (((1,), (1,)),...]
    pallas_call x0 -> x14, Pallas kernels: none -> 33.4 us  [the longest x10 23.8 us: call(): pl.pallas_call(kernel, in_specs=specs, out_specs=[whole(s) for s, _ in ou...]
    ppermute x8 -> x24, waiting for transfers between devices: 12.2 us -> 30.2 us  [the longest x2 14.9 us: to_owner(): near = lax.ppermute(piece(2 - parity), ('seq', 'chan'), link((1, 2)))]
    all_gather x1 -> x0, waiting for transfers between devices: 14 us -> none  [channel_gather(): return lax.all_gather(block, 'chan', axis=1, tiled=True)]
    convert_element_type x6 -> x0, other arithmetic: 11.4 us -> none  [the longest x2 6.34 us: weight_grad(): lax.optimization_barrier(rounded).astype(jnp.float32)]
    unnamed x31 -> x52, local copies, waits for them, and re-layouts: 0.12 us -> 11.3 us
    all_gather x1 -> x0, blocking collectives: 8.34 us -> none  [channel_gather(): return lax.all_gather(block, 'chan', axis=1, tiled=True)]
  transfers between devices with their start and end apart: 13 -> 24, of which waited for: 9 -> 11; matrix products, arithmetic and copies ran while one was open for 6% -> 1% of each run, Pallas kernels for 0% -> 17%
where the time goes in v2:
time: 104 us
  Pallas kernels  33.4 us (32%)
  waiting for transfers between devices  30.2 us (29%)
  starting transfers between devices  26.4 us (25%)
  local copies, waits for them, and re-layouts  11.6 us (11%)
  other arithmetic  1.49 us (1%)
    pallas_call x10, Pallas kernels, call(): pl.pallas_call(kernel, in_specs=specs, out_specs=[whole(s) for s, _ in ou...  23.8 us
    ppermute x2, waiting for transfers between devices, to_owner(): near = lax.ppermute(piece(2 - parity), ('seq', 'chan'), link((1, 2)))  14.9 us
    unnamed x52, local copies, waits for them, and re-layouts  11.3 us
    ppermute x5, starting transfers between devices, ring(): lax.ppermute(array, 'seq', [(i, (i + step) % devices) for i in range(devi...  9.01 us
    ppermute x3, waiting for transfers between devices, swap(): lax.ppermute(array, 'seq', [(i, i ^ distance) for i in range(devices)])  7.69 us
    ppermute x3, starting transfers between devices, swap(): lax.ppermute(array, 'seq', [(i, i ^ distance) for i in range(devices)])  4.59 us
    pallas_call x1, Pallas kernels, shards(): pl.pallas_call(enc_grad_kernel, grid=(KW,), in_specs=[SCALARS, pl.BlockSp...  4.57 us
    ppermute x4, starting transfers between devices, to_owner(): return (mine, [lax.ppermute(m, 'chan', cores) for m in mine])  4.39 us
  transfers between devices with their start and end apart: 24, of which 11 were waited for; matrix products, arithmetic and copies ran while one was open for 1% of the time, Pallas kernels for 17%

profile of v2, /device:TPU:0, one launch (start us, length us, event | category | flops | bytes accessed | tf_op | source)
XLA Modules:
  0.0 104.1 jit_solution(1813719290206461447)
XLA Ops:
  0.7 1.8 %copy-done.3 = bf16[1536,5,192]{0,2,1:T(8,128)(2,1)S(1)} copy-done((bf16[1536,5,192]{0,2,1:T(8,128)(2,1)S(1)}, bf16[1536,5,192]{0,2,1:T(8,128)(2,1)}, u32[]{:S(2)}) %copy-start.3) | copy-done | bytes 2949144
  2.6 1.9 %enc_pick.1 = bf16[5,192,768]{2,1,0:T(8,128)(2,1)} custom-call(s32[4]{0:T(128)S(1)} %pad_add_fusion.place, bf16[5,192,1536]{2,1,0:T(8,128)(2,1)S(1)} %bitcast.28), custom_call_target="tpu_custom_call" | custom-call | tf_op jit(solution)/shard_map/enc_pick/pallas_call | solution.py:349
  5.3 3.0 %collective-permute-start = (s32[2,256]{1,0:T(2,128)S(1)}, s32[2,256]{1,0:T(2,128)S(1)}, u32[]{:S(2)}, u32[]{:S(2)}) collective-permute-start(s32[2,256]{1,0:T(2,128)S(1)} %bitcast.37), channel_id=1, source_target_pairs={{0,4},{4,8},{8,12},{12,0},{1,5},{5,9},{9,13},{13,1},{2,6},{6,10},{... | collective-permute-start | bytes 6152 | tf_op jit(solution)/shard_map/ppermute | solution.py:338
  8.4 2.1 %collective-permute-start.1 = (s32[2,256]{1,0:T(2,128)S(1)}, s32[2,256]{1,0:T(2,128)S(1)}, u32[]{:S(2)}, u32[]{:S(2)}) collective-permute-start(s32[2,256]{1,0:T(2,128)S(1)} %bitcast.38), channel_id=1, source_target_pairs={{0,12},{4,0},{8,4},{12,8},{1,13},{5,1},{9,5},{13,9},{2,14},{6,2},{... | collective-permute-start | bytes 6152 | tf_op jit(solution)/shard_map/ppermute | solution.py:338
  10.4 2.5 %dec_pick.1 = (bf16[5,2,192,384]{3,2,1,0:T(8,128)(2,1)S(1)}, bf16[5,2,192,384]{3,2,1,0:T(8,128)(2,1)}, bf16[3,2,2,192,384]{4,3,2,1,0:T(8,128)(2,1)S(1)}) custom-call(s32[4]{0:T(128)S(1)} %pad_add_fusion.place, bf16[5,4,192,384]{3,2,1,0:T(8,128)(2,1)S(1)} %bitcast.26, bf16[5,4,192,384]{3,2,1,0:T(8,128)(2,1)S(1)} %bitcast.27), custom_call_target="tpu_custom_call" | custom-call | tf_op jit(solution)/shard_map/dec_pick/pallas_call | solution.py:365
  12.9 1.3 %copy-done.5 = bf16[3,2,2,192,384]{4,3,2,1,0:T(8,128)(2,1)} copy-done((bf16[3,2,2,192,384]{4,3,2,1,0:T(8,128)(2,1)}, bf16[3,2,2,192,384]{4,3,2,1,0:T(8,128)(2,1)S(1)}, u32[]{:S(2)}) %copy-start.5) | copy-done | bytes 1769496
  14.2 1.1 %copy-done.7 = bf16[5,2,192,384]{3,2,1,0:T(8,128)(2,1)} copy-done((bf16[5,2,192,384]{3,2,1,0:T(8,128)(2,1)}, bf16[5,2,192,384]{3,2,1,0:T(8,128)(2,1)S(1)}, u32[]{:S(2)}) %copy-start.7) | copy-done | bytes 1474584
  15.4 2.9 %stem_conv.1 = (f32[544,768]{1,0:T(8,128)S(1)}, bf16[2,272,192]{2,1,0:T(8,128)(2,1)S(1)}, bf16[6,272,192]{2,1,0:T(8,128)(2,1)S(1)}) custom-call(s32[4]{0:T(128)S(1)} %pad_add_fusion.place, s32[2,256]{1,0:T(2,128)S(1)} %bitcast.39, s32[2,256]{1,0:T(2,128)S(1)} %collective-permute-done.1.after.refs_3_, s32[2,256]{1,0:T(2,128)S(1)} %collective-permute-done.before.refs_1_, ...), custom_call_target="tpu_custom_call" | custom-call | flops 802160640 | bytes 5477392 | tf_op jit(solution)/shard_map/stem_conv/pallas_call | solution.py:307
  18.3 3.8 %enc_conv.1 = (f32[544,384]{1,0:T(8,128)S(1)}, bf16[544,384]{1,0:T(8,128)(2,1)}) custom-call(s32[4]{0:T(128)S(1)} %pad_add_fusion.place, f32[544,768]{1,0:T(8,128)S(1)} %get-tuple-element.38.acc, bf16[6,272,192]{2,1,0:T(8,128)(2,1)S(1)} %get-tuple-element.39.lhs, bf16[5,192,768]{2,1,0:T(8,128)(2,1)} %collective-permute-done.3.w_oth), custom_call_target="tpu_custom_call" | custom-call | flops 802160640 | bytes 5025808 | tf_op jit(solution)/shard_map/enc_conv/pallas_call | solution.py:307
  22.1 1.7 %collective-permute-start.4 = (bf16[544,384]{1,0:T(8,128)(2,1)}, bf16[544,384]{1,0:T(8,128)(2,1)S(1)}, u32[]{:S(2)}, u32[]{:S(2)}) collective-permute-start(bf16[544,384]{1,0:T(8,128)(2,1)} %get-tuple-element.41), channel_id=1, source_target_pairs={{0,2},{1,3},{2,0},{3,1},{4,6},{5,7},{6,4},{7,5},{8,10},{9,11},{10,... | collective-permute-start | bytes 1253384 | tf_op jit(solution)/shard_map/ppermute | solution.py:410
  23.8 3.8 %collective-permute-start.7 = (bf16[192,128]{1,0:T(8,128)(2,1)S(1)}, bf16[192,128]{1,0:T(8,128)(2,1)S(1)}, u32[]{:S(2)}, u32[]{:S(2)}) collective-permute-start(bf16[192,128]{1,0:T(8,128)(2,1)S(1)} %get-tuple-element.72), channel_id=1, source_target_pairs={{0,12},{4,0},{8,4},{12,8},{1,13},{5,1},{9,5},{13,9},{2,14},{6,2},{... | collective-permute-start | bytes 147464 | tf_op jit(solution)/shard_map/ppermute | solution.py:338
  27.8 2.2 %collective-permute-done.6.before = bf16[192,128]{1,0:T(8,128)(2,1)S(1)} collective-permute-done((bf16[192,128]{1,0:T(8,128)(2,1)S(1)}, bf16[192,128]{1,0:T(8,128)(2,1)S(1)}, u32[]{:S(2)}, u32[]{:S(2)}) %collective-permute-start.6) | collective-permute-done | bytes 49184 | tf_op jit(solution)/shard_map/ppermute | solution.py:338
  30.0 0.9 targets.1
  31.0 0.6 dec_combine.1
  31.6 0.5 collective-permute-done.8.refs_2_
  32.1 0.6 copy-done.22
  32.7 1.6 %collective-permute-done.4.came = bf16[544,384]{1,0:T(8,128)(2,1)S(1)} collective-permute-done((bf16[544,384]{1,0:T(8,128)(2,1)}, bf16[544,384]{1,0:T(8,128)(2,1)S(1)}, u32[]{:S(2)}, u32[]{:S(2)}) %collective-permute-start.4) | collective-permute-done | bytes 417824 | tf_op jit(solution)/shard_map/ppermute | solution.py:410
  34.3 1.3 %gelu_pool.1 = (bf16[272,384]{1,0:T(8,128)(2,1)S(1)}, bf16[256,384]{1,0:T(8,128)(2,1)S(1)}, f32[2,256,384]{2,1,0:T(8,128)S(1)}) custom-call(s32[4]{0:T(128)S(1)} %pad_add_fusion.place, f32[544,384]{1,0:T(8,128)S(1)} %get-tuple-element.40.keep, bf16[544,384]{1,0:T(8,128)(2,1)S(1)} %collective-permute-done.4.came), custom_call_target="tpu_custom_call" | custom-call | bytes 2445328 | tf_op jit(solution)/shard_map/gelu_pool/pallas_call | solution.py:307
  35.6 0.9 copy-done.9
  36.5 1.5 %collective-permute-done.9.oth = bf16[272,384]{1,0:T(8,128)(2,1)S(1)} collective-permute-done((bf16[272,384]{1,0:T(8,128)(2,1)S(1)}, bf16[272,384]{1,0:T(8,128)(2,1)S(1)}, u32[]{:S(2)}, u32[]{:S(2)}) %collective-permute-start.9) | collective-permute-done | bytes 208928 | tf_op jit(solution)/shard_map/ppermute | solution.py:446
  38.0 2.3 %dec_conv.1 = (f32[272,768]{1,0:T(8,128)S(1)}, bf16[272,768]{1,0:T(8,128)(2,1)}) custom-call(bf16[272,384]{1,0:T(8,128)(2,1)S(1)} %get-tuple-element.47.own, bf16[272,384]{1,0:T(8,128)(2,1)S(1)} %collective-permute-done.9.oth, bf16[3,768,384]{2,1,0:T(8,128)(2,1)S(1)} %bitcast.31, bf16[3,768,384]{2,1,0:T(8,128)(2,1)S(1)} %bitcast.30, ...), custom_call_target="tpu_custom_call" | custom-call | flops 962592768 | bytes 6045696 | tf_op jit(solution)/shard_map/dec_conv/pallas_call | solution.py:307
  40.3 1.7 %collective-permute-start.10 = (bf16[272,768]{1,0:T(8,128)(2,1)}, bf16[272,768]{1,0:T(8,128)(2,1)S(1)}, u32[]{:S(2)}, u32[]{:S(2)}) collective-permute-start(bf16[272,768]{1,0:T(8,128)(2,1)} %get-tuple-element.49), channel_id=1, source_target_pairs={{0,2},{1,3},{2,0},{3,1},{4,6},{5,7},{6,4},{7,5},{8,10},{9,11},{10,... | collective-permute-start | bytes 1253384 | tf_op jit(solution)/shard_map/ppermute | solution.py:463
  41.9 0.8 collective-permute-start.11
  42.7 1.6 %collective-permute-start.12 = (bf16[256,384]{1,0:T(8,128)(2,1)S(1)}, bf16[256,384]{1,0:T(8,128)(2,1)}, u32[]{:S(2)}, u32[]{:S(2)}) collective-permute-start(bf16[256,384]{1,0:T(8,128)(2,1)S(1)} %get-tuple-element.51.pool0), channel_id=1, source_target_pairs={{0,4},{4,0},{8,12},{12,8},{1,5},{5,1},{9,13},{13,9},{2,6},{6,2},{1... | collective-permute-start | bytes 589832 | tf_op jit(solution)/shard_map/ppermute | solution.py:341
  44.5 2.3 %stem_taps.1.taps = bf16[960,2048]{1,0:T(8,128)(2,1)S(1)} custom-call(s32[4]{0:T(128)S(1)} %pad_add_fusion.place, s32[2,256]{1,0:T(2,128)S(1)} %bitcast.41, s32[2,256]{1,0:T(2,128)S(1)} %copy-done.19, s32[2,256]{1,0:T(2,128)S(1)} %copy-done.23, s32[2,256]{1,0:T(2,128)S(1)} %copy-done.21, bf16[192,20]{1,0:T(8,128)(2,1)S(1)} %bitcast.36), custom_call_target="tpu_custom_call" | custom-call | bytes 3948048 | tf_op jit(solution)/shard_map/stem_taps/pallas_call | solution.py:307
  46.7 1.9 %copy-done = bf16[960,2048]{1,0:T(8,128)(2,1)} copy-done((bf16[960,2048]{1,0:T(8,128)(2,1)}, bf16[960,2048]{1,0:T(8,128)(2,1)S(1)}, u32[]{:S(2)}) %copy-start) | copy-done | bytes 3932184
  48.6 4.5 %collective-permute-done.11.pool2 = bf16[256,384]{1,0:T(8,128)(2,1)} collective-permute-done((bf16[256,384]{1,0:T(8,128)(2,1)S(1)}, bf16[256,384]{1,0:T(8,128)(2,1)}, u32[]{:S(2)}, u32[]{:S(2)}) %collective-permute-start.11) | collective-permute-done | bytes 196640 | tf_op jit(solution)/shard_map/ppermute | solution.py:341
  53.4 0.8 copy-done.12
  54.2 1.0 copy-done.13
  55.2 1.7 %out_slope.1 = (bf16[2,256,384]{2,1,0:T(8,128)(2,1)S(1)}, bf16[2,272,384]{2,1,0:T(8,128)(2,1)}, bf16[2,272,192]{2,1,0:T(8,128)(2,1)S(1)}, bf16[2,272,192]{2,1,0:T(8,128)(2,1)S(1)}) custom-call(s32[4]{0:T(128)S(1)} %pad_add_fusion.place, f32[272,768]{1,0:T(8,128)S(1)} %get-tuple-element.48.part, bf16[272,768]{1,0:T(8,128)(2,1)S(1)} %copy-done.13, ...), custom_call_target="tpu_custom_call" | custom-call | bytes 2899984 | tf_op jit(solution)/shard_map/out_slope/pallas_call | solution.py:307
  56.9 0.8 copy-done.14
  57.6 0.8 broadcast_select_fusion.5
  58.7 1.4 %collective-permute-start.16 = (bf16[2,272,192]{2,1,0:T(8,128)(2,1)}, bf16[2,272,192]{2,1,0:T(8,128)(2,1)}, u32[]{:S(2)}, u32[]{:S(2)}) collective-permute-start(bf16[2,272,192]{2,1,0:T(8,128)(2,1)} %get-tuple-element.66), channel_id=1, source_target_pairs={{1,12},{3,14},{4,1},{6,3},{9,4},{11,6},{12,9},{14,11},{17,28},{19,... | collective-permute-start | bytes 626696 | tf_op jit(solution)/shard_map/ppermute | solution.py:530
  60.1 1.1 %copy-done.10 = f32[2,256,384]{2,1,0:T(8,128)S(1)} copy-done((f32[2,256,384]{2,1,0:T(8,128)S(1)}, f32[2,256,384]{2,1,0:T(8,128)}, u32[]{:S(2)}) %copy-start.10) | copy-done | bytes 786456
  61.2 2.9 %up_grad.1 = bf16[2,256,384]{2,1,0:T(8,128)(2,1)S(1)} custom-call(bf16[2,272,384]{2,1,0:T(8,128)(2,1)} %get-tuple-element.54.own, bf16[2,272,384]{2,1,0:T(8,128)(2,1)S(1)} %collective-permute-done.13.oth, bf16[5,384,384]{2,1,0:T(8,128)(2,1)S(1)} %bitcast.33, bf16[5,384,384]{2,1,0:T(8,128)(2,1)} %bitcast.15.w_oth, f32[2,256,384]{2,1,0:T(8,128)S(1)} %copy-done.10), custom_call_target="tpu_custom_call" | custom-call | flops 754974720 | bytes 4964352 | tf_op jit(solution)/shard_map/up_grad/pallas_call | solution.py:307
  64.1 1.0 %collective-permute-start.14 = (bf16[512,384]{1,0:T(8,128)(2,1)S(1)}, bf16[512,384]{1,0:T(8,128)(2,1)S(1)}, u32[]{:S(2)}, u32[]{:S(2)}) collective-permute-start(bf16[512,384]{1,0:T(8,128)(2,1)S(1)} %bitcast.32), channel_id=1, source_target_pairs={{0,2},{1,3},{2,0},{3,1},{4,6},{5,7},{6,4},{7,5},{8,10},{9,11},{10,... | collective-permute-start | bytes 1179656 | tf_op jit(solution)/shard_map/ppermute | solution.py:539
  65.1 2.2 %collective-permute-start.17 = (bf16[256,384]{1,0:T(8,128)(2,1)}, bf16[256,384]{1,0:T(8,128)(2,1)S(1)}, u32[]{:S(2)}, u32[]{:S(2)}) collective-permute-start(bf16[256,384]{1,0:T(8,128)(2,1)} %collective-permute-done.11.pool2), channel_id=1, source_target_pairs={{0,4},{4,0},{8,12},{12,8},{1,5},{5,1},{9,13},{13,9},{2,6},{6,2},{1... | collective-permute-start | bytes 589832 | tf_op jit(solution)/shard_map/ppermute | solution.py:341
  67.4 7.0 %collective-permute-done.15 = bf16[2,272,192]{2,1,0:T(8,128)(2,1)S(1)} collective-permute-done((bf16[2,272,192]{2,1,0:T(8,128)(2,1)}, bf16[2,272,192]{2,1,0:T(8,128)(2,1)S(1)}, u32[]{:S(2)}, u32[]{:S(2)}) %collective-permute-start.15) | collective-permute-done | bytes 208928 | tf_op jit(solution)/shard_map/ppermute | solution.py:529
  74.4 2.9 %collective-permute-done.17.pool3 = bf16[256,384]{1,0:T(8,128)(2,1)S(1)} collective-permute-done((bf16[256,384]{1,0:T(8,128)(2,1)}, bf16[256,384]{1,0:T(8,128)(2,1)S(1)}, u32[]{:S(2)}, u32[]{:S(2)}) %collective-permute-start.17) | collective-permute-done | bytes 196640 | tf_op jit(solution)/shard_map/ppermute | solution.py:341
  77.5 1.3 %collective-permute-start.18 = (bf16[512,384]{1,0:T(8,128)(2,1)S(1)}, bf16[512,384]{1,0:T(8,128)(2,1)S(1)}, u32[]{:S(2)}, u32[]{:S(2)}) collective-permute-start(bf16[512,384]{1,0:T(8,128)(2,1)S(1)} %broadcast_select_fusion.1), channel_id=1, source_target_pairs={{1,4},{3,6},{0,8},{2,10},{4,9},{6,11},{5,13},{7,15},{9,12},{11,14}... | collective-permute-start | bytes 1179656 | tf_op jit(solution)/shard_map/ppermute | solution.py:529
  78.8 0.7 collective-permute-start.19
  79.4 3.7 %collective-permute-start.20 = (bf16[2,272,192]{2,1,0:T(8,128)(2,1)S(1)}, bf16[2,272,192]{2,1,0:T(8,128)(2,1)S(1)}, u32[]{:S(2)}, u32[]{:S(2)}) collective-permute-start(bf16[2,272,192]{2,1,0:T(8,128)(2,1)S(1)} %get-tuple-element.71.own0), channel_id=1, source_target_pairs={{0,1},{1,0},{2,3},{3,2},{4,5},{5,4},{6,7},{7,6},{8,9},{9,8},{10,11... | collective-permute-start | bytes 626696 | tf_op jit(solution)/shard_map/ppermute | solution.py:535
  83.3 1.7 %pred_.1 = bf16[192,512]{1,0:T(8,128)(2,1)} custom-call(s32[4]{0:T(128)S(1)} %pad_add_fusion.place, bf16[2,256,384]{2,1,0:T(8,128)(2,1)S(1)} %copy-done.15), custom_call_target="tpu_custom_call" | custom-call | bytes 589840 | tf_op jit(solution)/shard_map/pred/pallas_call | solution.py:307
  85.0 4.1 %dec_grad.1 = f32[5,192,384]{2,1,0:T(8,128)} custom-call(s32[4]{0:T(128)S(1)} %pad_add_fusion.place, bf16[2,272,192]{2,1,0:T(8,128)(2,1)S(1)} %get-tuple-element.71.own0, bf16[2,272,192]{2,1,0:T(8,128)(2,1)S(1)} %get-tuple-element.70.own1, bf16[2,272,192]{2,1,0:T(8,128)(2,1)S(1)} %collective-permute-done.20.oth0, ...), custom_call_target="tpu_custom_call" | custom-call | flops 754974720 | bytes 3096592 | tf_op jit(solution)/shard_map/dec_grad/pallas_call | solution.py:307
  89.1 8.0 %collective-permute-done.18 = bf16[512,384]{1,0:T(8,128)(2,1)S(1)} collective-permute-done((bf16[512,384]{1,0:T(8,128)(2,1)S(1)}, bf16[512,384]{1,0:T(8,128)(2,1)S(1)}, u32[]{:S(2)}, u32[]{:S(2)}) %collective-permute-start.18) | collective-permute-done | bytes 393248 | tf_op jit(solution)/shard_map/ppermute | solution.py:529
  97.8 1.2 %collective-permute-done.22.oth0 = bf16[512,384]{1,0:T(8,128)(2,1)S(1)} collective-permute-done((bf16[512,384]{1,0:T(8,128)(2,1)S(1)}, bf16[512,384]{1,0:T(8,128)(2,1)S(1)}, u32[]{:S(2)}, u32[]{:S(2)}) %collective-permute-start.22) | collective-permute-done | bytes 393248 | tf_op jit(solution)/shard_map/ppermute | solution.py:535
  99.0 0.6 collective-permute-done.23.oth1
  99.6 4.6 %enc_grad.1 = f32[960,384]{1,0:T(8,128)} custom-call(s32[4]{0:T(128)S(1)} %pad_add_fusion.place, bf16[960,2048]{1,0:T(8,128)(2,1)S(1)} %copy-done.1, bf16[512,384]{1,0:T(8,128)(2,1)S(1)} %get-tuple-element.69.own0, bf16[512,384]{1,0:T(8,128)(2,1)S(1)} %get-tuple-element.68.own1, bf16[512,384]{1,0:T(8,128)(2,1)S(1)} %collective-permute-done.22.oth0, ...), custom_call_target="tpu_custom_call" | custom-call | tf_op jit(solution)/shard_map/enc_grad/pallas_call | solution.py:560
  (78 shorter events, 2.9 us)
Async XLA Ops:
  0.7 1.8 %copy-start.3 = (bf16[1536,5,192]{0,2,1:T(8,128)(2,1)S(1)}, bf16[1536,5,192]{0,2,1:T(8,128)(2,1)}, u32[]{:S(2)}) copy-start(bf16[1536,5,192]{0,2,1:T(8,128)(2,1)} %param.7) | copy-start | bytes 8847364
  2.6 2.4 %copy-start.24 = (bf16[192,5,4]{0,2,1:T(4,128)(2,1)S(1)}, bf16[192,5,4]{0,2,1:T(4,128)(2,1)}, u32[]{:S(2)}) copy-start(bf16[192,5,4]{0,2,1:T(4,128)(2,1)} %param.6) | copy-start | bytes 23044
  2.6 2.5 %copy-start.25 = (s32[512]{0:T(512)S(1)}, s32[512]{0:T(512)}, u32[]{:S(2)}) copy-start(s32[512]{0:T(512)} %param.5) | copy-start | bytes 6148
  2.6 7.9 %copy-start.2 = (bf16[768,5,384]{2,0,1:T(8,128)(2,1)S(1)}, bf16[768,5,384]{2,0,1:T(8,128)(2,1)}, u32[]{:S(2)}) copy-start(bf16[768,5,384]{2,0,1:T(8,128)(2,1)} %param.8) | copy-start | bytes 8847364
  4.5 13.8 %collective-permute-start.3 = (bf16[5,192,768]{2,1,0:T(8,128)(2,1)}, bf16[5,192,768]{2,1,0:T(8,128)(2,1)}, u32[]{:S(2)}, u32[]{:S(2)}) collective-permute-start(bf16[5,192,768]{2,1,0:T(8,128)(2,1)} %enc_pick.1), channel_id=1, source_target_pairs={{0,1},{1,0},{2,3},{3,2},{4,5},{5,4},{6,7},{7,6},{8,9},{9,8},{10,11... | collective-permute-start | bytes 4423688 | tf_op jit(solution)/shard_map/ppermute | solution.py:361
  5.0 10.4 %collective-permute-start.2 = (bf16[20,192]{1,0:T(8,128)(2,1)S(1)}, bf16[20,192]{1,0:T(8,128)(2,1)S(1)}, u32[]{:S(2)}, u32[]{:S(2)}) collective-permute-start(bf16[20,192]{1,0:T(8,128)(2,1)S(1)} %reshape.35.stem_own), channel_id=1, source_target_pairs={{0,1},{1,0},{2,3},{3,2},{4,5},{5,4},{6,7},{7,6},{8,9},{9,8},{10,11... | collective-permute-start | bytes 23048 | tf_op jit(solution)/shard_map/ppermute | solution.py:347
  5.3 22.3 %copy-start.16 = (s32[256,2]{0,1:T(2,128)}, s32[256,2]{0,1:T(2,128)S(1)}, u32[]{:S(2)}) copy-start(s32[256,2]{0,1:T(2,128)S(1)} %copy.11) | copy-start | bytes 6148
  5.3 10.0 %collective-permute-start = (s32[2,256]{1,0:T(2,128)S(1)}, s32[2,256]{1,0:T(2,128)S(1)}, u32[]{:S(2)}, u32[]{:S(2)}) collective-permute-start(s32[2,256]{1,0:T(2,128)S(1)} %bitcast.37), channel_id=1, source_target_pairs={{0,4},{4,8},{8,12},{12,0},{1,5},{5,9},{9,13},{13,1},{2,6},{6,10},{... | collective-permute-start | bytes 6152 | tf_op jit(solution)/shard_map/ppermute | solution.py:338
  8.4 7.0 %collective-permute-start.1 = (s32[2,256]{1,0:T(2,128)S(1)}, s32[2,256]{1,0:T(2,128)S(1)}, u32[]{:S(2)}, u32[]{:S(2)}) collective-permute-start(s32[2,256]{1,0:T(2,128)S(1)} %bitcast.38), channel_id=1, source_target_pairs={{0,12},{4,0},{8,4},{12,8},{1,13},{5,1},{9,5},{13,9},{2,14},{6,2},{... | collective-permute-start | bytes 6152 | tf_op jit(solution)/shard_map/ppermute | solution.py:338
  10.4 4.9 %copy-start.4 = (bf16[1536,5,192]{0,2,1:T(8,128)(2,1)S(1)}, bf16[1536,5,192]{0,2,1:T(8,128)(2,1)}, u32[]{:S(2)}) copy-start(bf16[1536,5,192]{0,2,1:T(8,128)(2,1)} %param.7) | copy-start | bytes 8847364
  12.9 1.3 %copy-start.5 = (bf16[3,2,2,192,384]{4,3,2,1,0:T(8,128)(2,1)}, bf16[3,2,2,192,384]{4,3,2,1,0:T(8,128)(2,1)S(1)}, u32[]{:S(2)}) copy-start(bf16[3,2,2,192,384]{4,3,2,1,0:T(8,128)(2,1)S(1)} %get-tuple-element.35) | copy-start | bytes 5308420
  14.2 1.1 %copy-start.7 = (bf16[5,2,192,384]{3,2,1,0:T(8,128)(2,1)}, bf16[5,2,192,384]{3,2,1,0:T(8,128)(2,1)S(1)}, u32[]{:S(2)}) copy-start(bf16[5,2,192,384]{3,2,1,0:T(8,128)(2,1)S(1)} %get-tuple-element.33) | copy-start | bytes 4423684
  15.3 2.9 %copy-start.18 = (s32[2,256]{1,0:T(2,128)}, s32[2,256]{1,0:T(2,128)S(1)}, u32[]{:S(2)}) copy-start(s32[2,256]{1,0:T(2,128)S(1)} %collective-permute-done.before.refs_1_) | copy-start | bytes 6148
  15.3 2.9 %copy-start.20 = (s32[2,256]{1,0:T(2,128)}, s32[2,256]{1,0:T(2,128)S(1)}, u32[]{:S(2)}) copy-start(s32[2,256]{1,0:T(2,128)S(1)} %collective-permute-done.1.after.refs_3_) | copy-start | bytes 6148
  18.3 5.5 %copy-start.11 = (bf16[512,192]{0,1:T(8,128)(2,1)S(1)}, bf16[512,192]{0,1:T(8,128)(2,1)}, u32[]{:S(2)}) copy-start(bf16[512,192]{0,1:T(8,128)(2,1)} %param.9) | copy-start | bytes 589828
  22.1 8.9 %collective-permute-start.5 = (bf16[5,2,192,384]{3,2,1,0:T(8,128)(2,1)}, bf16[5,2,192,384]{3,2,1,0:T(8,128)(2,1)S(1)}, u32[]{:S(2)}, u32[]{:S(2)}) collective-permute-start(bf16[5,2,192,384]{3,2,1,0:T(8,128)(2,1)} %get-tuple-element.42), channel_id=1, source_target_pairs={{0,1},{1,0},{2,3},{3,2},{4,5},{5,4},{6,7},{7,6},{8,9},{9,8},{10,11... | collective-permute-start | bytes 4423688 | tf_op jit(solution)/shard_map/ppermute | solution.py:415
  22.1 12.3 %collective-permute-start.4 = (bf16[544,384]{1,0:T(8,128)(2,1)}, bf16[544,384]{1,0:T(8,128)(2,1)S(1)}, u32[]{:S(2)}, u32[]{:S(2)}) collective-permute-start(bf16[544,384]{1,0:T(8,128)(2,1)} %get-tuple-element.41), channel_id=1, source_target_pairs={{0,2},{1,3},{2,0},{3,1},{4,6},{5,7},{6,4},{7,5},{8,10},{9,11},{10,... | collective-permute-start | bytes 1253384 | tf_op jit(solution)/shard_map/ppermute | solution.py:410
  23.8 6.3 %collective-permute-start.6 = (bf16[192,128]{1,0:T(8,128)(2,1)S(1)}, bf16[192,128]{1,0:T(8,128)(2,1)S(1)}, u32[]{:S(2)}, u32[]{:S(2)}) collective-permute-start(bf16[192,128]{1,0:T(8,128)(2,1)S(1)} %get-tuple-element.73), channel_id=1, source_target_pairs={{0,4},{4,8},{8,12},{12,0},{1,5},{5,9},{9,13},{13,1},{2,6},{6,10},{... | collective-permute-start | bytes 147464 | tf_op jit(solution)/shard_map/ppermute | solution.py:338
  23.8 6.2 %collective-permute-start.7 = (bf16[192,128]{1,0:T(8,128)(2,1)S(1)}, bf16[192,128]{1,0:T(8,128)(2,1)S(1)}, u32[]{:S(2)}, u32[]{:S(2)}) collective-permute-start(bf16[192,128]{1,0:T(8,128)(2,1)S(1)} %get-tuple-element.72), channel_id=1, source_target_pairs={{0,12},{4,0},{8,4},{12,8},{1,13},{5,1},{9,5},{13,9},{2,14},{6,2},{... | collective-permute-start | bytes 147464 | tf_op jit(solution)/shard_map/ppermute | solution.py:338
  27.6 4.5 %collective-permute-start.8 = (s32[2,256]{1,0:T(2,128)S(1)}, s32[2,256]{1,0:T(2,128)S(1)}, u32[]{:S(2)}, u32[]{:S(2)}) collective-permute-start(s32[2,256]{1,0:T(2,128)S(1)} %bitcast.40), channel_id=1, source_target_pairs={{0,8},{4,12},{8,0},{12,4},{1,9},{5,13},{9,1},{13,5},{2,10},{6,14},... | collective-permute-start | bytes 6152 | tf_op jit(solution)/shard_map/ppermute | solution.py:338
  31.0 7.0 %copy-start.6 = (bf16[3,2,2,192,384]{4,3,2,1,0:T(8,128)(2,1)S(1)}, bf16[3,2,2,192,384]{4,3,2,1,0:T(8,128)(2,1)}, u32[]{:S(2)}) copy-start(bf16[3,2,2,192,384]{4,3,2,1,0:T(8,128)(2,1)} %copy-done.5) | copy-start | bytes 5308420
  35.6 0.9 copy-start.9
  36.5 1.5 %collective-permute-start.9 = (bf16[272,384]{1,0:T(8,128)(2,1)S(1)}, bf16[272,384]{1,0:T(8,128)(2,1)S(1)}, u32[]{:S(2)}, u32[]{:S(2)}) collective-permute-start(bf16[272,384]{1,0:T(8,128)(2,1)S(1)} %get-tuple-element.47.own), channel_id=1, source_target_pairs={{0,1},{1,0},{2,3},{3,2},{4,5},{5,4},{6,7},{7,6},{8,9},{9,8},{10,11... | collective-permute-start | bytes 626696 | tf_op jit(solution)/shard_map/ppermute | solution.py:446
  38.0 6.5 %copy-start.17 = (s32[256,2]{0,1:T(2,128)S(1)}, s32[256,2]{0,1:T(2,128)}, u32[]{:S(2)}) copy-start(s32[256,2]{0,1:T(2,128)} %copy-done.16) | copy-start | bytes 6148
  38.0 6.5 %copy-start.19 = (s32[2,256]{1,0:T(2,128)S(1)}, s32[2,256]{1,0:T(2,128)}, u32[]{:S(2)}) copy-start(s32[2,256]{1,0:T(2,128)} %copy-done.18) | copy-start | bytes 6148
  38.0 6.5 %copy-start.21 = (s32[2,256]{1,0:T(2,128)S(1)}, s32[2,256]{1,0:T(2,128)}, u32[]{:S(2)}) copy-start(s32[2,256]{1,0:T(2,128)} %copy-done.20) | copy-start | bytes 6148
  38.0 6.5 %copy-start.23 = (s32[2,256]{1,0:T(2,128)S(1)}, s32[2,256]{1,0:T(2,128)}, u32[]{:S(2)}) copy-start(s32[2,256]{1,0:T(2,128)} %copy-done.22) | copy-start | bytes 6148
  40.3 13.2 %collective-permute-start.10 = (bf16[272,768]{1,0:T(8,128)(2,1)}, bf16[272,768]{1,0:T(8,128)(2,1)S(1)}, u32[]{:S(2)}, u32[]{:S(2)}) collective-permute-start(bf16[272,768]{1,0:T(8,128)(2,1)} %get-tuple-element.49), channel_id=1, source_target_pairs={{0,2},{1,3},{2,0},{3,1},{4,6},{5,7},{6,4},{7,5},{8,10},{9,11},{10,... | collective-permute-start | bytes 1253384 | tf_op jit(solution)/shard_map/ppermute | solution.py:463
  41.9 11.2 %collective-permute-start.11 = (bf16[256,384]{1,0:T(8,128)(2,1)S(1)}, bf16[256,384]{1,0:T(8,128)(2,1)}, u32[]{:S(2)}, u32[]{:S(2)}) collective-permute-start(bf16[256,384]{1,0:T(8,128)(2,1)S(1)} %get-tuple-element.51.pool0), channel_id=1, source_target_pairs={{0,8},{4,12},{8,0},{12,4},{1,9},{5,13},{9,1},{13,5},{2,10},{6,14},... | collective-permute-start | bytes 589832 | tf_op jit(solution)/shard_map/ppermute | solution.py:341
  42.7 10.7 %collective-permute-start.12 = (bf16[256,384]{1,0:T(8,128)(2,1)S(1)}, bf16[256,384]{1,0:T(8,128)(2,1)}, u32[]{:S(2)}, u32[]{:S(2)}) collective-permute-start(bf16[256,384]{1,0:T(8,128)(2,1)S(1)} %get-tuple-element.51.pool0), channel_id=1, source_target_pairs={{0,4},{4,0},{8,12},{12,8},{1,5},{5,1},{9,13},{13,9},{2,6},{6,2},{1... | collective-permute-start | bytes 589832 | tf_op jit(solution)/shard_map/ppermute | solution.py:341
  46.7 1.9 %copy-start = (bf16[960,2048]{1,0:T(8,128)(2,1)}, bf16[960,2048]{1,0:T(8,128)(2,1)S(1)}, u32[]{:S(2)}) copy-start(bf16[960,2048]{1,0:T(8,128)(2,1)S(1)} %stem_taps.1.taps) | copy-start | bytes 11796484
  48.6 11.4 %copy-start.8 = (bf16[5,2,192,384]{3,2,1,0:T(8,128)(2,1)S(1)}, bf16[5,2,192,384]{3,2,1,0:T(8,128)(2,1)}, u32[]{:S(2)}) copy-start(bf16[5,2,192,384]{3,2,1,0:T(8,128)(2,1)} %copy-done.7) | copy-start | bytes 4423684
  54.2 1.0 copy-start.13
  56.9 0.8 copy-start.14
  57.6 2.4 %collective-permute-start.13 = (bf16[2,272,384]{2,1,0:T(8,128)(2,1)}, bf16[2,272,384]{2,1,0:T(8,128)(2,1)S(1)}, u32[]{:S(2)}, u32[]{:S(2)}) collective-permute-start(bf16[2,272,384]{2,1,0:T(8,128)(2,1)} %get-tuple-element.54.own), channel_id=1, source_target_pairs={{0,1},{1,0},{2,3},{3,2},{4,5},{5,4},{6,7},{7,6},{8,9},{9,8},{10,11... | collective-permute-start | bytes 1253384 | tf_op jit(solution)/shard_map/ppermute | solution.py:490
  58.5 15.8 %collective-permute-start.15 = (bf16[2,272,192]{2,1,0:T(8,128)(2,1)}, bf16[2,272,192]{2,1,0:T(8,128)(2,1)S(1)}, u32[]{:S(2)}, u32[]{:S(2)}) collective-permute-start(bf16[2,272,192]{2,1,0:T(8,128)(2,1)} %get-tuple-element.67), channel_id=1, source_target_pairs={{1,4},{3,6},{0,8},{2,10},{4,9},{6,11},{5,13},{7,15},{9,12},{11,14}... | collective-permute-start | bytes 626696 | tf_op jit(solution)/shard_map/ppermute | solution.py:529
  58.7 15.6 %collective-permute-start.16 = (bf16[2,272,192]{2,1,0:T(8,128)(2,1)}, bf16[2,272,192]{2,1,0:T(8,128)(2,1)}, u32[]{:S(2)}, u32[]{:S(2)}) collective-permute-start(bf16[2,272,192]{2,1,0:T(8,128)(2,1)} %get-tuple-element.66), channel_id=1, source_target_pairs={{1,12},{3,14},{4,1},{6,3},{9,4},{11,6},{12,9},{14,11},{17,28},{19,... | collective-permute-start | bytes 626696 | tf_op jit(solution)/shard_map/ppermute | solution.py:530
  60.1 1.1 %copy-start.10 = (f32[2,256,384]{2,1,0:T(8,128)S(1)}, f32[2,256,384]{2,1,0:T(8,128)}, u32[]{:S(2)}) copy-start(f32[2,256,384]{2,1,0:T(8,128)} %copy-done.9) | copy-start | bytes 2359300
  64.1 13.2 %collective-permute-start.14 = (bf16[512,384]{1,0:T(8,128)(2,1)S(1)}, bf16[512,384]{1,0:T(8,128)(2,1)S(1)}, u32[]{:S(2)}, u32[]{:S(2)}) collective-permute-start(bf16[512,384]{1,0:T(8,128)(2,1)S(1)} %bitcast.32), channel_id=1, source_target_pairs={{0,2},{1,3},{2,0},{3,1},{4,6},{5,7},{6,4},{7,5},{8,10},{9,11},{10,... | collective-permute-start | bytes 1179656 | tf_op jit(solution)/shard_map/ppermute | solution.py:539
  65.1 12.1 %collective-permute-start.17 = (bf16[256,384]{1,0:T(8,128)(2,1)}, bf16[256,384]{1,0:T(8,128)(2,1)S(1)}, u32[]{:S(2)}, u32[]{:S(2)}) collective-permute-start(bf16[256,384]{1,0:T(8,128)(2,1)} %collective-permute-done.11.pool2), channel_id=1, source_target_pairs={{0,4},{4,0},{8,12},{12,8},{1,5},{5,1},{9,13},{13,9},{2,6},{6,2},{1... | collective-permute-start | bytes 589832 | tf_op jit(solution)/shard_map/ppermute | solution.py:341
  77.3 6.0 %copy-start.15 = (bf16[2,256,384]{2,1,0:T(8,128)(2,1)S(1)}, bf16[2,256,384]{2,1,0:T(8,128)(2,1)}, u32[]{:S(2)}) copy-start(bf16[2,256,384]{2,1,0:T(8,128)(2,1)} %copy-done.14) | copy-start | bytes 1179652
  77.5 19.6 %collective-permute-start.18 = (bf16[512,384]{1,0:T(8,128)(2,1)S(1)}, bf16[512,384]{1,0:T(8,128)(2,1)S(1)}, u32[]{:S(2)}, u32[]{:S(2)}) collective-permute-start(bf16[512,384]{1,0:T(8,128)(2,1)S(1)} %broadcast_select_fusion.1), channel_id=1, source_target_pairs={{1,4},{3,6},{0,8},{2,10},{4,9},{6,11},{5,13},{7,15},{9,12},{11,14}... | collective-permute-start | bytes 1179656 | tf_op jit(solution)/shard_map/ppermute | solution.py:529
  78.8 18.3 %collective-permute-start.19 = (bf16[512,384]{1,0:T(8,128)(2,1)S(1)}, bf16[512,384]{1,0:T(8,128)(2,1)S(1)}, u32[]{:S(2)}, u32[]{:S(2)}) collective-permute-start(bf16[512,384]{1,0:T(8,128)(2,1)S(1)} %get-tuple-element.63), channel_id=1, source_target_pairs={{1,12},{3,14},{4,1},{6,3},{9,4},{11,6},{12,9},{14,11},{17,28},{19,... | collective-permute-start | bytes 1179656 | tf_op jit(solution)/shard_map/ppermute | solution.py:530
  79.4 5.5 %collective-permute-start.20 = (bf16[2,272,192]{2,1,0:T(8,128)(2,1)S(1)}, bf16[2,272,192]{2,1,0:T(8,128)(2,1)S(1)}, u32[]{:S(2)}, u32[]{:S(2)}) collective-permute-start(bf16[2,272,192]{2,1,0:T(8,128)(2,1)S(1)} %get-tuple-element.71.own0), channel_id=1, source_target_pairs={{0,1},{1,0},{2,3},{3,2},{4,5},{5,4},{6,7},{7,6},{8,9},{9,8},{10,11... | collective-permute-start | bytes 626696 | tf_op jit(solution)/shard_map/ppermute | solution.py:535
  83.2 1.8 %collective-permute-start.21 = (bf16[2,272,192]{2,1,0:T(8,128)(2,1)S(1)}, bf16[2,272,192]{2,1,0:T(8,128)(2,1)S(1)}, u32[]{:S(2)}, u32[]{:S(2)}) collective-permute-start(bf16[2,272,192]{2,1,0:T(8,128)(2,1)S(1)} %get-tuple-element.70.own1), channel_id=1, source_target_pairs={{0,1},{1,0},{2,3},{3,2},{4,5},{5,4},{6,7},{7,6},{8,9},{9,8},{10,11... | collective-permute-start | bytes 626696 | tf_op jit(solution)/shard_map/ppermute | solution.py:535
  85.0 14.6 %copy-start.1 = (bf16[960,2048]{1,0:T(8,128)(2,1)S(1)}, bf16[960,2048]{1,0:T(8,128)(2,1)}, u32[]{:S(2)}) copy-start(bf16[960,2048]{1,0:T(8,128)(2,1)} %copy-done) | copy-start | bytes 11796484
  97.2 1.8 %collective-permute-start.22 = (bf16[512,384]{1,0:T(8,128)(2,1)S(1)}, bf16[512,384]{1,0:T(8,128)(2,1)S(1)}, u32[]{:S(2)}, u32[]{:S(2)}) collective-permute-start(bf16[512,384]{1,0:T(8,128)(2,1)S(1)} %get-tuple-element.69.own0), channel_id=1, source_target_pairs={{0,1},{1,0},{2,3},{3,2},{4,5},{5,4},{6,7},{7,6},{8,9},{9,8},{10,11... | collective-permute-start | bytes 1179656 | tf_op jit(solution)/shard_map/ppermute | solution.py:535
  97.3 2.3 %collective-permute-start.23 = (bf16[512,384]{1,0:T(8,128)(2,1)S(1)}, bf16[512,384]{1,0:T(8,128)(2,1)S(1)}, u32[]{:S(2)}, u32[]{:S(2)}) collective-permute-start(bf16[512,384]{1,0:T(8,128)(2,1)S(1)} %get-tuple-element.68.own1), channel_id=1, source_target_pairs={{0,1},{1,0},{2,3},{3,2},{4,5},{5,4},{6,7},{7,6},{8,9},{9,8},{10,11... | collective-permute-start | bytes 1179656 | tf_op jit(solution)/shard_map/ppermute | solution.py:535
  (2 other events, 1.4 us)

commit v3 on v2

v3 whole, which is shorter than its diff:
```python
import functools
import math

import jax
import jax.numpy as jnp
from jax import lax
from jax.experimental import pallas as pl
from jax.experimental.pallas import tpu as pltpu
from jax.sharding import PartitionSpec as P

KW = 5

SQRT_TWO_PI = 0.7978845608028654
CUBIC = 0.044715

STEM_ROWS = 32
SIDE = 64
OUTER = 16
INNER = 8
F32 = jnp.float32
BF16 = jnp.bfloat16
MIB = 1024 * 1024


def gelu_value(value):
    inner = jnp.tanh(SQRT_TWO_PI * (value + CUBIC * value * value * value))
    return 0.5 * value * (1.0 + inner)


def gelu_slope(value):
    inner = jnp.tanh(SQRT_TWO_PI * (value + CUBIC * value * value * value))
    return 0.5 * (1.0 + inner) + 0.5 * value * (1.0 - inner * inner) * SQRT_TWO_PI * (
        1.0 + 3.0 * CUBIC * value * value
    )


def dot(a, b, contract):
    return lax.dot_general(a, b, (contract, ((), ())), preferred_element_type=F32)


def assemble(own, after, before, block, devices):
    side = 2 * SIDE
    pairs = own.shape[1]
    column = lax.broadcasted_iota(jnp.int32, (2, side), 1)
    after = jnp.where(block == devices - 1, -1, after[:, :side])
    before = jnp.where(block == 0, -1, before[:, pairs - side :])
    return jnp.concatenate([own, jnp.where(column < SIDE, after, before)], axis=1)


def split_parity(bases):
    count = bases.shape[1]
    row = lax.broadcasted_iota(jnp.int32, (count, count), 0)
    column = lax.broadcasted_iota(jnp.int32, (count, count), 1)
    source = jnp.where(column < count // 2, 2 * column, 2 * column - count + 1)
    chosen = jnp.where(row == source, 1.0, 0.0).astype(BF16)
    wide = jnp.broadcast_to(bases, (16, count)).astype(F32).astype(BF16)
    value = dot(wide, chosen, ((1,), (0,))).astype(jnp.int32)
    return jnp.concatenate([value[0:1, : count // 2], value[0:1, count // 2 :]], axis=0)


def tap_onehots(bases, start, width):
    total = bases.shape[1]
    before = pltpu.roll(bases, (1 - start) % total, 1)[:, :width]
    here = bases[:, :width] if start == 0 else pltpu.roll(bases, -start % total, 1)[:, :width]
    after = pltpu.roll(bases, (-1 - start) % total, 1)[:, :width]
    taps = [before[0:1], before[1:2], here[0:1], here[1:2], after[0:1], after[1:2]]
    row = lax.broadcasted_iota(jnp.int32, (4 * KW, width), 0)
    tap, base = row >> 2, row & 3
    out = []
    for first in (0, 1):
        value = jnp.full((4 * KW, width), -1, jnp.int32)
        for k in range(KW):
            value = jnp.where(tap == k, jnp.broadcast_to(taps[first + k], value.shape), value)
        out.append(jnp.where(value == base, 1.0, 0.0).astype(BF16))
    return out


def valid_pairs(shape, dim, first, total):
    pair = lax.broadcasted_iota(jnp.int32, shape, dim) + first
    return (pair >= 0) & (pair < total)


def stem_kernel(
    place, own, after, before, stem_own, w_oth, w_own, acc, stem_out, lhs_oth, split, even, odd, lhs, *, pairs, devices
):
    seq, hi, lo = place[0], place[1], place[2]
    rows = pairs + 2 * INNER
    wide = pairs + 2 * OUTER
    block = acc.shape[1] // 2
    swapped = lax.rem(seq, 2) == 1
    first, second = after[...], before[...]
    for i, raw in enumerate((own[...], jnp.where(swapped, second, first), jnp.where(swapped, first, second))):
        split[i] = split_parity(raw)
    hots = tap_onehots(assemble(split[0], split[1], split[2], seq, devices), -OUTER, wide)
    gap = OUTER - INNER
    stem_oth = w_oth[: stem_own.shape[0], : stem_own.shape[1]]
    for weight, held_lhs in ((stem_own[...], lhs), (stem_oth, lhs_oth)):
        for hot, held in zip(hots, (even, odd)):
            raw = dot(hot, weight, ((0,), (0,)))
            ok = valid_pairs(raw.shape, 0, seq * pairs - OUTER, pairs * devices)
            held[...] = jnp.where(ok, gelu_value(raw), 0.0).astype(BF16).astype(F32)
        for k in range(6):
            source = even if k % 2 == 0 else odd
            held_lhs[k] = source[gap + k // 2 - 1 : gap + k // 2 - 1 + rows, :].astype(BF16)
    stem_out[0] = lhs[2]
    stem_out[1] = lhs[3]
    for part in range(2):
        at = pl.multiple_of((2 * (hi if part == 0 else 1 - hi) + lo) * block, 128)
        total = jnp.zeros((2 * rows, block), F32)
        for k in range(KW):
            total = total + dot(lhs[k : k + 2].reshape(2 * rows, -1), w_own[k, :, pl.ds(at, block)], ((1,), (0,)))
        acc[:, part * block : (part + 1) * block] = total


def enc_kernel(place, acc, lhs, w_oth, keep, send):
    hi = place[1]
    rows, block = keep.shape
    for part in range(2):
        at = pl.multiple_of((hi if part == 0 else 1 - hi) * block, 128)
        total = acc[:, part * block : (part + 1) * block]
        for k in range(KW):
            total = total + dot(lhs[k : k + 2].reshape(rows, -1), w_oth[k * lhs.shape[2] : (k + 1) * lhs.shape[2], pl.ds(at, block)], ((1,), (0,)))
        if part == 0:
            keep[...] = total
        else:
            send[...] = total.astype(BF16)


def pool_kernel(place, keep, came, pooled, centre, *, pairs, total):
    rows = pairs + 2 * INNER
    value = keep[...] + came[...].astype(F32)
    active = gelu_value(value).astype(BF16).astype(F32)
    both = 0.5 * (active[:rows] + active[rows:])
    ok = valid_pairs(both.shape, 0, place[0] * pairs - INNER, total)
    both = jnp.where(ok, both, 0.0).astype(BF16)
    pooled[...] = both
    centre[...] = both[INNER : INNER + pairs].astype(BF16)


def dec_kernel(own, oth, w_own, w_oth, stem, targets, part, send, held, *, pairs):
    rows = pairs + 2 * INNER
    held[:8] = jnp.zeros((8, held.shape[1]), F32)
    held[8 + rows :] = jnp.zeros((8, held.shape[1]), F32)
    acc = jnp.zeros(part.shape, F32)
    for source, weight in ((own, w_own), (oth, w_oth)):
        held[8 : 8 + rows] = source[...].astype(F32)
        for k in range(3):
            acc = acc + dot(held[7 + k : 7 + k + rows].astype(BF16), weight[k], ((1,), (1,)))
    half = part.shape[1] // 2
    for parity in range(2):
        value = acc[:, parity * half : (parity + 1) * half]
        value = value + stem[parity].astype(F32) - targets[parity].astype(F32)
        part[:, parity * half : (parity + 1) * half] = value
        send[:, parity * half : (parity + 1) * half] = value.astype(BF16)


def slope_kernel(place, part, came, targets, pred, sums, local, near, far, held, *, pairs, total, scale):
    rows = pairs + 2 * INNER
    half = part.shape[1] // 2
    quarter = half // 2
    ok = valid_pairs((rows, half), 0, place[0] * pairs - INNER, total)
    second = place[1] == 1
    slopes = []
    for parity in range(2):
        cols = slice(parity * half, (parity + 1) * half)
        value = part[:, cols] + came[:, cols].astype(F32)
        out = (value + targets[parity].astype(F32))[INNER : INNER + pairs]
        pred[parity] = jnp.where(second, out[:, quarter:], out[:, :quarter]).astype(BF16)
        slopes.append(jnp.where(ok, value * scale, 0.0).astype(BF16).astype(F32))
    held[:rows] = slopes[0]
    held[rows:] = jnp.zeros((8, half), F32)
    both = slopes[0] + slopes[1], slopes[1] + held[1 : 1 + rows]
    for i in range(2):
        for h in range(2):
            sums[h, i] = both[i][:, h * quarter : (h + 1) * quarter].astype(BF16)
    for out, step in ((local, 0), (near, 2 - place[3]), (far, 3)):
        out[...] = sums[lax.rem(place[0] + step, 4) // 2]


def lane_tiles(channels):
    return [(first, min(first + 128, channels)) for first in range(0, channels, 128)]


def targets_kernel(place, own, before, after, out, held):
    channels, count = own.shape
    side = before.shape[1]
    rows = count // 2 + 2 * INNER
    high = place[1] == 1
    for first, last in lane_tiles(channels):
        wide = last - first
        held[:side, :wide] = before[first:last].astype(F32).T
        held[side : side + count, :wide] = own[first:last].astype(F32).T
        held[side + count :, :wide] = after[first:last].astype(F32).T
        for parity in range(2):
            value = held[pl.ds(side - 2 * INNER + parity, rows, stride=2), :][:, :wide].astype(BF16)
            blank = jnp.zeros_like(value)
            out[parity, :, first:last] = jnp.where(high, blank, value)
            out[parity, :, channels + first : channels + last] = jnp.where(high, value, blank)


def pred_kernel(source, out, held):
    channels, count = out.shape
    for first, last in lane_tiles(channels):
        wide = last - first
        for parity in range(2):
            value = source[parity, :, first:last].astype(F32)
            if wide < 128:
                value = jnp.concatenate([value, jnp.zeros((count // 2, 128 - wide), F32)], axis=1)
            held[pl.ds(parity, count // 2, stride=2), :] = value
        out[first:last] = held[:, :wide].T.astype(BF16)


def shifted_sums(held, pairs):
    return [
        held[0, INNER + 1 : INNER + 1 + pairs].astype(BF16),
        held[1, INNER : INNER + pairs].astype(BF16),
        held[0, INNER : INNER + pairs].astype(BF16),
        held[1, INNER - 1 : INNER - 1 + pairs].astype(BF16),
        held[0, INNER - 1 : INNER - 1 + pairs].astype(BF16),
    ]


def back_kernel(place, own, oth, weight, out, held, *, pairs):
    acc = jnp.zeros(out.shape, F32)
    for source, core in ((own, place[2]), (oth, 1 - place[2])):
        for h in range(2):
            held[...] = source[h].astype(F32)
            for k, tap in enumerate(shifted_sums(held, pairs)):
                acc = acc + dot(tap, weight[k, 2 * h + core], ((1,), (0,)))
    out[...] = (0.5 * acc).astype(BF16)


def owner_slope_kernel(place, *refs, slot, pairs, devices):
    blocks, weights = refs[:devices], refs[devices : devices + 4]
    out, bases, even, odd, lhs = refs[devices + 4 :]
    for r in range(devices):
        bases[r] = blocks[r][...]
    wide = pairs + 2 * INNER
    step = 2 * slot + place[3]
    block = lax.rem(place[0] - step + devices, devices)
    before, after = lax.rem(step + 1, devices), lax.rem(step + devices - 1, devices)
    joined = assemble(bases[step], bases[after], bases[before], block, devices)
    hots = tap_onehots(joined, -INNER, wide)
    total = jnp.zeros(out.shape, F32)
    for kernel in weights:
        channels = lhs.shape[2]
        weight = kernel[KW * channels : KW * channels + 4 * KW, :channels]
        for hot, held in zip(hots, (even, odd)):
            raw = dot(hot, weight, ((0,), (0,)))
            ok = valid_pairs(raw.shape, 0, block * pairs - INNER, pairs * devices)
            held[...] = jnp.where(ok, gelu_value(raw), 0.0).astype(BF16).astype(F32)
        for k in range(6):
            source = even if k % 2 == 0 else odd
            lhs[k] = source[INNER + k // 2 - 1 : INNER + k // 2 - 1 + pairs, :].astype(BF16)
        for k in range(KW):
            total = total + dot(
                lhs[k : k + 2].reshape(2 * pairs, -1), kernel[k * channels : (k + 1) * channels, :], ((1,), (0,))
            )
    out[...] = gelu_slope(total).astype(BF16)


def taps_kernel(place, *refs, pairs, devices):
    blocks, (stem_w, out) = refs[:devices], refs[devices:]
    channels = stem_w.shape[1]
    for r in range(devices):
        block = lax.rem(place[0] - r + devices, devices)
        bases = assemble(blocks[r][...], blocks[r - 1][...], blocks[(r + 1) % devices][...], block, devices)
        width = bases.shape[1]
        parts = []
        for hot in tap_onehots(bases, 0, width):
            raw = dot(stem_w[...], hot, ((0,), (0,)))
            column = lax.broadcasted_iota(jnp.int32, raw.shape, 1)
            pair = jnp.where(column >= width - SIDE, column - width, column) + block * pairs
            ok = (pair >= 0) & (pair < pairs * devices)
            parts.append(jnp.where(ok, gelu_value(raw), 0.0))
        taps = []
        for step in (-1, 0, 1):
            for held in parts:
                moved = held if step == 0 else pltpu.roll(held, -step % width, 1)
                taps.append(moved[:, :pairs].astype(BF16))
        at = 2 * r * pairs
        for k in range(KW):
            out[k * channels : (k + 1) * channels, at : at + pairs] = taps[k]
            out[k * channels : (k + 1) * channels, at + pairs : at + 2 * pairs] = taps[k + 1]


def picks_kernel(place, stem, enc, mine, enc_oth, sems):
    seq, core = place[0], 1 - place[2]
    taps, channels, _ = enc.shape
    block = mine.shape[1]

    def columns(index):
        return pl.ds(pl.multiple_of(index * block, 128), block)

    copies = []
    for k in range(taps):
        rows = pl.ds(k * channels, channels)
        for h in range(2):
            copies.append((enc.at[k, :, columns(2 * h + core)], enc_oth.at[rows, h * block : (h + 1) * block]))
        copies.append((enc.at[k, :, columns(seq)], mine.at[rows]))
    copies = [pltpu.make_async_copy(*ends, sems.at[i]) for i, ends in enumerate(copies)]
    for copy in copies:
        copy.start()
    enc_oth[taps * channels :, : stem.shape[1]] = stem[...]
    mine[taps * channels :, : stem.shape[1]] = stem[...]
    for copy in copies:
        copy.wait()


def pick_kernel(place, source, out):
    out[...] = source[...]


def comb_kernel(place, own, came, comb_own, comb_came):
    combine(own, comb_own)
    combine(came, comb_came)


def combine(weight, comb):
    comb[0, 0] = weight[0] + weight[1]
    comb[1, 0] = weight[2] + weight[3]
    comb[2, 0] = weight[4]
    comb[0, 1] = weight[0]
    comb[1, 1] = weight[1] + weight[2]
    comb[2, 1] = weight[3] + weight[4]


def dec_grad_kernel(place, own, came, pool0, pool1, pool2, pool3, out, held, taps, pooled, *, pairs):
    blocks = (pool0, pool1, pool2, pool3)
    parity = place[3]
    odd = lax.rem(place[0], 2)
    for block, step in zip(blocks, (0, 3 - 2 * odd, 2, 1 + 2 * odd)):
        pooled[pl.ds(pl.multiple_of(step * pairs, pairs), pairs), :] = block[...]
    for i in range(4):
        slots = own if i < 2 else came
        held[...] = slots[i % 2].astype(F32)
        step = 2 * (i % 2) + (parity if i < 2 else 1 - parity)
        at = pl.ds(pl.multiple_of(step * pairs, pairs), pairs)
        for k, tap in enumerate(shifted_sums(held, pairs)):
            taps[k, at, :] = tap
    for k in range(KW):
        out[k] = dot(taps[k], pooled[...], ((0,), (0,)))


def enc_grad_kernel(place, taps, own, came, slope0, slope1, slope2, slope3, out, joined):
    @pl.when(pl.program_id(0) == 0)
    def _():
        pairs = own.shape[1]
        for i, slope in enumerate((slope0, slope1, slope2, slope3)):
            step = 2 * (i % 2) + (place[3] if i < 2 else 1 - place[3])
            grad = (own if i < 2 else came)[i % 2].astype(F32)
            for parity in range(2):
                value = grad * slope[parity * pairs : (parity + 1) * pairs].astype(F32)
                at = pl.multiple_of((2 * step + parity) * pairs, pairs)
                joined[pl.ds(at, pairs), :] = value.astype(BF16)

    out[...] = dot(taps[...], joined[...], ((1,), (0,)))


def whole(shape):
    return pl.BlockSpec(shape, lambda *_: (0,) * len(shape))


SCALARS = pl.BlockSpec(memory_space=pltpu.SMEM)


def call(kernel, ins, outs, scratch=(), limit=16, name=None, last=()):
    specs = [SCALARS if i.dtype == jnp.int32 and i.ndim == 1 else whole(i.shape) for i in ins]
    for at in last:
        shape = ins[at].shape
        specs[at] = pl.BlockSpec((STEM_ROWS,) + shape[1:], lambda *_: (shape[0] // STEM_ROWS - 1, 0))
    return pl.pallas_call(
        kernel,
        grid=(1,) if last else (),
        in_specs=specs,
        out_specs=[whole(s) for s, _ in outs],
        out_shape=[jax.ShapeDtypeStruct(s, d) for s, d in outs],
        scratch_shapes=[pltpu.VMEM(s, d) for s, d in scratch],
        compiler_params=pltpu.CompilerParams(vmem_limit_bytes=limit * MIB),
        name=name,
    )(*ins)


def gated(values, gates):
    return lax.optimization_barrier((values, gates))[0]


def shards(dna_bases, w_stem, w_enc, w_dec, targets):
    devices = lax.axis_size("seq")
    seq, chan = lax.axis_index("seq"), lax.axis_index("chan")
    hi, lo = chan // 2, chan % 2
    parity = (lo + seq) % 2
    pairs = dna_bases.shape[0] // 2
    total = pairs * devices
    rows = pairs + 2 * INNER
    stem_c = w_stem.shape[0]
    enc_c = w_dec.shape[2]
    across = [(c, c ^ 2) for c in range(4)]
    cores = [(c, c ^ 1) for c in range(4)]

    def ring(array, step):
        return lax.ppermute(array, "seq", [(i, (i + step) % devices) for i in range(devices)])

    def swap(array, distance):
        return lax.ppermute(array, "seq", [(i, i ^ distance) for i in range(devices)])

    place = jnp.stack([seq, hi, lo, parity]).astype(jnp.int32)
    first_chip, even = hi == 0, parity == 0
    target = [(seq + step) % devices // 2 == hi for step in (0, 2 - parity, 3)]
    own = dna_bases.reshape(1, 2 * pairs)
    stem_w = w_stem.transpose(1, 2, 0).reshape(4 * KW, stem_c)
    own, place, first_chip, even, target = lax.optimization_barrier((own, place, first_chip, even, target))

    first = swap(own, 1)
    second = lax.ppermute(own, "seq", [(i, (i + 1 - 2 * (1 - i % 2)) % devices) for i in range(devices)])
    enc_w = w_enc.transpose(1, 2, 0)
    dec_w = w_dec.transpose(1, 0, 2).reshape(KW, 4, stem_c, enc_c)
    picked = (KW, 1, stem_c, enc_c)
    stem_rows = jnp.concatenate([stem_w, jnp.zeros((STEM_ROWS - 4 * KW, stem_c), BF16)])
    mine, enc_send = pl.pallas_call(
        picks_kernel,
        in_specs=[SCALARS, whole(stem_rows.shape), pl.BlockSpec(memory_space=pl.ANY)],
        out_specs=[pl.BlockSpec(memory_space=pltpu.VMEM)] * 2,
        out_shape=[
            jax.ShapeDtypeStruct((KW * stem_c + STEM_ROWS, enc_c), BF16),
            jax.ShapeDtypeStruct((KW * stem_c + STEM_ROWS, 2 * enc_c), BF16),
        ],
        scratch_shapes=[pltpu.SemaphoreType.DMA((3 * KW,))],
        compiler_params=pltpu.CompilerParams(vmem_limit_bytes=5 * MIB),
        name="picks",
    )(place, stem_rows, enc_w)
    enc_oth = lax.ppermute(enc_send, "chan", cores)
    mine_far = lax.ppermute(mine, "chan", across)
    dec_send = pl.pallas_call(
        pick_kernel,
        grid_spec=pltpu.PrefetchScalarGridSpec(
            num_scalar_prefetch=1,
            grid=(2,),
            in_specs=[pl.BlockSpec(picked, lambda h, at: (0, 2 * h + 1 - at[2], 0, 0))],
            out_specs=pl.BlockSpec(picked, lambda h, at: (0, h, 0, 0)),
        ),
        out_shape=jax.ShapeDtypeStruct((KW, 2, stem_c, enc_c), BF16),
        compiler_params=pltpu.CompilerParams(vmem_limit_bytes=8 * MIB),
        name="dec_pick",
    )(place, dec_w)
    dec_came = lax.ppermute(dec_send, "chan", cores)

    acc, stem, lhs, split = call(
        functools.partial(stem_kernel, pairs=pairs, devices=devices),
        [place, own, first, second, stem_w, enc_oth, enc_w],
        [
            ((2 * rows, 2 * enc_c), F32),
            ((2, rows, stem_c), BF16),
            ((6, rows, stem_c), BF16),
            ((3, 2, pairs), jnp.int32),
        ],
        [
            ((pairs + 2 * OUTER, stem_c), F32),
            ((pairs + 2 * OUTER, stem_c), F32),
            ((6, rows, stem_c), BF16),
        ],
        limit=14,
        name="stem_conv",
        last=(5,),
    )
    keep, send = call(
        enc_kernel,
        [place, acc, lhs, enc_oth],
        [((2 * rows, enc_c), F32), ((2 * rows, enc_c), BF16)],
        limit=12,
        name="enc_conv",
    )
    came = lax.ppermute(gated(send, mine_far), "chan", across)

    targets_in, place_in = gated((targets, place), send)
    blocks = {0: split[0], 1: split[2], devices - 1: split[1]}
    for r in range(2, devices - 1):
        blocks[r] = ring(split[0], r)
    comb_own, comb_came = pl.pallas_call(
        comb_kernel,
        grid_spec=pltpu.PrefetchScalarGridSpec(
            num_scalar_prefetch=1,
            grid=(2,),
            in_specs=[
                pl.BlockSpec(picked, lambda h, at: (0, 2 * h + at[2], 0, 0)),
                pl.BlockSpec(picked, lambda h, at: (0, h, 0, 0)),
            ],
            out_specs=[pl.BlockSpec((3, 2, 1, stem_c, enc_c), lambda h, at: (0, 0, h, 0, 0))] * 2,
        ),
        out_shape=[jax.ShapeDtypeStruct((3, 2, 2, stem_c, enc_c), BF16)] * 2,
        compiler_params=pltpu.CompilerParams(vmem_limit_bytes=12 * MIB),
        name="dec_taps",
    )(place_in, dec_w, dec_came)
    targets_in = targets_in.T
    count, edge = 2 * pairs, 2 * SIDE
    (targets_at,) = call(
        targets_kernel,
        [place, targets_in, ring(targets_in[:, count - edge :], 1), ring(targets_in[:, :edge], devices - 1)],
        [((2, rows, 2 * stem_c), BF16)],
        [((count + 2 * edge, 128), F32)],
        limit=6,
        name="targets",
    )
    blank = jnp.zeros_like(stem)
    stem_at = jnp.where(
        first_chip, jnp.concatenate([stem, blank], axis=2), jnp.concatenate([blank, stem], axis=2)
    )
    place_in = gated(place, (comb_own, comb_came, targets_at, stem_at, list(blocks.values())))

    pooled, centre = call(
        functools.partial(pool_kernel, pairs=pairs, total=total),
        [place_in, keep, came],
        [((rows, enc_c), BF16), ((pairs, enc_c), BF16)],
        limit=8,
        name="gelu_pool",
    )
    pooled_oth = lax.ppermute(pooled, "chan", cores)
    part, send = call(
        functools.partial(dec_kernel, pairs=pairs),
        [
            pooled,
            pooled_oth,
            comb_own.reshape(3, 4 * stem_c, enc_c),
            comb_came.reshape(3, 4 * stem_c, enc_c),
            stem_at,
            targets_at,
        ],
        [((rows, 4 * stem_c), F32), ((rows, 4 * stem_c), BF16)],
        [((rows + 16, enc_c), F32)],
        limit=11,
        name="dec_conv",
    )
    came = lax.ppermute(send, "chan", across)

    centre, place_in = gated((centre, place), send)
    beyond, beside = swap(centre, 2), swap(centre, 1)
    (taps,) = call(
        functools.partial(taps_kernel, pairs=pairs, devices=devices),
        [place_in] + [blocks[r] for r in range(devices)] + [stem_w],
        [((KW * stem_c, 2 * pairs * devices), BF16)],
        limit=12,
        name="stem_taps",
    )

    weights = [mine, mine_far]
    weights += [lax.ppermute(w, "chan", cores) for w in gated(weights, keep)]

    def owner_slope(slot, at):
        (out,) = call(
            functools.partial(owner_slope_kernel, slot=slot, pairs=pairs, devices=devices),
            [at] + [blocks[r] for r in range(devices)] + weights,
            [((2 * pairs, enc_c), BF16)],
            [
                ((devices, 2, pairs), jnp.int32),
                ((rows, stem_c), F32),
                ((rows, stem_c), F32),
                ((6, pairs, stem_c), BF16),
            ],
            limit=10,
            name="owner_slope",
        )
        return out, lax.ppermute(out, "chan", cores)

    slope0, slope0_came = owner_slope(0, gated(place, taps))

    pred, sums, local, near, far = call(
        functools.partial(slope_kernel, pairs=pairs, total=total, scale=1.0 / math.sqrt(2 * total)),
        [gated(place, (beyond, beside, slope0)), part, came, targets_at],
        [((2, pairs, stem_c), BF16), ((2, 2, rows, stem_c), BF16)] + [((2, rows, stem_c), BF16)] * 3,
        [((rows + 8, 2 * stem_c), F32)],
        limit=7,
        name="out_slope",
    )
    sums_oth = lax.ppermute(sums, "chan", cores)
    (pre,) = call(
        functools.partial(back_kernel, pairs=pairs),
        [place, sums, sums_oth, dec_w],
        [((pairs, enc_c), BF16)],
        [((2, rows, stem_c), F32)],
        limit=11,
        name="up_grad",
    )

    def link(steps):
        out = []
        for s in range(devices):
            for step in steps:
                t = (s + step) % devices
                for x in range(2):
                    out.append((s * 4 + 2 * x + t % 2, t * 4 + 2 * x + (t + step) % 2))
        return out

    def to_owner(local, near, far):
        near = lax.ppermute(near, ("seq", "chan"), link((1, 2)))
        far = lax.ppermute(far, ("seq", "chan"), link((3,)))
        return local, near, far

    def slots(local, near, far):
        return jnp.stack([jnp.where(even, local, near), jnp.where(even, near, far)])

    local, near, far = to_owner(local, near, far)
    pre_oth = lax.ppermute(pre, "chan", across)
    slope1, slope1_came = owner_slope(1, gated(place, pre))
    near, far = gated((near, far), slope1)
    far_pooled = swap(beyond, 1)
    sums_pieces = local, near, far
    pre_oth = gated(pre_oth, (near, far, slope1))
    pieces = [jnp.where(own_block, pre, pre_oth) for own_block in target]
    local, near, far = to_owner(*pieces)
    sums_mine = gated(slots(*sums_pieces), pieces)
    sums_came = lax.ppermute(sums_mine, "chan", cores)

    (pred,) = call(
        pred_kernel,
        [pred],
        [((stem_c, 2 * pairs), BF16)],
        [((2 * pairs, 128), F32)],
        limit=5,
        name="pred",
    )
    pred = pred.T
    (g_dec,) = call(
        functools.partial(dec_grad_kernel, pairs=pairs),
        [place, sums_mine, sums_came, centre, beside, beyond, far_pooled],
        [((KW, stem_c, enc_c), F32)],
        [
            ((2, rows, stem_c), F32),
            ((KW, devices * pairs, stem_c), BF16),
            ((devices * pairs, enc_c), BF16),
        ],
        limit=12,
        name="dec_grad",
    )
    near, far = gated((near, far), (g_dec, pred))
    pre_mine = slots(local, near, far)
    pre_came = lax.ppermute(pre_mine, "chan", cores)
    g_enc = pl.pallas_call(
        enc_grad_kernel,
        grid=(2,),
        in_specs=[SCALARS, pl.BlockSpec((KW * stem_c // 2, 2 * pairs * devices), lambda k: (k, 0))]
        + [whole(pre_mine.shape)] * 2
        + [whole(slope0.shape)] * 4,
        out_specs=pl.BlockSpec((KW * stem_c // 2, enc_c), lambda k: (k, 0)),
        out_shape=jax.ShapeDtypeStruct((KW * stem_c, enc_c), F32),
        scratch_shapes=[pltpu.VMEM((2 * pairs * devices, enc_c), BF16)],
        compiler_params=pltpu.CompilerParams(vmem_limit_bytes=13 * MIB),
        name="enc_grad",
    )(place, taps, pre_mine, pre_came, slope0, slope1, slope0_came, slope1_came)
    g_enc = g_enc.reshape(KW, stem_c, enc_c).transpose(2, 0, 1)
    return (pred, g_enc, g_dec.transpose(1, 0, 2))


def extended(block, sides, width):
    for axis, dim in sides:
        count = lax.axis_size(axis)
        forward = [(i, i + 1) for i in range(count - 1)]
        backward = [(target, source) for source, target in forward]
        low = lax.ppermute(
            lax.slice_in_dim(block, block.shape[dim] - width, None, axis=dim), axis, forward
        )
        high = lax.ppermute(lax.slice_in_dim(block, 0, width, axis=dim), axis, backward)
        block = jnp.concatenate([low, block, high], axis=dim)
    return block


def rim_cells(block, margin):
    return extended(block, (("seq", 0),), margin)


def channel_sum(partial_value):
    return lax.psum_scatter(partial_value, "chan", scatter_dimension=1, tiled=True)


def channel_gather(block):
    return lax.all_gather(block, "chan", axis=1, tiled=True)


def conv_rows(padded, weight):
    row_count = padded.shape[0] - 4
    total = jnp.zeros((row_count, weight.shape[0]), jnp.float32)
    for k in range(KW):
        total = total + lax.dot_general(
            padded[k : k + row_count],
            weight[:, k, :],
            (((1,), (1,)), ((), ())),
            preferred_element_type=jnp.float32,
        )
    return total


def grad_taps(picked, padded):
    row_count = picked.shape[0]
    pieces = [
        lax.dot_general(
            picked,
            padded[k : k + row_count],
            (((0,), (0,)), ((), ())),
            preferred_element_type=jnp.float32,
        )
        for k in range(KW)
    ]
    return jnp.stack(pieces, axis=1)


def weight_grad(cotangent, padded):
    rounded = grad_taps(cotangent, padded).astype(jnp.bfloat16)
    return lax.psum_scatter(
        lax.optimization_barrier(rounded).astype(jnp.float32),
        "seq",
        scatter_dimension=0,
        tiled=True,
    )


def general_shards(dna_bases, w_stem, w_enc, w_dec, targets):
    row_count = dna_bases.shape[0]
    devices = lax.axis_size("seq")
    length = row_count * devices
    onehot = (dna_bases[:, None] == jnp.arange(4, dtype=jnp.int32)[None, :]).astype(jnp.bfloat16)
    onehot_pad = rim_cells(onehot, 2)
    stem_out = gelu_value(conv_rows(onehot_pad, w_stem)).astype(jnp.bfloat16)
    stem_pad = rim_cells(stem_out, 2)
    enc_pre = channel_sum(conv_rows(stem_pad, w_enc))
    active = gelu_value(enc_pre).astype(jnp.bfloat16).astype(jnp.float32)
    pooled = (0.5 * active.reshape(row_count // 2, 2, -1).sum(axis=1)).astype(jnp.bfloat16)
    pooled_pad = rim_cells(pooled, 1)
    up_pad = jnp.repeat(pooled_pad, 2, axis=0)
    output = channel_sum(conv_rows(up_pad, w_dec)) + stem_out.astype(jnp.float32)
    pred = output.astype(jnp.bfloat16)
    scale = 1.0 / math.sqrt(length)
    slope_out = ((output - targets.astype(jnp.float32)) * scale).astype(jnp.bfloat16)
    slope_all = channel_gather(slope_out)
    g_dec = weight_grad(slope_all, up_pad)
    slope_pad = rim_cells(slope_all, 2)
    up_grad = jnp.zeros((row_count, w_dec.shape[2]), jnp.float32)
    for k in range(KW):
        up_grad = up_grad + jnp.dot(
            slope_pad[4 - k : 4 - k + row_count], w_dec[:, k, :], preferred_element_type=jnp.float32
        )
    pool_grad = up_grad.reshape(row_count // 2, 2, -1).sum(axis=1)
    act_grad = 0.5 * jnp.repeat(pool_grad, 2, axis=0)
    pre_grad = (act_grad * gelu_slope(enc_pre)).astype(jnp.bfloat16)
    pre_all = channel_gather(pre_grad)
    g_enc = weight_grad(pre_all, stem_pad)
    return (pred, g_enc, g_dec)


def solution(mesh):
    sizes = mesh.shape["seq"], mesh.shape["chan"]
    return jax.shard_map(
        shards if sizes == (4, 4) else general_shards,
        mesh=mesh,
        in_specs=(
            P(("groups", "seq")),
            P("chan", None, None),
            P(None, None, "chan"),
            P(None, None, "chan"),
            P(("groups", "seq"), "chan"),
        ),
        out_specs=(
            P(("groups", "seq"), "chan"),
            P(("groups", "seq"), None, "chan"),
            P(("groups", "seq"), None, "chan"),
        ),
        check_vma=False,
    )
```

time: 104 us -> 92.3 us (0.89)
  waiting for transfers between devices: 30.2 us -> 20.7 us
  local copies, waits for them, and re-layouts: 11.6 us -> 2.74 us
  Pallas kernels: 33.4 us -> 37.5 us
  starting transfers between devices: 26.4 us -> 29.5 us
    unnamed x52 -> x10, local copies, waits for them, and re-layouts: 11.3 us -> 1.85 us
    ppermute x10 -> x14, starting transfers between devices: 8.01 us -> 16.1 us  [the longest x2 4.02 us: owner_slope(): return (out, lax.ppermute(out, 'chan', cores))]
    ppermute x3 -> x4, waiting for transfers between devices: 7.69 us -> 1.94 us  [swap(): lax.ppermute(array, 'seq', [(i, i ^ distance) for i in range(devices)])]
    pallas_call x13 -> x15, Pallas kernels: 31.5 us -> 36.5 us  [the longest x12 29.7 us: call(): pl.pallas_call(kernel, grid=(1,) if last else (), in_specs=specs, out_spe...]
    ppermute x5 -> x3, starting transfers between devices: 9.01 us -> 4.56 us  [ring(): lax.ppermute(array, 'seq', [(i, (i + step) % devices) for i in range(devi...]
    ppermute x2 -> x1, starting transfers between devices: 3.31 us -> 0.38 us  [shards(): came = lax.ppermute(send, 'chan', across)]
    ppermute x10 -> x14, waiting for transfers between devices: 16.7 us -> 14.7 us  [the longest x2 5.48 us: to_owner(): near = lax.ppermute(near, ('seq', 'chan'), link((1, 2)))]
    ppermute x3 -> x4, starting transfers between devices: 4.59 us -> 6.6 us  [swap(): lax.ppermute(array, 'seq', [(i, i ^ distance) for i in range(devices)])]
  transfers between devices with their start and end apart: 24 -> 26, of which waited for: 11 -> 9; matrix products, arithmetic and copies ran while one was open for 1% -> 0% of each run, Pallas kernels for 17% -> 34%
where the time goes in v3:
time: 92.3 us; the launch traced here: 92 us
  Pallas kernels  37.5 us (41%)
  starting transfers between devices  29.5 us (32%)
  waiting for transfers between devices  20.7 us (22%)
  local copies, waits for them, and re-layouts  2.74 us (3%)
  between operations  1.02 us (1%)
    pallas_call x12, Pallas kernels, call(): pl.pallas_call(kernel, grid=(1,) if last else (), in_specs=specs, out_spe...  29.7 us
    ppermute x4, starting transfers between devices, swap(): lax.ppermute(array, 'seq', [(i, i ^ distance) for i in range(devices)])  6.6 us
    ppermute x2, waiting for transfers between devices, to_owner(): near = lax.ppermute(near, ('seq', 'chan'), link((1, 2)))  5.48 us
    ppermute x1, waiting for transfers between devices, shards(): mine_far = lax.ppermute(mine, 'chan', across)  4.9 us
    ppermute x3, starting transfers between devices, ring(): lax.ppermute(array, 'seq', [(i, (i + step) % devices) for i in range(devi...  4.56 us
    pallas_call x1, Pallas kernels, shards(): pl.pallas_call(enc_grad_kernel, grid=(2,), in_specs=[SCALARS, pl.BlockSpe...  4.15 us
    ppermute x2, starting transfers between devices, owner_slope(): return (out, lax.ppermute(out, 'chan', cores))  4.02 us
    ppermute x1, starting transfers between devices, shards(): mine_far = lax.ppermute(mine, 'chan', across)  2.94 us
  transfers between devices with their start and end apart: 26, of which 9 were waited for; matrix products, arithmetic and copies ran while one was open for 0% of the time, Pallas kernels for 34%

profile of v3, /device:TPU:0, one launch (start us, length us, event | category | flops | bytes accessed | tf_op | source)
XLA Modules:
  0.0 92.0 jit_solution(13444344938347252318)
XLA Ops:
  0.9 0.9 reshape.25.stem_own.refs_4_
  1.8 1.8 %copy-done.1 = bf16[1536,5,192]{0,2,1:T(8,128)(2,1)S(1)} copy-done((bf16[1536,5,192]{0,2,1:T(8,128)(2,1)S(1)}, bf16[1536,5,192]{0,2,1:T(8,128)(2,1)}, u32[]{:S(2)}) %copy-start.1) | copy-done | bytes 2949144
  3.6 1.0 %picks.1 = (bf16[992,384]{1,0:T(8,128)(2,1)S(1)}, bf16[992,768]{1,0:T(8,128)(2,1)S(1)}) custom-call(s32[4]{0:T(128)S(1)} %pad_add_fusion.place, bf16[32,192]{1,0:T(8,128)(2,1)S(1)} %concatenate.9.stem, bf16[5,192,1536]{2,1,0:T(8,128)(2,1)S(1)} %bitcast.35), custom_call_target="tpu_custom_call" | custom-call | tf_op jit(solution)/shard_map/picks/pallas_call | solution.py:420
  4.5 0.5 collective-permute-start.2
  5.1 1.1 %dec_pick.1 = bf16[5,2,192,384]{3,2,1,0:T(8,128)(2,1)S(1)} custom-call(s32[4]{0:T(128)S(1)} %pad_add_fusion.place, bf16[5,4,192,384]{3,2,1,0:T(8,128)(2,1)S(1)} %bitcast.32), custom_call_target="tpu_custom_call" | custom-call | tf_op jit(solution)/shard_map/dec_pick/pallas_call | solution.py:434
  6.2 2.9 %collective-permute-start.7 = (bf16[992,384]{1,0:T(8,128)(2,1)S(1)}, bf16[992,384]{1,0:T(8,128)(2,1)S(1)}, u32[]{:S(2)}, u32[]{:S(2)}) collective-permute-start(bf16[992,384]{1,0:T(8,128)(2,1)S(1)} %get-tuple-element.69.refs_4_), channel_id=1, source_target_pairs={{0,2},{1,3},{2,0},{3,1},{4,6},{5,7},{6,4},{7,5},{8,10},{9,11},{10,... | collective-permute-start | bytes 2285576 | tf_op jit(solution)/shard_map/ppermute | solution.py:433
  9.2 1.6 %collective-permute-start = (s32[1,512]{1,0:T(1,128)S(1)}, s32[1,512]{1,0:T(1,128)S(1)}, u32[]{:S(2)}, u32[]{:S(2)}) collective-permute-start(s32[1,512]{1,0:T(1,128)S(1)} %bitcast.41), channel_id=1, source_target_pairs={{0,4},{4,0},{8,12},{12,8},{1,5},{5,1},{9,13},{13,9},{2,6},{6,2},{1... | collective-permute-start | bytes 6152 | tf_op jit(solution)/shard_map/ppermute | solution.py:405
  10.8 2.5 %collective-permute-start.1 = (s32[1,512]{1,0:T(1,128)S(1)}, s32[1,512]{1,0:T(1,128)S(1)}, u32[]{:S(2)}, u32[]{:S(2)}) collective-permute-start(s32[1,512]{1,0:T(1,128)S(1)} %bitcast.42), channel_id=1, source_target_pairs={{0,12},{4,8},{8,4},{12,0},{1,13},{5,9},{9,5},{13,1},{2,14},{6,10},... | collective-permute-start | bytes 6152 | tf_op jit(solution)/shard_map/ppermute | solution.py:415
  13.2 2.9 %collective-permute-done.1.before = s32[1,512]{1,0:T(1,128)S(1)} collective-permute-done((s32[1,512]{1,0:T(1,128)S(1)}, s32[1,512]{1,0:T(1,128)S(1)}, u32[]{:S(2)}, u32[]{:S(2)}) %collective-permute-start.1) | collective-permute-done | bytes 2080 | tf_op jit(solution)/shard_map/ppermute | solution.py:415
  16.2 3.2 %stem_conv.1 = (f32[544,768]{1,0:T(8,128)S(1)}, bf16[2,272,192]{2,1,0:T(8,128)(2,1)S(1)}, bf16[6,272,192]{2,1,0:T(8,128)(2,1)S(1)}, s32[3,2,256]{2,1,0:T(2,128)S(1)}) custom-call(s32[4]{0:T(128)S(1)} %pad_add_fusion.place, s32[1,512]{1,0:T(1,128)S(1)} %bitcast.43, s32[1,512]{1,0:T(1,128)S(1)} %collective-permute-done.after, ...), custom_call_target="tpu_custom_call" | custom-call | tf_op jit(solution)/shard_map/stem_conv/pallas_call | solution.py:372
  19.4 2.1 %enc_conv.1 = (f32[544,384]{1,0:T(8,128)S(1)}, bf16[544,384]{1,0:T(8,128)(2,1)S(1)}) custom-call(s32[4]{0:T(128)S(1)} %pad_add_fusion.place, f32[544,768]{1,0:T(8,128)S(1)} %get-tuple-element.49.acc, bf16[6,272,192]{2,1,0:T(8,128)(2,1)S(1)} %get-tuple-element.50.lhs, bf16[992,768]{1,0:T(8,128)(2,1)S(1)} %collective-permute-done.2.w_oth), custom_call_target="tpu_custom_call" | custom-call | tf_op jit(solution)/shard_map/enc_conv/pallas_call | solution.py:372
  21.5 4.9 %collective-permute-done.7.refs_5_ = bf16[992,384]{1,0:T(8,128)(2,1)S(1)} collective-permute-done((bf16[992,384]{1,0:T(8,128)(2,1)S(1)}, bf16[992,384]{1,0:T(8,128)(2,1)S(1)}, u32[]{:S(2)}, u32[]{:S(2)}) %collective-permute-start.7) | collective-permute-done | bytes 761888 | tf_op jit(solution)/shard_map/ppermute | solution.py:433
  26.4 1.7 %collective-permute-start.8 = (bf16[544,384]{1,0:T(8,128)(2,1)S(1)}, bf16[544,384]{1,0:T(8,128)(2,1)S(1)}, u32[]{:S(2)}, u32[]{:S(2)}) collective-permute-start(bf16[544,384]{1,0:T(8,128)(2,1)S(1)} %get-tuple-element.62), channel_id=1, source_target_pairs={{0,2},{1,3},{2,0},{3,1},{4,6},{5,7},{6,4},{7,5},{8,10},{9,11},{10,... | collective-permute-start | bytes 1253384 | tf_op jit(solution)/shard_map/ppermute | solution.py:473
  28.2 1.6 %collective-permute-start.4 = (bf16[192,128]{1,0:T(8,128)(2,1)S(1)}, bf16[192,128]{1,0:T(8,128)(2,1)S(1)}, u32[]{:S(2)}, u32[]{:S(2)}) collective-permute-start(bf16[192,128]{1,0:T(8,128)(2,1)S(1)} %get-tuple-element.97), channel_id=1, source_target_pairs={{0,4},{4,8},{8,12},{12,0},{1,5},{5,9},{9,13},{13,1},{2,6},{6,10},{... | collective-permute-start | bytes 147464 | tf_op jit(solution)/shard_map/ppermute | solution.py:402
  29.8 0.5 collective-permute-start.13
  30.3 2.2 %collective-permute-start.5 = (bf16[192,128]{1,0:T(8,128)(2,1)S(1)}, bf16[192,128]{1,0:T(8,128)(2,1)S(1)}, u32[]{:S(2)}, u32[]{:S(2)}) collective-permute-start(bf16[192,128]{1,0:T(8,128)(2,1)S(1)} %get-tuple-element.96), channel_id=1, source_target_pairs={{0,12},{4,0},{8,4},{12,8},{1,13},{5,1},{9,5},{13,9},{2,14},{6,2},{... | collective-permute-start | bytes 147464 | tf_op jit(solution)/shard_map/ppermute | solution.py:402
  32.6 1.7 %collective-permute-done.4.before = bf16[192,128]{1,0:T(8,128)(2,1)S(1)} collective-permute-done((bf16[192,128]{1,0:T(8,128)(2,1)S(1)}, bf16[192,128]{1,0:T(8,128)(2,1)S(1)}, u32[]{:S(2)}, u32[]{:S(2)}) %collective-permute-start.4) | collective-permute-done | bytes 49184 | tf_op jit(solution)/shard_map/ppermute | solution.py:402
  34.2 0.7 collective-permute-start.6
  34.9 0.2 pad_select_fusion.stem
  35.1 1.7 %dec_taps.1 = (bf16[3,2,2,192,384]{4,3,2,1,0:T(8,128)(2,1)S(1)}, bf16[3,2,2,192,384]{4,3,2,1,0:T(8,128)(2,1)S(1)}) custom-call(s32[4]{0:T(128)S(1)} %pad_add_fusion.place, bf16[5,4,192,384]{3,2,1,0:T(8,128)(2,1)S(1)} %bitcast.33, bf16[5,2,192,384]{3,2,1,0:T(8,128)(2,1)S(1)} %collective-permute-done.3.came), custom_call_target="tpu_custom_call" | custom-call | tf_op jit(solution)/shard_map/dec_taps/pallas_call | solution.py:479
  36.8 0.9 %targets.1 = bf16[2,272,384]{2,1,0:T(8,128)(2,1)S(1)} custom-call(s32[4]{0:T(128)S(1)} %pad_add_fusion.place, bf16[192,512]{1,0:T(8,128)(2,1)S(1)} %bitcast.40, bf16[192,128]{1,0:T(8,128)(2,1)S(1)} %collective-permute-done.4.before, bf16[192,128]{1,0:T(8,128)(2,1)S(1)} %collective-permute-done.5.after), custom_call_target="tpu_custom_call" | custom-call | tf_op jit(solution)/shard_map/targets/pallas_call | solution.py:372
  37.8 1.0 %collective-permute-done.6.refs_2_ = s32[2,256]{1,0:T(2,128)S(1)} collective-permute-done((s32[2,256]{1,0:T(2,128)S(1)}, s32[2,256]{1,0:T(2,128)S(1)}, u32[]{:S(2)}, u32[]{:S(2)}) %collective-permute-start.6) | collective-permute-done | bytes 2080 | tf_op jit(solution)/shard_map/ppermute | solution.py:402
  38.7 1.0 %gelu_pool.1 = (bf16[272,384]{1,0:T(8,128)(2,1)S(1)}, bf16[256,384]{1,0:T(8,128)(2,1)S(1)}) custom-call(s32[4]{0:T(128)S(1)} %pad_add_fusion.place, f32[544,384]{1,0:T(8,128)S(1)} %get-tuple-element.60.keep, bf16[544,384]{1,0:T(8,128)(2,1)S(1)} %collective-permute-done.8.came), custom_call_target="tpu_custom_call" | custom-call | tf_op jit(solution)/shard_map/gelu_pool/pallas_call | solution.py:372
  39.8 1.4 %collective-permute-done.9.oth = bf16[272,384]{1,0:T(8,128)(2,1)S(1)} collective-permute-done((bf16[272,384]{1,0:T(8,128)(2,1)S(1)}, bf16[272,384]{1,0:T(8,128)(2,1)S(1)}, u32[]{:S(2)}, u32[]{:S(2)}) %collective-permute-start.9) | collective-permute-done | bytes 208928 | tf_op jit(solution)/shard_map/ppermute | solution.py:517
  41.2 1.5 %dec_conv.1 = (f32[272,768]{1,0:T(8,128)S(1)}, bf16[272,768]{1,0:T(8,128)(2,1)S(1)}) custom-call(bf16[272,384]{1,0:T(8,128)(2,1)S(1)} %get-tuple-element.64.own, bf16[272,384]{1,0:T(8,128)(2,1)S(1)} %collective-permute-done.9.oth, bf16[3,768,384]{2,1,0:T(8,128)(2,1)S(1)} %bitcast.37, bf16[3,768,384]{2,1,0:T(8,128)(2,1)S(1)} %bitcast.38, ...), custom_call_target="tpu_custom_call" | custom-call | tf_op jit(solution)/shard_map/dec_conv/pallas_call | solution.py:372
  42.8 0.4 collective-permute-start.14
  43.2 2.5 %collective-permute-start.10 = (bf16[256,384]{1,0:T(8,128)(2,1)S(1)}, bf16[256,384]{1,0:T(8,128)(2,1)S(1)}, u32[]{:S(2)}, u32[]{:S(2)}) collective-permute-start(bf16[256,384]{1,0:T(8,128)(2,1)S(1)} %get-tuple-element.66.pool0), channel_id=1, source_target_pairs={{0,8},{4,12},{8,0},{12,4},{1,9},{5,13},{9,1},{13,5},{2,10},{6,14},... | collective-permute-start | bytes 589832 | tf_op jit(solution)/shard_map/ppermute | solution.py:405
  45.7 1.6 %collective-permute-start.11 = (bf16[256,384]{1,0:T(8,128)(2,1)S(1)}, bf16[256,384]{1,0:T(8,128)(2,1)S(1)}, u32[]{:S(2)}, u32[]{:S(2)}) collective-permute-start(bf16[256,384]{1,0:T(8,128)(2,1)S(1)} %get-tuple-element.66.pool0), channel_id=1, source_target_pairs={{0,4},{4,0},{8,12},{12,8},{1,5},{5,1},{9,13},{13,9},{2,6},{6,2},{1... | collective-permute-start | bytes 589832 | tf_op jit(solution)/shard_map/ppermute | solution.py:405
  47.2 2.6 %stem_taps.1.taps = bf16[960,2048]{1,0:T(8,128)(2,1)S(1)} custom-call(s32[4]{0:T(128)S(1)} %pad_add_fusion.place, s32[2,256]{1,0:T(2,128)S(1)} %get-tuple-element.100.refs_0_, s32[2,256]{1,0:T(2,128)S(1)} %get-tuple-element.99.refs_1_, s32[2,256]{1,0:T(2,128)S(1)} %collective-permute-done.6.refs_2_, s32[2,256]{1,0:T(2,128)S(1)} %get-tuple-element.98.refs_3_, ...), custom_call_target="tpu_custom_call" | custom-call | tf_op jit(solution)/shard_map/stem_taps/pallas_call | solution.py:372
  49.8 5.4 %owner_slope.2.slope0 = bf16[512,384]{1,0:T(8,128)(2,1)S(1)} custom-call(s32[4]{0:T(128)S(1)} %pad_add_fusion.place, s32[2,256]{1,0:T(2,128)S(1)} %get-tuple-element.100.refs_0_, s32[2,256]{1,0:T(2,128)S(1)} %get-tuple-element.99.refs_1_, s32[2,256]{1,0:T(2,128)S(1)} %collective-permute-done.6.refs_2_, s32[2,256]{1,0:T(2,128)S(1)} %get-tuple-element.98.refs_3_, ...), custom_call_target="tpu_custom_call" | custom-call | tf_op jit(solution)/shard_map/owner_slope/pallas_call | solution.py:372
  55.3 1.1 %out_slope.1 = (bf16[2,256,192]{2,1,0:T(8,128)(2,1)S(1)}, bf16[2,2,272,192]{3,2,1,0:T(8,128)(2,1)S(1)}, bf16[2,272,192]{2,1,0:T(8,128)(2,1)S(1)}, bf16[2,272,192...) custom-call(s32[4]{0:T(128)S(1)} %pad_add_fusion.place, f32[272,768]{1,0:T(8,128)S(1)} %get-tuple-element.72.part, ...), custom_call_target="tpu_custom_call" | custom-call | tf_op jit(solution)/shard_map/out_slope/pallas_call | solution.py:372
  56.4 1.2 %collective-permute-start.17 = (bf16[2,272,192]{2,1,0:T(8,128)(2,1)S(1)}, bf16[2,272,192]{2,1,0:T(8,128)(2,1)S(1)}, u32[]{:S(2)}, u32[]{:S(2)}) collective-permute-start(bf16[2,272,192]{2,1,0:T(8,128)(2,1)S(1)} %get-tuple-element.77), channel_id=1, source_target_pairs={{1,4},{3,6},{0,8},{2,10},{4,9},{6,11},{5,13},{7,15},{9,12},{11,14}... | collective-permute-start | bytes 626696 | tf_op jit(solution)/shard_map/ppermute | solution.py:594
  57.7 0.9 collective-permute-start.18
  58.6 2.1 %up_grad.1 = bf16[256,384]{1,0:T(8,128)(2,1)S(1)} custom-call(s32[4]{0:T(128)S(1)} %pad_add_fusion.place, bf16[2,2,272,192]{3,2,1,0:T(8,128)(2,1)S(1)} %get-tuple-element.76.own, bf16[2,2,272,192]{3,2,1,0:T(8,128)(2,1)S(1)} %collective-permute-done.15.oth, bf16[5,4,192,384]{3,2,1,0:T(8,128)(2,1)S(1)} %bitcast.34), custom_call_target="tpu_custom_call" | custom-call | tf_op jit(solution)/shard_map/up_grad/pallas_call | solution.py:372
  60.7 1.2 %collective-permute-start.16 = (bf16[256,384]{1,0:T(8,128)(2,1)S(1)}, bf16[256,384]{1,0:T(8,128)(2,1)S(1)}, u32[]{:S(2)}, u32[]{:S(2)}) collective-permute-start(bf16[256,384]{1,0:T(8,128)(2,1)S(1)} %up_grad.1), channel_id=1, source_target_pairs={{0,2},{1,3},{2,0},{3,1},{4,6},{5,7},{6,4},{7,5},{8,10},{9,11},{10,... | collective-permute-start | bytes 589832 | tf_op jit(solution)/shard_map/ppermute | solution.py:602
  61.9 5.4 %owner_slope.3.slope1 = bf16[512,384]{1,0:T(8,128)(2,1)S(1)} custom-call(s32[4]{0:T(128)S(1)} %pad_add_fusion.place, s32[2,256]{1,0:T(2,128)S(1)} %get-tuple-element.100.refs_0_, s32[2,256]{1,0:T(2,128)S(1)} %get-tuple-element.99.refs_1_, s32[2,256]{1,0:T(2,128)S(1)} %collective-permute-done.6.refs_2_, s32[2,256]{1,0:T(2,128)S(1)} %get-tuple-element.98.refs_3_, ...), custom_call_target="tpu_custom_call" | custom-call | tf_op jit(solution)/shard_map/owner_slope/pallas_call | solution.py:372
  67.3 5.3 %collective-permute-done.17 = bf16[2,272,192]{2,1,0:T(8,128)(2,1)S(1)} collective-permute-done((bf16[2,272,192]{2,1,0:T(8,128)(2,1)S(1)}, bf16[2,272,192]{2,1,0:T(8,128)(2,1)S(1)}, u32[]{:S(2)}, u32[]{:S(2)}) %collective-permute-start.17) | collective-permute-done | bytes 208928 | tf_op jit(solution)/shard_map/ppermute | solution.py:594
  72.9 0.9 %collective-permute-start.22 = (bf16[256,384]{1,0:T(8,128)(2,1)S(1)}, bf16[256,384]{1,0:T(8,128)(2,1)S(1)}, u32[]{:S(2)}, u32[]{:S(2)}) collective-permute-start(bf16[256,384]{1,0:T(8,128)(2,1)S(1)} %collective-permute-done.10.pool2), channel_id=1, source_target_pairs={{0,4},{4,0},{8,12},{12,8},{1,5},{5,1},{9,13},{13,9},{2,6},{6,2},{1... | collective-permute-start | bytes 589832 | tf_op jit(solution)/shard_map/ppermute | solution.py:405
  73.9 1.0 %collective-permute-start.19 = (bf16[256,384]{1,0:T(8,128)(2,1)S(1)}, bf16[256,384]{1,0:T(8,128)(2,1)S(1)}, u32[]{:S(2)}, u32[]{:S(2)}) collective-permute-start(bf16[256,384]{1,0:T(8,128)(2,1)S(1)} %get-tuple-element.91), channel_id=1, source_target_pairs={{1,4},{3,6},{0,8},{2,10},{4,9},{6,11},{5,13},{7,15},{9,12},{11,14}... | collective-permute-start | bytes 589832 | tf_op jit(solution)/shard_map/ppermute | solution.py:594
  74.8 0.7 collective-permute-start.20
  75.5 4.0 %collective-permute-start.24 = (bf16[512,384]{1,0:T(8,128)(2,1)S(1)}, bf16[512,384]{1,0:T(8,128)(2,1)S(1)}, u32[]{:S(2)}, u32[]{:S(2)}) collective-permute-start(bf16[512,384]{1,0:T(8,128)(2,1)S(1)} %owner_slope.2.slope0), channel_id=1, source_target_pairs={{0,1},{1,0},{2,3},{3,2},{4,5},{5,4},{6,7},{7,6},{8,9},{9,8},{10,11... | collective-permute-start | bytes 1179656 | tf_op jit(solution)/shard_map/ppermute | solution.py:562
  79.5 0.8 pred_.1
  80.4 1.9 %collective-permute-done.22.pool3 = bf16[256,384]{1,0:T(8,128)(2,1)S(1)} collective-permute-done((bf16[256,384]{1,0:T(8,128)(2,1)S(1)}, bf16[256,384]{1,0:T(8,128)(2,1)S(1)}, u32[]{:S(2)}, u32[]{:S(2)}) %collective-permute-start.22) | collective-permute-done | bytes 196640 | tf_op jit(solution)/shard_map/ppermute | solution.py:405
  82.3 3.5 %dec_grad.1 = f32[5,192,384]{2,1,0:T(8,128)} custom-call(s32[4]{0:T(128)S(1)} %pad_add_fusion.place, bf16[2,2,272,192]{3,2,1,0:T(8,128)(2,1)S(1)} %pad_maximum_fusion.own, bf16[2,2,272,192]{3,2,1,0:T(8,128)(2,1)S(1)} %collective-permute-done.21.came, bf16[256,384]{1,0:T(8,128)(2,1)S(1)} %get-tuple-element.66.pool0, ...), custom_call_target="tpu_custom_call" | custom-call | tf_op jit(solution)/shard_map/dec_grad/pallas_call | solution.py:372
  85.8 0.2 collective-permute-done.19
  86.1 0.4 collective-permute-start.23
  86.5 1.4 %collective-permute-done.23.came = bf16[2,256,384]{2,1,0:T(8,128)(2,1)S(1)} collective-permute-done((bf16[2,256,384]{2,1,0:T(8,128)(2,1)S(1)}, bf16[2,256,384]{2,1,0:T(8,128)(2,1)S(1)}, u32[]{:S(2)}, u32[]{:S(2)}) %collective-permute-start.23) | collective-permute-done | bytes 393248 | tf_op jit(solution)/shard_map/ppermute | solution.py:636
  87.9 4.2 %enc_grad.1 = f32[960,384]{1,0:T(8,128)} custom-call(s32[4]{0:T(128)S(1)} %pad_add_fusion.place, bf16[960,2048]{1,0:T(8,128)(2,1)S(1)} %stem_taps.1.taps, bf16[2,256,384]{2,1,0:T(8,128)(2,1)S(1)} %pad_maximum_fusion.1.own, bf16[2,256,384]{2,1,0:T(8,128)(2,1)S(1)} %collective-permute-done.23.came, bf16[512,384]{1,0:T(8,128)(2,1)S(1)} %owner_slope.2.slope0, ...), custom_call_target="tpu_custom_call" | custom-call | tf_op jit(solution)/shard_map/enc_grad/pallas_call | solution.py:637
  (41 shorter events, 0.8 us)
Async XLA Ops:
  0.6 4.4 %copy-start = (bf16[768,5,384]{2,0,1:T(8,128)(2,1)S(1)}, bf16[768,5,384]{2,0,1:T(8,128)(2,1)}, u32[]{:S(2)}) copy-start(bf16[768,5,384]{2,0,1:T(8,128)(2,1)} %param.8) | copy-start | bytes 8847364
  1.7 1.8 %copy-start.1 = (bf16[1536,5,192]{0,2,1:T(8,128)(2,1)S(1)}, bf16[1536,5,192]{0,2,1:T(8,128)(2,1)}, u32[]{:S(2)}) copy-start(bf16[1536,5,192]{0,2,1:T(8,128)(2,1)} %param.7) | copy-start | bytes 8847364
  4.5 11.6 %collective-permute-start.2 = (bf16[992,768]{1,0:T(8,128)(2,1)S(1)}, bf16[992,768]{1,0:T(8,128)(2,1)S(1)}, u32[]{:S(2)}, u32[]{:S(2)}) collective-permute-start(bf16[992,768]{1,0:T(8,128)(2,1)S(1)} %get-tuple-element.48), channel_id=1, source_target_pairs={{0,1},{1,0},{2,3},{3,2},{4,5},{5,4},{6,7},{7,6},{8,9},{9,8},{10,11... | collective-permute-start | bytes 4571144 | tf_op jit(solution)/shard_map/ppermute | solution.py:432
  5.1 4.1 %copy-start.4 = (s32[512]{0:T(512)S(1)}, s32[512]{0:T(512)}, u32[]{:S(2)}) copy-start(s32[512]{0:T(512)} %param.5) | copy-start | bytes 6148
  5.1 11.1 %copy-start.2 = (bf16[1536,5,192]{0,2,1:T(8,128)(2,1)S(1)}, bf16[1536,5,192]{0,2,1:T(8,128)(2,1)}, u32[]{:S(2)}) copy-start(bf16[1536,5,192]{0,2,1:T(8,128)(2,1)} %param.7) | copy-start | bytes 8847364
  6.1 24.2 %collective-permute-start.3 = (bf16[5,2,192,384]{3,2,1,0:T(8,128)(2,1)S(1)}, bf16[5,2,192,384]{3,2,1,0:T(8,128)(2,1)S(1)}, u32[]{:S(2)}, u32[]{:S(2)}) collective-permute-start(bf16[5,2,192,384]{3,2,1,0:T(8,128)(2,1)S(1)} %dec_pick.1), channel_id=1, source_target_pairs={{0,1},{1,0},{2,3},{3,2},{4,5},{5,4},{6,7},{7,6},{8,9},{9,8},{10,11... | collective-permute-start | bytes 4423688 | tf_op jit(solution)/shard_map/ppermute | solution.py:446
  6.2 20.2 %collective-permute-start.7 = (bf16[992,384]{1,0:T(8,128)(2,1)S(1)}, bf16[992,384]{1,0:T(8,128)(2,1)S(1)}, u32[]{:S(2)}, u32[]{:S(2)}) collective-permute-start(bf16[992,384]{1,0:T(8,128)(2,1)S(1)} %get-tuple-element.69.refs_4_), channel_id=1, source_target_pairs={{0,2},{1,3},{2,0},{3,1},{4,6},{5,7},{6,4},{7,5},{8,10},{9,11},{10,... | collective-permute-start | bytes 2285576 | tf_op jit(solution)/shard_map/ppermute | solution.py:433
  9.2 4.1 %collective-permute-start = (s32[1,512]{1,0:T(1,128)S(1)}, s32[1,512]{1,0:T(1,128)S(1)}, u32[]{:S(2)}, u32[]{:S(2)}) collective-permute-start(s32[1,512]{1,0:T(1,128)S(1)} %bitcast.41), channel_id=1, source_target_pairs={{0,4},{4,0},{8,12},{12,8},{1,5},{5,1},{9,13},{13,9},{2,6},{6,2},{1... | collective-permute-start | bytes 6152 | tf_op jit(solution)/shard_map/ppermute | solution.py:405
  10.8 5.4 %collective-permute-start.1 = (s32[1,512]{1,0:T(1,128)S(1)}, s32[1,512]{1,0:T(1,128)S(1)}, u32[]{:S(2)}, u32[]{:S(2)}) collective-permute-start(s32[1,512]{1,0:T(1,128)S(1)} %bitcast.42), channel_id=1, source_target_pairs={{0,12},{4,8},{8,4},{12,0},{1,13},{5,9},{9,5},{13,1},{2,14},{6,10},... | collective-permute-start | bytes 6152 | tf_op jit(solution)/shard_map/ppermute | solution.py:415
  19.4 8.8 %copy-start.3 = (bf16[512,192]{0,1:T(8,128)(2,1)S(1)}, bf16[512,192]{0,1:T(8,128)(2,1)}, u32[]{:S(2)}) copy-start(bf16[512,192]{0,1:T(8,128)(2,1)} %param.9) | copy-start | bytes 589828
  26.4 12.3 %collective-permute-start.8 = (bf16[544,384]{1,0:T(8,128)(2,1)S(1)}, bf16[544,384]{1,0:T(8,128)(2,1)S(1)}, u32[]{:S(2)}, u32[]{:S(2)}) collective-permute-start(bf16[544,384]{1,0:T(8,128)(2,1)S(1)} %get-tuple-element.62), channel_id=1, source_target_pairs={{0,2},{1,3},{2,0},{3,1},{4,6},{5,7},{6,4},{7,5},{8,10},{9,11},{10,... | collective-permute-start | bytes 1253384 | tf_op jit(solution)/shard_map/ppermute | solution.py:473
  28.2 6.0 %collective-permute-start.4 = (bf16[192,128]{1,0:T(8,128)(2,1)S(1)}, bf16[192,128]{1,0:T(8,128)(2,1)S(1)}, u32[]{:S(2)}, u32[]{:S(2)}) collective-permute-start(bf16[192,128]{1,0:T(8,128)(2,1)S(1)} %get-tuple-element.97), channel_id=1, source_target_pairs={{0,4},{4,8},{8,12},{12,0},{1,5},{5,9},{9,13},{13,1},{2,6},{6,10},{... | collective-permute-start | bytes 147464 | tf_op jit(solution)/shard_map/ppermute | solution.py:402
  29.8 20.0 %collective-permute-start.12 = (bf16[992,384]{1,0:T(8,128)(2,1)S(1)}, bf16[992,384]{1,0:T(8,128)(2,1)S(1)}, u32[]{:S(2)}, u32[]{:S(2)}) collective-permute-start(bf16[992,384]{1,0:T(8,128)(2,1)S(1)} %get-tuple-element.69.refs_4_), channel_id=1, source_target_pairs={{0,1},{1,0},{2,3},{3,2},{4,5},{5,4},{6,7},{7,6},{8,9},{9,8},{10,11... | collective-permute-start | bytes 2285576 | tf_op jit(solution)/shard_map/ppermute | solution.py:546
  29.8 20.0 %collective-permute-start.13 = (bf16[992,384]{1,0:T(8,128)(2,1)S(1)}, bf16[992,384]{1,0:T(8,128)(2,1)S(1)}, u32[]{:S(2)}, u32[]{:S(2)}) collective-permute-start(bf16[992,384]{1,0:T(8,128)(2,1)S(1)} %collective-permute-done.7.refs_5_), channel_id=1, source_target_pairs={{0,1},{1,0},{2,3},{3,2},{4,5},{5,4},{6,7},{7,6},{8,9},{9,8},{10,11... | collective-permute-start | bytes 2285576 | tf_op jit(solution)/shard_map/ppermute | solution.py:546
  30.3 6.5 %collective-permute-start.5 = (bf16[192,128]{1,0:T(8,128)(2,1)S(1)}, bf16[192,128]{1,0:T(8,128)(2,1)S(1)}, u32[]{:S(2)}, u32[]{:S(2)}) collective-permute-start(bf16[192,128]{1,0:T(8,128)(2,1)S(1)} %get-tuple-element.96), channel_id=1, source_target_pairs={{0,12},{4,0},{8,4},{12,8},{1,13},{5,1},{9,5},{13,9},{2,14},{6,2},{... | collective-permute-start | bytes 147464 | tf_op jit(solution)/shard_map/ppermute | solution.py:402
  34.2 4.5 %collective-permute-start.6 = (s32[2,256]{1,0:T(2,128)S(1)}, s32[2,256]{1,0:T(2,128)S(1)}, u32[]{:S(2)}, u32[]{:S(2)}) collective-permute-start(s32[2,256]{1,0:T(2,128)S(1)} %get-tuple-element.100.refs_0_), channel_id=1, source_target_pairs={{0,8},{4,12},{8,0},{12,4},{1,9},{5,13},{9,1},{13,5},{2,10},{6,14},... | collective-permute-start | bytes 6152 | tf_op jit(solution)/shard_map/ppermute | solution.py:402
  39.7 1.5 %collective-permute-start.9 = (bf16[272,384]{1,0:T(8,128)(2,1)S(1)}, bf16[272,384]{1,0:T(8,128)(2,1)S(1)}, u32[]{:S(2)}, u32[]{:S(2)}) collective-permute-start(bf16[272,384]{1,0:T(8,128)(2,1)S(1)} %get-tuple-element.64.own), channel_id=1, source_target_pairs={{0,1},{1,0},{2,3},{3,2},{4,5},{5,4},{6,7},{7,6},{8,9},{9,8},{10,11... | collective-permute-start | bytes 626696 | tf_op jit(solution)/shard_map/ppermute | solution.py:517
  42.8 12.5 %collective-permute-start.14 = (bf16[272,768]{1,0:T(8,128)(2,1)S(1)}, bf16[272,768]{1,0:T(8,128)(2,1)S(1)}, u32[]{:S(2)}, u32[]{:S(2)}) collective-permute-start(bf16[272,768]{1,0:T(8,128)(2,1)S(1)} %get-tuple-element.65), channel_id=1, source_target_pairs={{0,2},{1,3},{2,0},{3,1},{4,6},{5,7},{6,4},{7,5},{8,10},{9,11},{10,... | collective-permute-start | bytes 1253384 | tf_op jit(solution)/shard_map/ppermute | solution.py:533
  43.2 12.1 %collective-permute-start.10 = (bf16[256,384]{1,0:T(8,128)(2,1)S(1)}, bf16[256,384]{1,0:T(8,128)(2,1)S(1)}, u32[]{:S(2)}, u32[]{:S(2)}) collective-permute-start(bf16[256,384]{1,0:T(8,128)(2,1)S(1)} %get-tuple-element.66.pool0), channel_id=1, source_target_pairs={{0,8},{4,12},{8,0},{12,4},{1,9},{5,13},{9,1},{13,5},{2,10},{6,14},... | collective-permute-start | bytes 589832 | tf_op jit(solution)/shard_map/ppermute | solution.py:405
  45.7 9.6 %collective-permute-start.11 = (bf16[256,384]{1,0:T(8,128)(2,1)S(1)}, bf16[256,384]{1,0:T(8,128)(2,1)S(1)}, u32[]{:S(2)}, u32[]{:S(2)}) collective-permute-start(bf16[256,384]{1,0:T(8,128)(2,1)S(1)} %get-tuple-element.66.pool0), channel_id=1, source_target_pairs={{0,4},{4,0},{8,12},{12,8},{1,5},{5,1},{9,13},{13,9},{2,6},{6,2},{1... | collective-permute-start | bytes 589832 | tf_op jit(solution)/shard_map/ppermute | solution.py:405
  56.4 2.2 %collective-permute-start.15 = (bf16[2,2,272,192]{3,2,1,0:T(8,128)(2,1)S(1)}, bf16[2,2,272,192]{3,2,1,0:T(8,128)(2,1)S(1)}, u32[]{:S(2)}, u32[]{:S(2)}) collective-permute-start(bf16[2,2,272,192]{3,2,1,0:T(8,128)(2,1)S(1)} %get-tuple-element.76.own), channel_id=1, source_target_pairs={{0,1},{1,0},{2,3},{3,2},{4,5},{5,4},{6,7},{7,6},{8,9},{9,8},{10,11... | collective-permute-start | bytes 1253384 | tf_op jit(solution)/shard_map/ppermute | solution.py:574
  56.4 16.1 %collective-permute-start.17 = (bf16[2,272,192]{2,1,0:T(8,128)(2,1)S(1)}, bf16[2,272,192]{2,1,0:T(8,128)(2,1)S(1)}, u32[]{:S(2)}, u32[]{:S(2)}) collective-permute-start(bf16[2,272,192]{2,1,0:T(8,128)(2,1)S(1)} %get-tuple-element.77), channel_id=1, source_target_pairs={{1,4},{3,6},{0,8},{2,10},{4,9},{6,11},{5,13},{7,15},{9,12},{11,14}... | collective-permute-start | bytes 626696 | tf_op jit(solution)/shard_map/ppermute | solution.py:594
  57.7 14.9 %collective-permute-start.18 = (bf16[2,272,192]{2,1,0:T(8,128)(2,1)S(1)}, bf16[2,272,192]{2,1,0:T(8,128)(2,1)S(1)}, u32[]{:S(2)}, u32[]{:S(2)}) collective-permute-start(bf16[2,272,192]{2,1,0:T(8,128)(2,1)S(1)} %get-tuple-element.78), channel_id=1, source_target_pairs={{1,12},{3,14},{4,1},{6,3},{9,4},{11,6},{12,9},{14,11},{17,28},{19,... | collective-permute-start | bytes 626696 | tf_op jit(solution)/shard_map/ppermute | solution.py:595
  60.7 12.1 %collective-permute-start.16 = (bf16[256,384]{1,0:T(8,128)(2,1)S(1)}, bf16[256,384]{1,0:T(8,128)(2,1)S(1)}, u32[]{:S(2)}, u32[]{:S(2)}) collective-permute-start(bf16[256,384]{1,0:T(8,128)(2,1)S(1)} %up_grad.1), channel_id=1, source_target_pairs={{0,2},{1,3},{2,0},{3,1},{4,6},{5,7},{6,4},{7,5},{8,10},{9,11},{10,... | collective-permute-start | bytes 589832 | tf_op jit(solution)/shard_map/ppermute | solution.py:602
  72.8 9.4 %collective-permute-start.21 = (bf16[2,2,272,192]{3,2,1,0:T(8,128)(2,1)S(1)}, bf16[2,2,272,192]{3,2,1,0:T(8,128)(2,1)S(1)}, u32[]{:S(2)}, u32[]{:S(2)}) collective-permute-start(bf16[2,2,272,192]{3,2,1,0:T(8,128)(2,1)S(1)} %pad_maximum_fusion.own), channel_id=1, source_target_pairs={{0,1},{1,0},{2,3},{3,2},{4,5},{5,4},{6,7},{7,6},{8,9},{9,8},{10,11... | collective-permute-start | bytes 1253384 | tf_op jit(solution)/shard_map/ppermute | solution.py:611
  72.9 9.4 %collective-permute-start.22 = (bf16[256,384]{1,0:T(8,128)(2,1)S(1)}, bf16[256,384]{1,0:T(8,128)(2,1)S(1)}, u32[]{:S(2)}, u32[]{:S(2)}) collective-permute-start(bf16[256,384]{1,0:T(8,128)(2,1)S(1)} %collective-permute-done.10.pool2), channel_id=1, source_target_pairs={{0,4},{4,0},{8,12},{12,8},{1,5},{5,1},{9,13},{13,9},{2,6},{6,2},{1... | collective-permute-start | bytes 589832 | tf_op jit(solution)/shard_map/ppermute | solution.py:405
  73.9 12.1 %collective-permute-start.19 = (bf16[256,384]{1,0:T(8,128)(2,1)S(1)}, bf16[256,384]{1,0:T(8,128)(2,1)S(1)}, u32[]{:S(2)}, u32[]{:S(2)}) collective-permute-start(bf16[256,384]{1,0:T(8,128)(2,1)S(1)} %get-tuple-element.91), channel_id=1, source_target_pairs={{1,4},{3,6},{0,8},{2,10},{4,9},{6,11},{5,13},{7,15},{9,12},{11,14}... | collective-permute-start | bytes 589832 | tf_op jit(solution)/shard_map/ppermute | solution.py:594
  74.8 11.2 %collective-permute-start.20 = (bf16[256,384]{1,0:T(8,128)(2,1)S(1)}, bf16[256,384]{1,0:T(8,128)(2,1)S(1)}, u32[]{:S(2)}, u32[]{:S(2)}) collective-permute-start(bf16[256,384]{1,0:T(8,128)(2,1)S(1)} %get-tuple-element.90), channel_id=1, source_target_pairs={{1,12},{3,14},{4,1},{6,3},{9,4},{11,6},{12,9},{14,11},{17,28},{19,... | collective-permute-start | bytes 589832 | tf_op jit(solution)/shard_map/ppermute | solution.py:595
  75.5 11.0 %collective-permute-start.24 = (bf16[512,384]{1,0:T(8,128)(2,1)S(1)}, bf16[512,384]{1,0:T(8,128)(2,1)S(1)}, u32[]{:S(2)}, u32[]{:S(2)}) collective-permute-start(bf16[512,384]{1,0:T(8,128)(2,1)S(1)} %owner_slope.2.slope0), channel_id=1, source_target_pairs={{0,1},{1,0},{2,3},{3,2},{4,5},{5,4},{6,7},{7,6},{8,9},{9,8},{10,11... | collective-permute-start | bytes 1179656 | tf_op jit(solution)/shard_map/ppermute | solution.py:562
  82.3 4.3 %collective-permute-start.25 = (bf16[512,384]{1,0:T(8,128)(2,1)S(1)}, bf16[512,384]{1,0:T(8,128)(2,1)S(1)}, u32[]{:S(2)}, u32[]{:S(2)}) collective-permute-start(bf16[512,384]{1,0:T(8,128)(2,1)S(1)} %owner_slope.3.slope1), channel_id=1, source_target_pairs={{0,1},{1,0},{2,3},{3,2},{4,5},{5,4},{6,7},{7,6},{8,9},{9,8},{10,11... | collective-permute-start | bytes 1179656 | tf_op jit(solution)/shard_map/ppermute | solution.py:562
  86.1 1.8 %collective-permute-start.23 = (bf16[2,256,384]{2,1,0:T(8,128)(2,1)S(1)}, bf16[2,256,384]{2,1,0:T(8,128)(2,1)S(1)}, u32[]{:S(2)}, u32[]{:S(2)}) collective-permute-start(bf16[2,256,384]{2,1,0:T(8,128)(2,1)S(1)} %pad_maximum_fusion.1.own), channel_id=1, source_target_pairs={{0,1},{1,0},{2,3},{3,2},{4,5},{5,4},{6,7},{7,6},{8,9},{9,8},{10,11... | collective-permute-start | bytes 1179656 | tf_op jit(solution)/shard_map/ppermute | solution.py:636

commit v4 on v3

--- a/solution.py
+++ b/solution.py
@@ -14,6 +14,7 @@
 CUBIC = 0.044715
 
 STEM_ROWS = 32
+FIRST = 3
 SIDE = 64
 OUTER = 16
 INNER = 8
@@ -231,8 +232,8 @@
 
 
 def owner_slope_kernel(place, *refs, slot, pairs, devices):
-    blocks, weights = refs[:devices], refs[devices : devices + 4]
-    out, bases, even, odd, lhs = refs[devices + 4 :]
+    blocks, weights = refs[:devices], refs[devices : devices + 6]
+    out, bases, even, odd, lhs = refs[devices + 6 :]
     for r in range(devices):
         bases[r] = blocks[r][...]
     wide = pairs + 2 * INNER
@@ -242,9 +243,10 @@
     joined = assemble(bases[step], bases[after], bases[before], block, devices)
     hots = tap_onehots(joined, -INNER, wide)
     total = jnp.zeros(out.shape, F32)
-    for kernel in weights:
-        channels = lhs.shape[2]
-        weight = kernel[KW * channels : KW * channels + 4 * KW, :channels]
+    channels = lhs.shape[2]
+    for some, others in ((0, None), (1, None), (2, 3), (4, 5)):
+        count = KW if others is None else FIRST
+        weight = weights[some][count * channels : count * channels + 4 * KW, :channels]
         for hot, held in zip(hots, (even, odd)):
             raw = dot(hot, weight, ((0,), (0,)))
             ok = valid_pairs(raw.shape, 0, block * pairs - INNER, pairs * devices)
@@ -253,9 +255,9 @@
             source = even if k % 2 == 0 else odd
             lhs[k] = source[INNER + k // 2 - 1 : INNER + k // 2 - 1 + pairs, :].astype(BF16)
         for k in range(KW):
-            total = total + dot(
-                lhs[k : k + 2].reshape(2 * pairs, -1), kernel[k * channels : (k + 1) * channels, :], ((1,), (0,))
-            )
+            at, step = (some, k) if k < count else (others, k - count)
+            tap = weights[at][step * channels : (step + 1) * channels, :]
+            total = total + dot(lhs[k : k + 2].reshape(2 * pairs, -1), tap, ((1,), (0,)))
     out[...] = gelu_slope(total).astype(BF16)
 
 
@@ -284,10 +286,10 @@
             out[k * channels : (k + 1) * channels, at + pairs : at + 2 * pairs] = taps[k + 1]
 
 
-def picks_kernel(place, stem, enc, mine, enc_oth, sems):
+def picks_kernel(place, stem, enc, mine, mine0, mine1, enc_oth, sems):
     seq, core = place[0], 1 - place[2]
     taps, channels, _ = enc.shape
-    block = mine.shape[1]
+    block = mine0.shape[1]
 
     def columns(index):
         return pl.ds(pl.multiple_of(index * block, 128), block)
@@ -298,10 +300,15 @@
         for h in range(2):
             copies.append((enc.at[k, :, columns(2 * h + core)], enc_oth.at[rows, h * block : (h + 1) * block]))
         copies.append((enc.at[k, :, columns(seq)], mine.at[rows]))
+        if k < FIRST:
+            copies.append((enc.at[k, :, columns(seq)], mine0.at[rows]))
+        else:
+            copies.append((enc.at[k, :, columns(seq)], mine1.at[pl.ds((k - FIRST) * channels, channels)]))
     copies = [pltpu.make_async_copy(*ends, sems.at[i]) for i, ends in enumerate(copies)]
     for copy in copies:
         copy.start()
     enc_oth[taps * channels :, : stem.shape[1]] = stem[...]
+    mine0[FIRST * channels :, : stem.shape[1]] = stem[...]
     mine[taps * channels :, : stem.shape[1]] = stem[...]
     for copy in copies:
         copy.wait()
@@ -417,20 +424,22 @@
     dec_w = w_dec.transpose(1, 0, 2).reshape(KW, 4, stem_c, enc_c)
     picked = (KW, 1, stem_c, enc_c)
     stem_rows = jnp.concatenate([stem_w, jnp.zeros((STEM_ROWS - 4 * KW, stem_c), BF16)])
-    mine, enc_send = pl.pallas_call(
+    mine, mine0, mine1, enc_send = pl.pallas_call(
         picks_kernel,
         in_specs=[SCALARS, whole(stem_rows.shape), pl.BlockSpec(memory_space=pl.ANY)],
-        out_specs=[pl.BlockSpec(memory_space=pltpu.VMEM)] * 2,
+        out_specs=[pl.BlockSpec(memory_space=pltpu.VMEM)] * 4,
         out_shape=[
             jax.ShapeDtypeStruct((KW * stem_c + STEM_ROWS, enc_c), BF16),
+            jax.ShapeDtypeStruct((FIRST * stem_c + STEM_ROWS, enc_c), BF16),
+            jax.ShapeDtypeStruct(((KW - FIRST) * stem_c, enc_c), BF16),
             jax.ShapeDtypeStruct((KW * stem_c + STEM_ROWS, 2 * enc_c), BF16),
         ],
-        scratch_shapes=[pltpu.SemaphoreType.DMA((3 * KW,))],
-        compiler_params=pltpu.CompilerParams(vmem_limit_bytes=5 * MIB),
+        scratch_shapes=[pltpu.SemaphoreType.DMA((4 * KW,))],
+        compiler_params=pltpu.CompilerParams(vmem_limit_bytes=6 * MIB),
         name="picks",
     )(place, stem_rows, enc_w)
     enc_oth = lax.ppermute(enc_send, "chan", cores)
-    mine_far = lax.ppermute(mine, "chan", across)
+    mine0_far = lax.ppermute(mine0, "chan", across)
     dec_send = pl.pallas_call(
         pick_kernel,
         grid_spec=pltpu.PrefetchScalarGridSpec(
@@ -470,7 +479,7 @@
         limit=12,
         name="enc_conv",
     )
-    came = lax.ppermute(gated(send, mine_far), "chan", across)
+    came = lax.ppermute(gated(send, mine0_far), "chan", across)
 
     targets_in, place_in = gated((targets, place), send)
     blocks = {0: split[0], 1: split[2], devices - 1: split[1]}
@@ -493,9 +502,11 @@
     )(place_in, dec_w, dec_came)
     targets_in = targets_in.T
     count, edge = 2 * pairs, 2 * SIDE
+    below, above = ring(targets_in[:, count - edge :], 1), ring(targets_in[:, :edge], devices - 1)
+    mine1_far = lax.ppermute(gated(mine1, below), "chan", across)
     (targets_at,) = call(
         targets_kernel,
-        [place, targets_in, ring(targets_in[:, count - edge :], 1), ring(targets_in[:, :edge], devices - 1)],
+        [place, targets_in, below, above],
         [((2, rows, 2 * stem_c), BF16)],
         [((count + 2 * edge, 128), F32)],
         limit=6,
@@ -530,20 +541,13 @@
         limit=11,
         name="dec_conv",
     )
-    came = lax.ppermute(send, "chan", across)
+    came = lax.ppermute(gated(send, mine1_far), "chan", across)
 
     centre, place_in = gated((centre, place), send)
     beyond, beside = swap(centre, 2), swap(centre, 1)
-    (taps,) = call(
-        functools.partial(taps_kernel, pairs=pairs, devices=devices),
-        [place_in] + [blocks[r] for r in range(devices)] + [stem_w],
-        [((KW * stem_c, 2 * pairs * devices), BF16)],
-        limit=12,
-        name="stem_taps",
-    )
-
-    weights = [mine, mine_far]
-    weights += [lax.ppermute(w, "chan", cores) for w in gated(weights, keep)]
+
+    weights = [mine, lax.ppermute(gated(mine, keep), "chan", cores), mine0_far, mine1_far]
+    weights += [lax.ppermute(w, "chan", cores) for w in weights[2:]]
 
     def owner_slope(slot, at):
         (out,) = call(
@@ -561,7 +565,7 @@
         )
         return out, lax.ppermute(out, "chan", cores)
 
-    slope0, slope0_came = owner_slope(0, gated(place, taps))
+    slope0, slope0_came = owner_slope(0, gated(place, send))
 
     pred, sums, local, near, far = call(
         functools.partial(slope_kernel, pairs=pairs, total=total, scale=1.0 / math.sqrt(2 * total)),
@@ -601,10 +605,17 @@
     local, near, far = to_owner(local, near, far)
     pre_oth = lax.ppermute(pre, "chan", across)
     slope1, slope1_came = owner_slope(1, gated(place, pre))
-    near, far = gated((near, far), slope1)
+    (taps,) = call(
+        functools.partial(taps_kernel, pairs=pairs, devices=devices),
+        [gated(place, slope1)] + [blocks[r] for r in range(devices)] + [stem_w],
+        [((KW * stem_c, 2 * pairs * devices), BF16)],
+        limit=12,
+        name="stem_taps",
+    )
+    near, far = gated((near, far), taps)
     far_pooled = swap(beyond, 1)
     sums_pieces = local, near, far
-    pre_oth = gated(pre_oth, (near, far, slope1))
+    pre_oth = gated(pre_oth, (near, far, slope1, taps))
     pieces = [jnp.where(own_block, pre, pre_oth) for own_block in target]
     local, near, far = to_owner(*pieces)
     sums_mine = gated(slots(*sums_pieces), pieces)

time: 92.3 us -> 90.4 us (0.979)
  waiting for transfers between devices: 20.7 us -> 18.4 us
    ppermute x4, waiting for transfers between devices: 1.94 us -> 6.1 us  [swap(): lax.ppermute(array, 'seq', [(i, i ^ distance) for i in range(devices)])]
    ppermute x5 -> x7, waiting for transfers between devices: 4.91 us -> 1.56 us  [the longest x1 1.54 us: shards(): mine1_far = lax.ppermute(gated(mine1, below), 'chan', across)]
    ppermute x2, waiting for transfers between devices: 5.48 us -> 2.98 us  [to_owner(): near = lax.ppermute(near, ('seq', 'chan'), link((1, 2)))]
    ppermute x5 -> x7, starting transfers between devices: 5.57 us -> 5.21 us  [the longest x1 2.94 us: shards(): mine0_far = lax.ppermute(mine0, 'chan', across)]
  transfers between devices with their start and end apart: 26 -> 28, of which waited for: 9 -> 10; matrix products, arithmetic and copies ran while one was open for 0% -> 0% of each run, Pallas kernels for 34% -> 35%
where the time goes in v4:
time: 90.4 us; the launch traced here: 89.6 us
  Pallas kernels  37.6 us (42%)
  starting transfers between devices  29.2 us (32%)
  waiting for transfers between devices  18.4 us (20%)
  local copies, waits for them, and re-layouts  2.74 us (3%)
  between operations  0.98 us (1%)
    pallas_call x12, Pallas kernels, call(): pl.pallas_call(kernel, grid=(1,) if last else (), in_specs=specs, out_spe...  29.6 us
    ppermute x4, waiting for transfers between devices, swap(): lax.ppermute(array, 'seq', [(i, i ^ distance) for i in range(devices)])  6.1 us
    ppermute x4, starting transfers between devices, swap(): lax.ppermute(array, 'seq', [(i, i ^ distance) for i in range(devices)])  6.07 us
    ppermute x3, starting transfers between devices, ring(): lax.ppermute(array, 'seq', [(i, (i + step) % devices) for i in range(devi...  4.8 us
    pallas_call x1, Pallas kernels, shards(): pl.pallas_call(enc_grad_kernel, grid=(2,), in_specs=[SCALARS, pl.BlockSpe...  4.15 us
    ppermute x2, starting transfers between devices, owner_slope(): return (out, lax.ppermute(out, 'chan', cores))  4 us
    ppermute x2, waiting for transfers between devices, to_owner(): near = lax.ppermute(near, ('seq', 'chan'), link((1, 2)))  2.98 us
    ppermute x1, starting transfers between devices, shards(): mine0_far = lax.ppermute(mine0, 'chan', across)  2.94 us
  transfers between devices with their start and end apart: 28, of which 10 were waited for; matrix products, arithmetic and copies ran while one was open for 0% of the time, Pallas kernels for 35%

profile of v4, /device:TPU:0, one launch (start us, length us, event | category | flops | bytes accessed | tf_op | source)
XLA Modules:
  0.0 89.6 jit_solution(5714957001125886316)
XLA Ops:
  0.9 0.9 reshape.25.stem_own.refs_4_
  1.8 1.8 %copy-done.1 = bf16[1536,5,192]{0,2,1:T(8,128)(2,1)S(1)} copy-done((bf16[1536,5,192]{0,2,1:T(8,128)(2,1)S(1)}, bf16[1536,5,192]{0,2,1:T(8,128)(2,1)}, u32[]{:S(2)}) %copy-start.1) | copy-done | bytes 2949144
  3.6 1.1 %picks.1 = (bf16[992,384]{1,0:T(8,128)(2,1)S(1)}, bf16[608,384]{1,0:T(8,128)(2,1)S(1)}, bf16[384,384]{1,0:T(8,128)(2,1)S(1)}, bf16[992,768]{1,0:T(8,128)(2,1)S(1)}) custom-call(s32[4]{0:T(128)S(1)} %pad_add_fusion.place, bf16[32,192]{1,0:T(8,128)(2,1)S(1)} %concatenate.9.stem, bf16[5,192,1536]{2,1,0:T(8,128)(2,1)S(1)} %bitcast.35), custom_call_target="tpu_custom_call" | custom-call | tf_op jit(solution)/shard_map/picks/pallas_call | solution.py:427
  4.7 0.5 collective-permute-start.2
  5.2 1.1 %dec_pick.1 = bf16[5,2,192,384]{3,2,1,0:T(8,128)(2,1)S(1)} custom-call(s32[4]{0:T(128)S(1)} %pad_add_fusion.place, bf16[5,4,192,384]{3,2,1,0:T(8,128)(2,1)S(1)} %bitcast.32), custom_call_target="tpu_custom_call" | custom-call | tf_op jit(solution)/shard_map/dec_pick/pallas_call | solution.py:443
  6.4 2.9 %collective-permute-start.7 = (bf16[608,384]{1,0:T(8,128)(2,1)S(1)}, bf16[608,384]{1,0:T(8,128)(2,1)S(1)}, u32[]{:S(2)}, u32[]{:S(2)}) collective-permute-start(bf16[608,384]{1,0:T(8,128)(2,1)S(1)} %get-tuple-element.64), channel_id=1, source_target_pairs={{0,2},{1,3},{2,0},{3,1},{4,6},{5,7},{6,4},{7,5},{8,10},{9,11},{10,... | collective-permute-start | bytes 1400840 | tf_op jit(solution)/shard_map/ppermute | solution.py:442
  9.3 1.6 %collective-permute-start = (s32[1,512]{1,0:T(1,128)S(1)}, s32[1,512]{1,0:T(1,128)S(1)}, u32[]{:S(2)}, u32[]{:S(2)}) collective-permute-start(s32[1,512]{1,0:T(1,128)S(1)} %bitcast.41), channel_id=1, source_target_pairs={{0,4},{4,0},{8,12},{12,8},{1,5},{5,1},{9,13},{13,9},{2,6},{6,2},{1... | collective-permute-start | bytes 6152 | tf_op jit(solution)/shard_map/ppermute | solution.py:412
  10.9 2.5 %collective-permute-start.1 = (s32[1,512]{1,0:T(1,128)S(1)}, s32[1,512]{1,0:T(1,128)S(1)}, u32[]{:S(2)}, u32[]{:S(2)}) collective-permute-start(s32[1,512]{1,0:T(1,128)S(1)} %bitcast.42), channel_id=1, source_target_pairs={{0,12},{4,8},{8,4},{12,0},{1,13},{5,9},{9,5},{13,1},{2,14},{6,10},... | collective-permute-start | bytes 6152 | tf_op jit(solution)/shard_map/ppermute | solution.py:422
  13.4 2.9 %collective-permute-done.1.before = s32[1,512]{1,0:T(1,128)S(1)} collective-permute-done((s32[1,512]{1,0:T(1,128)S(1)}, s32[1,512]{1,0:T(1,128)S(1)}, u32[]{:S(2)}, u32[]{:S(2)}) %collective-permute-start.1) | collective-permute-done | bytes 2080 | tf_op jit(solution)/shard_map/ppermute | solution.py:422
  16.3 3.2 %stem_conv.1 = (f32[544,768]{1,0:T(8,128)S(1)}, bf16[2,272,192]{2,1,0:T(8,128)(2,1)S(1)}, bf16[6,272,192]{2,1,0:T(8,128)(2,1)S(1)}, s32[3,2,256]{2,1,0:T(2,128)S(1)}) custom-call(s32[4]{0:T(128)S(1)} %pad_add_fusion.place, s32[1,512]{1,0:T(1,128)S(1)} %bitcast.43, s32[1,512]{1,0:T(1,128)S(1)} %collective-permute-done.after, ...), custom_call_target="tpu_custom_call" | custom-call | tf_op jit(solution)/shard_map/stem_conv/pallas_call | solution.py:379
  19.5 2.1 %enc_conv.1 = (f32[544,384]{1,0:T(8,128)S(1)}, bf16[544,384]{1,0:T(8,128)(2,1)S(1)}) custom-call(s32[4]{0:T(128)S(1)} %pad_add_fusion.place, f32[544,768]{1,0:T(8,128)S(1)} %get-tuple-element.52.acc, bf16[6,272,192]{2,1,0:T(8,128)(2,1)S(1)} %get-tuple-element.53.lhs, bf16[992,768]{1,0:T(8,128)(2,1)S(1)} %collective-permute-done.2.w_oth), custom_call_target="tpu_custom_call" | custom-call | tf_op jit(solution)/shard_map/enc_conv/pallas_call | solution.py:379
  21.7 0.6 collective-permute-start.8
  22.3 1.4 %collective-permute-start.4 = (bf16[192,128]{1,0:T(8,128)(2,1)S(1)}, bf16[192,128]{1,0:T(8,128)(2,1)S(1)}, u32[]{:S(2)}, u32[]{:S(2)}) collective-permute-start(bf16[192,128]{1,0:T(8,128)(2,1)S(1)} %get-tuple-element.103), channel_id=1, source_target_pairs={{0,4},{4,8},{8,12},{12,0},{1,5},{5,9},{9,13},{13,1},{2,6},{6,10},{... | collective-permute-start | bytes 147464 | tf_op jit(solution)/shard_map/ppermute | solution.py:409
  23.6 2.5 %collective-permute-start.5 = (bf16[192,128]{1,0:T(8,128)(2,1)S(1)}, bf16[192,128]{1,0:T(8,128)(2,1)S(1)}, u32[]{:S(2)}, u32[]{:S(2)}) collective-permute-start(bf16[192,128]{1,0:T(8,128)(2,1)S(1)} %get-tuple-element.102), channel_id=1, source_target_pairs={{0,12},{4,0},{8,4},{12,8},{1,13},{5,1},{9,5},{13,9},{2,14},{6,2},{... | collective-permute-start | bytes 147464 | tf_op jit(solution)/shard_map/ppermute | solution.py:409
  26.2 2.1 %collective-permute-done.4.before = bf16[192,128]{1,0:T(8,128)(2,1)S(1)} collective-permute-done((bf16[192,128]{1,0:T(8,128)(2,1)S(1)}, bf16[192,128]{1,0:T(8,128)(2,1)S(1)}, u32[]{:S(2)}, u32[]{:S(2)}) %collective-permute-start.4) | collective-permute-done | bytes 49184 | tf_op jit(solution)/shard_map/ppermute | solution.py:409
  28.3 0.9 %collective-permute-start.6 = (s32[2,256]{1,0:T(2,128)S(1)}, s32[2,256]{1,0:T(2,128)S(1)}, u32[]{:S(2)}, u32[]{:S(2)}) collective-permute-start(s32[2,256]{1,0:T(2,128)S(1)} %get-tuple-element.106.refs_0_), channel_id=1, source_target_pairs={{0,8},{4,12},{8,0},{12,4},{1,9},{5,13},{9,1},{13,5},{2,10},{6,14},... | collective-permute-start | bytes 6152 | tf_op jit(solution)/shard_map/ppermute | solution.py:409
  29.2 0.7 collective-permute-start.13
  30.1 1.7 %dec_taps.1 = (bf16[3,2,2,192,384]{4,3,2,1,0:T(8,128)(2,1)S(1)}, bf16[3,2,2,192,384]{4,3,2,1,0:T(8,128)(2,1)S(1)}) custom-call(s32[4]{0:T(128)S(1)} %pad_add_fusion.place, bf16[5,4,192,384]{3,2,1,0:T(8,128)(2,1)S(1)} %bitcast.33, bf16[5,2,192,384]{3,2,1,0:T(8,128)(2,1)S(1)} %collective-permute-done.3.came), custom_call_target="tpu_custom_call" | custom-call | tf_op jit(solution)/shard_map/dec_taps/pallas_call | solution.py:488
  31.8 0.9 %targets.1 = bf16[2,272,384]{2,1,0:T(8,128)(2,1)S(1)} custom-call(s32[4]{0:T(128)S(1)} %pad_add_fusion.place, bf16[192,512]{1,0:T(8,128)(2,1)S(1)} %bitcast.40, bf16[192,128]{1,0:T(8,128)(2,1)S(1)} %collective-permute-done.4.before, bf16[192,128]{1,0:T(8,128)(2,1)S(1)} %collective-permute-done.5.after), custom_call_target="tpu_custom_call" | custom-call | tf_op jit(solution)/shard_map/targets/pallas_call | solution.py:379
  32.8 1.0 %gelu_pool.1 = (bf16[272,384]{1,0:T(8,128)(2,1)S(1)}, bf16[256,384]{1,0:T(8,128)(2,1)S(1)}) custom-call(s32[4]{0:T(128)S(1)} %pad_add_fusion.place, f32[544,384]{1,0:T(8,128)S(1)} %get-tuple-element.63.keep, bf16[544,384]{1,0:T(8,128)(2,1)S(1)} %collective-permute-done.8.came), custom_call_target="tpu_custom_call" | custom-call | tf_op jit(solution)/shard_map/gelu_pool/pallas_call | solution.py:379
  34.0 1.3 %collective-permute-done.9.oth = bf16[272,384]{1,0:T(8,128)(2,1)S(1)} collective-permute-done((bf16[272,384]{1,0:T(8,128)(2,1)S(1)}, bf16[272,384]{1,0:T(8,128)(2,1)S(1)}, u32[]{:S(2)}, u32[]{:S(2)}) %collective-permute-start.9) | collective-permute-done | bytes 208928 | tf_op jit(solution)/shard_map/ppermute | solution.py:528
  35.2 1.5 %dec_conv.1 = (f32[272,768]{1,0:T(8,128)S(1)}, bf16[272,768]{1,0:T(8,128)(2,1)S(1)}) custom-call(bf16[272,384]{1,0:T(8,128)(2,1)S(1)} %get-tuple-element.67.own, bf16[272,384]{1,0:T(8,128)(2,1)S(1)} %collective-permute-done.9.oth, bf16[3,768,384]{2,1,0:T(8,128)(2,1)S(1)} %bitcast.37, bf16[3,768,384]{2,1,0:T(8,128)(2,1)S(1)} %bitcast.38, ...), custom_call_target="tpu_custom_call" | custom-call | tf_op jit(solution)/shard_map/dec_conv/pallas_call | solution.py:379
  36.8 1.5 %collective-permute-done.13.refs_7_ = bf16[384,384]{1,0:T(8,128)(2,1)S(1)} collective-permute-done((bf16[384,384]{1,0:T(8,128)(2,1)S(1)}, bf16[384,384]{1,0:T(8,128)(2,1)S(1)}, u32[]{:S(2)}, u32[]{:S(2)}) %collective-permute-start.13) | collective-permute-done | bytes 294944 | tf_op jit(solution)/shard_map/ppermute | solution.py:506
  38.3 1.0 %collective-permute-start.16 = (bf16[272,768]{1,0:T(8,128)(2,1)S(1)}, bf16[272,768]{1,0:T(8,128)(2,1)S(1)}, u32[]{:S(2)}, u32[]{:S(2)}) collective-permute-start(bf16[272,768]{1,0:T(8,128)(2,1)S(1)} %get-tuple-element.77), channel_id=1, source_target_pairs={{0,2},{1,3},{2,0},{3,1},{4,6},{5,7},{6,4},{7,5},{8,10},{9,11},{10,... | collective-permute-start | bytes 1253384 | tf_op jit(solution)/shard_map/ppermute | solution.py:544
  39.3 2.6 %collective-permute-start.10 = (bf16[256,384]{1,0:T(8,128)(2,1)S(1)}, bf16[256,384]{1,0:T(8,128)(2,1)S(1)}, u32[]{:S(2)}, u32[]{:S(2)}) collective-permute-start(bf16[256,384]{1,0:T(8,128)(2,1)S(1)} %get-tuple-element.69.pool0), channel_id=1, source_target_pairs={{0,8},{4,12},{8,0},{12,4},{1,9},{5,13},{9,1},{13,5},{2,10},{6,14},... | collective-permute-start | bytes 589832 | tf_op jit(solution)/shard_map/ppermute | solution.py:412
  41.9 1.4 %collective-permute-start.11 = (bf16[256,384]{1,0:T(8,128)(2,1)S(1)}, bf16[256,384]{1,0:T(8,128)(2,1)S(1)}, u32[]{:S(2)}, u32[]{:S(2)}) collective-permute-start(bf16[256,384]{1,0:T(8,128)(2,1)S(1)} %get-tuple-element.69.pool0), channel_id=1, source_target_pairs={{0,4},{4,0},{8,12},{12,8},{1,5},{5,1},{9,13},{13,9},{2,6},{6,2},{1... | collective-permute-start | bytes 589832 | tf_op jit(solution)/shard_map/ppermute | solution.py:412
  43.3 5.4 %owner_slope.2.slope0 = bf16[512,384]{1,0:T(8,128)(2,1)S(1)} custom-call(s32[4]{0:T(128)S(1)} %pad_add_fusion.place, s32[2,256]{1,0:T(2,128)S(1)} %get-tuple-element.106.refs_0_, s32[2,256]{1,0:T(2,128)S(1)} %get-tuple-element.105.refs_1_, s32[2,256]{1,0:T(2,128)S(1)} %collective-permute-done.6.refs_2_, s32[2,256]{1,0:T(2,128)S(1)} %get-tuple-element.104.refs_3_, ...), custom_call_target="tpu_custom_call" | custom-call | tf_op jit(solution)/shard_map/owner_slope/pallas_call | solution.py:379
  48.7 3.2 %collective-permute-done.10.pool2 = bf16[256,384]{1,0:T(8,128)(2,1)S(1)} collective-permute-done((bf16[256,384]{1,0:T(8,128)(2,1)S(1)}, bf16[256,384]{1,0:T(8,128)(2,1)S(1)}, u32[]{:S(2)}, u32[]{:S(2)}) %collective-permute-start.10) | collective-permute-done | bytes 196640 | tf_op jit(solution)/shard_map/ppermute | solution.py:412
  51.8 0.4 collective-permute-done.11.pool1
  52.2 1.1 %out_slope.1 = (bf16[2,256,192]{2,1,0:T(8,128)(2,1)S(1)}, bf16[2,2,272,192]{3,2,1,0:T(8,128)(2,1)S(1)}, bf16[2,272,192]{2,1,0:T(8,128)(2,1)S(1)}, bf16[2,272,192...) custom-call(s32[4]{0:T(128)S(1)} %pad_add_fusion.place, f32[272,768]{1,0:T(8,128)S(1)} %get-tuple-element.76.part, ...), custom_call_target="tpu_custom_call" | custom-call | tf_op jit(solution)/shard_map/out_slope/pallas_call | solution.py:379
  53.4 1.0 %collective-permute-start.19 = (bf16[2,272,192]{2,1,0:T(8,128)(2,1)S(1)}, bf16[2,272,192]{2,1,0:T(8,128)(2,1)S(1)}, u32[]{:S(2)}, u32[]{:S(2)}) collective-permute-start(bf16[2,272,192]{2,1,0:T(8,128)(2,1)S(1)} %get-tuple-element.84), channel_id=1, source_target_pairs={{1,4},{3,6},{0,8},{2,10},{4,9},{6,11},{5,13},{7,15},{9,12},{11,14}... | collective-permute-start | bytes 626696 | tf_op jit(solution)/shard_map/ppermute | solution.py:598
  54.4 0.8 collective-permute-start.20
  55.3 2.1 %up_grad.1 = bf16[256,384]{1,0:T(8,128)(2,1)S(1)} custom-call(s32[4]{0:T(128)S(1)} %pad_add_fusion.place, bf16[2,2,272,192]{3,2,1,0:T(8,128)(2,1)S(1)} %get-tuple-element.79.own, bf16[2,2,272,192]{3,2,1,0:T(8,128)(2,1)S(1)} %collective-permute-done.17.oth, bf16[5,4,192,384]{3,2,1,0:T(8,128)(2,1)S(1)} %bitcast.34), custom_call_target="tpu_custom_call" | custom-call | tf_op jit(solution)/shard_map/up_grad/pallas_call | solution.py:379
  57.4 1.2 %collective-permute-start.18 = (bf16[256,384]{1,0:T(8,128)(2,1)S(1)}, bf16[256,384]{1,0:T(8,128)(2,1)S(1)}, u32[]{:S(2)}, u32[]{:S(2)}) collective-permute-start(bf16[256,384]{1,0:T(8,128)(2,1)S(1)} %up_grad.1), channel_id=1, source_target_pairs={{0,2},{1,3},{2,0},{3,1},{4,6},{5,7},{6,4},{7,5},{8,10},{9,11},{10,... | collective-permute-start | bytes 589832 | tf_op jit(solution)/shard_map/ppermute | solution.py:606
  58.7 5.4 %owner_slope.3.slope1 = bf16[512,384]{1,0:T(8,128)(2,1)S(1)} custom-call(s32[4]{0:T(128)S(1)} %pad_add_fusion.place, s32[2,256]{1,0:T(2,128)S(1)} %get-tuple-element.106.refs_0_, s32[2,256]{1,0:T(2,128)S(1)} %get-tuple-element.105.refs_1_, s32[2,256]{1,0:T(2,128)S(1)} %collective-permute-done.6.refs_2_, s32[2,256]{1,0:T(2,128)S(1)} %get-tuple-element.104.refs_3_, ...), custom_call_target="tpu_custom_call" | custom-call | tf_op jit(solution)/shard_map/owner_slope/pallas_call | solution.py:379
  64.1 2.6 %stem_taps.1.taps = bf16[960,2048]{1,0:T(8,128)(2,1)S(1)} custom-call(s32[4]{0:T(128)S(1)} %pad_add_fusion.place, s32[2,256]{1,0:T(2,128)S(1)} %get-tuple-element.106.refs_0_, s32[2,256]{1,0:T(2,128)S(1)} %get-tuple-element.105.refs_1_, s32[2,256]{1,0:T(2,128)S(1)} %collective-permute-done.6.refs_2_, s32[2,256]{1,0:T(2,128)S(1)} %get-tuple-element.104.refs_3_, ...), custom_call_target="tpu_custom_call" | custom-call | tf_op jit(solution)/shard_map/stem_taps/pallas_call | solution.py:379
  66.6 3.0 %collective-permute-done.19 = bf16[2,272,192]{2,1,0:T(8,128)(2,1)S(1)} collective-permute-done((bf16[2,272,192]{2,1,0:T(8,128)(2,1)S(1)}, bf16[2,272,192]{2,1,0:T(8,128)(2,1)S(1)}, u32[]{:S(2)}, u32[]{:S(2)}) %collective-permute-start.19) | collective-permute-done | bytes 208928 | tf_op jit(solution)/shard_map/ppermute | solution.py:598
  69.9 0.4 collective-permute-start.23
  70.3 0.5 collective-permute-start.24
  70.8 1.0 %collective-permute-start.21 = (bf16[256,384]{1,0:T(8,128)(2,1)S(1)}, bf16[256,384]{1,0:T(8,128)(2,1)S(1)}, u32[]{:S(2)}, u32[]{:S(2)}) collective-permute-start(bf16[256,384]{1,0:T(8,128)(2,1)S(1)} %get-tuple-element.97), channel_id=1, source_target_pairs={{1,4},{3,6},{0,8},{2,10},{4,9},{6,11},{5,13},{7,15},{9,12},{11,14}... | collective-permute-start | bytes 589832 | tf_op jit(solution)/shard_map/ppermute | solution.py:598
  71.8 0.7 collective-permute-start.22
  72.5 4.0 %collective-permute-start.26 = (bf16[512,384]{1,0:T(8,128)(2,1)S(1)}, bf16[512,384]{1,0:T(8,128)(2,1)S(1)}, u32[]{:S(2)}, u32[]{:S(2)}) collective-permute-start(bf16[512,384]{1,0:T(8,128)(2,1)S(1)} %owner_slope.2.slope0), channel_id=1, source_target_pairs={{0,1},{1,0},{2,3},{3,2},{4,5},{5,4},{6,7},{7,6},{8,9},{9,8},{10,11... | collective-permute-start | bytes 1179656 | tf_op jit(solution)/shard_map/ppermute | solution.py:566
  76.5 0.8 pred_.1
  77.3 2.5 %collective-permute-done.24.pool3 = bf16[256,384]{1,0:T(8,128)(2,1)S(1)} collective-permute-done((bf16[256,384]{1,0:T(8,128)(2,1)S(1)}, bf16[256,384]{1,0:T(8,128)(2,1)S(1)}, u32[]{:S(2)}, u32[]{:S(2)}) %collective-permute-start.24) | collective-permute-done | bytes 196640 | tf_op jit(solution)/shard_map/ppermute | solution.py:412
  79.9 3.5 %dec_grad.1 = f32[5,192,384]{2,1,0:T(8,128)} custom-call(s32[4]{0:T(128)S(1)} %pad_add_fusion.place, bf16[2,2,272,192]{3,2,1,0:T(8,128)(2,1)S(1)} %pad_maximum_fusion.own, bf16[2,2,272,192]{3,2,1,0:T(8,128)(2,1)S(1)} %collective-permute-done.23.came, bf16[256,384]{1,0:T(8,128)(2,1)S(1)} %get-tuple-element.69.pool0, ...), custom_call_target="tpu_custom_call" | custom-call | tf_op jit(solution)/shard_map/dec_grad/pallas_call | solution.py:379
  83.5 0.6 collective-permute-start.25
  84.1 1.3 %collective-permute-done.25.came = bf16[2,256,384]{2,1,0:T(8,128)(2,1)S(1)} collective-permute-done((bf16[2,256,384]{2,1,0:T(8,128)(2,1)S(1)}, bf16[2,256,384]{2,1,0:T(8,128)(2,1)S(1)}, u32[]{:S(2)}, u32[]{:S(2)}) %collective-permute-start.25) | collective-permute-done | bytes 393248 | tf_op jit(solution)/shard_map/ppermute | solution.py:647
  85.4 4.2 %enc_grad.1 = f32[960,384]{1,0:T(8,128)} custom-call(s32[4]{0:T(128)S(1)} %pad_add_fusion.place, bf16[960,2048]{1,0:T(8,128)(2,1)S(1)} %stem_taps.1.taps, bf16[2,256,384]{2,1,0:T(8,128)(2,1)S(1)} %pad_maximum_fusion.1.own, bf16[2,256,384]{2,1,0:T(8,128)(2,1)S(1)} %collective-permute-done.25.came, bf16[512,384]{1,0:T(8,128)(2,1)S(1)} %owner_slope.2.slope0, ...), custom_call_target="tpu_custom_call" | custom-call | tf_op jit(solution)/shard_map/enc_grad/pallas_call | solution.py:648
  (45 shorter events, 1.3 us)
Async XLA Ops:
  0.6 4.6 %copy-start = (bf16[768,5,384]{2,0,1:T(8,128)(2,1)S(1)}, bf16[768,5,384]{2,0,1:T(8,128)(2,1)}, u32[]{:S(2)}) copy-start(bf16[768,5,384]{2,0,1:T(8,128)(2,1)} %param.8) | copy-start | bytes 8847364
  1.7 1.8 %copy-start.1 = (bf16[1536,5,192]{0,2,1:T(8,128)(2,1)S(1)}, bf16[1536,5,192]{0,2,1:T(8,128)(2,1)}, u32[]{:S(2)}) copy-start(bf16[1536,5,192]{0,2,1:T(8,128)(2,1)} %param.7) | copy-start | bytes 8847364
  4.7 11.6 %collective-permute-start.2 = (bf16[992,768]{1,0:T(8,128)(2,1)S(1)}, bf16[992,768]{1,0:T(8,128)(2,1)S(1)}, u32[]{:S(2)}, u32[]{:S(2)}) collective-permute-start(bf16[992,768]{1,0:T(8,128)(2,1)S(1)} %get-tuple-element.51), channel_id=1, source_target_pairs={{0,1},{1,0},{2,3},{3,2},{4,5},{5,4},{6,7},{7,6},{8,9},{9,8},{10,11... | collective-permute-start | bytes 4571144 | tf_op jit(solution)/shard_map/ppermute | solution.py:441
  5.2 4.1 %copy-start.4 = (s32[512]{0:T(512)S(1)}, s32[512]{0:T(512)}, u32[]{:S(2)}) copy-start(s32[512]{0:T(512)} %param.5) | copy-start | bytes 6148
  5.2 11.1 %copy-start.2 = (bf16[1536,5,192]{0,2,1:T(8,128)(2,1)S(1)}, bf16[1536,5,192]{0,2,1:T(8,128)(2,1)}, u32[]{:S(2)}) copy-start(bf16[1536,5,192]{0,2,1:T(8,128)(2,1)} %param.7) | copy-start | bytes 8847364
  6.3 22.0 %collective-permute-start.3 = (bf16[5,2,192,384]{3,2,1,0:T(8,128)(2,1)S(1)}, bf16[5,2,192,384]{3,2,1,0:T(8,128)(2,1)S(1)}, u32[]{:S(2)}, u32[]{:S(2)}) collective-permute-start(bf16[5,2,192,384]{3,2,1,0:T(8,128)(2,1)S(1)} %dec_pick.1), channel_id=1, source_target_pairs={{0,1},{1,0},{2,3},{3,2},{4,5},{5,4},{6,7},{7,6},{8,9},{9,8},{10,11... | collective-permute-start | bytes 4423688 | tf_op jit(solution)/shard_map/ppermute | solution.py:455
  6.4 15.3 %collective-permute-start.7 = (bf16[608,384]{1,0:T(8,128)(2,1)S(1)}, bf16[608,384]{1,0:T(8,128)(2,1)S(1)}, u32[]{:S(2)}, u32[]{:S(2)}) collective-permute-start(bf16[608,384]{1,0:T(8,128)(2,1)S(1)} %get-tuple-element.64), channel_id=1, source_target_pairs={{0,2},{1,3},{2,0},{3,1},{4,6},{5,7},{6,4},{7,5},{8,10},{9,11},{10,... | collective-permute-start | bytes 1400840 | tf_op jit(solution)/shard_map/ppermute | solution.py:442
  9.3 4.1 %collective-permute-start = (s32[1,512]{1,0:T(1,128)S(1)}, s32[1,512]{1,0:T(1,128)S(1)}, u32[]{:S(2)}, u32[]{:S(2)}) collective-permute-start(s32[1,512]{1,0:T(1,128)S(1)} %bitcast.41), channel_id=1, source_target_pairs={{0,4},{4,0},{8,12},{12,8},{1,5},{5,1},{9,13},{13,9},{2,6},{6,2},{1... | collective-permute-start | bytes 6152 | tf_op jit(solution)/shard_map/ppermute | solution.py:412
  10.9 5.4 %collective-permute-start.1 = (s32[1,512]{1,0:T(1,128)S(1)}, s32[1,512]{1,0:T(1,128)S(1)}, u32[]{:S(2)}, u32[]{:S(2)}) collective-permute-start(s32[1,512]{1,0:T(1,128)S(1)} %bitcast.42), channel_id=1, source_target_pairs={{0,12},{4,8},{8,4},{12,0},{1,13},{5,9},{9,5},{13,1},{2,14},{6,10},... | collective-permute-start | bytes 6152 | tf_op jit(solution)/shard_map/ppermute | solution.py:422
  19.5 2.8 %copy-start.3 = (bf16[512,192]{0,1:T(8,128)(2,1)S(1)}, bf16[512,192]{0,1:T(8,128)(2,1)}, u32[]{:S(2)}) copy-start(bf16[512,192]{0,1:T(8,128)(2,1)} %param.9) | copy-start | bytes 589828
  21.7 11.1 %collective-permute-start.8 = (bf16[544,384]{1,0:T(8,128)(2,1)S(1)}, bf16[544,384]{1,0:T(8,128)(2,1)S(1)}, u32[]{:S(2)}, u32[]{:S(2)}) collective-permute-start(bf16[544,384]{1,0:T(8,128)(2,1)S(1)} %get-tuple-element.65), channel_id=1, source_target_pairs={{0,2},{1,3},{2,0},{3,1},{4,6},{5,7},{6,4},{7,5},{8,10},{9,11},{10,... | collective-permute-start | bytes 1253384 | tf_op jit(solution)/shard_map/ppermute | solution.py:482
  22.3 6.0 %collective-permute-start.4 = (bf16[192,128]{1,0:T(8,128)(2,1)S(1)}, bf16[192,128]{1,0:T(8,128)(2,1)S(1)}, u32[]{:S(2)}, u32[]{:S(2)}) collective-permute-start(bf16[192,128]{1,0:T(8,128)(2,1)S(1)} %get-tuple-element.103), channel_id=1, source_target_pairs={{0,4},{4,8},{8,12},{12,0},{1,5},{5,9},{9,13},{13,1},{2,6},{6,10},{... | collective-permute-start | bytes 147464 | tf_op jit(solution)/shard_map/ppermute | solution.py:409
  23.6 5.6 %collective-permute-start.5 = (bf16[192,128]{1,0:T(8,128)(2,1)S(1)}, bf16[192,128]{1,0:T(8,128)(2,1)S(1)}, u32[]{:S(2)}, u32[]{:S(2)}) collective-permute-start(bf16[192,128]{1,0:T(8,128)(2,1)S(1)} %get-tuple-element.102), channel_id=1, source_target_pairs={{0,12},{4,0},{8,4},{12,8},{1,13},{5,1},{9,5},{13,9},{2,14},{6,2},{... | collective-permute-start | bytes 147464 | tf_op jit(solution)/shard_map/ppermute | solution.py:409
  26.2 17.1 %collective-permute-start.12 = (bf16[992,384]{1,0:T(8,128)(2,1)S(1)}, bf16[992,384]{1,0:T(8,128)(2,1)S(1)}, u32[]{:S(2)}, u32[]{:S(2)}) collective-permute-start(bf16[992,384]{1,0:T(8,128)(2,1)S(1)} %get-tuple-element.72.refs_4_), channel_id=1, source_target_pairs={{0,1},{1,0},{2,3},{3,2},{4,5},{5,4},{6,7},{7,6},{8,9},{9,8},{10,11... | collective-permute-start | bytes 2285576 | tf_op jit(solution)/shard_map/ppermute | solution.py:549
  28.3 13.6 %collective-permute-start.14 = (bf16[608,384]{1,0:T(8,128)(2,1)S(1)}, bf16[608,384]{1,0:T(8,128)(2,1)S(1)}, u32[]{:S(2)}, u32[]{:S(2)}) collective-permute-start(bf16[608,384]{1,0:T(8,128)(2,1)S(1)} %collective-permute-done.7.refs_6_), channel_id=1, source_target_pairs={{0,1},{1,0},{2,3},{3,2},{4,5},{5,4},{6,7},{7,6},{8,9},{9,8},{10,11... | collective-permute-start | bytes 1400840 | tf_op jit(solution)/shard_map/ppermute | solution.py:550
  28.3 4.5 %collective-permute-start.6 = (s32[2,256]{1,0:T(2,128)S(1)}, s32[2,256]{1,0:T(2,128)S(1)}, u32[]{:S(2)}, u32[]{:S(2)}) collective-permute-start(s32[2,256]{1,0:T(2,128)S(1)} %get-tuple-element.106.refs_0_), channel_id=1, source_target_pairs={{0,8},{4,12},{8,0},{12,4},{1,9},{5,13},{9,1},{13,5},{2,10},{6,14},... | collective-permute-start | bytes 6152 | tf_op jit(solution)/shard_map/ppermute | solution.py:409
  29.2 9.1 %collective-permute-start.13 = (bf16[384,384]{1,0:T(8,128)(2,1)S(1)}, bf16[384,384]{1,0:T(8,128)(2,1)S(1)}, u32[]{:S(2)}, u32[]{:S(2)}) collective-permute-start(bf16[384,384]{1,0:T(8,128)(2,1)S(1)} %get-tuple-element.74), channel_id=1, source_target_pairs={{0,2},{1,3},{2,0},{3,1},{4,6},{5,7},{6,4},{7,5},{8,10},{9,11},{10,... | collective-permute-start | bytes 884744 | tf_op jit(solution)/shard_map/ppermute | solution.py:506
  33.7 1.5 %collective-permute-start.9 = (bf16[272,384]{1,0:T(8,128)(2,1)S(1)}, bf16[272,384]{1,0:T(8,128)(2,1)S(1)}, u32[]{:S(2)}, u32[]{:S(2)}) collective-permute-start(bf16[272,384]{1,0:T(8,128)(2,1)S(1)} %get-tuple-element.67.own), channel_id=1, source_target_pairs={{0,1},{1,0},{2,3},{3,2},{4,5},{5,4},{6,7},{7,6},{8,9},{9,8},{10,11... | collective-permute-start | bytes 626696 | tf_op jit(solution)/shard_map/ppermute | solution.py:528
  38.3 13.9 %collective-permute-start.16 = (bf16[272,768]{1,0:T(8,128)(2,1)S(1)}, bf16[272,768]{1,0:T(8,128)(2,1)S(1)}, u32[]{:S(2)}, u32[]{:S(2)}) collective-permute-start(bf16[272,768]{1,0:T(8,128)(2,1)S(1)} %get-tuple-element.77), channel_id=1, source_target_pairs={{0,2},{1,3},{2,0},{3,1},{4,6},{5,7},{6,4},{7,5},{8,10},{9,11},{10,... | collective-permute-start | bytes 1253384 | tf_op jit(solution)/shard_map/ppermute | solution.py:544
  39.3 4.0 %collective-permute-start.15 = (bf16[384,384]{1,0:T(8,128)(2,1)S(1)}, bf16[384,384]{1,0:T(8,128)(2,1)S(1)}, u32[]{:S(2)}, u32[]{:S(2)}) collective-permute-start(bf16[384,384]{1,0:T(8,128)(2,1)S(1)} %collective-permute-done.13.refs_7_), channel_id=1, source_target_pairs={{0,1},{1,0},{2,3},{3,2},{4,5},{5,4},{6,7},{7,6},{8,9},{9,8},{10,11... | collective-permute-start | bytes 884744 | tf_op jit(solution)/shard_map/ppermute | solution.py:550
  39.3 12.5 %collective-permute-start.10 = (bf16[256,384]{1,0:T(8,128)(2,1)S(1)}, bf16[256,384]{1,0:T(8,128)(2,1)S(1)}, u32[]{:S(2)}, u32[]{:S(2)}) collective-permute-start(bf16[256,384]{1,0:T(8,128)(2,1)S(1)} %get-tuple-element.69.pool0), channel_id=1, source_target_pairs={{0,8},{4,12},{8,0},{12,4},{1,9},{5,13},{9,1},{13,5},{2,10},{6,14},... | collective-permute-start | bytes 589832 | tf_op jit(solution)/shard_map/ppermute | solution.py:412
  41.9 10.3 %collective-permute-start.11 = (bf16[256,384]{1,0:T(8,128)(2,1)S(1)}, bf16[256,384]{1,0:T(8,128)(2,1)S(1)}, u32[]{:S(2)}, u32[]{:S(2)}) collective-permute-start(bf16[256,384]{1,0:T(8,128)(2,1)S(1)} %get-tuple-element.69.pool0), channel_id=1, source_target_pairs={{0,4},{4,0},{8,12},{12,8},{1,5},{5,1},{9,13},{13,9},{2,6},{6,2},{1... | collective-permute-start | bytes 589832 | tf_op jit(solution)/shard_map/ppermute | solution.py:412
  53.3 2.0 %collective-permute-start.17 = (bf16[2,2,272,192]{3,2,1,0:T(8,128)(2,1)S(1)}, bf16[2,2,272,192]{3,2,1,0:T(8,128)(2,1)S(1)}, u32[]{:S(2)}, u32[]{:S(2)}) collective-permute-start(bf16[2,2,272,192]{3,2,1,0:T(8,128)(2,1)S(1)} %get-tuple-element.79.own), channel_id=1, source_target_pairs={{0,1},{1,0},{2,3},{3,2},{4,5},{5,4},{6,7},{7,6},{8,9},{9,8},{10,11... | collective-permute-start | bytes 1253384 | tf_op jit(solution)/shard_map/ppermute | solution.py:578
  53.4 16.2 %collective-permute-start.19 = (bf16[2,272,192]{2,1,0:T(8,128)(2,1)S(1)}, bf16[2,272,192]{2,1,0:T(8,128)(2,1)S(1)}, u32[]{:S(2)}, u32[]{:S(2)}) collective-permute-start(bf16[2,272,192]{2,1,0:T(8,128)(2,1)S(1)} %get-tuple-element.84), channel_id=1, source_target_pairs={{1,4},{3,6},{0,8},{2,10},{4,9},{6,11},{5,13},{7,15},{9,12},{11,14}... | collective-permute-start | bytes 626696 | tf_op jit(solution)/shard_map/ppermute | solution.py:598
  54.4 15.2 %collective-permute-start.20 = (bf16[2,272,192]{2,1,0:T(8,128)(2,1)S(1)}, bf16[2,272,192]{2,1,0:T(8,128)(2,1)S(1)}, u32[]{:S(2)}, u32[]{:S(2)}) collective-permute-start(bf16[2,272,192]{2,1,0:T(8,128)(2,1)S(1)} %get-tuple-element.85), channel_id=1, source_target_pairs={{1,12},{3,14},{4,1},{6,3},{9,4},{11,6},{12,9},{14,11},{17,28},{19,... | collective-permute-start | bytes 626696 | tf_op jit(solution)/shard_map/ppermute | solution.py:599
  57.4 12.4 %collective-permute-start.18 = (bf16[256,384]{1,0:T(8,128)(2,1)S(1)}, bf16[256,384]{1,0:T(8,128)(2,1)S(1)}, u32[]{:S(2)}, u32[]{:S(2)}) collective-permute-start(bf16[256,384]{1,0:T(8,128)(2,1)S(1)} %up_grad.1), channel_id=1, source_target_pairs={{0,2},{1,3},{2,0},{3,1},{4,6},{5,7},{6,4},{7,5},{8,10},{9,11},{10,... | collective-permute-start | bytes 589832 | tf_op jit(solution)/shard_map/ppermute | solution.py:606
  69.9 10.0 %collective-permute-start.23 = (bf16[2,2,272,192]{3,2,1,0:T(8,128)(2,1)S(1)}, bf16[2,2,272,192]{3,2,1,0:T(8,128)(2,1)S(1)}, u32[]{:S(2)}, u32[]{:S(2)}) collective-permute-start(bf16[2,2,272,192]{3,2,1,0:T(8,128)(2,1)S(1)} %pad_maximum_fusion.own), channel_id=1, source_target_pairs={{0,1},{1,0},{2,3},{3,2},{4,5},{5,4},{6,7},{7,6},{8,9},{9,8},{10,11... | collective-permute-start | bytes 1253384 | tf_op jit(solution)/shard_map/ppermute | solution.py:622
  70.3 9.6 %collective-permute-start.24 = (bf16[256,384]{1,0:T(8,128)(2,1)S(1)}, bf16[256,384]{1,0:T(8,128)(2,1)S(1)}, u32[]{:S(2)}, u32[]{:S(2)}) collective-permute-start(bf16[256,384]{1,0:T(8,128)(2,1)S(1)} %collective-permute-done.10.pool2), channel_id=1, source_target_pairs={{0,4},{4,0},{8,12},{12,8},{1,5},{5,1},{9,13},{13,9},{2,6},{6,2},{1... | collective-permute-start | bytes 589832 | tf_op jit(solution)/shard_map/ppermute | solution.py:412
  70.8 12.6 %collective-permute-start.21 = (bf16[256,384]{1,0:T(8,128)(2,1)S(1)}, bf16[256,384]{1,0:T(8,128)(2,1)S(1)}, u32[]{:S(2)}, u32[]{:S(2)}) collective-permute-start(bf16[256,384]{1,0:T(8,128)(2,1)S(1)} %get-tuple-element.97), channel_id=1, source_target_pairs={{1,4},{3,6},{0,8},{2,10},{4,9},{6,11},{5,13},{7,15},{9,12},{11,14}... | collective-permute-start | bytes 589832 | tf_op jit(solution)/shard_map/ppermute | solution.py:598
  71.8 11.6 %collective-permute-start.22 = (bf16[256,384]{1,0:T(8,128)(2,1)S(1)}, bf16[256,384]{1,0:T(8,128)(2,1)S(1)}, u32[]{:S(2)}, u32[]{:S(2)}) collective-permute-start(bf16[256,384]{1,0:T(8,128)(2,1)S(1)} %get-tuple-element.96), channel_id=1, source_target_pairs={{1,12},{3,14},{4,1},{6,3},{9,4},{11,6},{12,9},{14,11},{17,28},{19,... | collective-permute-start | bytes 589832 | tf_op jit(solution)/shard_map/ppermute | solution.py:599
  72.5 11.6 %collective-permute-start.26 = (bf16[512,384]{1,0:T(8,128)(2,1)S(1)}, bf16[512,384]{1,0:T(8,128)(2,1)S(1)}, u32[]{:S(2)}, u32[]{:S(2)}) collective-permute-start(bf16[512,384]{1,0:T(8,128)(2,1)S(1)} %owner_slope.2.slope0), channel_id=1, source_target_pairs={{0,1},{1,0},{2,3},{3,2},{4,5},{5,4},{6,7},{7,6},{8,9},{9,8},{10,11... | collective-permute-start | bytes 1179656 | tf_op jit(solution)/shard_map/ppermute | solution.py:566
  79.9 4.2 %collective-permute-start.27 = (bf16[512,384]{1,0:T(8,128)(2,1)S(1)}, bf16[512,384]{1,0:T(8,128)(2,1)S(1)}, u32[]{:S(2)}, u32[]{:S(2)}) collective-permute-start(bf16[512,384]{1,0:T(8,128)(2,1)S(1)} %owner_slope.3.slope1), channel_id=1, source_target_pairs={{0,1},{1,0},{2,3},{3,2},{4,5},{5,4},{6,7},{7,6},{8,9},{9,8},{10,11... | collective-permute-start | bytes 1179656 | tf_op jit(solution)/shard_map/ppermute | solution.py:566
  83.5 1.9 %collective-permute-start.25 = (bf16[2,256,384]{2,1,0:T(8,128)(2,1)S(1)}, bf16[2,256,384]{2,1,0:T(8,128)(2,1)S(1)}, u32[]{:S(2)}, u32[]{:S(2)}) collective-permute-start(bf16[2,256,384]{2,1,0:T(8,128)(2,1)S(1)} %pad_maximum_fusion.1.own), channel_id=1, source_target_pairs={{0,1},{1,0},{2,3},{3,2},{4,5},{5,4},{6,7},{7,6},{8,9},{9,8},{10,11... | collective-permute-start | bytes 1179656 | tf_op jit(solution)/shard_map/ppermute | solution.py:647

commit v5 on v4

--- a/solution.py
+++ b/solution.py
@@ -48,15 +48,21 @@
     return jnp.concatenate([own, jnp.where(column < SIDE, after, before)], axis=1)
 
 
-def split_parity(bases):
-    count = bases.shape[1]
+def split_parity(blocks):
+    count = blocks[0].shape[1]
     row = lax.broadcasted_iota(jnp.int32, (count, count), 0)
     column = lax.broadcasted_iota(jnp.int32, (count, count), 1)
     source = jnp.where(column < count // 2, 2 * column, 2 * column - count + 1)
     chosen = jnp.where(row == source, 1.0, 0.0).astype(BF16)
-    wide = jnp.broadcast_to(bases, (16, count)).astype(F32).astype(BF16)
-    value = dot(wide, chosen, ((1,), (0,))).astype(jnp.int32)
-    return jnp.concatenate([value[0:1, : count // 2], value[0:1, count // 2 :]], axis=0)
+    place = lax.broadcasted_iota(jnp.int32, (16, count), 0)
+    wide = jnp.broadcast_to(blocks[0], (16, count))
+    for i, block in enumerate(blocks[1:]):
+        wide = jnp.where(place == i + 1, jnp.broadcast_to(block, (16, count)), wide)
+    value = dot(wide.astype(F32).astype(BF16), chosen, ((1,), (0,))).astype(jnp.int32)
+    return [
+        jnp.concatenate([value[i : i + 1, : count // 2], value[i : i + 1, count // 2 :]], axis=0)
+        for i in range(len(blocks))
+    ]
 
 
 def tap_onehots(bases, start, width):
@@ -82,17 +88,17 @@
 
 
 def stem_kernel(
-    place, own, after, before, stem_own, w_oth, w_own, acc, stem_out, lhs_oth, split, even, odd, lhs, *, pairs, devices
+    place, own, after, before, stem_own, w_oth, w_own, acc, stem_out, lhs, lhs_oth, split, even, odd, *, pairs, devices
 ):
-    seq, hi, lo = place[0], place[1], place[2]
+    seq = place[0]
     rows = pairs + 2 * INNER
     wide = pairs + 2 * OUTER
-    block = acc.shape[1] // 2
     swapped = lax.rem(seq, 2) == 1
     first, second = after[...], before[...]
-    for i, raw in enumerate((own[...], jnp.where(swapped, second, first), jnp.where(swapped, first, second))):
-        split[i] = split_parity(raw)
-    hots = tap_onehots(assemble(split[0], split[1], split[2], seq, devices), -OUTER, wide)
+    parts = split_parity([own[...], jnp.where(swapped, second, first), jnp.where(swapped, first, second)])
+    for i, part in enumerate(parts):
+        split[i] = part
+    hots = tap_onehots(assemble(*parts, seq, devices), -OUTER, wide)
     gap = OUTER - INNER
     stem_oth = w_oth[: stem_own.shape[0], : stem_own.shape[1]]
     for weight, held_lhs in ((stem_own[...], lhs), (stem_oth, lhs_oth)):
@@ -105,26 +111,34 @@
             held_lhs[k] = source[gap + k // 2 - 1 : gap + k // 2 - 1 + rows, :].astype(BF16)
     stem_out[0] = lhs[2]
     stem_out[1] = lhs[3]
-    for part in range(2):
-        at = pl.multiple_of((2 * (hi if part == 0 else 1 - hi) + lo) * block, 128)
-        total = jnp.zeros((2 * rows, block), F32)
-        for k in range(KW):
-            total = total + dot(lhs[k : k + 2].reshape(2 * rows, -1), w_own[k, :, pl.ds(at, block)], ((1,), (0,)))
-        acc[:, part * block : (part + 1) * block] = total
-
-
-def enc_kernel(place, acc, lhs, w_oth, keep, send):
-    hi = place[1]
-    rows, block = keep.shape
-    for part in range(2):
-        at = pl.multiple_of((hi if part == 0 else 1 - hi) * block, 128)
-        total = acc[:, part * block : (part + 1) * block]
-        for k in range(KW):
-            total = total + dot(lhs[k : k + 2].reshape(rows, -1), w_oth[k * lhs.shape[2] : (k + 1) * lhs.shape[2], pl.ds(at, block)], ((1,), (0,)))
-        if part == 0:
-            keep[...] = total
-        else:
-            send[...] = total.astype(BF16)
+    acc[...] = own_sums(lhs, w_own, 2 * (1 - place[1]) + place[2], acc.shape)
+
+
+def own_sums(lhs, weight, index, shape):
+    at = pl.ds(pl.multiple_of(index * shape[1], 128), shape[1])
+    total = jnp.zeros(shape, F32)
+    for k in range(KW):
+        total = total + dot(lhs[k : k + 2].reshape(shape[0], -1), weight[k, :, at], ((1,), (0,)))
+    return total
+
+
+def other_sums(lhs, weight, index, total):
+    rows, block = total.shape
+    channels = lhs.shape[2]
+    at = pl.ds(pl.multiple_of(index * block, 128), block)
+    for k in range(KW):
+        tap = weight[k * channels : (k + 1) * channels, at]
+        total = total + dot(lhs[k : k + 2].reshape(rows, -1), tap, ((1,), (0,)))
+    return total
+
+
+def send_kernel(place, acc, lhs, w_oth, send):
+    send[...] = other_sums(lhs, w_oth, 1 - place[1], acc[...]).astype(BF16)
+
+
+def keep_kernel(place, lhs, lhs_oth, w_own, w_oth, keep):
+    total = own_sums(lhs, w_own, 2 * place[1] + place[2], keep.shape)
+    keep[...] = other_sums(lhs_oth, w_oth, place[1], total)
 
 
 def pool_kernel(place, keep, came, pooled, centre, *, pairs, total):
@@ -349,19 +363,24 @@
         out[k] = dot(taps[k], pooled[...], ((0,), (0,)))
 
 
-def enc_grad_kernel(place, taps, own, came, slope0, slope1, slope2, slope3, out, joined):
+def enc_grad_kernel(place, taps, slots, slope0, slope1, *refs, first):
+    prior, (out, joined) = refs[:-2], refs[-2:]
+    pairs = slots.shape[1]
+    size = 2 * pairs
+    offset = place[3] if first else 1 - place[3]
+
     @pl.when(pl.program_id(0) == 0)
     def _():
-        pairs = own.shape[1]
-        for i, slope in enumerate((slope0, slope1, slope2, slope3)):
-            step = 2 * (i % 2) + (place[3] if i < 2 else 1 - place[3])
-            grad = (own if i < 2 else came)[i % 2].astype(F32)
+        for i, slope in enumerate((slope0, slope1)):
+            grad = slots[i].astype(F32)
             for parity in range(2):
+                at = i * size + parity * pairs
                 value = grad * slope[parity * pairs : (parity + 1) * pairs].astype(F32)
-                at = pl.multiple_of((2 * step + parity) * pairs, pairs)
-                joined[pl.ds(at, pairs), :] = value.astype(BF16)
-
-    out[...] = dot(taps[...], joined[...], ((1,), (0,)))
+                joined[at : at + pairs] = value.astype(BF16)
+
+    used = [taps[:, pl.ds(pl.multiple_of((2 * i + offset) * size, 128), size)] for i in range(2)]
+    value = dot(jnp.concatenate(used, axis=1), joined[...], ((1,), (0,)))
+    out[...] = value if first else value + prior[0][...]
 
 
 def whole(shape):
@@ -454,33 +473,38 @@
     )(place, dec_w)
     dec_came = lax.ppermute(dec_send, "chan", cores)
 
-    acc, stem, lhs, split = call(
+    held = (6, rows, stem_c)
+    acc, stem, lhs, lhs_oth, split = call(
         functools.partial(stem_kernel, pairs=pairs, devices=devices),
         [place, own, first, second, stem_w, enc_oth, enc_w],
         [
-            ((2 * rows, 2 * enc_c), F32),
+            ((2 * rows, enc_c), F32),
             ((2, rows, stem_c), BF16),
-            ((6, rows, stem_c), BF16),
+            (held, BF16),
+            (held, BF16),
             ((3, 2, pairs), jnp.int32),
         ],
-        [
-            ((pairs + 2 * OUTER, stem_c), F32),
-            ((pairs + 2 * OUTER, stem_c), F32),
-            ((6, rows, stem_c), BF16),
-        ],
+        [((pairs + 2 * OUTER, stem_c), F32), ((pairs + 2 * OUTER, stem_c), F32)],
         limit=14,
         name="stem_conv",
         last=(5,),
     )
-    keep, send = call(
-        enc_kernel,
-        [place, acc, lhs, enc_oth],
-        [((2 * rows, enc_c), F32), ((2 * rows, enc_c), BF16)],
+    (send,) = call(
+        send_kernel,
+        [place, acc, lhs_oth, enc_oth],
+        [((2 * rows, enc_c), BF16)],
         limit=12,
         name="enc_conv",
     )
-    came = lax.ppermute(gated(send, mine0_far), "chan", across)
-
+    came = lax.ppermute(send, "chan", across)
+
+    (keep,) = call(
+        keep_kernel,
+        [gated(place, send), lhs, lhs_oth, enc_w, enc_oth],
+        [((2 * rows, enc_c), F32)],
+        limit=14,
+        name="enc_keep",
+    )
     targets_in, place_in = gated((targets, place), send)
     blocks = {0: split[0], 1: split[2], devices - 1: split[1]}
     for r in range(2, devices - 1):
@@ -503,7 +527,7 @@
     targets_in = targets_in.T
     count, edge = 2 * pairs, 2 * SIDE
     below, above = ring(targets_in[:, count - edge :], 1), ring(targets_in[:, :edge], devices - 1)
-    mine1_far = lax.ppermute(gated(mine1, below), "chan", across)
+    mine1_far = lax.ppermute(gated(mine1, (below, mine0_far)), "chan", across)
     (targets_at,) = call(
         targets_kernel,
         [place, targets_in, below, above],
@@ -613,7 +637,7 @@
         name="stem_taps",
     )
     near, far = gated((near, far), taps)
-    far_pooled = swap(beyond, 1)
+    far_pooled = swap(gated(beyond, taps), 1)
     sums_pieces = local, near, far
     pre_oth = gated(pre_oth, (near, far, slope1, taps))
     pieces = [jnp.where(own_block, pre, pre_oth) for own_block in target]
@@ -645,18 +669,24 @@
     near, far = gated((near, far), (g_dec, pred))
     pre_mine = slots(local, near, far)
     pre_came = lax.ppermute(pre_mine, "chan", cores)
-    g_enc = pl.pallas_call(
-        enc_grad_kernel,
-        grid=(2,),
-        in_specs=[SCALARS, pl.BlockSpec((KW * stem_c // 2, 2 * pairs * devices), lambda k: (k, 0))]
-        + [whole(pre_mine.shape)] * 2
-        + [whole(slope0.shape)] * 4,
-        out_specs=pl.BlockSpec((KW * stem_c // 2, enc_c), lambda k: (k, 0)),
-        out_shape=jax.ShapeDtypeStruct((KW * stem_c, enc_c), F32),
-        scratch_shapes=[pltpu.VMEM((2 * pairs * devices, enc_c), BF16)],
-        compiler_params=pltpu.CompilerParams(vmem_limit_bytes=13 * MIB),
-        name="enc_grad",
-    )(place, taps, pre_mine, pre_came, slope0, slope1, slope0_came, slope1_came)
+
+    def enc_grad(first, *arrays):
+        half = (KW * stem_c // 2, enc_c)
+        return pl.pallas_call(
+            functools.partial(enc_grad_kernel, first=first),
+            grid=(2,),
+            in_specs=[SCALARS, pl.BlockSpec((half[0], 2 * pairs * devices), lambda k: (k, 0))]
+            + [whole(p.shape) for p in arrays[:3]]
+            + [pl.BlockSpec(half, lambda k: (k, 0))] * len(arrays[3:]),
+            out_specs=pl.BlockSpec(half, lambda k: (k, 0)),
+            out_shape=jax.ShapeDtypeStruct((KW * stem_c, enc_c), F32),
+            scratch_shapes=[pltpu.VMEM((4 * pairs, enc_c), BF16)],
+            compiler_params=pltpu.CompilerParams(vmem_limit_bytes=13 * MIB),
+            name="enc_grad",
+        )(place, taps, *arrays)
+
+    g_enc = enc_grad(True, pre_mine, slope0, slope1)
+    g_enc = enc_grad(False, pre_came, slope0_came, slope1_came, g_enc)
     g_enc = g_enc.reshape(KW, stem_c, enc_c).transpose(2, 0, 1)
     return (pred, g_enc, g_dec.transpose(1, 0, 2))
 

time: 90.4 us -> 88.3 us (0.977)
  waiting for transfers between devices: 18.4 us -> 12.6 us
  starting transfers between devices: 29.2 us -> 31.7 us
  Pallas kernels: 37.6 us -> 39.4 us
    ppermute x2, starting transfers between devices: 1.98 us -> 4.72 us  [to_owner(): near = lax.ppermute(near, ('seq', 'chan'), link((1, 2)))]
    ppermute x1, starting transfers between devices: 0.41 us -> 2.69 us  [shards(): sums_came = lax.ppermute(sums_mine, 'chan', cores)]
    ppermute x3, waiting for transfers between devices: 2.12 us -> 0.1 us  [ring(): lax.ppermute(array, 'seq', [(i, (i + step) % devices) for i in range(devi...]
    ppermute x2, waiting for transfers between devices: 2.98 us -> 1.05 us  [to_owner(): near = lax.ppermute(near, ('seq', 'chan'), link((1, 2)))]
    ppermute x2, starting transfers between devices: 4 us -> 2.47 us  [owner_slope(): return (out, lax.ppermute(out, 'chan', cores))]
    ppermute x1, waiting for transfers between devices: 1.34 us -> 0.01 us  [shards(): pre_came = lax.ppermute(pre_mine, 'chan', cores)]
    ppermute x4, starting transfers between devices: 6.07 us -> 4.88 us  [swap(): lax.ppermute(array, 'seq', [(i, i ^ distance) for i in range(devices)])]
    ppermute x2, waiting for transfers between devices: 1.54 us -> 0.57 us  [the longest x1 0.57 us: shards(): mine1_far = lax.ppermute(gated(mine1, (below, mine0_far)), 'chan', across)]
  transfers between devices with their start and end apart: 28 -> 28, of which waited for: 10 -> 7; matrix products, arithmetic and copies ran while one was open for 0% -> 0% of each run, Pallas kernels for 35% -> 39%
where the time goes in v5:
time: 88.3 us; the launch traced here: 88 us
  Pallas kernels  39.4 us (45%)
  starting transfers between devices  31.7 us (36%)
  waiting for transfers between devices  12.6 us (14%)
  local copies, waits for them, and re-layouts  2.74 us (3%)
  between operations  1.06 us (1%)
    pallas_call x13, Pallas kernels, call(): pl.pallas_call(kernel, grid=(1,) if last else (), in_specs=specs, out_spe...  30.4 us
    ppermute x4, waiting for transfers between devices, swap(): lax.ppermute(array, 'seq', [(i, i ^ distance) for i in range(devices)])  6.46 us
    pallas_call x2, Pallas kernels, enc_grad(): pl.pallas_call(functools.partial(enc_grad_kernel, first=first), grid=(2,)...  5.12 us
    ppermute x4, starting transfers between devices, swap(): lax.ppermute(array, 'seq', [(i, i ^ distance) for i in range(devices)])  4.88 us
    ppermute x2, starting transfers between devices, to_owner(): near = lax.ppermute(near, ('seq', 'chan'), link((1, 2)))  4.72 us
    ppermute x3, starting transfers between devices, ring(): lax.ppermute(array, 'seq', [(i, (i + step) % devices) for i in range(devi...  3.87 us
    ppermute x1, starting transfers between devices, shards(): mine0_far = lax.ppermute(mine0, 'chan', across)  2.94 us
    ppermute x1, waiting for transfers between devices, shards(): lax.ppermute(own, 'seq', [(i, (i + 1 - 2 * (1 - i % 2)) % devices) for i...  2.9 us
  transfers between devices with their start and end apart: 28, of which 7 were waited for; matrix products, arithmetic and copies ran while one was open for 0% of the time, Pallas kernels for 39%

profile of v5, /device:TPU:0, one launch (start us, length us, event | category | flops | bytes accessed | tf_op | source)
XLA Modules:
  0.0 88.0 jit_solution(8557276712459891929)
XLA Ops:
  0.9 0.9 reshape.25.stem_own.refs_4_
  1.8 1.8 %copy-done.1 = bf16[1536,5,192]{0,2,1:T(8,128)(2,1)S(1)} copy-done((bf16[1536,5,192]{0,2,1:T(8,128)(2,1)S(1)}, bf16[1536,5,192]{0,2,1:T(8,128)(2,1)}, u32[]{:S(2)}) %copy-start.1) | copy-done | bytes 2949144
  3.6 1.1 %picks.1 = (bf16[992,384]{1,0:T(8,128)(2,1)S(1)}, bf16[608,384]{1,0:T(8,128)(2,1)S(1)}, bf16[384,384]{1,0:T(8,128)(2,1)S(1)}, bf16[992,768]{1,0:T(8,128)(2,1)S(1)}) custom-call(s32[4]{0:T(128)S(1)} %pad_add_fusion.place, bf16[32,192]{1,0:T(8,128)(2,1)S(1)} %concatenate.9.stem, bf16[5,192,1536]{2,1,0:T(8,128)(2,1)S(1)} %bitcast.35), custom_call_target="tpu_custom_call" | custom-call | tf_op jit(solution)/shard_map/picks/pallas_call | solution.py:446
  4.7 0.5 collective-permute-start.2
  5.2 1.1 %dec_pick.1 = bf16[5,2,192,384]{3,2,1,0:T(8,128)(2,1)S(1)} custom-call(s32[4]{0:T(128)S(1)} %pad_add_fusion.place, bf16[5,4,192,384]{3,2,1,0:T(8,128)(2,1)S(1)} %bitcast.32), custom_call_target="tpu_custom_call" | custom-call | tf_op jit(solution)/shard_map/dec_pick/pallas_call | solution.py:462
  6.3 0.1 collective-permute-start.3
  6.4 2.9 %collective-permute-start.12 = (bf16[608,384]{1,0:T(8,128)(2,1)S(1)}, bf16[608,384]{1,0:T(8,128)(2,1)S(1)}, u32[]{:S(2)}, u32[]{:S(2)}) collective-permute-start(bf16[608,384]{1,0:T(8,128)(2,1)S(1)} %get-tuple-element.71), channel_id=1, source_target_pairs={{0,2},{1,3},{2,0},{3,1},{4,6},{5,7},{6,4},{7,5},{8,10},{9,11},{10,... | collective-permute-start | bytes 1400840 | tf_op jit(solution)/shard_map/ppermute | solution.py:461
  9.3 1.6 %collective-permute-start = (s32[1,512]{1,0:T(1,128)S(1)}, s32[1,512]{1,0:T(1,128)S(1)}, u32[]{:S(2)}, u32[]{:S(2)}) collective-permute-start(s32[1,512]{1,0:T(1,128)S(1)} %bitcast.42), channel_id=1, source_target_pairs={{0,4},{4,0},{8,12},{12,8},{1,5},{5,1},{9,13},{13,9},{2,6},{6,2},{1... | collective-permute-start | bytes 6152 | tf_op jit(solution)/shard_map/ppermute | solution.py:431
  10.9 2.5 %collective-permute-start.1 = (s32[1,512]{1,0:T(1,128)S(1)}, s32[1,512]{1,0:T(1,128)S(1)}, u32[]{:S(2)}, u32[]{:S(2)}) collective-permute-start(s32[1,512]{1,0:T(1,128)S(1)} %bitcast.43), channel_id=1, source_target_pairs={{0,12},{4,8},{8,4},{12,0},{1,13},{5,9},{9,5},{13,1},{2,14},{6,10},... | collective-permute-start | bytes 6152 | tf_op jit(solution)/shard_map/ppermute | solution.py:441
  13.4 2.9 %collective-permute-done.1.before = s32[1,512]{1,0:T(1,128)S(1)} collective-permute-done((s32[1,512]{1,0:T(1,128)S(1)}, s32[1,512]{1,0:T(1,128)S(1)}, u32[]{:S(2)}, u32[]{:S(2)}) %collective-permute-start.1) | collective-permute-done | bytes 2080 | tf_op jit(solution)/shard_map/ppermute | solution.py:441
  16.3 2.6 %stem_conv.1 = (f32[544,384]{1,0:T(8,128)S(1)}, bf16[2,272,192]{2,1,0:T(8,128)(2,1)S(1)}, bf16[6,272,192]{2,1,0:T(8,128)(2,1)S(1)}, bf16[6,272,192]{2,1,0:T(8,128)(2,1)S(1)}, s32[3,2,256]{2,1,0:T(2,128)S(1)}) custom-call(s32[4]{0:T(128)S(1)} %pad_add_fusion.place, s32[1,512]{1,0:T(1,128)S(1)} %bitcast.44, s32[1,512]{1,0:T(1,128)S(1)} %collective-permute-done.after, ...), custom_call_target="tpu_custom_call" | custom-call | tf_op jit(solution)/shard_map/stem_conv/pallas_call | solution.py:398
  18.9 1.4 %enc_conv.1 = bf16[544,384]{1,0:T(8,128)(2,1)S(1)} custom-call(s32[4]{0:T(128)S(1)} %pad_add_fusion.place, f32[544,384]{1,0:T(8,128)S(1)} %get-tuple-element.52.acc, bf16[6,272,192]{2,1,0:T(8,128)(2,1)S(1)} %get-tuple-element.53.lhs.lhs_oth, bf16[992,768]{1,0:T(8,128)(2,1)S(1)} %collective-permute-done.2.w_oth), custom_call_target="tpu_custom_call" | custom-call | tf_op jit(solution)/shard_map/enc_conv/pallas_call | solution.py:398
  20.3 0.6 collective-permute-start.7
  21.0 3.8 %collective-permute-start.5 = (bf16[192,128]{1,0:T(8,128)(2,1)S(1)}, bf16[192,128]{1,0:T(8,128)(2,1)S(1)}, u32[]{:S(2)}, u32[]{:S(2)}) collective-permute-start(bf16[192,128]{1,0:T(8,128)(2,1)S(1)} %get-tuple-element.102), channel_id=1, source_target_pairs={{0,12},{4,0},{8,4},{12,8},{1,13},{5,1},{9,5},{13,9},{2,14},{6,2},{... | collective-permute-start | bytes 147464 | tf_op jit(solution)/shard_map/ppermute | solution.py:428
  24.8 2.1 %enc_keep.1.keep = f32[544,384]{1,0:T(8,128)S(1)} custom-call(s32[4]{0:T(128)S(1)} %pad_add_fusion.place, bf16[6,272,192]{2,1,0:T(8,128)(2,1)S(1)} %get-tuple-element.63.lhs, bf16[6,272,192]{2,1,0:T(8,128)(2,1)S(1)} %get-tuple-element.53.lhs.lhs_oth, bf16[5,192,1536]{2,1,0:T(8,128)(2,1)S(1)} %bitcast.37, bf16[992,768]{1,0:T(8,128)(2,1)S(1)} %collective-permute-done.2.w_oth), custom_call_target="tpu_custom_call" | custom-call | tf_op jit(solution)/shard_map/enc_keep/pallas_call | solution.py:398
  27.1 0.5 collective-permute-start.14
  27.6 1.6 %collective-permute-start.13 = (bf16[384,384]{1,0:T(8,128)(2,1)S(1)}, bf16[384,384]{1,0:T(8,128)(2,1)S(1)}, u32[]{:S(2)}, u32[]{:S(2)}) collective-permute-start(bf16[384,384]{1,0:T(8,128)(2,1)S(1)} %get-tuple-element.73), channel_id=1, source_target_pairs={{0,2},{1,3},{2,0},{3,1},{4,6},{5,7},{6,4},{7,5},{8,10},{9,11},{10,... | collective-permute-start | bytes 884744 | tf_op jit(solution)/shard_map/ppermute | solution.py:530
  29.1 0.2 pad_select_fusion.stem
  29.3 1.7 %dec_taps.1 = (bf16[3,2,2,192,384]{4,3,2,1,0:T(8,128)(2,1)S(1)}, bf16[3,2,2,192,384]{4,3,2,1,0:T(8,128)(2,1)S(1)}) custom-call(s32[4]{0:T(128)S(1)} %pad_add_fusion.place, bf16[5,4,192,384]{3,2,1,0:T(8,128)(2,1)S(1)} %bitcast.33, bf16[5,2,192,384]{3,2,1,0:T(8,128)(2,1)S(1)} %collective-permute-done.3.came), custom_call_target="tpu_custom_call" | custom-call | tf_op jit(solution)/shard_map/dec_taps/pallas_call | solution.py:512
  31.0 0.9 %targets.1 = bf16[2,272,384]{2,1,0:T(8,128)(2,1)S(1)} custom-call(s32[4]{0:T(128)S(1)} %pad_add_fusion.place, bf16[192,512]{1,0:T(8,128)(2,1)S(1)} %bitcast.41, bf16[192,128]{1,0:T(8,128)(2,1)S(1)} %collective-permute-done.4.before, bf16[192,128]{1,0:T(8,128)(2,1)S(1)} %collective-permute-done.5.after), custom_call_target="tpu_custom_call" | custom-call | tf_op jit(solution)/shard_map/targets/pallas_call | solution.py:398
  32.0 1.0 %gelu_pool.1 = (bf16[272,384]{1,0:T(8,128)(2,1)S(1)}, bf16[256,384]{1,0:T(8,128)(2,1)S(1)}) custom-call(s32[4]{0:T(128)S(1)} %pad_add_fusion.place, f32[544,384]{1,0:T(8,128)S(1)} %enc_keep.1.keep, bf16[544,384]{1,0:T(8,128)(2,1)S(1)} %collective-permute-done.7.came), custom_call_target="tpu_custom_call" | custom-call | tf_op jit(solution)/shard_map/gelu_pool/pallas_call | solution.py:398
  33.1 1.4 %collective-permute-done.8.oth = bf16[272,384]{1,0:T(8,128)(2,1)S(1)} collective-permute-done((bf16[272,384]{1,0:T(8,128)(2,1)S(1)}, bf16[272,384]{1,0:T(8,128)(2,1)S(1)}, u32[]{:S(2)}, u32[]{:S(2)}) %collective-permute-start.8) | collective-permute-done | bytes 208928 | tf_op jit(solution)/shard_map/ppermute | solution.py:552
  34.5 1.5 %dec_conv.1 = (f32[272,768]{1,0:T(8,128)S(1)}, bf16[272,768]{1,0:T(8,128)(2,1)S(1)}) custom-call(bf16[272,384]{1,0:T(8,128)(2,1)S(1)} %get-tuple-element.65.own, bf16[272,384]{1,0:T(8,128)(2,1)S(1)} %collective-permute-done.8.oth, bf16[3,768,384]{2,1,0:T(8,128)(2,1)S(1)} %bitcast.38, bf16[3,768,384]{2,1,0:T(8,128)(2,1)S(1)} %bitcast.39, ...), custom_call_target="tpu_custom_call" | custom-call | tf_op jit(solution)/shard_map/dec_conv/pallas_call | solution.py:398
  36.1 0.6 collective-permute-done.13.refs_7_
  36.6 1.5 %collective-permute-start.16 = (bf16[272,768]{1,0:T(8,128)(2,1)S(1)}, bf16[272,768]{1,0:T(8,128)(2,1)S(1)}, u32[]{:S(2)}, u32[]{:S(2)}) collective-permute-start(bf16[272,768]{1,0:T(8,128)(2,1)S(1)} %get-tuple-element.76), channel_id=1, source_target_pairs={{0,2},{1,3},{2,0},{3,1},{4,6},{5,7},{6,4},{7,5},{8,10},{9,11},{10,... | collective-permute-start | bytes 1253384 | tf_op jit(solution)/shard_map/ppermute | solution.py:568
  38.1 1.2 %collective-permute-start.10 = (bf16[256,384]{1,0:T(8,128)(2,1)S(1)}, bf16[256,384]{1,0:T(8,128)(2,1)S(1)}, u32[]{:S(2)}, u32[]{:S(2)}) collective-permute-start(bf16[256,384]{1,0:T(8,128)(2,1)S(1)} %get-tuple-element.67.pool0), channel_id=1, source_target_pairs={{0,4},{4,0},{8,12},{12,8},{1,5},{5,1},{9,13},{13,9},{2,6},{6,2},{1... | collective-permute-start | bytes 589832 | tf_op jit(solution)/shard_map/ppermute | solution.py:431
  39.3 2.1 %collective-permute-start.9 = (bf16[256,384]{1,0:T(8,128)(2,1)S(1)}, bf16[256,384]{1,0:T(8,128)(2,1)S(1)}, u32[]{:S(2)}, u32[]{:S(2)}) collective-permute-start(bf16[256,384]{1,0:T(8,128)(2,1)S(1)} %get-tuple-element.67.pool0), channel_id=1, source_target_pairs={{0,8},{4,12},{8,0},{12,4},{1,9},{5,13},{9,1},{13,5},{2,10},{6,14},... | collective-permute-start | bytes 589832 | tf_op jit(solution)/shard_map/ppermute | solution.py:431
  41.5 5.4 %owner_slope.2.slope0 = bf16[512,384]{1,0:T(8,128)(2,1)S(1)} custom-call(s32[4]{0:T(128)S(1)} %pad_add_fusion.place, s32[2,256]{1,0:T(2,128)S(1)} %get-tuple-element.106.refs_0_, s32[2,256]{1,0:T(2,128)S(1)} %get-tuple-element.105.refs_1_, s32[2,256]{1,0:T(2,128)S(1)} %collective-permute-done.6.refs_2_, s32[2,256]{1,0:T(2,128)S(1)} %get-tuple-element.104.refs_3_, ...), custom_call_target="tpu_custom_call" | custom-call | tf_op jit(solution)/shard_map/owner_slope/pallas_call | solution.py:398
  46.8 2.8 %collective-permute-done.10.pool1 = bf16[256,384]{1,0:T(8,128)(2,1)S(1)} collective-permute-done((bf16[256,384]{1,0:T(8,128)(2,1)S(1)}, bf16[256,384]{1,0:T(8,128)(2,1)S(1)}, u32[]{:S(2)}, u32[]{:S(2)}) %collective-permute-start.10) | collective-permute-done | bytes 196640 | tf_op jit(solution)/shard_map/ppermute | solution.py:431
  49.7 1.1 %out_slope.1 = (bf16[2,256,192]{2,1,0:T(8,128)(2,1)S(1)}, bf16[2,2,272,192]{3,2,1,0:T(8,128)(2,1)S(1)}, bf16[2,272,192]{2,1,0:T(8,128)(2,1)S(1)}, bf16[2,272,192...) custom-call(s32[4]{0:T(128)S(1)} %pad_add_fusion.place, f32[272,768]{1,0:T(8,128)S(1)} %get-tuple-element.75.part, ...), custom_call_target="tpu_custom_call" | custom-call | tf_op jit(solution)/shard_map/out_slope/pallas_call | solution.py:398
  50.9 2.2 %collective-permute-start.19 = (bf16[2,272,192]{2,1,0:T(8,128)(2,1)S(1)}, bf16[2,272,192]{2,1,0:T(8,128)(2,1)S(1)}, u32[]{:S(2)}, u32[]{:S(2)}) collective-permute-start(bf16[2,272,192]{2,1,0:T(8,128)(2,1)S(1)} %get-tuple-element.83), channel_id=1, source_target_pairs={{1,4},{3,6},{0,8},{2,10},{4,9},{6,11},{5,13},{7,15},{9,12},{11,14}... | collective-permute-start | bytes 626696 | tf_op jit(solution)/shard_map/ppermute | solution.py:622
  53.1 0.8 collective-permute-start.20
  53.9 2.1 %up_grad.1 = bf16[256,384]{1,0:T(8,128)(2,1)S(1)} custom-call(s32[4]{0:T(128)S(1)} %pad_add_fusion.place, bf16[2,2,272,192]{3,2,1,0:T(8,128)(2,1)S(1)} %get-tuple-element.78.own, bf16[2,2,272,192]{3,2,1,0:T(8,128)(2,1)S(1)} %collective-permute-done.17.oth, bf16[5,4,192,384]{3,2,1,0:T(8,128)(2,1)S(1)} %bitcast.34), custom_call_target="tpu_custom_call" | custom-call | tf_op jit(solution)/shard_map/up_grad/pallas_call | solution.py:398
  56.0 0.6 collective-permute-start.18
  56.6 5.4 %owner_slope.3.slope1 = bf16[512,384]{1,0:T(8,128)(2,1)S(1)} custom-call(s32[4]{0:T(128)S(1)} %pad_add_fusion.place, s32[2,256]{1,0:T(2,128)S(1)} %get-tuple-element.106.refs_0_, s32[2,256]{1,0:T(2,128)S(1)} %get-tuple-element.105.refs_1_, s32[2,256]{1,0:T(2,128)S(1)} %collective-permute-done.6.refs_2_, s32[2,256]{1,0:T(2,128)S(1)} %get-tuple-element.104.refs_3_, ...), custom_call_target="tpu_custom_call" | custom-call | tf_op jit(solution)/shard_map/owner_slope/pallas_call | solution.py:398
  62.0 2.6 %stem_taps.1.taps = bf16[960,2048]{1,0:T(8,128)(2,1)S(1)} custom-call(s32[4]{0:T(128)S(1)} %pad_add_fusion.place, s32[2,256]{1,0:T(2,128)S(1)} %get-tuple-element.106.refs_0_, s32[2,256]{1,0:T(2,128)S(1)} %get-tuple-element.105.refs_1_, s32[2,256]{1,0:T(2,128)S(1)} %collective-permute-done.6.refs_2_, s32[2,256]{1,0:T(2,128)S(1)} %get-tuple-element.104.refs_3_, ...), custom_call_target="tpu_custom_call" | custom-call | tf_op jit(solution)/shard_map/stem_taps/pallas_call | solution.py:398
  64.6 1.0 %collective-permute-done.19 = bf16[2,272,192]{2,1,0:T(8,128)(2,1)S(1)} collective-permute-done((bf16[2,272,192]{2,1,0:T(8,128)(2,1)S(1)}, bf16[2,272,192]{2,1,0:T(8,128)(2,1)S(1)}, u32[]{:S(2)}, u32[]{:S(2)}) %collective-permute-start.19) | collective-permute-done | bytes 208928 | tf_op jit(solution)/shard_map/ppermute | solution.py:622
  65.7 0.1 pad_maximum_fusion.own
  65.9 2.7 %collective-permute-start.23 = (bf16[2,2,272,192]{3,2,1,0:T(8,128)(2,1)S(1)}, bf16[2,2,272,192]{3,2,1,0:T(8,128)(2,1)S(1)}, u32[]{:S(2)}, u32[]{:S(2)}) collective-permute-start(bf16[2,2,272,192]{3,2,1,0:T(8,128)(2,1)S(1)} %pad_maximum_fusion.own), channel_id=1, source_target_pairs={{0,1},{1,0},{2,3},{3,2},{4,5},{5,4},{6,7},{7,6},{8,9},{9,8},{10,11... | collective-permute-start | bytes 1253384 | tf_op jit(solution)/shard_map/ppermute | solution.py:646
  68.5 2.5 %collective-permute-start.21 = (bf16[256,384]{1,0:T(8,128)(2,1)S(1)}, bf16[256,384]{1,0:T(8,128)(2,1)S(1)}, u32[]{:S(2)}, u32[]{:S(2)}) collective-permute-start(bf16[256,384]{1,0:T(8,128)(2,1)S(1)} %get-tuple-element.97), channel_id=1, source_target_pairs={{1,4},{3,6},{0,8},{2,10},{4,9},{6,11},{5,13},{7,15},{9,12},{11,14}... | collective-permute-start | bytes 589832 | tf_op jit(solution)/shard_map/ppermute | solution.py:622
  71.1 0.7 collective-permute-start.22
  71.7 2.5 %collective-permute-start.26 = (bf16[512,384]{1,0:T(8,128)(2,1)S(1)}, bf16[512,384]{1,0:T(8,128)(2,1)S(1)}, u32[]{:S(2)}, u32[]{:S(2)}) collective-permute-start(bf16[512,384]{1,0:T(8,128)(2,1)S(1)} %owner_slope.2.slope0), channel_id=1, source_target_pairs={{0,1},{1,0},{2,3},{3,2},{4,5},{5,4},{6,7},{7,6},{8,9},{9,8},{10,11... | collective-permute-start | bytes 1179656 | tf_op jit(solution)/shard_map/ppermute | solution.py:590
  74.2 0.8 pred_.1
  75.0 3.6 %collective-permute-done.24.pool3 = bf16[256,384]{1,0:T(8,128)(2,1)S(1)} collective-permute-done((bf16[256,384]{1,0:T(8,128)(2,1)S(1)}, bf16[256,384]{1,0:T(8,128)(2,1)S(1)}, u32[]{:S(2)}, u32[]{:S(2)}) %collective-permute-start.24) | collective-permute-done | bytes 196640 | tf_op jit(solution)/shard_map/ppermute | solution.py:431
  78.7 3.5 %dec_grad.1 = f32[5,192,384]{2,1,0:T(8,128)} custom-call(s32[4]{0:T(128)S(1)} %pad_add_fusion.place, bf16[2,2,272,192]{3,2,1,0:T(8,128)(2,1)S(1)} %pad_maximum_fusion.own, bf16[2,2,272,192]{3,2,1,0:T(8,128)(2,1)S(1)} %collective-permute-done.23.came, bf16[256,384]{1,0:T(8,128)(2,1)S(1)} %get-tuple-element.67.pool0, ...), custom_call_target="tpu_custom_call" | custom-call | tf_op jit(solution)/shard_map/dec_grad/pallas_call | solution.py:398
  82.3 0.6 collective-permute-start.25
  82.9 2.1 %enc_grad.2.refs_0_ = f32[960,384]{1,0:T(8,128)S(1)} custom-call(s32[4]{0:T(128)S(1)} %pad_add_fusion.place, bf16[960,2048]{1,0:T(8,128)(2,1)S(1)} %stem_taps.1.taps, bf16[2,256,384]{2,1,0:T(8,128)(2,1)S(1)} %pad_maximum_fusion.1.slots, bf16[512,384]{1,0:T(8,128)(2,1)S(1)} %owner_slope.2.slope0, bf16[512,384]{1,0:T(8,128)(2,1)S(1)} %owner_slope.3.slope1), custom_call_target="tpu_custom_call" | custom-call | tf_op jit(solution)/shard_map/enc_grad/pallas_call | solution.py:675
  85.0 3.0 %enc_grad.3 = f32[960,384]{1,0:T(8,128)} custom-call(s32[4]{0:T(128)S(1)} %pad_add_fusion.place, bf16[960,2048]{1,0:T(8,128)(2,1)S(1)} %stem_taps.1.taps, bf16[2,256,384]{2,1,0:T(8,128)(2,1)S(1)} %collective-permute-done.25.slots, bf16[512,384]{1,0:T(8,128)(2,1)S(1)} %collective-permute-done.26.slope0, bf16[512,384]{1,0:T(8,128)(2,1)S(1)} %collective-permute-done.27.slope1, ...), custom_call_target="tpu_custom_call" | custom-call | tf_op jit(solution)/shard_map/enc_grad/pallas_call | solution.py:675
  (47 shorter events, 0.8 us)
Async XLA Ops:
  0.8 4.4 %copy-start = (bf16[768,5,384]{2,0,1:T(8,128)(2,1)S(1)}, bf16[768,5,384]{2,0,1:T(8,128)(2,1)}, u32[]{:S(2)}) copy-start(bf16[768,5,384]{2,0,1:T(8,128)(2,1)} %param.8) | copy-start | bytes 8847364
  1.7 1.8 %copy-start.1 = (bf16[1536,5,192]{0,2,1:T(8,128)(2,1)S(1)}, bf16[1536,5,192]{0,2,1:T(8,128)(2,1)}, u32[]{:S(2)}) copy-start(bf16[1536,5,192]{0,2,1:T(8,128)(2,1)} %param.7) | copy-start | bytes 8847364
  4.7 11.6 %collective-permute-start.2 = (bf16[992,768]{1,0:T(8,128)(2,1)S(1)}, bf16[992,768]{1,0:T(8,128)(2,1)S(1)}, u32[]{:S(2)}, u32[]{:S(2)}) collective-permute-start(bf16[992,768]{1,0:T(8,128)(2,1)S(1)} %get-tuple-element.51), channel_id=1, source_target_pairs={{0,1},{1,0},{2,3},{3,2},{4,5},{5,4},{6,7},{7,6},{8,9},{9,8},{10,11... | collective-permute-start | bytes 4571144 | tf_op jit(solution)/shard_map/ppermute | solution.py:460
  5.2 4.1 %copy-start.4 = (s32[512]{0:T(512)S(1)}, s32[512]{0:T(512)}, u32[]{:S(2)}) copy-start(s32[512]{0:T(512)} %param.5) | copy-start | bytes 6148
  5.2 11.1 %copy-start.2 = (bf16[1536,5,192]{0,2,1:T(8,128)(2,1)S(1)}, bf16[1536,5,192]{0,2,1:T(8,128)(2,1)}, u32[]{:S(2)}) copy-start(bf16[1536,5,192]{0,2,1:T(8,128)(2,1)} %param.7) | copy-start | bytes 8847364
  6.3 21.3 %collective-permute-start.3 = (bf16[5,2,192,384]{3,2,1,0:T(8,128)(2,1)S(1)}, bf16[5,2,192,384]{3,2,1,0:T(8,128)(2,1)S(1)}, u32[]{:S(2)}, u32[]{:S(2)}) collective-permute-start(bf16[5,2,192,384]{3,2,1,0:T(8,128)(2,1)S(1)} %dec_pick.1), channel_id=1, source_target_pairs={{0,1},{1,0},{2,3},{3,2},{4,5},{5,4},{6,7},{7,6},{8,9},{9,8},{10,11... | collective-permute-start | bytes 4423688 | tf_op jit(solution)/shard_map/ppermute | solution.py:474
  6.4 20.6 %collective-permute-start.12 = (bf16[608,384]{1,0:T(8,128)(2,1)S(1)}, bf16[608,384]{1,0:T(8,128)(2,1)S(1)}, u32[]{:S(2)}, u32[]{:S(2)}) collective-permute-start(bf16[608,384]{1,0:T(8,128)(2,1)S(1)} %get-tuple-element.71), channel_id=1, source_target_pairs={{0,2},{1,3},{2,0},{3,1},{4,6},{5,7},{6,4},{7,5},{8,10},{9,11},{10,... | collective-permute-start | bytes 1400840 | tf_op jit(solution)/shard_map/ppermute | solution.py:461
  9.3 4.1 %collective-permute-start = (s32[1,512]{1,0:T(1,128)S(1)}, s32[1,512]{1,0:T(1,128)S(1)}, u32[]{:S(2)}, u32[]{:S(2)}) collective-permute-start(s32[1,512]{1,0:T(1,128)S(1)} %bitcast.42), channel_id=1, source_target_pairs={{0,4},{4,0},{8,12},{12,8},{1,5},{5,1},{9,13},{13,9},{2,6},{6,2},{1... | collective-permute-start | bytes 6152 | tf_op jit(solution)/shard_map/ppermute | solution.py:431
  10.9 5.4 %collective-permute-start.1 = (s32[1,512]{1,0:T(1,128)S(1)}, s32[1,512]{1,0:T(1,128)S(1)}, u32[]{:S(2)}, u32[]{:S(2)}) collective-permute-start(s32[1,512]{1,0:T(1,128)S(1)} %bitcast.43), channel_id=1, source_target_pairs={{0,12},{4,8},{8,4},{12,0},{1,13},{5,9},{9,5},{13,1},{2,14},{6,10},... | collective-permute-start | bytes 6152 | tf_op jit(solution)/shard_map/ppermute | solution.py:441
  18.9 2.0 %copy-start.3 = (bf16[512,192]{0,1:T(8,128)(2,1)S(1)}, bf16[512,192]{0,1:T(8,128)(2,1)}, u32[]{:S(2)}) copy-start(bf16[512,192]{0,1:T(8,128)(2,1)} %param.9) | copy-start | bytes 589828
  20.3 11.7 %collective-permute-start.7 = (bf16[544,384]{1,0:T(8,128)(2,1)S(1)}, bf16[544,384]{1,0:T(8,128)(2,1)S(1)}, u32[]{:S(2)}, u32[]{:S(2)}) collective-permute-start(bf16[544,384]{1,0:T(8,128)(2,1)S(1)} %enc_conv.1), channel_id=1, source_target_pairs={{0,2},{1,3},{2,0},{3,1},{4,6},{5,7},{6,4},{7,5},{8,10},{9,11},{10,... | collective-permute-start | bytes 1253384 | tf_op jit(solution)/shard_map/ppermute | solution.py:499
  20.9 6.1 %collective-permute-start.4 = (bf16[192,128]{1,0:T(8,128)(2,1)S(1)}, bf16[192,128]{1,0:T(8,128)(2,1)S(1)}, u32[]{:S(2)}, u32[]{:S(2)}) collective-permute-start(bf16[192,128]{1,0:T(8,128)(2,1)S(1)} %get-tuple-element.103), channel_id=1, source_target_pairs={{0,4},{4,8},{8,12},{12,0},{1,5},{5,9},{9,13},{13,1},{2,6},{6,10},{... | collective-permute-start | bytes 147464 | tf_op jit(solution)/shard_map/ppermute | solution.py:428
  21.0 6.5 %collective-permute-start.5 = (bf16[192,128]{1,0:T(8,128)(2,1)S(1)}, bf16[192,128]{1,0:T(8,128)(2,1)S(1)}, u32[]{:S(2)}, u32[]{:S(2)}) collective-permute-start(bf16[192,128]{1,0:T(8,128)(2,1)S(1)} %get-tuple-element.102), channel_id=1, source_target_pairs={{0,12},{4,0},{8,4},{12,8},{1,13},{5,1},{9,5},{13,9},{2,14},{6,2},{... | collective-permute-start | bytes 147464 | tf_op jit(solution)/shard_map/ppermute | solution.py:428
  27.0 14.5 %collective-permute-start.11 = (bf16[992,384]{1,0:T(8,128)(2,1)S(1)}, bf16[992,384]{1,0:T(8,128)(2,1)S(1)}, u32[]{:S(2)}, u32[]{:S(2)}) collective-permute-start(bf16[992,384]{1,0:T(8,128)(2,1)S(1)} %get-tuple-element.70.refs_4_), channel_id=1, source_target_pairs={{0,1},{1,0},{2,3},{3,2},{4,5},{5,4},{6,7},{7,6},{8,9},{9,8},{10,11... | collective-permute-start | bytes 2285576 | tf_op jit(solution)/shard_map/ppermute | solution.py:573
  27.1 12.2 %collective-permute-start.14 = (bf16[608,384]{1,0:T(8,128)(2,1)S(1)}, bf16[608,384]{1,0:T(8,128)(2,1)S(1)}, u32[]{:S(2)}, u32[]{:S(2)}) collective-permute-start(bf16[608,384]{1,0:T(8,128)(2,1)S(1)} %collective-permute-done.12.refs_6_), channel_id=1, source_target_pairs={{0,1},{1,0},{2,3},{3,2},{4,5},{5,4},{6,7},{7,6},{8,9},{9,8},{10,11... | collective-permute-start | bytes 1400840 | tf_op jit(solution)/shard_map/ppermute | solution.py:574
  27.6 4.5 %collective-permute-start.6 = (s32[2,256]{1,0:T(2,128)S(1)}, s32[2,256]{1,0:T(2,128)S(1)}, u32[]{:S(2)}, u32[]{:S(2)}) collective-permute-start(s32[2,256]{1,0:T(2,128)S(1)} %get-tuple-element.106.refs_0_), channel_id=1, source_target_pairs={{0,8},{4,12},{8,0},{12,4},{1,9},{5,13},{9,1},{13,5},{2,10},{6,14},... | collective-permute-start | bytes 6152 | tf_op jit(solution)/shard_map/ppermute | solution.py:428
  27.6 9.1 %collective-permute-start.13 = (bf16[384,384]{1,0:T(8,128)(2,1)S(1)}, bf16[384,384]{1,0:T(8,128)(2,1)S(1)}, u32[]{:S(2)}, u32[]{:S(2)}) collective-permute-start(bf16[384,384]{1,0:T(8,128)(2,1)S(1)} %get-tuple-element.73), channel_id=1, source_target_pairs={{0,2},{1,3},{2,0},{3,1},{4,6},{5,7},{6,4},{7,5},{8,10},{9,11},{10,... | collective-permute-start | bytes 884744 | tf_op jit(solution)/shard_map/ppermute | solution.py:530
  33.0 1.5 %collective-permute-start.8 = (bf16[272,384]{1,0:T(8,128)(2,1)S(1)}, bf16[272,384]{1,0:T(8,128)(2,1)S(1)}, u32[]{:S(2)}, u32[]{:S(2)}) collective-permute-start(bf16[272,384]{1,0:T(8,128)(2,1)S(1)} %get-tuple-element.65.own), channel_id=1, source_target_pairs={{0,1},{1,0},{2,3},{3,2},{4,5},{5,4},{6,7},{7,6},{8,9},{9,8},{10,11... | collective-permute-start | bytes 626696 | tf_op jit(solution)/shard_map/ppermute | solution.py:552
  36.6 13.0 %collective-permute-start.16 = (bf16[272,768]{1,0:T(8,128)(2,1)S(1)}, bf16[272,768]{1,0:T(8,128)(2,1)S(1)}, u32[]{:S(2)}, u32[]{:S(2)}) collective-permute-start(bf16[272,768]{1,0:T(8,128)(2,1)S(1)} %get-tuple-element.76), channel_id=1, source_target_pairs={{0,2},{1,3},{2,0},{3,1},{4,6},{5,7},{6,4},{7,5},{8,10},{9,11},{10,... | collective-permute-start | bytes 1253384 | tf_op jit(solution)/shard_map/ppermute | solution.py:568
  38.1 3.3 %collective-permute-start.15 = (bf16[384,384]{1,0:T(8,128)(2,1)S(1)}, bf16[384,384]{1,0:T(8,128)(2,1)S(1)}, u32[]{:S(2)}, u32[]{:S(2)}) collective-permute-start(bf16[384,384]{1,0:T(8,128)(2,1)S(1)} %collective-permute-done.13.refs_7_), channel_id=1, source_target_pairs={{0,1},{1,0},{2,3},{3,2},{4,5},{5,4},{6,7},{7,6},{8,9},{9,8},{10,11... | collective-permute-start | bytes 884744 | tf_op jit(solution)/shard_map/ppermute | solution.py:574
  38.1 11.5 %collective-permute-start.10 = (bf16[256,384]{1,0:T(8,128)(2,1)S(1)}, bf16[256,384]{1,0:T(8,128)(2,1)S(1)}, u32[]{:S(2)}, u32[]{:S(2)}) collective-permute-start(bf16[256,384]{1,0:T(8,128)(2,1)S(1)} %get-tuple-element.67.pool0), channel_id=1, source_target_pairs={{0,4},{4,0},{8,12},{12,8},{1,5},{5,1},{9,13},{13,9},{2,6},{6,2},{1... | collective-permute-start | bytes 589832 | tf_op jit(solution)/shard_map/ppermute | solution.py:431
  39.3 10.4 %collective-permute-start.9 = (bf16[256,384]{1,0:T(8,128)(2,1)S(1)}, bf16[256,384]{1,0:T(8,128)(2,1)S(1)}, u32[]{:S(2)}, u32[]{:S(2)}) collective-permute-start(bf16[256,384]{1,0:T(8,128)(2,1)S(1)} %get-tuple-element.67.pool0), channel_id=1, source_target_pairs={{0,8},{4,12},{8,0},{12,4},{1,9},{5,13},{9,1},{13,5},{2,10},{6,14},... | collective-permute-start | bytes 589832 | tf_op jit(solution)/shard_map/ppermute | solution.py:431
  50.8 3.1 %collective-permute-start.17 = (bf16[2,2,272,192]{3,2,1,0:T(8,128)(2,1)S(1)}, bf16[2,2,272,192]{3,2,1,0:T(8,128)(2,1)S(1)}, u32[]{:S(2)}, u32[]{:S(2)}) collective-permute-start(bf16[2,2,272,192]{3,2,1,0:T(8,128)(2,1)S(1)} %get-tuple-element.78.own), channel_id=1, source_target_pairs={{0,1},{1,0},{2,3},{3,2},{4,5},{5,4},{6,7},{7,6},{8,9},{9,8},{10,11... | collective-permute-start | bytes 1253384 | tf_op jit(solution)/shard_map/ppermute | solution.py:602
  50.9 14.8 %collective-permute-start.19 = (bf16[2,272,192]{2,1,0:T(8,128)(2,1)S(1)}, bf16[2,272,192]{2,1,0:T(8,128)(2,1)S(1)}, u32[]{:S(2)}, u32[]{:S(2)}) collective-permute-start(bf16[2,272,192]{2,1,0:T(8,128)(2,1)S(1)} %get-tuple-element.83), channel_id=1, source_target_pairs={{1,4},{3,6},{0,8},{2,10},{4,9},{6,11},{5,13},{7,15},{9,12},{11,14}... | collective-permute-start | bytes 626696 | tf_op jit(solution)/shard_map/ppermute | solution.py:622
  53.1 12.5 %collective-permute-start.20 = (bf16[2,272,192]{2,1,0:T(8,128)(2,1)S(1)}, bf16[2,272,192]{2,1,0:T(8,128)(2,1)S(1)}, u32[]{:S(2)}, u32[]{:S(2)}) collective-permute-start(bf16[2,272,192]{2,1,0:T(8,128)(2,1)S(1)} %get-tuple-element.84), channel_id=1, source_target_pairs={{1,12},{3,14},{4,1},{6,3},{9,4},{11,6},{12,9},{14,11},{17,28},{19,... | collective-permute-start | bytes 626696 | tf_op jit(solution)/shard_map/ppermute | solution.py:623
  56.0 9.8 %collective-permute-start.18 = (bf16[256,384]{1,0:T(8,128)(2,1)S(1)}, bf16[256,384]{1,0:T(8,128)(2,1)S(1)}, u32[]{:S(2)}, u32[]{:S(2)}) collective-permute-start(bf16[256,384]{1,0:T(8,128)(2,1)S(1)} %up_grad.1), channel_id=1, source_target_pairs={{0,2},{1,3},{2,0},{3,1},{4,6},{5,7},{6,4},{7,5},{8,10},{9,11},{10,... | collective-permute-start | bytes 589832 | tf_op jit(solution)/shard_map/ppermute | solution.py:630
  65.9 12.8 %collective-permute-start.23 = (bf16[2,2,272,192]{3,2,1,0:T(8,128)(2,1)S(1)}, bf16[2,2,272,192]{3,2,1,0:T(8,128)(2,1)S(1)}, u32[]{:S(2)}, u32[]{:S(2)}) collective-permute-start(bf16[2,2,272,192]{3,2,1,0:T(8,128)(2,1)S(1)} %pad_maximum_fusion.own), channel_id=1, source_target_pairs={{0,1},{1,0},{2,3},{3,2},{4,5},{5,4},{6,7},{7,6},{8,9},{9,8},{10,11... | collective-permute-start | bytes 1253384 | tf_op jit(solution)/shard_map/ppermute | solution.py:646
  68.5 10.1 %collective-permute-start.24 = (bf16[256,384]{1,0:T(8,128)(2,1)S(1)}, bf16[256,384]{1,0:T(8,128)(2,1)S(1)}, u32[]{:S(2)}, u32[]{:S(2)}) collective-permute-start(bf16[256,384]{1,0:T(8,128)(2,1)S(1)} %collective-permute-done.9.pool2), channel_id=1, source_target_pairs={{0,4},{4,0},{8,12},{12,8},{1,5},{5,1},{9,13},{13,9},{2,6},{6,2},{1... | collective-permute-start | bytes 589832 | tf_op jit(solution)/shard_map/ppermute | solution.py:431
  68.5 13.6 %collective-permute-start.21 = (bf16[256,384]{1,0:T(8,128)(2,1)S(1)}, bf16[256,384]{1,0:T(8,128)(2,1)S(1)}, u32[]{:S(2)}, u32[]{:S(2)}) collective-permute-start(bf16[256,384]{1,0:T(8,128)(2,1)S(1)} %get-tuple-element.97), channel_id=1, source_target_pairs={{1,4},{3,6},{0,8},{2,10},{4,9},{6,11},{5,13},{7,15},{9,12},{11,14}... | collective-permute-start | bytes 589832 | tf_op jit(solution)/shard_map/ppermute | solution.py:622
  71.1 11.1 %collective-permute-start.22 = (bf16[256,384]{1,0:T(8,128)(2,1)S(1)}, bf16[256,384]{1,0:T(8,128)(2,1)S(1)}, u32[]{:S(2)}, u32[]{:S(2)}) collective-permute-start(bf16[256,384]{1,0:T(8,128)(2,1)S(1)} %get-tuple-element.96), channel_id=1, source_target_pairs={{1,12},{3,14},{4,1},{6,3},{9,4},{11,6},{12,9},{14,11},{17,28},{19,... | collective-permute-start | bytes 589832 | tf_op jit(solution)/shard_map/ppermute | solution.py:623
  71.7 13.3 %collective-permute-start.26 = (bf16[512,384]{1,0:T(8,128)(2,1)S(1)}, bf16[512,384]{1,0:T(8,128)(2,1)S(1)}, u32[]{:S(2)}, u32[]{:S(2)}) collective-permute-start(bf16[512,384]{1,0:T(8,128)(2,1)S(1)} %owner_slope.2.slope0), channel_id=1, source_target_pairs={{0,1},{1,0},{2,3},{3,2},{4,5},{5,4},{6,7},{7,6},{8,9},{9,8},{10,11... | collective-permute-start | bytes 1179656 | tf_op jit(solution)/shard_map/ppermute | solution.py:590
  78.7 6.3 %collective-permute-start.27 = (bf16[512,384]{1,0:T(8,128)(2,1)S(1)}, bf16[512,384]{1,0:T(8,128)(2,1)S(1)}, u32[]{:S(2)}, u32[]{:S(2)}) collective-permute-start(bf16[512,384]{1,0:T(8,128)(2,1)S(1)} %owner_slope.3.slope1), channel_id=1, source_target_pairs={{0,1},{1,0},{2,3},{3,2},{4,5},{5,4},{6,7},{7,6},{8,9},{9,8},{10,11... | collective-permute-start | bytes 1179656 | tf_op jit(solution)/shard_map/ppermute | solution.py:590
  82.3 2.7 %collective-permute-start.25 = (bf16[2,256,384]{2,1,0:T(8,128)(2,1)S(1)}, bf16[2,256,384]{2,1,0:T(8,128)(2,1)S(1)}, u32[]{:S(2)}, u32[]{:S(2)}) collective-permute-start(bf16[2,256,384]{2,1,0:T(8,128)(2,1)S(1)} %pad_maximum_fusion.1.slots), channel_id=1, source_target_pairs={{0,1},{1,0},{2,3},{3,2},{4,5},{5,4},{6,7},{7,6},{8,9},{9,8},{10,11... | collective-permute-start | bytes 1179656 | tf_op jit(solution)/shard_map/ppermute | solution.py:671

commit v6 on v5

--- a/solution.py
+++ b/solution.py
@@ -590,10 +590,17 @@
         return out, lax.ppermute(out, "chan", cores)
 
     slope0, slope0_came = owner_slope(0, gated(place, send))
+    (taps,) = call(
+        functools.partial(taps_kernel, pairs=pairs, devices=devices),
+        [gated(place, slope0)] + [blocks[r] for r in range(devices)] + [stem_w],
+        [((KW * stem_c, 2 * pairs * devices), BF16)],
+        limit=12,
+        name="stem_taps",
+    )
 
     pred, sums, local, near, far = call(
         functools.partial(slope_kernel, pairs=pairs, total=total, scale=1.0 / math.sqrt(2 * total)),
-        [gated(place, (beyond, beside, slope0)), part, came, targets_at],
+        [gated(place, (beyond, beside, slope0, taps)), part, came, targets_at],
         [((2, pairs, stem_c), BF16), ((2, 2, rows, stem_c), BF16)] + [((2, rows, stem_c), BF16)] * 3,
         [((rows + 8, 2 * stem_c), F32)],
         limit=7,
@@ -629,17 +636,10 @@
     local, near, far = to_owner(local, near, far)
     pre_oth = lax.ppermute(pre, "chan", across)
     slope1, slope1_came = owner_slope(1, gated(place, pre))
-    (taps,) = call(
-        functools.partial(taps_kernel, pairs=pairs, devices=devices),
-        [gated(place, slope1)] + [blocks[r] for r in range(devices)] + [stem_w],
-        [((KW * stem_c, 2 * pairs * devices), BF16)],
-        limit=12,
-        name="stem_taps",
-    )
-    near, far = gated((near, far), taps)
-    far_pooled = swap(gated(beyond, taps), 1)
+    near, far = gated((near, far), slope1)
+    far_pooled = swap(gated(beyond, pre), 1)
     sums_pieces = local, near, far
-    pre_oth = gated(pre_oth, (near, far, slope1, taps))
+    pre_oth = gated(pre_oth, (near, far, slope1))
     pieces = [jnp.where(own_block, pre, pre_oth) for own_block in target]
     local, near, far = to_owner(*pieces)
     sums_mine = gated(slots(*sums_pieces), pieces)

time: 88.3 us -> 85.5 us (0.968)
  waiting for transfers between devices: 12.6 us -> 10.1 us
    ppermute x4, waiting for transfers between devices: 6.46 us -> 1.34 us  [swap(): lax.ppermute(array, 'seq', [(i, i ^ distance) for i in range(devices)])]
    ppermute x2, waiting for transfers between devices: 1.05 us -> 3.73 us  [to_owner(): near = lax.ppermute(near, ('seq', 'chan'), link((1, 2)))]
    ppermute x1, starting transfers between devices: 2.69 us -> 0.16 us  [shards(): sums_came = lax.ppermute(sums_mine, 'chan', cores)]
    ppermute x4, starting transfers between devices: 4.88 us -> 7.12 us  [swap(): lax.ppermute(array, 'seq', [(i, i ^ distance) for i in range(devices)])]
  transfers between devices with their start and end apart: 28 -> 28, of which waited for: 7 -> 8; matrix products, arithmetic and copies ran while one was open for 0% -> 1% of each run, Pallas kernels for 39% -> 40%
where the time goes in v6:
time: 85.5 us; the launch traced here: 85.2 us
  Pallas kernels  39.4 us (46%)
  starting transfers between devices  31.3 us (37%)
  waiting for transfers between devices  10.1 us (12%)
  local copies, waits for them, and re-layouts  2.74 us (3%)
  between operations  1.05 us (1%)
    pallas_call x13, Pallas kernels, call(): pl.pallas_call(kernel, grid=(1,) if last else (), in_specs=specs, out_spe...  30.4 us
    ppermute x4, starting transfers between devices, swap(): lax.ppermute(array, 'seq', [(i, i ^ distance) for i in range(devices)])  7.12 us
    pallas_call x2, Pallas kernels, enc_grad(): pl.pallas_call(functools.partial(enc_grad_kernel, first=first), grid=(2,)...  5.11 us
    ppermute x2, starting transfers between devices, to_owner(): near = lax.ppermute(near, ('seq', 'chan'), link((1, 2)))  4.16 us
    ppermute x3, starting transfers between devices, ring(): lax.ppermute(array, 'seq', [(i, (i + step) % devices) for i in range(devi...  3.87 us
    ppermute x2, waiting for transfers between devices, to_owner(): near = lax.ppermute(near, ('seq', 'chan'), link((1, 2)))  3.73 us
    ppermute x2, starting transfers between devices, owner_slope(): return (out, lax.ppermute(out, 'chan', cores))  3.06 us
    ppermute x1, starting transfers between devices, shards(): mine0_far = lax.ppermute(mine0, 'chan', across)  2.94 us
  transfers between devices with their start and end apart: 28, of which 8 were waited for; matrix products, arithmetic and copies ran while one was open for 1% of the time, Pallas kernels for 40%

profile of v6, /device:TPU:0, one launch (start us, length us, event | category | flops | bytes accessed | tf_op | source)
XLA Modules:
  0.0 85.2 jit_solution(7686648910243621536)
XLA Ops:
  0.9 0.9 %reshape.25.stem_own.refs_4_ = bf16[20,192]{1,0:T(8,128)(2,1)S(1)} reshape(bf16[5,4,192]{2,1,0:T(4,128)(2,1)} %bitcast.48) | data formatting | bytes 15360 | tf_op jit(solution)/shard_map/reshape | solution.py:437
  1.8 1.8 %copy-done.1 = bf16[1536,5,192]{0,2,1:T(8,128)(2,1)S(1)} copy-done((bf16[1536,5,192]{0,2,1:T(8,128)(2,1)S(1)}, bf16[1536,5,192]{0,2,1:T(8,128)(2,1)}, u32[]{:S(2)}) %copy-start.1) | copy-done | bytes 2949144
  3.6 1.1 %picks.1 = (bf16[992,384]{1,0:T(8,128)(2,1)S(1)}, bf16[608,384]{1,0:T(8,128)(2,1)S(1)}, bf16[384,384]{1,0:T(8,128)(2,1)S(1)}, bf16[992,768]{1,0:T(8,128)(2,1)S(1)}) custom-call(s32[4]{0:T(128)S(1)} %pad_add_fusion.place, bf16[32,192]{1,0:T(8,128)(2,1)S(1)} %concatenate.9.stem, bf16[5,192,1536]{2,1,0:T(8,128)(2,1)S(1)} %bitcast.35), custom_call_target="tpu_custom_call" | custom-call | tf_op jit(solution)/shard_map/picks/pallas_call | solution.py:446
  4.7 0.5 collective-permute-start.2
  5.2 1.1 %dec_pick.1 = bf16[5,2,192,384]{3,2,1,0:T(8,128)(2,1)S(1)} custom-call(s32[4]{0:T(128)S(1)} %pad_add_fusion.place, bf16[5,4,192,384]{3,2,1,0:T(8,128)(2,1)S(1)} %bitcast.32), custom_call_target="tpu_custom_call" | custom-call | tf_op jit(solution)/shard_map/dec_pick/pallas_call | solution.py:462
  6.4 2.9 %collective-permute-start.12 = (bf16[608,384]{1,0:T(8,128)(2,1)S(1)}, bf16[608,384]{1,0:T(8,128)(2,1)S(1)}, u32[]{:S(2)}, u32[]{:S(2)}) collective-permute-start(bf16[608,384]{1,0:T(8,128)(2,1)S(1)} %get-tuple-element.71), channel_id=1, source_target_pairs={{0,2},{1,3},{2,0},{3,1},{4,6},{5,7},{6,4},{7,5},{8,10},{9,11},{10,... | collective-permute-start | bytes 1400840 | tf_op jit(solution)/shard_map/ppermute | solution.py:461
  9.3 1.6 %collective-permute-start = (s32[1,512]{1,0:T(1,128)S(1)}, s32[1,512]{1,0:T(1,128)S(1)}, u32[]{:S(2)}, u32[]{:S(2)}) collective-permute-start(s32[1,512]{1,0:T(1,128)S(1)} %bitcast.42), channel_id=1, source_target_pairs={{0,4},{4,0},{8,12},{12,8},{1,5},{5,1},{9,13},{13,9},{2,6},{6,2},{1... | collective-permute-start | bytes 6152 | tf_op jit(solution)/shard_map/ppermute | solution.py:431
  10.9 2.5 %collective-permute-start.1 = (s32[1,512]{1,0:T(1,128)S(1)}, s32[1,512]{1,0:T(1,128)S(1)}, u32[]{:S(2)}, u32[]{:S(2)}) collective-permute-start(s32[1,512]{1,0:T(1,128)S(1)} %bitcast.43), channel_id=1, source_target_pairs={{0,12},{4,8},{8,4},{12,0},{1,13},{5,9},{9,5},{13,1},{2,14},{6,10},... | collective-permute-start | bytes 6152 | tf_op jit(solution)/shard_map/ppermute | solution.py:441
  13.4 2.9 %collective-permute-done.1.before = s32[1,512]{1,0:T(1,128)S(1)} collective-permute-done((s32[1,512]{1,0:T(1,128)S(1)}, s32[1,512]{1,0:T(1,128)S(1)}, u32[]{:S(2)}, u32[]{:S(2)}) %collective-permute-start.1) | collective-permute-done | bytes 2080 | tf_op jit(solution)/shard_map/ppermute | solution.py:441
  16.3 2.6 %stem_conv.1 = (f32[544,384]{1,0:T(8,128)S(1)}, bf16[2,272,192]{2,1,0:T(8,128)(2,1)S(1)}, bf16[6,272,192]{2,1,0:T(8,128)(2,1)S(1)}, bf16[6,272,192]{2,1,0:T(8,128)(2,1)S(1)}, s32[3,2,256]{2,1,0:T(2,128)S(1)}) custom-call(s32[4]{0:T(128)S(1)} %pad_add_fusion.place, s32[1,512]{1,0:T(1,128)S(1)} %bitcast.44, s32[1,512]{1,0:T(1,128)S(1)} %collective-permute-done.after, ...), custom_call_target="tpu_custom_call" | custom-call | tf_op jit(solution)/shard_map/stem_conv/pallas_call | solution.py:398
  18.9 1.4 %enc_conv.1 = bf16[544,384]{1,0:T(8,128)(2,1)S(1)} custom-call(s32[4]{0:T(128)S(1)} %pad_add_fusion.place, f32[544,384]{1,0:T(8,128)S(1)} %get-tuple-element.52.acc, bf16[6,272,192]{2,1,0:T(8,128)(2,1)S(1)} %get-tuple-element.53.lhs.lhs_oth, bf16[992,768]{1,0:T(8,128)(2,1)S(1)} %collective-permute-done.2.w_oth), custom_call_target="tpu_custom_call" | custom-call | tf_op jit(solution)/shard_map/enc_conv/pallas_call | solution.py:398
  20.3 0.6 collective-permute-start.7
  21.0 3.8 %collective-permute-start.5 = (bf16[192,128]{1,0:T(8,128)(2,1)S(1)}, bf16[192,128]{1,0:T(8,128)(2,1)S(1)}, u32[]{:S(2)}, u32[]{:S(2)}) collective-permute-start(bf16[192,128]{1,0:T(8,128)(2,1)S(1)} %get-tuple-element.102), channel_id=1, source_target_pairs={{0,12},{4,0},{8,4},{12,8},{1,13},{5,1},{9,5},{13,9},{2,14},{6,2},{... | collective-permute-start | bytes 147464 | tf_op jit(solution)/shard_map/ppermute | solution.py:428
  24.8 2.1 %enc_keep.1.keep = f32[544,384]{1,0:T(8,128)S(1)} custom-call(s32[4]{0:T(128)S(1)} %pad_add_fusion.place, bf16[6,272,192]{2,1,0:T(8,128)(2,1)S(1)} %get-tuple-element.63.lhs, bf16[6,272,192]{2,1,0:T(8,128)(2,1)S(1)} %get-tuple-element.53.lhs.lhs_oth, bf16[5,192,1536]{2,1,0:T(8,128)(2,1)S(1)} %bitcast.37, bf16[992,768]{1,0:T(8,128)(2,1)S(1)} %collective-permute-done.2.w_oth), custom_call_target="tpu_custom_call" | custom-call | tf_op jit(solution)/shard_map/enc_keep/pallas_call | solution.py:398
  27.1 0.5 collective-permute-start.14
  27.6 1.6 %collective-permute-start.13 = (bf16[384,384]{1,0:T(8,128)(2,1)S(1)}, bf16[384,384]{1,0:T(8,128)(2,1)S(1)}, u32[]{:S(2)}, u32[]{:S(2)}) collective-permute-start(bf16[384,384]{1,0:T(8,128)(2,1)S(1)} %get-tuple-element.73), channel_id=1, source_target_pairs={{0,2},{1,3},{2,0},{3,1},{4,6},{5,7},{6,4},{7,5},{8,10},{9,11},{10,... | collective-permute-start | bytes 884744 | tf_op jit(solution)/shard_map/ppermute | solution.py:530
  29.1 0.2 pad_select_fusion.stem
  29.3 1.7 %dec_taps.1 = (bf16[3,2,2,192,384]{4,3,2,1,0:T(8,128)(2,1)S(1)}, bf16[3,2,2,192,384]{4,3,2,1,0:T(8,128)(2,1)S(1)}) custom-call(s32[4]{0:T(128)S(1)} %pad_add_fusion.place, bf16[5,4,192,384]{3,2,1,0:T(8,128)(2,1)S(1)} %bitcast.33, bf16[5,2,192,384]{3,2,1,0:T(8,128)(2,1)S(1)} %collective-permute-done.3.came), custom_call_target="tpu_custom_call" | custom-call | tf_op jit(solution)/shard_map/dec_taps/pallas_call | solution.py:512
  31.0 0.9 %targets.1 = bf16[2,272,384]{2,1,0:T(8,128)(2,1)S(1)} custom-call(s32[4]{0:T(128)S(1)} %pad_add_fusion.place, bf16[192,512]{1,0:T(8,128)(2,1)S(1)} %bitcast.41, bf16[192,128]{1,0:T(8,128)(2,1)S(1)} %collective-permute-done.4.before, bf16[192,128]{1,0:T(8,128)(2,1)S(1)} %collective-permute-done.5.after), custom_call_target="tpu_custom_call" | custom-call | tf_op jit(solution)/shard_map/targets/pallas_call | solution.py:398
  32.0 1.0 %gelu_pool.1 = (bf16[272,384]{1,0:T(8,128)(2,1)S(1)}, bf16[256,384]{1,0:T(8,128)(2,1)S(1)}) custom-call(s32[4]{0:T(128)S(1)} %pad_add_fusion.place, f32[544,384]{1,0:T(8,128)S(1)} %enc_keep.1.keep, bf16[544,384]{1,0:T(8,128)(2,1)S(1)} %collective-permute-done.7.came), custom_call_target="tpu_custom_call" | custom-call | tf_op jit(solution)/shard_map/gelu_pool/pallas_call | solution.py:398
  33.1 1.4 %collective-permute-done.8.oth = bf16[272,384]{1,0:T(8,128)(2,1)S(1)} collective-permute-done((bf16[272,384]{1,0:T(8,128)(2,1)S(1)}, bf16[272,384]{1,0:T(8,128)(2,1)S(1)}, u32[]{:S(2)}, u32[]{:S(2)}) %collective-permute-start.8) | collective-permute-done | bytes 208928 | tf_op jit(solution)/shard_map/ppermute | solution.py:552
  34.5 1.5 %dec_conv.1 = (f32[272,768]{1,0:T(8,128)S(1)}, bf16[272,768]{1,0:T(8,128)(2,1)S(1)}) custom-call(bf16[272,384]{1,0:T(8,128)(2,1)S(1)} %get-tuple-element.65.own, bf16[272,384]{1,0:T(8,128)(2,1)S(1)} %collective-permute-done.8.oth, bf16[3,768,384]{2,1,0:T(8,128)(2,1)S(1)} %bitcast.38, bf16[3,768,384]{2,1,0:T(8,128)(2,1)S(1)} %bitcast.39, ...), custom_call_target="tpu_custom_call" | custom-call | tf_op jit(solution)/shard_map/dec_conv/pallas_call | solution.py:398
  36.1 0.6 collective-permute-done.13.refs_7_
  36.6 1.5 %collective-permute-start.16 = (bf16[272,768]{1,0:T(8,128)(2,1)S(1)}, bf16[272,768]{1,0:T(8,128)(2,1)S(1)}, u32[]{:S(2)}, u32[]{:S(2)}) collective-permute-start(bf16[272,768]{1,0:T(8,128)(2,1)S(1)} %get-tuple-element.77), channel_id=1, source_target_pairs={{0,2},{1,3},{2,0},{3,1},{4,6},{5,7},{6,4},{7,5},{8,10},{9,11},{10,... | collective-permute-start | bytes 1253384 | tf_op jit(solution)/shard_map/ppermute | solution.py:568
  38.1 1.2 %collective-permute-start.10 = (bf16[256,384]{1,0:T(8,128)(2,1)S(1)}, bf16[256,384]{1,0:T(8,128)(2,1)S(1)}, u32[]{:S(2)}, u32[]{:S(2)}) collective-permute-start(bf16[256,384]{1,0:T(8,128)(2,1)S(1)} %get-tuple-element.67.pool0), channel_id=1, source_target_pairs={{0,4},{4,0},{8,12},{12,8},{1,5},{5,1},{9,13},{13,9},{2,6},{6,2},{1... | collective-permute-start | bytes 589832 | tf_op jit(solution)/shard_map/ppermute | solution.py:431
  39.3 2.1 %collective-permute-start.9 = (bf16[256,384]{1,0:T(8,128)(2,1)S(1)}, bf16[256,384]{1,0:T(8,128)(2,1)S(1)}, u32[]{:S(2)}, u32[]{:S(2)}) collective-permute-start(bf16[256,384]{1,0:T(8,128)(2,1)S(1)} %get-tuple-element.67.pool0), channel_id=1, source_target_pairs={{0,8},{4,12},{8,0},{12,4},{1,9},{5,13},{9,1},{13,5},{2,10},{6,14},... | collective-permute-start | bytes 589832 | tf_op jit(solution)/shard_map/ppermute | solution.py:431
  41.5 5.4 %owner_slope.2.slope0 = bf16[512,384]{1,0:T(8,128)(2,1)S(1)} custom-call(s32[4]{0:T(128)S(1)} %pad_add_fusion.place, s32[2,256]{1,0:T(2,128)S(1)} %get-tuple-element.106.refs_0_, s32[2,256]{1,0:T(2,128)S(1)} %get-tuple-element.105.refs_1_, s32[2,256]{1,0:T(2,128)S(1)} %collective-permute-done.6.refs_2_, s32[2,256]{1,0:T(2,128)S(1)} %get-tuple-element.104.refs_3_, ...), custom_call_target="tpu_custom_call" | custom-call | tf_op jit(solution)/shard_map/owner_slope/pallas_call | solution.py:398
  46.8 2.6 %stem_taps.1.taps = bf16[960,2048]{1,0:T(8,128)(2,1)S(1)} custom-call(s32[4]{0:T(128)S(1)} %pad_add_fusion.place, s32[2,256]{1,0:T(2,128)S(1)} %get-tuple-element.106.refs_0_, s32[2,256]{1,0:T(2,128)S(1)} %get-tuple-element.105.refs_1_, s32[2,256]{1,0:T(2,128)S(1)} %collective-permute-done.6.refs_2_, s32[2,256]{1,0:T(2,128)S(1)} %get-tuple-element.104.refs_3_, ...), custom_call_target="tpu_custom_call" | custom-call | tf_op jit(solution)/shard_map/stem_taps/pallas_call | solution.py:398
  49.4 0.2 collective-permute-done.10.pool1
  49.7 1.1 %out_slope.1 = (bf16[2,256,192]{2,1,0:T(8,128)(2,1)S(1)}, bf16[2,2,272,192]{3,2,1,0:T(8,128)(2,1)S(1)}, bf16[2,272,192]{2,1,0:T(8,128)(2,1)S(1)}, bf16[2,272,192...) custom-call(s32[4]{0:T(128)S(1)} %pad_add_fusion.place, f32[272,768]{1,0:T(8,128)S(1)} %get-tuple-element.76.part, ...), custom_call_target="tpu_custom_call" | custom-call | tf_op jit(solution)/shard_map/out_slope/pallas_call | solution.py:398
  50.8 2.2 %collective-permute-start.19 = (bf16[2,272,192]{2,1,0:T(8,128)(2,1)S(1)}, bf16[2,272,192]{2,1,0:T(8,128)(2,1)S(1)}, u32[]{:S(2)}, u32[]{:S(2)}) collective-permute-start(bf16[2,272,192]{2,1,0:T(8,128)(2,1)S(1)} %get-tuple-element.82), channel_id=1, source_target_pairs={{1,4},{3,6},{0,8},{2,10},{4,9},{6,11},{5,13},{7,15},{9,12},{11,14}... | collective-permute-start | bytes 626696 | tf_op jit(solution)/shard_map/ppermute | solution.py:629
  53.1 0.9 %collective-permute-start.20 = (bf16[2,272,192]{2,1,0:T(8,128)(2,1)S(1)}, bf16[2,272,192]{2,1,0:T(8,128)(2,1)S(1)}, u32[]{:S(2)}, u32[]{:S(2)}) collective-permute-start(bf16[2,272,192]{2,1,0:T(8,128)(2,1)S(1)} %get-tuple-element.83), channel_id=1, source_target_pairs={{1,12},{3,14},{4,1},{6,3},{9,4},{11,6},{12,9},{14,11},{17,28},{19,... | collective-permute-start | bytes 626696 | tf_op jit(solution)/shard_map/ppermute | solution.py:630
  54.0 2.1 %up_grad.1 = bf16[256,384]{1,0:T(8,128)(2,1)S(1)} custom-call(s32[4]{0:T(128)S(1)} %pad_add_fusion.place, bf16[2,2,272,192]{3,2,1,0:T(8,128)(2,1)S(1)} %get-tuple-element.81.own, bf16[2,2,272,192]{3,2,1,0:T(8,128)(2,1)S(1)} %collective-permute-done.17.oth, bf16[5,4,192,384]{3,2,1,0:T(8,128)(2,1)S(1)} %bitcast.34), custom_call_target="tpu_custom_call" | custom-call | tf_op jit(solution)/shard_map/up_grad/pallas_call | solution.py:398
  56.0 0.6 collective-permute-start.18
  56.6 5.4 %owner_slope.3.slope1 = bf16[512,384]{1,0:T(8,128)(2,1)S(1)} custom-call(s32[4]{0:T(128)S(1)} %pad_add_fusion.place, s32[2,256]{1,0:T(2,128)S(1)} %get-tuple-element.106.refs_0_, s32[2,256]{1,0:T(2,128)S(1)} %get-tuple-element.105.refs_1_, s32[2,256]{1,0:T(2,128)S(1)} %collective-permute-done.6.refs_2_, s32[2,256]{1,0:T(2,128)S(1)} %get-tuple-element.104.refs_3_, ...), custom_call_target="tpu_custom_call" | custom-call | tf_op jit(solution)/shard_map/owner_slope/pallas_call | solution.py:398
  62.0 3.6 %collective-permute-done.19 = bf16[2,272,192]{2,1,0:T(8,128)(2,1)S(1)} collective-permute-done((bf16[2,272,192]{2,1,0:T(8,128)(2,1)S(1)}, bf16[2,272,192]{2,1,0:T(8,128)(2,1)S(1)}, u32[]{:S(2)}, u32[]{:S(2)}) %collective-permute-start.19) | collective-permute-done | bytes 208928 | tf_op jit(solution)/shard_map/ppermute | solution.py:629
  65.9 0.2 collective-permute-start.23
  66.0 2.2 %collective-permute-start.24 = (bf16[256,384]{1,0:T(8,128)(2,1)S(1)}, bf16[256,384]{1,0:T(8,128)(2,1)S(1)}, u32[]{:S(2)}, u32[]{:S(2)}) collective-permute-start(bf16[256,384]{1,0:T(8,128)(2,1)S(1)} %collective-permute-done.9.pool2), channel_id=1, source_target_pairs={{0,4},{4,0},{8,12},{12,8},{1,5},{5,1},{9,13},{13,9},{2,6},{6,2},{1... | collective-permute-start | bytes 589832 | tf_op jit(solution)/shard_map/ppermute | solution.py:431
  68.3 2.0 %collective-permute-start.21 = (bf16[256,384]{1,0:T(8,128)(2,1)S(1)}, bf16[256,384]{1,0:T(8,128)(2,1)S(1)}, u32[]{:S(2)}, u32[]{:S(2)}) collective-permute-start(bf16[256,384]{1,0:T(8,128)(2,1)S(1)} %get-tuple-element.97), channel_id=1, source_target_pairs={{1,4},{3,6},{0,8},{2,10},{4,9},{6,11},{5,13},{7,15},{9,12},{11,14}... | collective-permute-start | bytes 589832 | tf_op jit(solution)/shard_map/ppermute | solution.py:629
  70.2 0.7 collective-permute-start.22
  70.9 3.1 %collective-permute-start.26 = (bf16[512,384]{1,0:T(8,128)(2,1)S(1)}, bf16[512,384]{1,0:T(8,128)(2,1)S(1)}, u32[]{:S(2)}, u32[]{:S(2)}) collective-permute-start(bf16[512,384]{1,0:T(8,128)(2,1)S(1)} %owner_slope.2.slope0), channel_id=1, source_target_pairs={{0,1},{1,0},{2,3},{3,2},{4,5},{5,4},{6,7},{7,6},{8,9},{9,8},{10,11... | collective-permute-start | bytes 1179656 | tf_op jit(solution)/shard_map/ppermute | solution.py:590
  73.9 0.8 pred_.1
  74.8 1.1 %collective-permute-done.24.pool3 = bf16[256,384]{1,0:T(8,128)(2,1)S(1)} collective-permute-done((bf16[256,384]{1,0:T(8,128)(2,1)S(1)}, bf16[256,384]{1,0:T(8,128)(2,1)S(1)}, u32[]{:S(2)}, u32[]{:S(2)}) %collective-permute-start.24) | collective-permute-done | bytes 196640 | tf_op jit(solution)/shard_map/ppermute | solution.py:431
  75.9 3.5 %dec_grad.1 = f32[5,192,384]{2,1,0:T(8,128)} custom-call(s32[4]{0:T(128)S(1)} %pad_add_fusion.place, bf16[2,2,272,192]{3,2,1,0:T(8,128)(2,1)S(1)} %pad_maximum_fusion.own, bf16[2,2,272,192]{3,2,1,0:T(8,128)(2,1)S(1)} %collective-permute-done.23.came, bf16[256,384]{1,0:T(8,128)(2,1)S(1)} %get-tuple-element.67.pool0, ...), custom_call_target="tpu_custom_call" | custom-call | tf_op jit(solution)/shard_map/dec_grad/pallas_call | solution.py:398
  79.4 0.2 collective-permute-done.21
  79.6 0.4 collective-permute-start.25
  80.1 2.1 %enc_grad.2.refs_0_ = f32[960,384]{1,0:T(8,128)S(1)} custom-call(s32[4]{0:T(128)S(1)} %pad_add_fusion.place, bf16[960,2048]{1,0:T(8,128)(2,1)S(1)} %stem_taps.1.taps, bf16[2,256,384]{2,1,0:T(8,128)(2,1)S(1)} %pad_maximum_fusion.1.slots, bf16[512,384]{1,0:T(8,128)(2,1)S(1)} %owner_slope.2.slope0, bf16[512,384]{1,0:T(8,128)(2,1)S(1)} %owner_slope.3.slope1), custom_call_target="tpu_custom_call" | custom-call | tf_op jit(solution)/shard_map/enc_grad/pallas_call | solution.py:675
  82.2 3.0 %enc_grad.3 = f32[960,384]{1,0:T(8,128)} custom-call(s32[4]{0:T(128)S(1)} %pad_add_fusion.place, bf16[960,2048]{1,0:T(8,128)(2,1)S(1)} %stem_taps.1.taps, bf16[2,256,384]{2,1,0:T(8,128)(2,1)S(1)} %collective-permute-done.25.slots, bf16[512,384]{1,0:T(8,128)(2,1)S(1)} %collective-permute-done.26.slope0, bf16[512,384]{1,0:T(8,128)(2,1)S(1)} %collective-permute-done.27.slope1, ...), custom_call_target="tpu_custom_call" | custom-call | tf_op jit(solution)/shard_map/enc_grad/pallas_call | solution.py:675
  (47 shorter events, 1.0 us)
Async XLA Ops:
  0.8 4.4 %copy-start = (bf16[768,5,384]{2,0,1:T(8,128)(2,1)S(1)}, bf16[768,5,384]{2,0,1:T(8,128)(2,1)}, u32[]{:S(2)}) copy-start(bf16[768,5,384]{2,0,1:T(8,128)(2,1)} %param.8) | copy-start | bytes 8847364
  1.7 1.8 %copy-start.1 = (bf16[1536,5,192]{0,2,1:T(8,128)(2,1)S(1)}, bf16[1536,5,192]{0,2,1:T(8,128)(2,1)}, u32[]{:S(2)}) copy-start(bf16[1536,5,192]{0,2,1:T(8,128)(2,1)} %param.7) | copy-start | bytes 8847364
  4.7 11.6 %collective-permute-start.2 = (bf16[992,768]{1,0:T(8,128)(2,1)S(1)}, bf16[992,768]{1,0:T(8,128)(2,1)S(1)}, u32[]{:S(2)}, u32[]{:S(2)}) collective-permute-start(bf16[992,768]{1,0:T(8,128)(2,1)S(1)} %get-tuple-element.51), channel_id=1, source_target_pairs={{0,1},{1,0},{2,3},{3,2},{4,5},{5,4},{6,7},{7,6},{8,9},{9,8},{10,11... | collective-permute-start | bytes 4571144 | tf_op jit(solution)/shard_map/ppermute | solution.py:460
  5.2 4.1 %copy-start.4 = (s32[512]{0:T(512)S(1)}, s32[512]{0:T(512)}, u32[]{:S(2)}) copy-start(s32[512]{0:T(512)} %param.5) | copy-start | bytes 6148
  5.2 11.1 %copy-start.2 = (bf16[1536,5,192]{0,2,1:T(8,128)(2,1)S(1)}, bf16[1536,5,192]{0,2,1:T(8,128)(2,1)}, u32[]{:S(2)}) copy-start(bf16[1536,5,192]{0,2,1:T(8,128)(2,1)} %param.7) | copy-start | bytes 8847364
  6.3 21.3 %collective-permute-start.3 = (bf16[5,2,192,384]{3,2,1,0:T(8,128)(2,1)S(1)}, bf16[5,2,192,384]{3,2,1,0:T(8,128)(2,1)S(1)}, u32[]{:S(2)}, u32[]{:S(2)}) collective-permute-start(bf16[5,2,192,384]{3,2,1,0:T(8,128)(2,1)S(1)} %dec_pick.1), channel_id=1, source_target_pairs={{0,1},{1,0},{2,3},{3,2},{4,5},{5,4},{6,7},{7,6},{8,9},{9,8},{10,11... | collective-permute-start | bytes 4423688 | tf_op jit(solution)/shard_map/ppermute | solution.py:474
  6.4 20.6 %collective-permute-start.12 = (bf16[608,384]{1,0:T(8,128)(2,1)S(1)}, bf16[608,384]{1,0:T(8,128)(2,1)S(1)}, u32[]{:S(2)}, u32[]{:S(2)}) collective-permute-start(bf16[608,384]{1,0:T(8,128)(2,1)S(1)} %get-tuple-element.71), channel_id=1, source_target_pairs={{0,2},{1,3},{2,0},{3,1},{4,6},{5,7},{6,4},{7,5},{8,10},{9,11},{10,... | collective-permute-start | bytes 1400840 | tf_op jit(solution)/shard_map/ppermute | solution.py:461
  9.3 4.1 %collective-permute-start = (s32[1,512]{1,0:T(1,128)S(1)}, s32[1,512]{1,0:T(1,128)S(1)}, u32[]{:S(2)}, u32[]{:S(2)}) collective-permute-start(s32[1,512]{1,0:T(1,128)S(1)} %bitcast.42), channel_id=1, source_target_pairs={{0,4},{4,0},{8,12},{12,8},{1,5},{5,1},{9,13},{13,9},{2,6},{6,2},{1... | collective-permute-start | bytes 6152 | tf_op jit(solution)/shard_map/ppermute | solution.py:431
  10.9 5.4 %collective-permute-start.1 = (s32[1,512]{1,0:T(1,128)S(1)}, s32[1,512]{1,0:T(1,128)S(1)}, u32[]{:S(2)}, u32[]{:S(2)}) collective-permute-start(s32[1,512]{1,0:T(1,128)S(1)} %bitcast.43), channel_id=1, source_target_pairs={{0,12},{4,8},{8,4},{12,0},{1,13},{5,9},{9,5},{13,1},{2,14},{6,10},... | collective-permute-start | bytes 6152 | tf_op jit(solution)/shard_map/ppermute | solution.py:441
  18.9 2.0 %copy-start.3 = (bf16[512,192]{0,1:T(8,128)(2,1)S(1)}, bf16[512,192]{0,1:T(8,128)(2,1)}, u32[]{:S(2)}) copy-start(bf16[512,192]{0,1:T(8,128)(2,1)} %param.9) | copy-start | bytes 589828
  20.3 11.7 %collective-permute-start.7 = (bf16[544,384]{1,0:T(8,128)(2,1)S(1)}, bf16[544,384]{1,0:T(8,128)(2,1)S(1)}, u32[]{:S(2)}, u32[]{:S(2)}) collective-permute-start(bf16[544,384]{1,0:T(8,128)(2,1)S(1)} %enc_conv.1), channel_id=1, source_target_pairs={{0,2},{1,3},{2,0},{3,1},{4,6},{5,7},{6,4},{7,5},{8,10},{9,11},{10,... | collective-permute-start | bytes 1253384 | tf_op jit(solution)/shard_map/ppermute | solution.py:499
  20.9 6.1 %collective-permute-start.4 = (bf16[192,128]{1,0:T(8,128)(2,1)S(1)}, bf16[192,128]{1,0:T(8,128)(2,1)S(1)}, u32[]{:S(2)}, u32[]{:S(2)}) collective-permute-start(bf16[192,128]{1,0:T(8,128)(2,1)S(1)} %get-tuple-element.103), channel_id=1, source_target_pairs={{0,4},{4,8},{8,12},{12,0},{1,5},{5,9},{9,13},{13,1},{2,6},{6,10},{... | collective-permute-start | bytes 147464 | tf_op jit(solution)/shard_map/ppermute | solution.py:428
  21.0 6.5 %collective-permute-start.5 = (bf16[192,128]{1,0:T(8,128)(2,1)S(1)}, bf16[192,128]{1,0:T(8,128)(2,1)S(1)}, u32[]{:S(2)}, u32[]{:S(2)}) collective-permute-start(bf16[192,128]{1,0:T(8,128)(2,1)S(1)} %get-tuple-element.102), channel_id=1, source_target_pairs={{0,12},{4,0},{8,4},{12,8},{1,13},{5,1},{9,5},{13,9},{2,14},{6,2},{... | collective-permute-start | bytes 147464 | tf_op jit(solution)/shard_map/ppermute | solution.py:428
  27.0 14.5 %collective-permute-start.11 = (bf16[992,384]{1,0:T(8,128)(2,1)S(1)}, bf16[992,384]{1,0:T(8,128)(2,1)S(1)}, u32[]{:S(2)}, u32[]{:S(2)}) collective-permute-start(bf16[992,384]{1,0:T(8,128)(2,1)S(1)} %get-tuple-element.70.refs_4_), channel_id=1, source_target_pairs={{0,1},{1,0},{2,3},{3,2},{4,5},{5,4},{6,7},{7,6},{8,9},{9,8},{10,11... | collective-permute-start | bytes 2285576 | tf_op jit(solution)/shard_map/ppermute | solution.py:573
  27.1 12.2 %collective-permute-start.14 = (bf16[608,384]{1,0:T(8,128)(2,1)S(1)}, bf16[608,384]{1,0:T(8,128)(2,1)S(1)}, u32[]{:S(2)}, u32[]{:S(2)}) collective-permute-start(bf16[608,384]{1,0:T(8,128)(2,1)S(1)} %collective-permute-done.12.refs_6_), channel_id=1, source_target_pairs={{0,1},{1,0},{2,3},{3,2},{4,5},{5,4},{6,7},{7,6},{8,9},{9,8},{10,11... | collective-permute-start | bytes 1400840 | tf_op jit(solution)/shard_map/ppermute | solution.py:574
  27.6 4.5 %collective-permute-start.6 = (s32[2,256]{1,0:T(2,128)S(1)}, s32[2,256]{1,0:T(2,128)S(1)}, u32[]{:S(2)}, u32[]{:S(2)}) collective-permute-start(s32[2,256]{1,0:T(2,128)S(1)} %get-tuple-element.106.refs_0_), channel_id=1, source_target_pairs={{0,8},{4,12},{8,0},{12,4},{1,9},{5,13},{9,1},{13,5},{2,10},{6,14},... | collective-permute-start | bytes 6152 | tf_op jit(solution)/shard_map/ppermute | solution.py:428
  27.6 9.1 %collective-permute-start.13 = (bf16[384,384]{1,0:T(8,128)(2,1)S(1)}, bf16[384,384]{1,0:T(8,128)(2,1)S(1)}, u32[]{:S(2)}, u32[]{:S(2)}) collective-permute-start(bf16[384,384]{1,0:T(8,128)(2,1)S(1)} %get-tuple-element.73), channel_id=1, source_target_pairs={{0,2},{1,3},{2,0},{3,1},{4,6},{5,7},{6,4},{7,5},{8,10},{9,11},{10,... | collective-permute-start | bytes 884744 | tf_op jit(solution)/shard_map/ppermute | solution.py:530
  33.0 1.5 %collective-permute-start.8 = (bf16[272,384]{1,0:T(8,128)(2,1)S(1)}, bf16[272,384]{1,0:T(8,128)(2,1)S(1)}, u32[]{:S(2)}, u32[]{:S(2)}) collective-permute-start(bf16[272,384]{1,0:T(8,128)(2,1)S(1)} %get-tuple-element.65.own), channel_id=1, source_target_pairs={{0,1},{1,0},{2,3},{3,2},{4,5},{5,4},{6,7},{7,6},{8,9},{9,8},{10,11... | collective-permute-start | bytes 626696 | tf_op jit(solution)/shard_map/ppermute | solution.py:552
  36.6 13.0 %collective-permute-start.16 = (bf16[272,768]{1,0:T(8,128)(2,1)S(1)}, bf16[272,768]{1,0:T(8,128)(2,1)S(1)}, u32[]{:S(2)}, u32[]{:S(2)}) collective-permute-start(bf16[272,768]{1,0:T(8,128)(2,1)S(1)} %get-tuple-element.77), channel_id=1, source_target_pairs={{0,2},{1,3},{2,0},{3,1},{4,6},{5,7},{6,4},{7,5},{8,10},{9,11},{10,... | collective-permute-start | bytes 1253384 | tf_op jit(solution)/shard_map/ppermute | solution.py:568
  38.1 3.3 %collective-permute-start.15 = (bf16[384,384]{1,0:T(8,128)(2,1)S(1)}, bf16[384,384]{1,0:T(8,128)(2,1)S(1)}, u32[]{:S(2)}, u32[]{:S(2)}) collective-permute-start(bf16[384,384]{1,0:T(8,128)(2,1)S(1)} %collective-permute-done.13.refs_7_), channel_id=1, source_target_pairs={{0,1},{1,0},{2,3},{3,2},{4,5},{5,4},{6,7},{7,6},{8,9},{9,8},{10,11... | collective-permute-start | bytes 884744 | tf_op jit(solution)/shard_map/ppermute | solution.py:574
  38.1 11.5 %collective-permute-start.10 = (bf16[256,384]{1,0:T(8,128)(2,1)S(1)}, bf16[256,384]{1,0:T(8,128)(2,1)S(1)}, u32[]{:S(2)}, u32[]{:S(2)}) collective-permute-start(bf16[256,384]{1,0:T(8,128)(2,1)S(1)} %get-tuple-element.67.pool0), channel_id=1, source_target_pairs={{0,4},{4,0},{8,12},{12,8},{1,5},{5,1},{9,13},{13,9},{2,6},{6,2},{1... | collective-permute-start | bytes 589832 | tf_op jit(solution)/shard_map/ppermute | solution.py:431
  39.3 10.4 %collective-permute-start.9 = (bf16[256,384]{1,0:T(8,128)(2,1)S(1)}, bf16[256,384]{1,0:T(8,128)(2,1)S(1)}, u32[]{:S(2)}, u32[]{:S(2)}) collective-permute-start(bf16[256,384]{1,0:T(8,128)(2,1)S(1)} %get-tuple-element.67.pool0), channel_id=1, source_target_pairs={{0,8},{4,12},{8,0},{12,4},{1,9},{5,13},{9,1},{13,5},{2,10},{6,14},... | collective-permute-start | bytes 589832 | tf_op jit(solution)/shard_map/ppermute | solution.py:431
  50.8 3.2 %collective-permute-start.17 = (bf16[2,2,272,192]{3,2,1,0:T(8,128)(2,1)S(1)}, bf16[2,2,272,192]{3,2,1,0:T(8,128)(2,1)S(1)}, u32[]{:S(2)}, u32[]{:S(2)}) collective-permute-start(bf16[2,2,272,192]{3,2,1,0:T(8,128)(2,1)S(1)} %get-tuple-element.81.own), channel_id=1, source_target_pairs={{0,1},{1,0},{2,3},{3,2},{4,5},{5,4},{6,7},{7,6},{8,9},{9,8},{10,11... | collective-permute-start | bytes 1253384 | tf_op jit(solution)/shard_map/ppermute | solution.py:609
  50.8 14.8 %collective-permute-start.19 = (bf16[2,272,192]{2,1,0:T(8,128)(2,1)S(1)}, bf16[2,272,192]{2,1,0:T(8,128)(2,1)S(1)}, u32[]{:S(2)}, u32[]{:S(2)}) collective-permute-start(bf16[2,272,192]{2,1,0:T(8,128)(2,1)S(1)} %get-tuple-element.82), channel_id=1, source_target_pairs={{1,4},{3,6},{0,8},{2,10},{4,9},{6,11},{5,13},{7,15},{9,12},{11,14}... | collective-permute-start | bytes 626696 | tf_op jit(solution)/shard_map/ppermute | solution.py:629
  53.1 12.5 %collective-permute-start.20 = (bf16[2,272,192]{2,1,0:T(8,128)(2,1)S(1)}, bf16[2,272,192]{2,1,0:T(8,128)(2,1)S(1)}, u32[]{:S(2)}, u32[]{:S(2)}) collective-permute-start(bf16[2,272,192]{2,1,0:T(8,128)(2,1)S(1)} %get-tuple-element.83), channel_id=1, source_target_pairs={{1,12},{3,14},{4,1},{6,3},{9,4},{11,6},{12,9},{14,11},{17,28},{19,... | collective-permute-start | bytes 626696 | tf_op jit(solution)/shard_map/ppermute | solution.py:630
  56.0 9.7 %collective-permute-start.18 = (bf16[256,384]{1,0:T(8,128)(2,1)S(1)}, bf16[256,384]{1,0:T(8,128)(2,1)S(1)}, u32[]{:S(2)}, u32[]{:S(2)}) collective-permute-start(bf16[256,384]{1,0:T(8,128)(2,1)S(1)} %up_grad.1), channel_id=1, source_target_pairs={{0,2},{1,3},{2,0},{3,1},{4,6},{5,7},{6,4},{7,5},{8,10},{9,11},{10,... | collective-permute-start | bytes 589832 | tf_op jit(solution)/shard_map/ppermute | solution.py:637
  65.9 10.0 %collective-permute-start.23 = (bf16[2,2,272,192]{3,2,1,0:T(8,128)(2,1)S(1)}, bf16[2,2,272,192]{3,2,1,0:T(8,128)(2,1)S(1)}, u32[]{:S(2)}, u32[]{:S(2)}) collective-permute-start(bf16[2,2,272,192]{3,2,1,0:T(8,128)(2,1)S(1)} %pad_maximum_fusion.own), channel_id=1, source_target_pairs={{0,1},{1,0},{2,3},{3,2},{4,5},{5,4},{6,7},{7,6},{8,9},{9,8},{10,11... | collective-permute-start | bytes 1253384 | tf_op jit(solution)/shard_map/ppermute | solution.py:646
  66.0 9.8 %collective-permute-start.24 = (bf16[256,384]{1,0:T(8,128)(2,1)S(1)}, bf16[256,384]{1,0:T(8,128)(2,1)S(1)}, u32[]{:S(2)}, u32[]{:S(2)}) collective-permute-start(bf16[256,384]{1,0:T(8,128)(2,1)S(1)} %collective-permute-done.9.pool2), channel_id=1, source_target_pairs={{0,4},{4,0},{8,12},{12,8},{1,5},{5,1},{9,13},{13,9},{2,6},{6,2},{1... | collective-permute-start | bytes 589832 | tf_op jit(solution)/shard_map/ppermute | solution.py:431
  68.3 11.3 %collective-permute-start.21 = (bf16[256,384]{1,0:T(8,128)(2,1)S(1)}, bf16[256,384]{1,0:T(8,128)(2,1)S(1)}, u32[]{:S(2)}, u32[]{:S(2)}) collective-permute-start(bf16[256,384]{1,0:T(8,128)(2,1)S(1)} %get-tuple-element.97), channel_id=1, source_target_pairs={{1,4},{3,6},{0,8},{2,10},{4,9},{6,11},{5,13},{7,15},{9,12},{11,14}... | collective-permute-start | bytes 589832 | tf_op jit(solution)/shard_map/ppermute | solution.py:629
  70.2 9.3 %collective-permute-start.22 = (bf16[256,384]{1,0:T(8,128)(2,1)S(1)}, bf16[256,384]{1,0:T(8,128)(2,1)S(1)}, u32[]{:S(2)}, u32[]{:S(2)}) collective-permute-start(bf16[256,384]{1,0:T(8,128)(2,1)S(1)} %get-tuple-element.96), channel_id=1, source_target_pairs={{1,12},{3,14},{4,1},{6,3},{9,4},{11,6},{12,9},{14,11},{17,28},{19,... | collective-permute-start | bytes 589832 | tf_op jit(solution)/shard_map/ppermute | solution.py:630
  70.9 11.3 %collective-permute-start.26 = (bf16[512,384]{1,0:T(8,128)(2,1)S(1)}, bf16[512,384]{1,0:T(8,128)(2,1)S(1)}, u32[]{:S(2)}, u32[]{:S(2)}) collective-permute-start(bf16[512,384]{1,0:T(8,128)(2,1)S(1)} %owner_slope.2.slope0), channel_id=1, source_target_pairs={{0,1},{1,0},{2,3},{3,2},{4,5},{5,4},{6,7},{7,6},{8,9},{9,8},{10,11... | collective-permute-start | bytes 1179656 | tf_op jit(solution)/shard_map/ppermute | solution.py:590
  75.9 6.3 %collective-permute-start.27 = (bf16[512,384]{1,0:T(8,128)(2,1)S(1)}, bf16[512,384]{1,0:T(8,128)(2,1)S(1)}, u32[]{:S(2)}, u32[]{:S(2)}) collective-permute-start(bf16[512,384]{1,0:T(8,128)(2,1)S(1)} %owner_slope.3.slope1), channel_id=1, source_target_pairs={{0,1},{1,0},{2,3},{3,2},{4,5},{5,4},{6,7},{7,6},{8,9},{9,8},{10,11... | collective-permute-start | bytes 1179656 | tf_op jit(solution)/shard_map/ppermute | solution.py:590
  79.6 2.6 %collective-permute-start.25 = (bf16[2,256,384]{2,1,0:T(8,128)(2,1)S(1)}, bf16[2,256,384]{2,1,0:T(8,128)(2,1)S(1)}, u32[]{:S(2)}, u32[]{:S(2)}) collective-permute-start(bf16[2,256,384]{2,1,0:T(8,128)(2,1)S(1)} %pad_maximum_fusion.1.slots), channel_id=1, source_target_pairs={{0,1},{1,0},{2,3},{3,2},{4,5},{5,4},{6,7},{7,6},{8,9},{9,8},{10,11... | collective-permute-start | bytes 1179656 | tf_op jit(solution)/shard_map/ppermute | solution.py:671

commit v7 on v6

--- a/solution.py
+++ b/solution.py
@@ -186,10 +186,11 @@
     held[rows:] = jnp.zeros((8, half), F32)
     both = slopes[0] + slopes[1], slopes[1] + held[1 : 1 + rows]
     for i in range(2):
-        for h in range(2):
-            sums[h, i] = both[i][:, h * quarter : (h + 1) * quarter].astype(BF16)
+        sums[i] = both[i].astype(BF16)
     for out, step in ((local, 0), (near, 2 - place[3]), (far, 3)):
-        out[...] = sums[lax.rem(place[0] + step, 4) // 2]
+        low = lax.rem(place[0] + step, 4) < 2
+        for i in range(2):
+            out[i] = jnp.where(low, both[i][:, :quarter], both[i][:, quarter:]).astype(BF16)
 
 
 def lane_tiles(channels):
@@ -236,12 +237,17 @@
 
 
 def back_kernel(place, own, oth, weight, out, held, *, pairs):
+    core = place[2]
+    sides = []
+    for source in (own, oth):
+        held[...] = source[...].astype(F32)
+        sides.append(shifted_sums(held, pairs))
     acc = jnp.zeros(out.shape, F32)
-    for source, core in ((own, place[2]), (oth, 1 - place[2])):
-        for h in range(2):
-            held[...] = source[h].astype(F32)
-            for k, tap in enumerate(shifted_sums(held, pairs)):
-                acc = acc + dot(tap, weight[k, 2 * h + core], ((1,), (0,)))
+    for k in range(KW):
+        kernel = [weight[k, 2 * h + c] for c in (core, 1 - core) for h in range(2)]
+        acc = acc + dot(
+            jnp.concatenate([sides[0][k], sides[1][k]], axis=1), jnp.concatenate(kernel, axis=0), ((1,), (0,))
+        )
     out[...] = (0.5 * acc).astype(BF16)
 
 
@@ -601,7 +607,7 @@
     pred, sums, local, near, far = call(
         functools.partial(slope_kernel, pairs=pairs, total=total, scale=1.0 / math.sqrt(2 * total)),
         [gated(place, (beyond, beside, slope0, taps)), part, came, targets_at],
-        [((2, pairs, stem_c), BF16), ((2, 2, rows, stem_c), BF16)] + [((2, rows, stem_c), BF16)] * 3,
+        [((2, pairs, stem_c), BF16), ((2, rows, 2 * stem_c), BF16)] + [((2, rows, stem_c), BF16)] * 3,
         [((rows + 8, 2 * stem_c), F32)],
         limit=7,
         name="out_slope",
@@ -611,7 +617,7 @@
         functools.partial(back_kernel, pairs=pairs),
         [place, sums, sums_oth, dec_w],
         [((pairs, enc_c), BF16)],
-        [((2, rows, stem_c), F32)],
+        [((2, rows, 2 * stem_c), F32)],
         limit=11,
         name="up_grad",
     )
@@ -671,10 +677,11 @@
     pre_came = lax.ppermute(pre_mine, "chan", cores)
 
     def enc_grad(first, *arrays):
-        half = (KW * stem_c // 2, enc_c)
+        count = 1 if first else 2
+        half = (KW * stem_c // count, enc_c)
         return pl.pallas_call(
             functools.partial(enc_grad_kernel, first=first),
-            grid=(2,),
+            grid=(count,),
             in_specs=[SCALARS, pl.BlockSpec((half[0], 2 * pairs * devices), lambda k: (k, 0))]
             + [whole(p.shape) for p in arrays[:3]]
             + [pl.BlockSpec(half, lambda k: (k, 0))] * len(arrays[3:]),

time: 85.5 us -> 85.2 us (level)
  no operation moved by 1% of the time
where the time goes in v7:
time: 85.2 us; the launch traced here: 84.9 us
  Pallas kernels  38.8 us (46%)
  starting transfers between devices  31.3 us (37%)
  waiting for transfers between devices  10.4 us (12%)
  local copies, waits for them, and re-layouts  2.74 us (3%)
  between operations  1.05 us (1%)
    pallas_call x13, Pallas kernels, call(): pl.pallas_call(kernel, grid=(1,) if last else (), in_specs=specs, out_spe...  30.1 us
    ppermute x4, starting transfers between devices, swap(): lax.ppermute(array, 'seq', [(i, i ^ distance) for i in range(devices)])  7.21 us
    pallas_call x2, Pallas kernels, enc_grad(): pl.pallas_call(functools.partial(enc_grad_kernel, first=first), grid=(cou...  4.81 us
    ppermute x2, starting transfers between devices, to_owner(): near = lax.ppermute(near, ('seq', 'chan'), link((1, 2)))  4.16 us
    ppermute x2, waiting for transfers between devices, to_owner(): near = lax.ppermute(near, ('seq', 'chan'), link((1, 2)))  4.04 us
    ppermute x3, starting transfers between devices, ring(): lax.ppermute(array, 'seq', [(i, (i + step) % devices) for i in range(devi...  3.87 us
    ppermute x2, starting transfers between devices, owner_slope(): return (out, lax.ppermute(out, 'chan', cores))  3.06 us
    ppermute x1, starting transfers between devices, shards(): mine0_far = lax.ppermute(mine0, 'chan', across)  2.94 us
  transfers between devices with their start and end apart: 28, of which 8 were waited for; matrix products, arithmetic and copies ran while one was open for 1% of the time, Pallas kernels for 40%

profile of v7, /device:TPU:0, one launch (start us, length us, event | category | flops | bytes accessed | tf_op | source)
XLA Modules:
  0.0 84.9 jit_solution(9076580203278567382)
XLA Ops:
  0.9 0.9 %reshape.25.stem_own.refs_4_ = bf16[20,192]{1,0:T(8,128)(2,1)S(1)} reshape(bf16[5,4,192]{2,1,0:T(4,128)(2,1)} %bitcast.48) | data formatting | bytes 15360 | tf_op jit(solution)/shard_map/reshape | solution.py:443
  1.8 1.8 %copy-done.1 = bf16[1536,5,192]{0,2,1:T(8,128)(2,1)S(1)} copy-done((bf16[1536,5,192]{0,2,1:T(8,128)(2,1)S(1)}, bf16[1536,5,192]{0,2,1:T(8,128)(2,1)}, u32[]{:S(2)}) %copy-start.1) | copy-done | bytes 2949144
  3.6 1.1 %picks.1 = (bf16[992,384]{1,0:T(8,128)(2,1)S(1)}, bf16[608,384]{1,0:T(8,128)(2,1)S(1)}, bf16[384,384]{1,0:T(8,128)(2,1)S(1)}, bf16[992,768]{1,0:T(8,128)(2,1)S(1)}) custom-call(s32[4]{0:T(128)S(1)} %pad_add_fusion.place, bf16[32,192]{1,0:T(8,128)(2,1)S(1)} %concatenate.9.stem, bf16[5,192,1536]{2,1,0:T(8,128)(2,1)S(1)} %bitcast.35), custom_call_target="tpu_custom_call" | custom-call | tf_op jit(solution)/shard_map/picks/pallas_call | solution.py:452
  4.7 0.5 collective-permute-start.2
  5.2 1.1 %dec_pick.1 = bf16[5,2,192,384]{3,2,1,0:T(8,128)(2,1)S(1)} custom-call(s32[4]{0:T(128)S(1)} %pad_add_fusion.place, bf16[5,4,192,384]{3,2,1,0:T(8,128)(2,1)S(1)} %bitcast.32), custom_call_target="tpu_custom_call" | custom-call | tf_op jit(solution)/shard_map/dec_pick/pallas_call | solution.py:468
  6.3 0.1 collective-permute-start.3
  6.4 2.9 %collective-permute-start.12 = (bf16[608,384]{1,0:T(8,128)(2,1)S(1)}, bf16[608,384]{1,0:T(8,128)(2,1)S(1)}, u32[]{:S(2)}, u32[]{:S(2)}) collective-permute-start(bf16[608,384]{1,0:T(8,128)(2,1)S(1)} %get-tuple-element.71), channel_id=1, source_target_pairs={{0,2},{1,3},{2,0},{3,1},{4,6},{5,7},{6,4},{7,5},{8,10},{9,11},{10,... | collective-permute-start | bytes 1400840 | tf_op jit(solution)/shard_map/ppermute | solution.py:467
  9.3 1.6 %collective-permute-start = (s32[1,512]{1,0:T(1,128)S(1)}, s32[1,512]{1,0:T(1,128)S(1)}, u32[]{:S(2)}, u32[]{:S(2)}) collective-permute-start(s32[1,512]{1,0:T(1,128)S(1)} %bitcast.42), channel_id=1, source_target_pairs={{0,4},{4,0},{8,12},{12,8},{1,5},{5,1},{9,13},{13,9},{2,6},{6,2},{1... | collective-permute-start | bytes 6152 | tf_op jit(solution)/shard_map/ppermute | solution.py:437
  10.9 2.5 %collective-permute-start.1 = (s32[1,512]{1,0:T(1,128)S(1)}, s32[1,512]{1,0:T(1,128)S(1)}, u32[]{:S(2)}, u32[]{:S(2)}) collective-permute-start(s32[1,512]{1,0:T(1,128)S(1)} %bitcast.43), channel_id=1, source_target_pairs={{0,12},{4,8},{8,4},{12,0},{1,13},{5,9},{9,5},{13,1},{2,14},{6,10},... | collective-permute-start | bytes 6152 | tf_op jit(solution)/shard_map/ppermute | solution.py:447
  13.4 2.9 %collective-permute-done.1.before = s32[1,512]{1,0:T(1,128)S(1)} collective-permute-done((s32[1,512]{1,0:T(1,128)S(1)}, s32[1,512]{1,0:T(1,128)S(1)}, u32[]{:S(2)}, u32[]{:S(2)}) %collective-permute-start.1) | collective-permute-done | bytes 2080 | tf_op jit(solution)/shard_map/ppermute | solution.py:447
  16.3 2.6 %stem_conv.1 = (f32[544,384]{1,0:T(8,128)S(1)}, bf16[2,272,192]{2,1,0:T(8,128)(2,1)S(1)}, bf16[6,272,192]{2,1,0:T(8,128)(2,1)S(1)}, bf16[6,272,192]{2,1,0:T(8,128)(2,1)S(1)}, s32[3,2,256]{2,1,0:T(2,128)S(1)}) custom-call(s32[4]{0:T(128)S(1)} %pad_add_fusion.place, s32[1,512]{1,0:T(1,128)S(1)} %bitcast.44, s32[1,512]{1,0:T(1,128)S(1)} %collective-permute-done.after, ...), custom_call_target="tpu_custom_call" | custom-call | tf_op jit(solution)/shard_map/stem_conv/pallas_call | solution.py:404
  18.9 1.4 %enc_conv.1 = bf16[544,384]{1,0:T(8,128)(2,1)S(1)} custom-call(s32[4]{0:T(128)S(1)} %pad_add_fusion.place, f32[544,384]{1,0:T(8,128)S(1)} %get-tuple-element.52.acc, bf16[6,272,192]{2,1,0:T(8,128)(2,1)S(1)} %get-tuple-element.53.lhs.lhs_oth, bf16[992,768]{1,0:T(8,128)(2,1)S(1)} %collective-permute-done.2.w_oth), custom_call_target="tpu_custom_call" | custom-call | tf_op jit(solution)/shard_map/enc_conv/pallas_call | solution.py:404
  20.3 0.6 collective-permute-start.7
  21.0 3.8 %collective-permute-start.5 = (bf16[192,128]{1,0:T(8,128)(2,1)S(1)}, bf16[192,128]{1,0:T(8,128)(2,1)S(1)}, u32[]{:S(2)}, u32[]{:S(2)}) collective-permute-start(bf16[192,128]{1,0:T(8,128)(2,1)S(1)} %get-tuple-element.102), channel_id=1, source_target_pairs={{0,12},{4,0},{8,4},{12,8},{1,13},{5,1},{9,5},{13,9},{2,14},{6,2},{... | collective-permute-start | bytes 147464 | tf_op jit(solution)/shard_map/ppermute | solution.py:434
  24.8 2.1 %enc_keep.1.keep = f32[544,384]{1,0:T(8,128)S(1)} custom-call(s32[4]{0:T(128)S(1)} %pad_add_fusion.place, bf16[6,272,192]{2,1,0:T(8,128)(2,1)S(1)} %get-tuple-element.63.lhs, bf16[6,272,192]{2,1,0:T(8,128)(2,1)S(1)} %get-tuple-element.53.lhs.lhs_oth, bf16[5,192,1536]{2,1,0:T(8,128)(2,1)S(1)} %bitcast.37, bf16[992,768]{1,0:T(8,128)(2,1)S(1)} %collective-permute-done.2.w_oth), custom_call_target="tpu_custom_call" | custom-call | tf_op jit(solution)/shard_map/enc_keep/pallas_call | solution.py:404
  27.1 0.5 collective-permute-start.14
  27.6 1.6 %collective-permute-start.13 = (bf16[384,384]{1,0:T(8,128)(2,1)S(1)}, bf16[384,384]{1,0:T(8,128)(2,1)S(1)}, u32[]{:S(2)}, u32[]{:S(2)}) collective-permute-start(bf16[384,384]{1,0:T(8,128)(2,1)S(1)} %get-tuple-element.73), channel_id=1, source_target_pairs={{0,2},{1,3},{2,0},{3,1},{4,6},{5,7},{6,4},{7,5},{8,10},{9,11},{10,... | collective-permute-start | bytes 884744 | tf_op jit(solution)/shard_map/ppermute | solution.py:536
  29.1 0.2 pad_select_fusion.stem
  29.3 1.7 %dec_taps.1 = (bf16[3,2,2,192,384]{4,3,2,1,0:T(8,128)(2,1)S(1)}, bf16[3,2,2,192,384]{4,3,2,1,0:T(8,128)(2,1)S(1)}) custom-call(s32[4]{0:T(128)S(1)} %pad_add_fusion.place, bf16[5,4,192,384]{3,2,1,0:T(8,128)(2,1)S(1)} %bitcast.33, bf16[5,2,192,384]{3,2,1,0:T(8,128)(2,1)S(1)} %collective-permute-done.3.came), custom_call_target="tpu_custom_call" | custom-call | tf_op jit(solution)/shard_map/dec_taps/pallas_call | solution.py:518
  31.0 0.9 %targets.1 = bf16[2,272,384]{2,1,0:T(8,128)(2,1)S(1)} custom-call(s32[4]{0:T(128)S(1)} %pad_add_fusion.place, bf16[192,512]{1,0:T(8,128)(2,1)S(1)} %bitcast.41, bf16[192,128]{1,0:T(8,128)(2,1)S(1)} %collective-permute-done.4.before, bf16[192,128]{1,0:T(8,128)(2,1)S(1)} %collective-permute-done.5.after), custom_call_target="tpu_custom_call" | custom-call | tf_op jit(solution)/shard_map/targets/pallas_call | solution.py:404
  32.0 1.0 %gelu_pool.1 = (bf16[272,384]{1,0:T(8,128)(2,1)S(1)}, bf16[256,384]{1,0:T(8,128)(2,1)S(1)}) custom-call(s32[4]{0:T(128)S(1)} %pad_add_fusion.place, f32[544,384]{1,0:T(8,128)S(1)} %enc_keep.1.keep, bf16[544,384]{1,0:T(8,128)(2,1)S(1)} %collective-permute-done.7.came), custom_call_target="tpu_custom_call" | custom-call | tf_op jit(solution)/shard_map/gelu_pool/pallas_call | solution.py:404
  33.1 1.4 %collective-permute-done.8.oth = bf16[272,384]{1,0:T(8,128)(2,1)S(1)} collective-permute-done((bf16[272,384]{1,0:T(8,128)(2,1)S(1)}, bf16[272,384]{1,0:T(8,128)(2,1)S(1)}, u32[]{:S(2)}, u32[]{:S(2)}) %collective-permute-start.8) | collective-permute-done | bytes 208928 | tf_op jit(solution)/shard_map/ppermute | solution.py:558
  34.5 1.5 %dec_conv.1 = (f32[272,768]{1,0:T(8,128)S(1)}, bf16[272,768]{1,0:T(8,128)(2,1)S(1)}) custom-call(bf16[272,384]{1,0:T(8,128)(2,1)S(1)} %get-tuple-element.65.own, bf16[272,384]{1,0:T(8,128)(2,1)S(1)} %collective-permute-done.8.oth, bf16[3,768,384]{2,1,0:T(8,128)(2,1)S(1)} %bitcast.38, bf16[3,768,384]{2,1,0:T(8,128)(2,1)S(1)} %bitcast.39, ...), custom_call_target="tpu_custom_call" | custom-call | tf_op jit(solution)/shard_map/dec_conv/pallas_call | solution.py:404
  36.1 0.6 collective-permute-done.13.refs_7_
  36.6 1.5 %collective-permute-start.16 = (bf16[272,768]{1,0:T(8,128)(2,1)S(1)}, bf16[272,768]{1,0:T(8,128)(2,1)S(1)}, u32[]{:S(2)}, u32[]{:S(2)}) collective-permute-start(bf16[272,768]{1,0:T(8,128)(2,1)S(1)} %get-tuple-element.77), channel_id=1, source_target_pairs={{0,2},{1,3},{2,0},{3,1},{4,6},{5,7},{6,4},{7,5},{8,10},{9,11},{10,... | collective-permute-start | bytes 1253384 | tf_op jit(solution)/shard_map/ppermute | solution.py:574
  38.1 1.2 %collective-permute-start.10 = (bf16[256,384]{1,0:T(8,128)(2,1)S(1)}, bf16[256,384]{1,0:T(8,128)(2,1)S(1)}, u32[]{:S(2)}, u32[]{:S(2)}) collective-permute-start(bf16[256,384]{1,0:T(8,128)(2,1)S(1)} %get-tuple-element.67.pool0), channel_id=1, source_target_pairs={{0,4},{4,0},{8,12},{12,8},{1,5},{5,1},{9,13},{13,9},{2,6},{6,2},{1... | collective-permute-start | bytes 589832 | tf_op jit(solution)/shard_map/ppermute | solution.py:437
  39.3 2.1 %collective-permute-start.9 = (bf16[256,384]{1,0:T(8,128)(2,1)S(1)}, bf16[256,384]{1,0:T(8,128)(2,1)S(1)}, u32[]{:S(2)}, u32[]{:S(2)}) collective-permute-start(bf16[256,384]{1,0:T(8,128)(2,1)S(1)} %get-tuple-element.67.pool0), channel_id=1, source_target_pairs={{0,8},{4,12},{8,0},{12,4},{1,9},{5,13},{9,1},{13,5},{2,10},{6,14},... | collective-permute-start | bytes 589832 | tf_op jit(solution)/shard_map/ppermute | solution.py:437
  41.5 5.4 %owner_slope.2.slope0 = bf16[512,384]{1,0:T(8,128)(2,1)S(1)} custom-call(s32[4]{0:T(128)S(1)} %pad_add_fusion.place, s32[2,256]{1,0:T(2,128)S(1)} %get-tuple-element.106.refs_0_, s32[2,256]{1,0:T(2,128)S(1)} %get-tuple-element.105.refs_1_, s32[2,256]{1,0:T(2,128)S(1)} %collective-permute-done.6.refs_2_, s32[2,256]{1,0:T(2,128)S(1)} %get-tuple-element.104.refs_3_, ...), custom_call_target="tpu_custom_call" | custom-call | tf_op jit(solution)/shard_map/owner_slope/pallas_call | solution.py:404
  46.8 2.6 %stem_taps.1.taps = bf16[960,2048]{1,0:T(8,128)(2,1)S(1)} custom-call(s32[4]{0:T(128)S(1)} %pad_add_fusion.place, s32[2,256]{1,0:T(2,128)S(1)} %get-tuple-element.106.refs_0_, s32[2,256]{1,0:T(2,128)S(1)} %get-tuple-element.105.refs_1_, s32[2,256]{1,0:T(2,128)S(1)} %collective-permute-done.6.refs_2_, s32[2,256]{1,0:T(2,128)S(1)} %get-tuple-element.104.refs_3_, ...), custom_call_target="tpu_custom_call" | custom-call | tf_op jit(solution)/shard_map/stem_taps/pallas_call | solution.py:404
  49.4 0.2 collective-permute-done.10.pool1
  49.7 1.1 %out_slope.1 = (bf16[2,256,192]{2,1,0:T(8,128)(2,1)S(1)}, bf16[2,272,384]{2,1,0:T(8,128)(2,1)S(1)}, bf16[2,272,192]{2,1,0:T(8,128)(2,1)S(1)}, bf16[2,272,192]{2,1,0:T(8,128)(2,1)S(1)}, bf16[2,272,192]{2,1,0:T(8,128)(2,1)S(1)}) custom-call(s32[4]{0:T(128)S(1)} %pad_add_fusion.place, f32[272,768]{1,0:T(8,128)S(1)} %get-tuple-element.76.part, ...), custom_call_target="tpu_custom_call" | custom-call | tf_op jit(solution)/shard_map/out_slope/pallas_call | solution.py:404
  50.9 2.2 %collective-permute-start.19 = (bf16[2,272,192]{2,1,0:T(8,128)(2,1)S(1)}, bf16[2,272,192]{2,1,0:T(8,128)(2,1)S(1)}, u32[]{:S(2)}, u32[]{:S(2)}) collective-permute-start(bf16[2,272,192]{2,1,0:T(8,128)(2,1)S(1)} %get-tuple-element.82), channel_id=1, source_target_pairs={{1,4},{3,6},{0,8},{2,10},{4,9},{6,11},{5,13},{7,15},{9,12},{11,14}... | collective-permute-start | bytes 626696 | tf_op jit(solution)/shard_map/ppermute | solution.py:635
  53.1 0.9 %collective-permute-start.20 = (bf16[2,272,192]{2,1,0:T(8,128)(2,1)S(1)}, bf16[2,272,192]{2,1,0:T(8,128)(2,1)S(1)}, u32[]{:S(2)}, u32[]{:S(2)}) collective-permute-start(bf16[2,272,192]{2,1,0:T(8,128)(2,1)S(1)} %get-tuple-element.83), channel_id=1, source_target_pairs={{1,12},{3,14},{4,1},{6,3},{9,4},{11,6},{12,9},{14,11},{17,28},{19,... | collective-permute-start | bytes 626696 | tf_op jit(solution)/shard_map/ppermute | solution.py:636
  54.0 1.8 %up_grad.1 = bf16[256,384]{1,0:T(8,128)(2,1)S(1)} custom-call(s32[4]{0:T(128)S(1)} %pad_add_fusion.place, bf16[2,272,384]{2,1,0:T(8,128)(2,1)S(1)} %get-tuple-element.81.own, bf16[2,272,384]{2,1,0:T(8,128)(2,1)S(1)} %collective-permute-done.17.oth, bf16[5,4,192,384]{3,2,1,0:T(8,128)(2,1)S(1)} %bitcast.34), custom_call_target="tpu_custom_call" | custom-call | tf_op jit(solution)/shard_map/up_grad/pallas_call | solution.py:404
  55.7 0.6 collective-permute-start.18
  56.3 5.4 %owner_slope.3.slope1 = bf16[512,384]{1,0:T(8,128)(2,1)S(1)} custom-call(s32[4]{0:T(128)S(1)} %pad_add_fusion.place, s32[2,256]{1,0:T(2,128)S(1)} %get-tuple-element.106.refs_0_, s32[2,256]{1,0:T(2,128)S(1)} %get-tuple-element.105.refs_1_, s32[2,256]{1,0:T(2,128)S(1)} %collective-permute-done.6.refs_2_, s32[2,256]{1,0:T(2,128)S(1)} %get-tuple-element.104.refs_3_, ...), custom_call_target="tpu_custom_call" | custom-call | tf_op jit(solution)/shard_map/owner_slope/pallas_call | solution.py:404
  61.7 3.9 %collective-permute-done.19 = bf16[2,272,192]{2,1,0:T(8,128)(2,1)S(1)} collective-permute-done((bf16[2,272,192]{2,1,0:T(8,128)(2,1)S(1)}, bf16[2,272,192]{2,1,0:T(8,128)(2,1)S(1)}, u32[]{:S(2)}, u32[]{:S(2)}) %collective-permute-start.19) | collective-permute-done | bytes 208928 | tf_op jit(solution)/shard_map/ppermute | solution.py:635
  66.0 2.3 %collective-permute-start.24 = (bf16[256,384]{1,0:T(8,128)(2,1)S(1)}, bf16[256,384]{1,0:T(8,128)(2,1)S(1)}, u32[]{:S(2)}, u32[]{:S(2)}) collective-permute-start(bf16[256,384]{1,0:T(8,128)(2,1)S(1)} %collective-permute-done.9.pool2), channel_id=1, source_target_pairs={{0,4},{4,0},{8,12},{12,8},{1,5},{5,1},{9,13},{13,9},{2,6},{6,2},{1... | collective-permute-start | bytes 589832 | tf_op jit(solution)/shard_map/ppermute | solution.py:437
  68.3 2.0 %collective-permute-start.21 = (bf16[256,384]{1,0:T(8,128)(2,1)S(1)}, bf16[256,384]{1,0:T(8,128)(2,1)S(1)}, u32[]{:S(2)}, u32[]{:S(2)}) collective-permute-start(bf16[256,384]{1,0:T(8,128)(2,1)S(1)} %get-tuple-element.97), channel_id=1, source_target_pairs={{1,4},{3,6},{0,8},{2,10},{4,9},{6,11},{5,13},{7,15},{9,12},{11,14}... | collective-permute-start | bytes 589832 | tf_op jit(solution)/shard_map/ppermute | solution.py:635
  70.2 0.7 collective-permute-start.22
  70.9 3.1 %collective-permute-start.26 = (bf16[512,384]{1,0:T(8,128)(2,1)S(1)}, bf16[512,384]{1,0:T(8,128)(2,1)S(1)}, u32[]{:S(2)}, u32[]{:S(2)}) collective-permute-start(bf16[512,384]{1,0:T(8,128)(2,1)S(1)} %owner_slope.2.slope0), channel_id=1, source_target_pairs={{0,1},{1,0},{2,3},{3,2},{4,5},{5,4},{6,7},{7,6},{8,9},{9,8},{10,11... | collective-permute-start | bytes 1179656 | tf_op jit(solution)/shard_map/ppermute | solution.py:596
  74.0 0.8 pred_.1
  74.8 1.1 %collective-permute-done.24.pool3 = bf16[256,384]{1,0:T(8,128)(2,1)S(1)} collective-permute-done((bf16[256,384]{1,0:T(8,128)(2,1)S(1)}, bf16[256,384]{1,0:T(8,128)(2,1)S(1)}, u32[]{:S(2)}, u32[]{:S(2)}) %collective-permute-start.24) | collective-permute-done | bytes 196640 | tf_op jit(solution)/shard_map/ppermute | solution.py:437
  75.9 3.5 %dec_grad.1 = f32[5,192,384]{2,1,0:T(8,128)} custom-call(s32[4]{0:T(128)S(1)} %pad_add_fusion.place, bf16[2,2,272,192]{3,2,1,0:T(8,128)(2,1)S(1)} %pad_maximum_fusion.own, bf16[2,2,272,192]{3,2,1,0:T(8,128)(2,1)S(1)} %collective-permute-done.23.came, bf16[256,384]{1,0:T(8,128)(2,1)S(1)} %get-tuple-element.67.pool0, ...), custom_call_target="tpu_custom_call" | custom-call | tf_op jit(solution)/shard_map/dec_grad/pallas_call | solution.py:404
  79.4 0.2 collective-permute-done.21
  79.7 0.4 collective-permute-start.25
  80.1 1.8 %enc_grad.2.refs_0_ = f32[960,384]{1,0:T(8,128)S(1)} custom-call(s32[4]{0:T(128)S(1)} %pad_add_fusion.place, bf16[960,2048]{1,0:T(8,128)(2,1)S(1)} %stem_taps.1.taps, bf16[2,256,384]{2,1,0:T(8,128)(2,1)S(1)} %pad_maximum_fusion.1.slots, bf16[512,384]{1,0:T(8,128)(2,1)S(1)} %owner_slope.2.slope0, bf16[512,384]{1,0:T(8,128)(2,1)S(1)} %owner_slope.3.slope1), custom_call_target="tpu_custom_call" | custom-call | tf_op jit(solution)/shard_map/enc_grad/pallas_call | solution.py:682
  81.9 3.0 %enc_grad.3 = f32[960,384]{1,0:T(8,128)} custom-call(s32[4]{0:T(128)S(1)} %pad_add_fusion.place, bf16[960,2048]{1,0:T(8,128)(2,1)S(1)} %stem_taps.1.taps, bf16[2,256,384]{2,1,0:T(8,128)(2,1)S(1)} %collective-permute-done.25.slots, bf16[512,384]{1,0:T(8,128)(2,1)S(1)} %collective-permute-done.26.slope0, bf16[512,384]{1,0:T(8,128)(2,1)S(1)} %collective-permute-done.27.slope1, ...), custom_call_target="tpu_custom_call" | custom-call | tf_op jit(solution)/shard_map/enc_grad/pallas_call | solution.py:682
  (47 shorter events, 0.9 us)
Async XLA Ops:
  0.8 4.4 %copy-start = (bf16[768,5,384]{2,0,1:T(8,128)(2,1)S(1)}, bf16[768,5,384]{2,0,1:T(8,128)(2,1)}, u32[]{:S(2)}) copy-start(bf16[768,5,384]{2,0,1:T(8,128)(2,1)} %param.8) | copy-start | bytes 8847364
  1.7 1.8 %copy-start.1 = (bf16[1536,5,192]{0,2,1:T(8,128)(2,1)S(1)}, bf16[1536,5,192]{0,2,1:T(8,128)(2,1)}, u32[]{:S(2)}) copy-start(bf16[1536,5,192]{0,2,1:T(8,128)(2,1)} %param.7) | copy-start | bytes 8847364
  4.7 11.6 %collective-permute-start.2 = (bf16[992,768]{1,0:T(8,128)(2,1)S(1)}, bf16[992,768]{1,0:T(8,128)(2,1)S(1)}, u32[]{:S(2)}, u32[]{:S(2)}) collective-permute-start(bf16[992,768]{1,0:T(8,128)(2,1)S(1)} %get-tuple-element.51), channel_id=1, source_target_pairs={{0,1},{1,0},{2,3},{3,2},{4,5},{5,4},{6,7},{7,6},{8,9},{9,8},{10,11... | collective-permute-start | bytes 4571144 | tf_op jit(solution)/shard_map/ppermute | solution.py:466
  5.2 4.1 %copy-start.4 = (s32[512]{0:T(512)S(1)}, s32[512]{0:T(512)}, u32[]{:S(2)}) copy-start(s32[512]{0:T(512)} %param.5) | copy-start | bytes 6148
  5.2 11.1 %copy-start.2 = (bf16[1536,5,192]{0,2,1:T(8,128)(2,1)S(1)}, bf16[1536,5,192]{0,2,1:T(8,128)(2,1)}, u32[]{:S(2)}) copy-start(bf16[1536,5,192]{0,2,1:T(8,128)(2,1)} %param.7) | copy-start | bytes 8847364
  6.3 21.3 %collective-permute-start.3 = (bf16[5,2,192,384]{3,2,1,0:T(8,128)(2,1)S(1)}, bf16[5,2,192,384]{3,2,1,0:T(8,128)(2,1)S(1)}, u32[]{:S(2)}, u32[]{:S(2)}) collective-permute-start(bf16[5,2,192,384]{3,2,1,0:T(8,128)(2,1)S(1)} %dec_pick.1), channel_id=1, source_target_pairs={{0,1},{1,0},{2,3},{3,2},{4,5},{5,4},{6,7},{7,6},{8,9},{9,8},{10,11... | collective-permute-start | bytes 4423688 | tf_op jit(solution)/shard_map/ppermute | solution.py:480
  6.4 20.6 %collective-permute-start.12 = (bf16[608,384]{1,0:T(8,128)(2,1)S(1)}, bf16[608,384]{1,0:T(8,128)(2,1)S(1)}, u32[]{:S(2)}, u32[]{:S(2)}) collective-permute-start(bf16[608,384]{1,0:T(8,128)(2,1)S(1)} %get-tuple-element.71), channel_id=1, source_target_pairs={{0,2},{1,3},{2,0},{3,1},{4,6},{5,7},{6,4},{7,5},{8,10},{9,11},{10,... | collective-permute-start | bytes 1400840 | tf_op jit(solution)/shard_map/ppermute | solution.py:467
  9.3 4.1 %collective-permute-start = (s32[1,512]{1,0:T(1,128)S(1)}, s32[1,512]{1,0:T(1,128)S(1)}, u32[]{:S(2)}, u32[]{:S(2)}) collective-permute-start(s32[1,512]{1,0:T(1,128)S(1)} %bitcast.42), channel_id=1, source_target_pairs={{0,4},{4,0},{8,12},{12,8},{1,5},{5,1},{9,13},{13,9},{2,6},{6,2},{1... | collective-permute-start | bytes 6152 | tf_op jit(solution)/shard_map/ppermute | solution.py:437
  10.9 5.4 %collective-permute-start.1 = (s32[1,512]{1,0:T(1,128)S(1)}, s32[1,512]{1,0:T(1,128)S(1)}, u32[]{:S(2)}, u32[]{:S(2)}) collective-permute-start(s32[1,512]{1,0:T(1,128)S(1)} %bitcast.43), channel_id=1, source_target_pairs={{0,12},{4,8},{8,4},{12,0},{1,13},{5,9},{9,5},{13,1},{2,14},{6,10},... | collective-permute-start | bytes 6152 | tf_op jit(solution)/shard_map/ppermute | solution.py:447
  18.9 2.0 %copy-start.3 = (bf16[512,192]{0,1:T(8,128)(2,1)S(1)}, bf16[512,192]{0,1:T(8,128)(2,1)}, u32[]{:S(2)}) copy-start(bf16[512,192]{0,1:T(8,128)(2,1)} %param.9) | copy-start | bytes 589828
  20.3 11.7 %collective-permute-start.7 = (bf16[544,384]{1,0:T(8,128)(2,1)S(1)}, bf16[544,384]{1,0:T(8,128)(2,1)S(1)}, u32[]{:S(2)}, u32[]{:S(2)}) collective-permute-start(bf16[544,384]{1,0:T(8,128)(2,1)S(1)} %enc_conv.1), channel_id=1, source_target_pairs={{0,2},{1,3},{2,0},{3,1},{4,6},{5,7},{6,4},{7,5},{8,10},{9,11},{10,... | collective-permute-start | bytes 1253384 | tf_op jit(solution)/shard_map/ppermute | solution.py:505
  20.9 6.1 %collective-permute-start.4 = (bf16[192,128]{1,0:T(8,128)(2,1)S(1)}, bf16[192,128]{1,0:T(8,128)(2,1)S(1)}, u32[]{:S(2)}, u32[]{:S(2)}) collective-permute-start(bf16[192,128]{1,0:T(8,128)(2,1)S(1)} %get-tuple-element.103), channel_id=1, source_target_pairs={{0,4},{4,8},{8,12},{12,0},{1,5},{5,9},{9,13},{13,1},{2,6},{6,10},{... | collective-permute-start | bytes 147464 | tf_op jit(solution)/shard_map/ppermute | solution.py:434
  21.0 6.5 %collective-permute-start.5 = (bf16[192,128]{1,0:T(8,128)(2,1)S(1)}, bf16[192,128]{1,0:T(8,128)(2,1)S(1)}, u32[]{:S(2)}, u32[]{:S(2)}) collective-permute-start(bf16[192,128]{1,0:T(8,128)(2,1)S(1)} %get-tuple-element.102), channel_id=1, source_target_pairs={{0,12},{4,0},{8,4},{12,8},{1,13},{5,1},{9,5},{13,9},{2,14},{6,2},{... | collective-permute-start | bytes 147464 | tf_op jit(solution)/shard_map/ppermute | solution.py:434
  27.0 14.5 %collective-permute-start.11 = (bf16[992,384]{1,0:T(8,128)(2,1)S(1)}, bf16[992,384]{1,0:T(8,128)(2,1)S(1)}, u32[]{:S(2)}, u32[]{:S(2)}) collective-permute-start(bf16[992,384]{1,0:T(8,128)(2,1)S(1)} %get-tuple-element.70.refs_4_), channel_id=1, source_target_pairs={{0,1},{1,0},{2,3},{3,2},{4,5},{5,4},{6,7},{7,6},{8,9},{9,8},{10,11... | collective-permute-start | bytes 2285576 | tf_op jit(solution)/shard_map/ppermute | solution.py:579
  27.1 12.2 %collective-permute-start.14 = (bf16[608,384]{1,0:T(8,128)(2,1)S(1)}, bf16[608,384]{1,0:T(8,128)(2,1)S(1)}, u32[]{:S(2)}, u32[]{:S(2)}) collective-permute-start(bf16[608,384]{1,0:T(8,128)(2,1)S(1)} %collective-permute-done.12.refs_6_), channel_id=1, source_target_pairs={{0,1},{1,0},{2,3},{3,2},{4,5},{5,4},{6,7},{7,6},{8,9},{9,8},{10,11... | collective-permute-start | bytes 1400840 | tf_op jit(solution)/shard_map/ppermute | solution.py:580
  27.6 4.5 %collective-permute-start.6 = (s32[2,256]{1,0:T(2,128)S(1)}, s32[2,256]{1,0:T(2,128)S(1)}, u32[]{:S(2)}, u32[]{:S(2)}) collective-permute-start(s32[2,256]{1,0:T(2,128)S(1)} %get-tuple-element.106.refs_0_), channel_id=1, source_target_pairs={{0,8},{4,12},{8,0},{12,4},{1,9},{5,13},{9,1},{13,5},{2,10},{6,14},... | collective-permute-start | bytes 6152 | tf_op jit(solution)/shard_map/ppermute | solution.py:434
  27.6 9.1 %collective-permute-start.13 = (bf16[384,384]{1,0:T(8,128)(2,1)S(1)}, bf16[384,384]{1,0:T(8,128)(2,1)S(1)}, u32[]{:S(2)}, u32[]{:S(2)}) collective-permute-start(bf16[384,384]{1,0:T(8,128)(2,1)S(1)} %get-tuple-element.73), channel_id=1, source_target_pairs={{0,2},{1,3},{2,0},{3,1},{4,6},{5,7},{6,4},{7,5},{8,10},{9,11},{10,... | collective-permute-start | bytes 884744 | tf_op jit(solution)/shard_map/ppermute | solution.py:536
  33.0 1.5 %collective-permute-start.8 = (bf16[272,384]{1,0:T(8,128)(2,1)S(1)}, bf16[272,384]{1,0:T(8,128)(2,1)S(1)}, u32[]{:S(2)}, u32[]{:S(2)}) collective-permute-start(bf16[272,384]{1,0:T(8,128)(2,1)S(1)} %get-tuple-element.65.own), channel_id=1, source_target_pairs={{0,1},{1,0},{2,3},{3,2},{4,5},{5,4},{6,7},{7,6},{8,9},{9,8},{10,11... | collective-permute-start | bytes 626696 | tf_op jit(solution)/shard_map/ppermute | solution.py:558
  36.6 13.0 %collective-permute-start.16 = (bf16[272,768]{1,0:T(8,128)(2,1)S(1)}, bf16[272,768]{1,0:T(8,128)(2,1)S(1)}, u32[]{:S(2)}, u32[]{:S(2)}) collective-permute-start(bf16[272,768]{1,0:T(8,128)(2,1)S(1)} %get-tuple-element.77), channel_id=1, source_target_pairs={{0,2},{1,3},{2,0},{3,1},{4,6},{5,7},{6,4},{7,5},{8,10},{9,11},{10,... | collective-permute-start | bytes 1253384 | tf_op jit(solution)/shard_map/ppermute | solution.py:574
  38.1 3.3 %collective-permute-start.15 = (bf16[384,384]{1,0:T(8,128)(2,1)S(1)}, bf16[384,384]{1,0:T(8,128)(2,1)S(1)}, u32[]{:S(2)}, u32[]{:S(2)}) collective-permute-start(bf16[384,384]{1,0:T(8,128)(2,1)S(1)} %collective-permute-done.13.refs_7_), channel_id=1, source_target_pairs={{0,1},{1,0},{2,3},{3,2},{4,5},{5,4},{6,7},{7,6},{8,9},{9,8},{10,11... | collective-permute-start | bytes 884744 | tf_op jit(solution)/shard_map/ppermute | solution.py:580
  38.1 11.5 %collective-permute-start.10 = (bf16[256,384]{1,0:T(8,128)(2,1)S(1)}, bf16[256,384]{1,0:T(8,128)(2,1)S(1)}, u32[]{:S(2)}, u32[]{:S(2)}) collective-permute-start(bf16[256,384]{1,0:T(8,128)(2,1)S(1)} %get-tuple-element.67.pool0), channel_id=1, source_target_pairs={{0,4},{4,0},{8,12},{12,8},{1,5},{5,1},{9,13},{13,9},{2,6},{6,2},{1... | collective-permute-start | bytes 589832 | tf_op jit(solution)/shard_map/ppermute | solution.py:437
  39.3 10.4 %collective-permute-start.9 = (bf16[256,384]{1,0:T(8,128)(2,1)S(1)}, bf16[256,384]{1,0:T(8,128)(2,1)S(1)}, u32[]{:S(2)}, u32[]{:S(2)}) collective-permute-start(bf16[256,384]{1,0:T(8,128)(2,1)S(1)} %get-tuple-element.67.pool0), channel_id=1, source_target_pairs={{0,8},{4,12},{8,0},{12,4},{1,9},{5,13},{9,1},{13,5},{2,10},{6,14},... | collective-permute-start | bytes 589832 | tf_op jit(solution)/shard_map/ppermute | solution.py:437
  50.8 3.2 %collective-permute-start.17 = (bf16[2,272,384]{2,1,0:T(8,128)(2,1)S(1)}, bf16[2,272,384]{2,1,0:T(8,128)(2,1)S(1)}, u32[]{:S(2)}, u32[]{:S(2)}) collective-permute-start(bf16[2,272,384]{2,1,0:T(8,128)(2,1)S(1)} %get-tuple-element.81.own), channel_id=1, source_target_pairs={{0,1},{1,0},{2,3},{3,2},{4,5},{5,4},{6,7},{7,6},{8,9},{9,8},{10,11... | collective-permute-start | bytes 1253384 | tf_op jit(solution)/shard_map/ppermute | solution.py:615
  50.9 14.8 %collective-permute-start.19 = (bf16[2,272,192]{2,1,0:T(8,128)(2,1)S(1)}, bf16[2,272,192]{2,1,0:T(8,128)(2,1)S(1)}, u32[]{:S(2)}, u32[]{:S(2)}) collective-permute-start(bf16[2,272,192]{2,1,0:T(8,128)(2,1)S(1)} %get-tuple-element.82), channel_id=1, source_target_pairs={{1,4},{3,6},{0,8},{2,10},{4,9},{6,11},{5,13},{7,15},{9,12},{11,14}... | collective-permute-start | bytes 626696 | tf_op jit(solution)/shard_map/ppermute | solution.py:635
  53.1 12.5 %collective-permute-start.20 = (bf16[2,272,192]{2,1,0:T(8,128)(2,1)S(1)}, bf16[2,272,192]{2,1,0:T(8,128)(2,1)S(1)}, u32[]{:S(2)}, u32[]{:S(2)}) collective-permute-start(bf16[2,272,192]{2,1,0:T(8,128)(2,1)S(1)} %get-tuple-element.83), channel_id=1, source_target_pairs={{1,12},{3,14},{4,1},{6,3},{9,4},{11,6},{12,9},{14,11},{17,28},{19,... | collective-permute-start | bytes 626696 | tf_op jit(solution)/shard_map/ppermute | solution.py:636
  55.7 10.1 %collective-permute-start.18 = (bf16[256,384]{1,0:T(8,128)(2,1)S(1)}, bf16[256,384]{1,0:T(8,128)(2,1)S(1)}, u32[]{:S(2)}, u32[]{:S(2)}) collective-permute-start(bf16[256,384]{1,0:T(8,128)(2,1)S(1)} %up_grad.1), channel_id=1, source_target_pairs={{0,2},{1,3},{2,0},{3,1},{4,6},{5,7},{6,4},{7,5},{8,10},{9,11},{10,... | collective-permute-start | bytes 589832 | tf_op jit(solution)/shard_map/ppermute | solution.py:643
  65.9 10.0 %collective-permute-start.23 = (bf16[2,2,272,192]{3,2,1,0:T(8,128)(2,1)S(1)}, bf16[2,2,272,192]{3,2,1,0:T(8,128)(2,1)S(1)}, u32[]{:S(2)}, u32[]{:S(2)}) collective-permute-start(bf16[2,2,272,192]{3,2,1,0:T(8,128)(2,1)S(1)} %pad_maximum_fusion.own), channel_id=1, source_target_pairs={{0,1},{1,0},{2,3},{3,2},{4,5},{5,4},{6,7},{7,6},{8,9},{9,8},{10,11... | collective-permute-start | bytes 1253384 | tf_op jit(solution)/shard_map/ppermute | solution.py:652
  66.0 9.9 %collective-permute-start.24 = (bf16[256,384]{1,0:T(8,128)(2,1)S(1)}, bf16[256,384]{1,0:T(8,128)(2,1)S(1)}, u32[]{:S(2)}, u32[]{:S(2)}) collective-permute-start(bf16[256,384]{1,0:T(8,128)(2,1)S(1)} %collective-permute-done.9.pool2), channel_id=1, source_target_pairs={{0,4},{4,0},{8,12},{12,8},{1,5},{5,1},{9,13},{13,9},{2,6},{6,2},{1... | collective-permute-start | bytes 589832 | tf_op jit(solution)/shard_map/ppermute | solution.py:437
  68.3 11.3 %collective-permute-start.21 = (bf16[256,384]{1,0:T(8,128)(2,1)S(1)}, bf16[256,384]{1,0:T(8,128)(2,1)S(1)}, u32[]{:S(2)}, u32[]{:S(2)}) collective-permute-start(bf16[256,384]{1,0:T(8,128)(2,1)S(1)} %get-tuple-element.97), channel_id=1, source_target_pairs={{1,4},{3,6},{0,8},{2,10},{4,9},{6,11},{5,13},{7,15},{9,12},{11,14}... | collective-permute-start | bytes 589832 | tf_op jit(solution)/shard_map/ppermute | solution.py:635
  70.2 9.3 %collective-permute-start.22 = (bf16[256,384]{1,0:T(8,128)(2,1)S(1)}, bf16[256,384]{1,0:T(8,128)(2,1)S(1)}, u32[]{:S(2)}, u32[]{:S(2)}) collective-permute-start(bf16[256,384]{1,0:T(8,128)(2,1)S(1)} %get-tuple-element.96), channel_id=1, source_target_pairs={{1,12},{3,14},{4,1},{6,3},{9,4},{11,6},{12,9},{14,11},{17,28},{19,... | collective-permute-start | bytes 589832 | tf_op jit(solution)/shard_map/ppermute | solution.py:636
  70.9 11.0 %collective-permute-start.26 = (bf16[512,384]{1,0:T(8,128)(2,1)S(1)}, bf16[512,384]{1,0:T(8,128)(2,1)S(1)}, u32[]{:S(2)}, u32[]{:S(2)}) collective-permute-start(bf16[512,384]{1,0:T(8,128)(2,1)S(1)} %owner_slope.2.slope0), channel_id=1, source_target_pairs={{0,1},{1,0},{2,3},{3,2},{4,5},{5,4},{6,7},{7,6},{8,9},{9,8},{10,11... | collective-permute-start | bytes 1179656 | tf_op jit(solution)/shard_map/ppermute | solution.py:596
  75.9 6.0 %collective-permute-start.27 = (bf16[512,384]{1,0:T(8,128)(2,1)S(1)}, bf16[512,384]{1,0:T(8,128)(2,1)S(1)}, u32[]{:S(2)}, u32[]{:S(2)}) collective-permute-start(bf16[512,384]{1,0:T(8,128)(2,1)S(1)} %owner_slope.3.slope1), channel_id=1, source_target_pairs={{0,1},{1,0},{2,3},{3,2},{4,5},{5,4},{6,7},{7,6},{8,9},{9,8},{10,11... | collective-permute-start | bytes 1179656 | tf_op jit(solution)/shard_map/ppermute | solution.py:596
  79.7 2.3 %collective-permute-start.25 = (bf16[2,256,384]{2,1,0:T(8,128)(2,1)S(1)}, bf16[2,256,384]{2,1,0:T(8,128)(2,1)S(1)}, u32[]{:S(2)}, u32[]{:S(2)}) collective-permute-start(bf16[2,256,384]{2,1,0:T(8,128)(2,1)S(1)} %pad_maximum_fusion.1.slots), channel_id=1, source_target_pairs={{0,1},{1,0},{2,3},{3,2},{4,5},{5,4},{6,7},{7,6},{8,9},{9,8},{10,11... | collective-permute-start | bytes 1179656 | tf_op jit(solution)/shard_map/ppermute | solution.py:677
